TPU v7x, 256 devices: a whole 4x4x8 slice. The times are simulated.
256 devices in a mesh: dp: 32 (over z_hi, y, core), shard: 8 (over z_lo, x).
Axes of the slice: x: 4, y: 4, z: 8 (z_hi: 4, z_lo: 2; z = z_hi * 2 + z_lo), core: 2. Of those that a mesh axis runs over, the one named last changes fastest.
Arguments:
- inputs: bfloat16 [16384, 8192], P('dp', 'shard'), may hold values from -6 to 6
- key_grads: bfloat16 [16384, 1024], P('dp'), may hold values from -6 to 6
- error: bfloat16 [32, 8192, 1024], P('dp', 'shard'), may hold values from -6 to 6
- momentum: bfloat16 [8192, 1024], P('shard'), may hold values from -0.59765625 to 0.59765625
- q_start: float32 [1024, 64], replicated, may hold values from -6 to 6
Outputs:
- new_error: bfloat16 [32, 8192, 1024], P('dp', 'shard')
- new_momentum: bfloat16 [8192, 1024], P('shard')
- q_factor: float32 [1024, 64], replicated
All inputs are finite; a program needn't handle non-finite values.
Results may differ from a plain program's by a relative error of at most 0.001.
Values sent between devices are 32-bit elements; how exact they have to be, the bound alone decides.
No kernel may reach another device: no remote copies, remote signals or barrier semaphores. Data moves between devices by JAX's collectives and lax.ppermute only.
A program may use at most 64 MiB of HBM per device.

v0:
```python
import math

import jax
import jax.numpy as jnp
from jax import lax
from jax.sharding import PartitionSpec as P

ITERS = 3


HIGH = lax.Precision.HIGHEST


def orthonormal(p_left, gram):
    lower = jnp.linalg.cholesky(gram)
    return lax.linalg.triangular_solve(lower, p_left, left_side=False, lower=True, transpose_a=True)


def left_factor(p_left):
    total = lax.psum(p_left, "dp")
    gram = lax.psum(jnp.dot(total.T, total, precision=HIGH), "shard")
    return orthonormal(total, gram)


def shards(inputs, key_grads, error, momentum, q_start):
    replicas = lax.axis_size("dp")
    factor = 1.0 / math.sqrt(inputs.shape[0])
    err_rows = error[0].astype(jnp.float32)
    contract = (((0,), (0,)), ((), ()))
    merged = (
        lax.dot_general(inputs, key_grads, contract, preferred_element_type=jnp.float32) * factor
        + err_rows
    )
    first_p = jnp.dot(merged, q_start, precision=HIGH)
    q_now = q_start
    p_hat = first_p
    for turn in range(ITERS):
        if turn == 0:
            p_left = first_p
        else:
            p_left = jnp.dot(merged, q_now, precision=HIGH)
        p_hat = left_factor(p_left)
        q_part = lax.dot_general(merged, p_hat, contract, precision=HIGH)
        q_now = lax.psum(q_part, ("dp", "shard")) / replicas
    approx = jnp.dot(p_hat, q_now.T, precision=HIGH)
    new_error = (merged - approx).astype(jnp.bfloat16)[None]
    new_momentum = (0.9 * momentum.astype(jnp.float32) + approx).astype(jnp.bfloat16)
    return (new_error, new_momentum, q_now)


def solution(mesh):
    return jax.shard_map(
        shards,
        mesh=mesh,
        in_specs=(P("dp", "shard"), P("dp", None), P("dp", "shard", None), P("shard", None), P()),
        out_specs=(P("dp", "shard", None), P("shard", None), P()),
        check_vma=False,
    )
```

profile of v0, /device:TPU:1, one launch (start us, length us, event | category | flops | bytes accessed | tf_op | source)
XLA Modules:
  0.0 1796.1 jit_solution(8203384575144374079)
XLA Ops:
  7.2 1.2 copy-done
  8.4 3.2 convert_add_fusion
  11.6 1.9 copy-done.1
  13.6 4.9 fusion.22
  18.5 286.6 %all-reduce.7.cloned.1.call-done = f32[1024,64]{0,1:T(8,128)} async-done(((f32[1024,64]{0,1:T(8,128)}), f32[1024,64]{0,1:T(8,128)}) %all-reduce.7.cloned.1.call-update) | async-done | bytes 262160 | tf_op jit(solution)/shard_map/psum | solution.py:20
  305.1 1.4 fusion.23
  306.5 26.2 %psum.64 = f32[64,64]{0,1:T(8,128)S(1)} all-reduce(f32[64,64]{0,1:T(8,128)S(1)} %fusion.23), channel_id=1, replica_groups=mesh['dp'=32,'shard'=8] {'shard'}, use_global_device_ids=true, to_apply=%region_1.0 | all-reduce | flops 4096 | bytes 32768 | tf_op jit(solution)/shard_map/psum | solution.py:21
  332.9 5.8 cholesky.59
  340.1 4.9 custom-call.7
  345.0 1.4 convolution_bitcast_fusion.2
  346.4 5.6 fusion.24
  352.3 251.4 %all-reduce.9.cloned.1.call-done = f32[1024,64]{0,1:T(8,128)} async-done(((f32[1024,64]{0,1:T(8,128)}), f32[1024,64]{0,1:T(8,128)}) %all-reduce.9.cloned.1.call-update) | async-done | bytes 262160 | tf_op jit(solution)/shard_map/psum | solution.py:44
  603.6 7.1 fusion.3
  610.8 283.1 %all-reduce.11.cloned.1.call-done = f32[1024,64]{0,1:T(8,128)} async-done(((f32[1024,64]{0,1:T(8,128)}), f32[1024,64]{0,1:T(8,128)}) %all-reduce.11.cloned.1.call-update) | async-done | bytes 262160 | tf_op jit(solution)/shard_map/psum | solution.py:20
  893.9 1.4 fusion.25
  895.3 26.2 %psum.67 = f32[64,64]{0,1:T(8,128)S(1)} all-reduce(f32[64,64]{0,1:T(8,128)S(1)} %fusion.25), channel_id=1, replica_groups=mesh['dp'=32,'shard'=8] {'shard'}, use_global_device_ids=true, to_apply=%region_6.9 | all-reduce | flops 4096 | bytes 32768 | tf_op jit(solution)/shard_map/psum | solution.py:21
  921.6 5.8 cholesky.70
  928.8 4.9 custom-call.8
  933.7 1.4 convolution_bitcast_fusion.1
  935.1 5.6 fusion.26
  940.8 251.5 %all-reduce.13.cloned.1.call-done = f32[1024,64]{0,1:T(8,128)} async-done(((f32[1024,64]{0,1:T(8,128)}), f32[1024,64]{0,1:T(8,128)}) %all-reduce.13.cloned.1.call-update) | async-done | bytes 262160 | tf_op jit(solution)/shard_map/psum | solution.py:44
  1192.3 7.1 fusion.1
  1199.5 283.2 %all-reduce.15.cloned.1.call-done = f32[1024,64]{0,1:T(8,128)} async-done(((f32[1024,64]{0,1:T(8,128)}), f32[1024,64]{0,1:T(8,128)}) %all-reduce.15.cloned.1.call-update) | async-done | bytes 262160 | tf_op jit(solution)/shard_map/psum | solution.py:20
  1482.7 1.4 fusion.27
  1484.0 26.3 %psum.70 = f32[64,64]{0,1:T(8,128)S(1)} all-reduce(f32[64,64]{0,1:T(8,128)S(1)} %fusion.27), channel_id=1, replica_groups=mesh['dp'=32,'shard'=8] {'shard'}, use_global_device_ids=true, to_apply=%region_9.12 | all-reduce | flops 4096 | bytes 32768 | tf_op jit(solution)/shard_map/psum | solution.py:21
  1510.4 5.8 cholesky.81
  1517.6 4.9 custom-call.9
  1522.5 1.4 convolution_bitcast_fusion
  1523.9 5.6 fusion.28
  1529.6 251.6 %all-reduce.17.cloned.1.call-done = f32[1024,64]{0,1:T(8,128)} async-done(((f32[1024,64]{0,1:T(8,128)}), f32[1024,64]{0,1:T(8,128)}) %all-reduce.17.cloned.1.call-update) | async-done | bytes 262160 | tf_op jit(solution)/shard_map/psum | solution.py:44
  1781.1 1.0 broadcast_multiply_fusion
  1782.1 7.1 add_convert_fusion
  (35 shorter events, 4.8 us)
Async XLA Ops:
  7.2 1.2 copy-start
  7.2 6.4 copy-start.4
  7.2 298.0 %all-reduce.7.cloned.1.call-start = ((), (), s32[]{:S(2)}) async-start(), calls=%async_computation | async-start | bytes 524288 | tf_op jit(solution)/shard_map/psum | solution.py:20
  11.6 1.9 copy-start.1
  18.5 585.2 %all-reduce.9.cloned.1.call-start = ((), (), s32[]{:S(2)}) async-start(), calls=%async_computation.1 | async-start | bytes 524288 | tf_op jit(solution)/shard_map/psum | solution.py:44
  352.0 541.8 %all-reduce.11.cloned.1.call-start = ((), (), s32[]{:S(2)}) async-start(), calls=%async_computation.2 | async-start | bytes 524288 | tf_op jit(solution)/shard_map/psum | solution.py:20
  610.7 581.6 %all-reduce.13.cloned.1.call-start = ((), (), s32[]{:S(2)}) async-start(), calls=%async_computation.3 | async-start | bytes 524288 | tf_op jit(solution)/shard_map/psum | solution.py:44
  940.7 541.9 %all-reduce.15.cloned.1.call-start = ((), (), s32[]{:S(2)}) async-start(), calls=%async_computation.4 | async-start | bytes 524288 | tf_op jit(solution)/shard_map/psum | solution.py:20
  1199.4 582.7 %copy-start.2 = (bf16[1024,1024]{1,0:T(8,128)(2,1)S(1)}, bf16[1024,1024]{1,0:T(8,128)(2,1)}, u32[]{:S(2)}) copy-start(bf16[1024,1024]{1,0:T(8,128)(2,1)} %param.11) | copy-start | bytes 6291460
  1199.4 581.7 %all-reduce.17.cloned.1.call-start = ((), (), s32[]{:S(2)}) async-start(), calls=%async_computation.5 | async-start | bytes 524288 | tf_op jit(solution)/shard_map/psum | solution.py:44
  1782.1 7.1 copy-start.3
Sparse Core Ops, SparseCore 0:
  18.6 286.4 all-reduce.6
  352.1 251.4 all-reduce.8
  610.9 282.9 all-reduce.10
  940.9 251.4 all-reduce.12
  1199.5 283.0 all-reduce.14
  1529.7 251.4 all-reduce.16
where the time goes:
time: 1800 us
  waiting for transfers between devices  1610 us (89%)
  blocking collectives  78.8 us (4%)
  matrix products  54.6 us (3%)
  other arithmetic  37.2 us (2%)
    psum x3, waiting for transfers between devices, left_factor(): total = lax.psum(p_left, 'dp')  853 us
    psum x3, waiting for transfers between devices, shards(): q_now = lax.psum(q_part, ('dp', 'shard')) / replicas  755 us
    psum x3, blocking collectives, left_factor(): gram = lax.psum(jnp.dot(total.T, total, precision=HIGH), 'shard')  78.8 us
  transfers between devices with their start and end apart: 6, of which 6 were waited for; matrix products, arithmetic and copies ran while one was open for 0% of the time, Pallas kernels for 0%

commit v1 on v0

v1 whole, which is shorter than its diff:
```python
import math

import jax
import jax.numpy as jnp
from jax import lax
from jax.experimental import pallas as pl
from jax.experimental.pallas import tpu as pltpu
from jax.sharding import PartitionSpec as P

ITERS = 3
HIGH = lax.Precision.HIGHEST
ROWS = (((0,), (0,)), ((), ()))
LANES = (((1,), (1,)), ((), ()))
F32 = jnp.float32
BF16 = jnp.bfloat16
VMEM = pl.BlockSpec(memory_space=pltpu.VMEM)
SMEM = pl.BlockSpec(memory_space=pltpu.SMEM)

Y_GROUPS = [[z * 8 + y * 2 + c for y in range(4)] for z in range(4) for c in range(2)]
Z_GROUPS = [[z * 8 + y * 2 + c for z in range(4)] for y in range(4) for c in range(2)]
ZY_GROUPS = [[z * 8 + y * 2 + c for z in range(4) for y in range(4)] for c in range(2)]


def dp_shift(x, dy, dc):
    pairs = []
    for i in range(32):
        z, y, c = i // 8, (i // 2) % 4, i % 2
        pairs.append((i, z * 8 + (y + dy) % 4 * 2 + (c + dc) % 2))
    return lax.ppermute(x, "dp", pairs)


def exchange(x, groups, axis="dp"):
    return lax.all_to_all(x, axis, 0, 0, axis_index_groups=groups)


def gather(x, n, groups, axis="dp"):
    return exchange(jnp.broadcast_to(x[None], (n,) + x.shape), groups, axis)


def params(mib, **more):
    return pltpu.CompilerParams(vmem_limit_bytes=mib << 20, **more)


def cost(flops, read):
    return pl.CostEstimate(flops=flops, bytes_accessed=read, transcendentals=0)


def split2(x):
    hi = x.astype(BF16)
    return hi, (x - hi.astype(F32)).astype(BF16)


def split3(x):
    hi = x.astype(BF16)
    rest = x - hi.astype(F32)
    mid = rest.astype(BF16)
    return hi, mid, (rest - mid.astype(F32)).astype(BF16)


def merge_kernel(half_ref, acts_ref, grads_ref, err_ref, out_ref):
    factor = 1.0 / math.sqrt(acts_ref.shape[0])
    product = lax.dot_general(acts_ref[...], grads_ref[...], ROWS, preferred_element_type=F32)
    out_ref[0] = product * factor + err_ref[0].astype(F32)


def merge(half, inputs, key_grads, error):
    tok, d = inputs.shape
    k = key_grads.shape[1]
    return pl.pallas_call(
        merge_kernel,
        out_shape=jax.ShapeDtypeStruct((4, d // 2, k // 4), F32),
        grid_spec=pltpu.PrefetchScalarGridSpec(
            num_scalar_prefetch=1,
            grid=(4,),
            in_specs=[
                pl.BlockSpec((tok, d // 2), lambda i, half: (0, half[0])),
                pl.BlockSpec((tok, k // 4), lambda i, half: (0, i)),
                pl.BlockSpec((1, d // 2, k // 4), lambda i, half: (0, half[0], i)),
            ],
            out_specs=pl.BlockSpec((1, d // 2, k // 4), lambda i, half: (i, 0, 0)),
        ),
        compiler_params=params(56),
        cost_estimate=cost(tok * d * k, 5 << 20),
        name="merge",
    )(half.reshape(1), inputs, key_grads, error)


def sum_turn_kernel(x_ref, out_ref):
    out_ref[...] = (x_ref[0] + x_ref[1] + x_ref[2] + x_ref[3]).T


def sum_turn(x):
    _, d, k = x.shape
    return pl.pallas_call(
        sum_turn_kernel,
        out_shape=jax.ShapeDtypeStruct((k, d), F32),
        grid=(d // 128,),
        in_specs=[pl.BlockSpec((4, 128, k), lambda i: (0, i, 0))],
        out_specs=pl.BlockSpec((k, 128), lambda i: (0, i)),
        compiler_params=params(24),
        cost_estimate=cost(4 * d * k, 20 * d * k),
        name="sum_turn",
    )(x)


def block_kernel(pos_ref, u0, u1, u2, of_y, sent_ref, mine_ref):
    core = pos_ref[0]
    rows = jnp.concatenate([u0[...], u1[...], u2[...]], axis=0)
    block = lax.dot_general(rows, of_y[...], LANES, precision=HIGH, preferred_element_type=F32)

    def put(ref, part):
        for e in range(3):
            for s in range(8):
                ref[s, e] = part[64 * e + 8 * s:64 * e + 8 * s + 8]

    @pl.when(core == 0)
    def _():
        put(mine_ref, block[:, :128])
        put(sent_ref, block[:, 128:])

    @pl.when(core == 1)
    def _():
        put(mine_ref, block[:, 128:])
        put(sent_ref, block[:, :128])


def g_block(pos, units, of_y):
    k, d = of_y.shape
    return pl.pallas_call(
        block_kernel,
        out_shape=(jax.ShapeDtypeStruct((8, 3, 8, 128), F32),) * 2,
        in_specs=[SMEM] + [VMEM] * 4,
        out_specs=(VMEM, VMEM),
        compiler_params=params(24),
        cost_estimate=cost(2 * 6 * 192 * k * d, 2 << 20),
        name="g_block",
    )(pos, *units, of_y)


def inverse_factor(gram):
    n = gram.shape[0]
    tiles = n // 8
    gram = 0.5 * (gram + gram.T)
    row = lax.broadcasted_iota(jnp.int32, (n, n), 0)
    col = lax.broadcasted_iota(jnp.int32, (n, n), 1)
    both = jnp.concatenate([gram, jnp.where(row == col, 1.0, 0.0)], axis=1)
    b = [both[8 * r:8 * r + 8] for r in range(tiles)]
    sub = lax.broadcasted_iota(jnp.int32, (8, 2 * n), 0)
    out = []
    for t in range(tiles):
        c = {
            (r, k): jnp.broadcast_to(b[r][:, 8 * t + k:8 * t + k + 1], (8, 2 * n))
            for r in range(t, tiles)
            for k in range(8)
        }
        pivots = jnp.ones((8, 2 * n), F32)
        for k in range(8):
            pivot = jnp.broadcast_to(c[t, k][k:k + 1], (8, 2 * n))
            pivots = jnp.where(sub == k, pivot, pivots)
            turn = 1.0 / pivot
            lead = jnp.broadcast_to(b[t][k:k + 1], (8, 2 * n))
            heads = {l: jnp.broadcast_to(c[t, l][k:k + 1], (8, 2 * n)) for l in range(k + 1, 8)}
            for r in range(t, tiles):
                m = c[r, k] * turn
                if r == t:
                    m = jnp.where(sub > k, m, 0.0)
                b[r] = b[r] - m * lead
                for l in range(k + 1, 8):
                    c[r, l] = c[r, l] - m * heads[l]
        out.append(b[t] / jnp.sqrt(pivots))
    return jnp.concatenate(out, axis=0)[:, n:]


def iterate_kernel(pos_ref, own_ref, away_ref, q_ref, q_out, w_out, hi_ref, mid_ref, low_ref):
    s = pl.program_id(0)
    parts = (hi_ref, mid_ref, low_ref)
    for ref, core in ((own_ref, pos_ref[0]), (away_ref, 1 - pos_ref[0])):
        for z in range(4):
            for y in range(4):
                to = pl.ds(pl.multiple_of(y * 256 + core * 128, 128), 128)
                for e in range(3):
                    start = (y - e) % 4 * 256 + z * 64 + s * 16
                    at = pl.ds(pl.multiple_of(start, 16), 16)
                    both = jnp.concatenate([ref[0, z * 4 + y, e], ref[1, z * 4 + y, e]], axis=0)
                    for part, value in zip(parts, split3(both)):
                        part[at, to] = value

    @pl.when(s == pl.num_programs(0) - 1)
    def _():
        for y in range(4):
            here, after = pl.ds(y * 256, 256), pl.ds((y + 1) % 4 * 256, 256)
            for part in parts:
                part[after, here] = part[here, after].T
        q = q_ref[...]
        n = q.shape[0]
        for turn in range(ITERS):
            hi, mid, low = split3(q)
            by_hi = jnp.dot(jnp.concatenate([hi, mid, low], axis=0), hi_ref[...], preferred_element_type=F32)
            by_mid = jnp.dot(jnp.concatenate([hi, mid], axis=0), mid_ref[...], preferred_element_type=F32)
            by_low = jnp.dot(hi, low_ref[...], preferred_element_type=F32)
            small = by_hi[2 * n:] + by_mid[n:] + by_low
            u = by_hi[:n] + (by_hi[n:2 * n] + by_mid[:n] + small)
            gram = lax.dot_general(q, u, LANES, precision=HIGH, preferred_element_type=F32)
            inv = inverse_factor(gram)
            if turn == ITERS - 1:
                w_out[...] = jnp.dot(inv, q, precision=HIGH, preferred_element_type=F32)
            q = jnp.dot(inv, u, precision=HIGH, preferred_element_type=F32) * (1.0 / 32)
        q_out[...] = q


def iterate(pos, own, away, q):
    n, k = q.shape
    part = pl.BlockSpec((2,) + own.shape[1:], lambda s: (s, 0, 0, 0, 0))
    whole = pl.BlockSpec((n, k), lambda s: (0, 0))
    return pl.pallas_call(
        iterate_kernel,
        out_shape=(jax.ShapeDtypeStruct(q.shape, F32),) * 2,
        grid=(own.shape[0] // 2,),
        in_specs=[SMEM, part, part, whole],
        out_specs=(whole, whole),
        scratch_shapes=[pltpu.VMEM((k, k), BF16)] * 3,
        compiler_params=params(40),
        cost_estimate=cost(36 * n * k * k, 4 * k * k),
        name="iterations",
    )(pos, own, away, q)


def left_kernel(pos_ref, w_ref, m0, m1, m2, m3, out_ref):
    total = None
    n = w_ref.shape[0]
    for turn, ref in enumerate((m0, m1, m2, m3)):
        at = pl.multiple_of(((pos_ref[1] + 4 - turn) % 4) * 256, 256)
        whi, wlow = split2(w_ref[:, pl.ds(at, 256)])
        mhi, mlow = split2(ref[...])
        both = jnp.dot(jnp.concatenate([whi, wlow], axis=0), mhi, preferred_element_type=F32)
        part = both[:n] + (both[n:] + jnp.dot(whi, mlow, preferred_element_type=F32))
        total = part if total is None else total + part
    out_ref[...] = total


def left(pos, w, blocks):
    n, d = w.shape[0], blocks[0].shape[1]
    return pl.pallas_call(
        left_kernel,
        out_shape=jax.ShapeDtypeStruct((n, d), F32),
        in_specs=[SMEM] + [VMEM] * 5,
        out_specs=VMEM,
        compiler_params=params(24),
        cost_estimate=cost(6 * n * d * 1024, 2 << 20),
        name="left",
    )(pos, w, *blocks)


def finish_kernel(pos_ref, mine, other, mom, own, away, q, err_out, mom_out, q_parts):
    i = pl.program_id(0)

    @pl.when(i == 0)
    def _():
        hi, low = split2(q[...])
        q_parts[...] = jnp.concatenate([hi, hi, low, low], axis=0)

    def step(merged, p_t):
        hi, low = split2(p_t[...])
        p_parts = jnp.concatenate([hi, low, hi, low], axis=0)
        for n in range(4):
            cols = pl.ds(256 * n, 256)
            approx = lax.dot_general(p_parts, q_parts[:, cols], ROWS, preferred_element_type=F32)
            err_out[0, :, cols] = (merged[n] - approx).astype(BF16)
            mom_out[:, cols] = (0.9 * mom[:, cols].astype(F32) + approx).astype(BF16)

    first = i < pl.num_programs(0) // 2

    @pl.when(first)
    def _():
        step(mine, own)

    @pl.when(jnp.logical_not(first))
    def _():
        step(other, away)


def finish(pos, mine, other, error, momentum, own, away, q):
    n, k = q.shape
    d = momentum.shape[0]
    rows = 256
    half = d // rows // 2

    def row(i, pos):
        return jnp.where(i < half, pos[0], 1 - pos[0]) * half + i % half

    def early(i):
        return jnp.minimum(i, half - 1)

    def late(i):
        return jnp.maximum(i - half, 0)

    return pl.pallas_call(
        finish_kernel,
        out_shape=(jax.ShapeDtypeStruct(error.shape, BF16), jax.ShapeDtypeStruct(momentum.shape, BF16)),
        grid_spec=pltpu.PrefetchScalarGridSpec(
            num_scalar_prefetch=1,
            grid=(d // rows,),
            in_specs=[
                pl.BlockSpec((4, rows, k // 4), lambda i, pos: (0, early(i), 0)),
                pl.BlockSpec((4, rows, k // 4), lambda i, pos: (0, late(i), 0)),
                pl.BlockSpec((rows, k), lambda i, pos: (row(i, pos), 0)),
                pl.BlockSpec((n, rows), lambda i, pos: (0, early(i))),
                pl.BlockSpec((n, rows), lambda i, pos: (0, late(i))),
                pl.BlockSpec((n, k), lambda i, pos: (0, 0)),
            ],
            out_specs=(
                pl.BlockSpec((1, rows, k), lambda i, pos: (0, row(i, pos), 0)),
                pl.BlockSpec((rows, k), lambda i, pos: (row(i, pos), 0)),
            ),
            scratch_shapes=[pltpu.VMEM((4 * n, k), BF16)],
        ),
        compiler_params=params(24),
        cost_estimate=cost(8 * n * d * k, 10 << 20),
        name="finish",
    )(pos, mine, other, momentum, own, away, q)


def shards(inputs, key_grads, error, momentum, q_start):
    i = lax.axis_index("dp")
    y, c = (i // 2) % 4, i % 2
    pos = jnp.stack([c, y])

    other = merge(1 - c, inputs, key_grads, error)
    sent = dp_shift(other, 0, 1)
    mine = merge(c, inputs, key_grads, error)
    pieces = exchange(mine + sent, Y_GROUPS)
    unit = exchange(sum_turn(pieces).reshape(4, 64, 512), Z_GROUPS).sum(axis=0)
    units = [unit] + [dp_shift(unit, dy, 0) for dy in (1, 2)]
    of_y = gather(unit, 4, Z_GROUPS).reshape(256, 512)

    to_core, part = g_block(pos, units, of_y)
    part = part + dp_shift(to_core, 0, 1)
    part = exchange(part, None, "shard").sum(axis=0)
    part = gather(part, 16, ZY_GROUPS)
    part, of_y = lax.optimization_barrier((part, of_y))
    blocks = [of_y] + [dp_shift(of_y, dy, 0) for dy in (1, 2, 3)]
    part = gather(part, 8, None, "shard")
    part, blocks = lax.optimization_barrier((part, blocks))
    q_t, w = iterate(pos, part, dp_shift(part, 0, 1), q_start.T)

    own = left(pos, w, blocks)
    away = dp_shift(own, 0, 1)
    new_error, new_momentum = finish(pos, mine, other, error, momentum, own, away, q_t)
    return (new_error, new_momentum, q_t.T)


def solution(mesh):
    return jax.shard_map(
        shards,
        mesh=mesh,
        in_specs=(P("dp", "shard"), P("dp", None), P("dp", "shard", None), P("shard", None), P()),
        out_specs=(P("dp", "shard", None), P("shard", None), P()),
        check_vma=False,
    )
```

time: 1800 us -> 172 us (0.10)
  waiting for transfers between devices: 1610 us -> 38.1 us
  matrix products: 54.6 us -> 0 us
  other arithmetic: 37.2 us -> 2 us
  Pallas kernels: 0 us -> 30.6 us
  starting transfers between devices: 0.43 us -> 22 us
    psum x6 -> x0, waiting for transfers between devices: 1610 us -> none  [the longest x3 853 us: left_factor(): total = lax.psum(p_left, 'dp')]
    psum x3 -> x0, blocking collectives: 78.8 us -> none  [left_factor(): gram = lax.psum(jnp.dot(total.T, total, precision=HIGH), 'shard')]
    all_to_all x0 -> x4, blocking collectives: none -> 74.7 us  [exchange(): return lax.all_to_all(x, axis, 0, 0, axis_index_groups=groups)]
    dot_general x11 -> x0, matrix products: 50.5 us -> none  [the longest x3 16.9 us: shards(): q_part = lax.dot_general(merged, p_hat, contract, precision=HIGH)]
    another operation x15 -> x1, other arithmetic: 36.2 us -> 0.07 us  [shards(): pos = jnp.stack([c, y])]
    ppermute x0 -> x9, waiting for transfers between devices: none -> 35 us  [dp_shift(): return lax.ppermute(x, 'dp', pairs)]
    pallas_call x0 -> x7, Pallas kernels: none -> 30.6 us  [the longest x1 14.4 us: iterate(): pl.pallas_call(iterate_kernel, out_shape=(jax.ShapeDtypeStruct(q.shape, F...]
  transfers between devices with their start and end apart: 6 -> 11, of which waited for: 6 -> 9; matrix products, arithmetic and copies ran while one was open for 0% -> 0% of each run, Pallas kernels for 0% -> 3%
where the time goes in v1:
time: 172 us; the launch traced here: 171 us
  blocking collectives  74.7 us (43%)
  waiting for transfers between devices  38.1 us (22%)
  Pallas kernels  30.6 us (18%)
  starting transfers between devices  22 us (13%)
  local copies, waits for them, and re-layouts  2.99 us (2%)
  other arithmetic  2 us (1%)
    all_to_all x4, blocking collectives, exchange(): return lax.all_to_all(x, axis, 0, 0, axis_index_groups=groups)  74.7 us
    ppermute x9, waiting for transfers between devices, dp_shift(): return lax.ppermute(x, 'dp', pairs)  35 us
    pallas_call x1, Pallas kernels, iterate(): pl.pallas_call(iterate_kernel, out_shape=(jax.ShapeDtypeStruct(q.shape, F...  14.4 us
    ppermute x9, starting transfers between devices, dp_shift(): return lax.ppermute(x, 'dp', pairs)  13.5 us
    pallas_call x2, Pallas kernels, merge(): pl.pallas_call(merge_kernel, out_shape=jax.ShapeDtypeStruct((4, d // 2, k...  9.17 us
    all_to_all x2, starting transfers between devices, exchange(): return lax.all_to_all(x, axis, 0, 0, axis_index_groups=groups)  8.56 us
    pallas_call x1, Pallas kernels, finish(): pl.pallas_call(finish_kernel, out_shape=(jax.ShapeDtypeStruct(error.shape...  4.02 us
  transfers between devices with their start and end apart: 11, of which 9 were waited for; matrix products, arithmetic and copies ran while one was open for 0% of the time, Pallas kernels for 3%

profile of v1, /device:TPU:1, one launch (start us, length us, event | category | flops | bytes accessed | tf_op | source)
XLA Modules:
  0.0 171.2 jit_solution(5304908828919394839)
XLA Ops:
  0.6 4.6 %merge.3.other = f32[4,512,256]{2,1,0:T(8,128)} custom-call(s32[1]{0:T(128)} %bitcast.2.half_ref, bf16[512,1024]{1,0:T(8,128)(2,1)} %acts_ref.3, bf16[512,1024]{1,0:T(8,128)(2,1)} %grads_ref.3, bf16[1,1024,1024]{2,1,0:T(8,128)(2,1)} %err_ref.3), custom_call_target="tpu_custom_call" | custom-call | flops 536870912 | bytes 5242880 | tf_op jit(solution)/shard_map/merge/pallas_call | solution.py:69
  5.2 3.2 %collective-permute-start = (f32[4,512,256]{2,1,0:T(8,128)}, f32[4,512,256]{2,1,0:T(8,128)S(1)}, u32[]{:S(2)}, u32[]{:S(2)}) collective-permute-start(f32[4,512,256]{2,1,0:T(8,128)} %merge.3.other), channel_id=1, source_target_pairs={{0,8},{8,0},{16,24},{24,16},{32,40},{40,32},{48,56},{56,48},{64,72... | collective-permute-start | bytes 6291464 | tf_op jit(solution)/shard_map/ppermute | solution.py:29
  8.5 4.6 %merge.2.mine = f32[4,512,256]{2,1,0:T(8,128)} custom-call(s32[1]{0:T(128)} %bitcast.half_ref, bf16[512,1024]{1,0:T(8,128)(2,1)} %acts_ref.3, bf16[512,1024]{1,0:T(8,128)(2,1)} %grads_ref.3, bf16[1,1024,1024]{2,1,0:T(8,128)(2,1)} %err_ref.3), custom_call_target="tpu_custom_call" | custom-call | flops 536870912 | bytes 5242880 | tf_op jit(solution)/shard_map/merge/pallas_call | solution.py:69
  13.1 1.9 %add.16 = f32[4,512,256]{2,1,0:T(8,128)S(1)} add(f32[4,512,256]{2,1,0:T(8,128)} %merge.2.mine, f32[4,512,256]{2,1,0:T(8,128)S(1)} %collective-permute-done) | non-fusion elementwise | flops 524288 | bytes 6291456 | tf_op jit(solution)/shard_map/add | solution.py:331
  14.9 28.6 %all_to_all.30.x_ref = f32[4,512,256]{2,1,0:T(8,128)S(1)} all-to-all(f32[4,512,256]{2,1,0:T(8,128)S(1)} %add.16), channel_id=1, replica_groups={{0,16,32,48},{8,24,40,56},{64,80,96,112},{72,88,104,120},{128,144,160,1..., dimensions={0} | all-to-all | bytes 4194304 | tf_op jit(solution)/shard_map/all_to_all | solution.py:33
  43.5 0.7 sum_turn.1
  44.2 21.2 %all_to_all.31 = f32[4,64,512]{2,1,0:T(8,128)S(1)} all-to-all(f32[4,64,512]{2,1,0:T(8,128)S(1)} %bitcast.7), channel_id=1, replica_groups={{0,64,128,192},{8,72,136,200},{16,80,144,208},{24,88,152,216},{32,96,16..., dimensions={0} | all-to-all | bytes 1048576 | tf_op jit(solution)/shard_map/all_to_all | solution.py:33
  65.5 0.9 broadcast_in_dim.6
  66.3 5.0 %all-to-all-start.2 = ((f32[4,64,512]{2,1,0:T(8,128)}), f32[4,64,512]{2,1,0:T(8,128)S(1)}, u32[]{:S(2)}, u32[]{:S(2)}) async-start(f32[4,64,512]{2,1,0:T(8,128)} %broadcast_in_dim.6), calls=%async_computation.2 | async-start | bytes 1048576 | tf_op jit(solution)/shard_map/all_to_all | solution.py:33
  71.3 1.5 collective-permute-start.1
  72.9 3.9 %collective-permute-done.2.u2 = f32[64,512]{1,0:T(8,128)S(1)} collective-permute-done((f32[64,512]{1,0:T(8,128)S(1)}, f32[64,512]{1,0:T(8,128)S(1)}, u32[]{:S(2)}, u32[]{:S(2)}) %collective-permute-start.2) | collective-permute-done | bytes 131104 | tf_op jit(solution)/shard_map/ppermute | solution.py:29
  76.7 1.0 collective-permute-done.1.u1
  77.7 3.1 %all-to-all-done.2 = f32[4,64,512]{2,1,0:T(8,128)S(1)} async-done(((f32[4,64,512]{2,1,0:T(8,128)}), f32[4,64,512]{2,1,0:T(8,128)S(1)}, u32[]{:S(2)}, u32[]{:S(2)}) %all-to-all-start.2) | async-done | bytes 524320 | tf_op jit(solution)/shard_map/all_to_all | solution.py:33
  80.9 1.2 g_block.1
  82.1 5.3 %collective-permute-start.3 = (f32[8,3,8,128]{3,2,1,0:T(8,128)S(1)}, f32[8,3,8,128]{3,2,1,0:T(8,128)S(1)}, u32[]{:S(2)}, u32[]{:S(2)}) collective-permute-start(f32[8,3,8,128]{3,2,1,0:T(8,128)S(1)} %get-tuple-element.17), channel_id=1, source_target_pairs={{0,8},{8,0},{16,24},{24,16},{32,40},{40,32},{48,56},{56,48},{64,72... | collective-permute-start | bytes 294920 | tf_op jit(solution)/shard_map/ppermute | solution.py:29
  87.4 0.9 collective-permute-done.3
  88.4 12.7 %all_to_all.32 = f32[8,3,8,128]{3,2,1,0:T(8,128)S(1)} all-to-all(f32[8,3,8,128]{3,2,1,0:T(8,128)S(1)} %add.17), channel_id=1, replica_groups=mesh['dp'=32,'shard'=8] {'shard'}, dimensions={0} | all-to-all | bytes 196608 | tf_op jit(solution)/shard_map/all_to_all | solution.py:33
  101.1 12.2 %all_to_all.33 = f32[16,3,8,128]{3,2,1,0:T(8,128)S(1)} all-to-all(f32[16,3,8,128]{3,2,1,0:T(8,128)S(1)} %broadcast_in_dim.7), channel_id=1, replica_groups={{0,16,32,48,64,80,96,112,128,144,160,176,192,208,224,240},{8,24,40,56,7..., dimensions={0} | all-to-all | bytes 393216 | tf_op jit(solution)/shard_map/all_to_all | solution.py:33
  113.3 1.3 broadcast_in_dim.8
  114.6 3.6 %all-to-all-start.5 = ((f32[8,16,3,8,128]{4,3,2,1,0:T(8,128)}), f32[8,16,3,8,128]{4,3,2,1,0:T(8,128)S(1)}, u32[]{:S(2)}, u32[]{:S(2)}) async-start(f32[8,16,3,8,128]{4,3,2,1,0:T(8,128)} %broadcast_in_dim.8), calls=%async_computation.5 | async-start | bytes 3145728 | tf_op jit(solution)/shard_map/all_to_all | solution.py:33
  118.2 1.1 collective-permute-start.6
  119.2 0.8 collective-permute-start.5
  120.1 0.6 collective-permute-start.4
  120.7 7.6 %collective-permute-done.6.m3 = f32[256,512]{1,0:T(8,128)S(1)} collective-permute-done((f32[256,512]{1,0:T(8,128)S(1)}, f32[256,512]{1,0:T(8,128)S(1)}, u32[]{:S(2)}, u32[]{:S(2)}) %collective-permute-start.6) | collective-permute-done | bytes 524320 | tf_op jit(solution)/shard_map/ppermute | solution.py:29
  128.2 2.5 %collective-permute-done.5.m2 = f32[256,512]{1,0:T(8,128)S(1)} collective-permute-done((f32[256,512]{1,0:T(8,128)S(1)}, f32[256,512]{1,0:T(8,128)S(1)}, u32[]{:S(2)}, u32[]{:S(2)}) %collective-permute-start.5) | collective-permute-done | bytes 524320 | tf_op jit(solution)/shard_map/ppermute | solution.py:29
  130.8 15.1 %collective-permute-done.4.m1 = f32[256,512]{1,0:T(8,128)S(1)} collective-permute-done((f32[256,512]{1,0:T(8,128)S(1)}, f32[256,512]{1,0:T(8,128)S(1)}, u32[]{:S(2)}, u32[]{:S(2)}) %collective-permute-start.4) | collective-permute-done | bytes 524320 | tf_op jit(solution)/shard_map/ppermute | solution.py:29
  145.8 0.8 copy-done.3
  147.2 3.0 %collective-permute-done.7.away_ref = f32[8,16,3,8,128]{4,3,2,1,0:T(8,128)S(1)} collective-permute-done((f32[8,16,3,8,128]{4,3,2,1,0:T(8,128)S(1)}, f32[8,16,3,8,128]{4,3,2,1,0:T(8,128)S(1)}, u32[]{:S(2)}, u32[]{:S(2)}) %collective-permute-start.7) | collective-permute-done | bytes 1572896 | tf_op jit(solution)/shard_map/ppermute | solution.py:29
  150.2 14.4 %iterations.1 = (f32[64,1024]{1,0:T(8,128)}, f32[64,1024]{1,0:T(8,128)S(1)}) custom-call(s32[2]{0:T(128)S(1)} %pad_add_fusion.pos_ref, f32[8,16,3,8,128]{4,3,2,1,0:T(8,128)S(1)} %all-to-all-done.5.own_ref, f32[8,16,3,8,128]{4,3,2,1,0:T(8,128)S(1)} %collective-permute-done.7.away_ref, f32[64,1024]{1,0:T(8,128)S(1)} %bitcast.14), custom_call_target="tpu_custom_call" | custom-call | flops 2415919104 | bytes 4194304 | tf_op jit(solution)/shard_map/iterations/pallas_call | solution.py:215
  164.6 1.1 left.1.own
  166.2 1.0 collective-permute-done.8.away
  167.2 4.0 %finish.1 = (bf16[1,1024,1024]{2,1,0:T(8,128)(2,1)}, bf16[1024,1024]{1,0:T(8,128)(2,1)}) custom-call(s32[2]{0:T(128)S(1)} %pad_add_fusion.pos_ref, f32[4,512,256]{2,1,0:T(8,128)S(1)} %copy-done, f32[4,512,256]{2,1,0:T(8,128)S(1)} %copy-done.1, bf16[1024,1024]{1,0:T(8,128)(2,1)S(1)} %copy-done.2, f32[64,512]{1,0:T(8,128)S(1)} %left.1.own, ...), custom_call_target="tpu_custom_call" | custom-call | flops 536870912 | bytes 10485760 | tf_op jit(solution)/shard_map/finish/pallas_call | solution.py:297
  (23 shorter events, 1.1 us)
Async XLA Ops:
  5.2 7.8 %collective-permute-start = (f32[4,512,256]{2,1,0:T(8,128)}, f32[4,512,256]{2,1,0:T(8,128)S(1)}, u32[]{:S(2)}, u32[]{:S(2)}) collective-permute-start(f32[4,512,256]{2,1,0:T(8,128)} %merge.3.other), channel_id=1, source_target_pairs={{0,8},{8,0},{16,24},{24,16},{32,40},{40,32},{48,56},{56,48},{64,72... | collective-permute-start | bytes 6291464 | tf_op jit(solution)/shard_map/ppermute | solution.py:29
  66.3 14.5 %all-to-all-start.2 = ((f32[4,64,512]{2,1,0:T(8,128)}), f32[4,64,512]{2,1,0:T(8,128)S(1)}, u32[]{:S(2)}, u32[]{:S(2)}) async-start(f32[4,64,512]{2,1,0:T(8,128)} %broadcast_in_dim.6), calls=%async_computation.2 | async-start | bytes 1048576 | tf_op jit(solution)/shard_map/all_to_all | solution.py:33
  71.3 5.4 %collective-permute-start.2 = (f32[64,512]{1,0:T(8,128)S(1)}, f32[64,512]{1,0:T(8,128)S(1)}, u32[]{:S(2)}, u32[]{:S(2)}) collective-permute-start(f32[64,512]{1,0:T(8,128)S(1)} %reduce_sum.18.u0), channel_id=1, source_target_pairs={{0,32},{8,40},{16,48},{24,56},{32,0},{40,8},{48,16},{56,24},{64,96... | collective-permute-start | bytes 393224 | tf_op jit(solution)/shard_map/ppermute | solution.py:29
  71.3 6.4 %collective-permute-start.1 = (f32[64,512]{1,0:T(8,128)S(1)}, f32[64,512]{1,0:T(8,128)S(1)}, u32[]{:S(2)}, u32[]{:S(2)}) collective-permute-start(f32[64,512]{1,0:T(8,128)S(1)} %reduce_sum.18.u0), channel_id=1, source_target_pairs={{0,16},{8,24},{16,32},{24,40},{32,48},{40,56},{48,0},{56,8},{64,80... | collective-permute-start | bytes 393224 | tf_op jit(solution)/shard_map/ppermute | solution.py:29
  82.1 6.2 %collective-permute-start.3 = (f32[8,3,8,128]{3,2,1,0:T(8,128)S(1)}, f32[8,3,8,128]{3,2,1,0:T(8,128)S(1)}, u32[]{:S(2)}, u32[]{:S(2)}) collective-permute-start(f32[8,3,8,128]{3,2,1,0:T(8,128)S(1)} %get-tuple-element.17), channel_id=1, source_target_pairs={{0,8},{8,0},{16,24},{24,16},{32,40},{40,32},{48,56},{56,48},{64,72... | collective-permute-start | bytes 294920 | tf_op jit(solution)/shard_map/ppermute | solution.py:29
  113.3 36.9 %copy-start.6 = (f32[1024,64]{0,1:T(8,128)S(1)}, f32[1024,64]{0,1:T(8,128)}, u32[]{:S(2)}) copy-start(f32[1024,64]{0,1:T(8,128)} %param.9) | copy-start | bytes 786436
  114.6 32.1 %all-to-all-start.5 = ((f32[8,16,3,8,128]{4,3,2,1,0:T(8,128)}), f32[8,16,3,8,128]{4,3,2,1,0:T(8,128)S(1)}, u32[]{:S(2)}, u32[]{:S(2)}) async-start(f32[8,16,3,8,128]{4,3,2,1,0:T(8,128)} %broadcast_in_dim.8), calls=%async_computation.5 | async-start | bytes 3145728 | tf_op jit(solution)/shard_map/all_to_all | solution.py:33
  118.2 10.1 %collective-permute-start.6 = (f32[256,512]{1,0:T(8,128)S(1)}, f32[256,512]{1,0:T(8,128)S(1)}, u32[]{:S(2)}, u32[]{:S(2)}) collective-permute-start(f32[256,512]{1,0:T(8,128)S(1)} %bitcast.9), channel_id=1, source_target_pairs={{0,48},{8,56},{16,0},{24,8},{32,16},{40,24},{48,32},{56,40},{64,11... | collective-permute-start | bytes 1572872 | tf_op jit(solution)/shard_map/ppermute | solution.py:29
  119.2 11.5 %collective-permute-start.5 = (f32[256,512]{1,0:T(8,128)S(1)}, f32[256,512]{1,0:T(8,128)S(1)}, u32[]{:S(2)}, u32[]{:S(2)}) collective-permute-start(f32[256,512]{1,0:T(8,128)S(1)} %bitcast.10), channel_id=1, source_target_pairs={{0,32},{8,40},{16,48},{24,56},{32,0},{40,8},{48,16},{56,24},{64,96... | collective-permute-start | bytes 1572872 | tf_op jit(solution)/shard_map/ppermute | solution.py:29
  120.1 25.8 %collective-permute-start.4 = (f32[256,512]{1,0:T(8,128)S(1)}, f32[256,512]{1,0:T(8,128)S(1)}, u32[]{:S(2)}, u32[]{:S(2)}) collective-permute-start(f32[256,512]{1,0:T(8,128)S(1)} %bitcast.11), channel_id=1, source_target_pairs={{0,16},{8,24},{16,32},{24,40},{32,48},{40,56},{48,0},{56,8},{64,80... | collective-permute-start | bytes 1572872 | tf_op jit(solution)/shard_map/ppermute | solution.py:29
  145.8 0.8 copy-start.3
  146.7 3.5 %collective-permute-start.7 = (f32[8,16,3,8,128]{4,3,2,1,0:T(8,128)S(1)}, f32[8,16,3,8,128]{4,3,2,1,0:T(8,128)S(1)}, u32[]{:S(2)}, u32[]{:S(2)}) collective-permute-start(f32[8,16,3,8,128]{4,3,2,1,0:T(8,128)S(1)} %all-to-all-done.5.own_ref), channel_id=1, source_target_pairs={{0,8},{8,0},{16,24},{24,16},{32,40},{40,32},{48,56},{56,48},{64,72... | collective-permute-start | bytes 4718600 | tf_op jit(solution)/shard_map/ppermute | solution.py:29
  150.2 14.4 %copy-start.4 = (f32[256,512]{1,0:T(8,128)S(1)}, f32[256,512]{1,0:T(8,128)}, u32[]{:S(2)}) copy-start(f32[256,512]{1,0:T(8,128)} %copy-done.3) | copy-start | bytes 1572868
  150.2 17.0 %copy-start.1 = (f32[4,512,256]{2,1,0:T(8,128)S(1)}, f32[4,512,256]{2,1,0:T(8,128)}, u32[]{:S(2)}) copy-start(f32[4,512,256]{2,1,0:T(8,128)} %merge.3.other) | copy-start | bytes 6291460
  150.2 17.0 %copy-start.2 = (bf16[1024,1024]{1,0:T(8,128)(2,1)S(1)}, bf16[1024,1024]{1,0:T(8,128)(2,1)}, u32[]{:S(2)}) copy-start(bf16[1024,1024]{1,0:T(8,128)(2,1)} %mom.1) | copy-start | bytes 6291460
  164.6 2.6 %copy-start = (f32[4,512,256]{2,1,0:T(8,128)S(1)}, f32[4,512,256]{2,1,0:T(8,128)}, u32[]{:S(2)}) copy-start(f32[4,512,256]{2,1,0:T(8,128)} %merge.2.mine) | copy-start | bytes 6291460
  164.6 2.6 %copy-start.5 = (f32[64,1024]{1,0:T(8,128)S(1)}, f32[64,1024]{1,0:T(8,128)}, u32[]{:S(2)}) copy-start(f32[64,1024]{1,0:T(8,128)} %get-tuple-element.26.q) | copy-start | bytes 786436
  165.7 1.5 collective-permute-start.8

commit v2 on v1

--- a/solution.py
+++ b/solution.py
@@ -1,3 +1,4 @@
+import functools
 import math
 
 import jax
@@ -16,17 +17,24 @@
 VMEM = pl.BlockSpec(memory_space=pltpu.VMEM)
 SMEM = pl.BlockSpec(memory_space=pltpu.SMEM)
 
-Y_GROUPS = [[z * 8 + y * 2 + c for y in range(4)] for z in range(4) for c in range(2)]
 Z_GROUPS = [[z * 8 + y * 2 + c for z in range(4)] for y in range(4) for c in range(2)]
 ZY_GROUPS = [[z * 8 + y * 2 + c for z in range(4) for y in range(4)] for c in range(2)]
 
 
-def dp_shift(x, dy, dc):
+def dp_shift(x, dz=0, dy=0, dc=0):
     pairs = []
     for i in range(32):
         z, y, c = i // 8, (i // 2) % 4, i % 2
-        pairs.append((i, z * 8 + (y + dy) % 4 * 2 + (c + dc) % 2))
+        pairs.append((i, (z + dz) % 4 * 8 + (y + dy) % 4 * 2 + (c + dc) % 2))
     return lax.ppermute(x, "dp", pairs)
+
+
+def ring_sum(opposite, following, before, step):
+    relay_on, relay_back = step(opposite[0], 1), step(opposite[1], -1)
+    second, first = step(following[1], 1), step(before[0], -1)
+    relay_on, relay_back, second, first = lax.optimization_barrier((relay_on, relay_back, second, first))
+    on, back = step(following[0] + relay_on, 1), step(before[1] + relay_back, -1)
+    return on, second, first, back
 
 
 def exchange(x, groups, axis="dp"):
@@ -57,50 +65,107 @@
     return hi, mid, (rest - mid.astype(F32)).astype(BF16)
 
 
-def merge_kernel(half_ref, acts_ref, grads_ref, err_ref, out_ref):
-    factor = 1.0 / math.sqrt(acts_ref.shape[0])
-    product = lax.dot_general(acts_ref[...], grads_ref[...], ROWS, preferred_element_type=F32)
-    out_ref[0] = product * factor + err_ref[0].astype(F32)
-
-
-def merge(half, inputs, key_grads, error):
+def merge_kernel(turns, added, pos_ref, acts, grads, err, *refs):
+    sent, refs = (refs[0], refs[1:]) if added else (None, refs)
+    out_ref, refs = refs[0], refs[1:]
+    sums, refs = (refs[:2 * len(turns)], refs[2 * len(turns):]) if added else ((), refs)
+    x_buf, k_buf, e_buf, sems = refs
+    half, y = pos_ref[0], pos_ref[1]
+    tok, d = x_buf.shape
+    at_d = pl.ds(pl.multiple_of(half * d, 128), d)
+    copies = [pltpu.make_async_copy(acts.at[:, at_d], x_buf, sems.at[0])]
+    for n, turn in enumerate(turns):
+        cols = pl.ds(pl.multiple_of((y + turn) % 4 * 256, 128), 256)
+        copies.append(pltpu.make_async_copy(grads.at[:, cols], k_buf.at[n], sems.at[1 + 2 * n]))
+        copies.append(pltpu.make_async_copy(err.at[0, at_d, cols], e_buf.at[n], sems.at[2 + 2 * n]))
+    for copy in copies:
+        copy.start()
+    copies[0].wait()
+    factor = 1.0 / math.sqrt(tok)
+    for n in range(len(turns)):
+        copies[1 + 2 * n].wait()
+        product = lax.dot_general(x_buf[...], k_buf[n], ROWS, preferred_element_type=F32)
+        copies[2 + 2 * n].wait()
+        merged = product * factor + e_buf[n].astype(F32)
+        out_ref[n] = merged
+        if added:
+            total = merged + sent[n]
+            sums[2 * n][...] = total[:d // 2]
+            sums[2 * n + 1][...] = total[d // 2:]
+
+
+def merge(half, y, turns, inputs, key_grads, error, sent=None):
     tok, d = inputs.shape
-    k = key_grads.shape[1]
-    return pl.pallas_call(
-        merge_kernel,
-        out_shape=jax.ShapeDtypeStruct((4, d // 2, k // 4), F32),
-        grid_spec=pltpu.PrefetchScalarGridSpec(
-            num_scalar_prefetch=1,
-            grid=(4,),
-            in_specs=[
-                pl.BlockSpec((tok, d // 2), lambda i, half: (0, half[0])),
-                pl.BlockSpec((tok, k // 4), lambda i, half: (0, i)),
-                pl.BlockSpec((1, d // 2, k // 4), lambda i, half: (0, half[0], i)),
-            ],
-            out_specs=pl.BlockSpec((1, d // 2, k // 4), lambda i, half: (i, 0, 0)),
-        ),
-        compiler_params=params(56),
-        cost_estimate=cost(tok * d * k, 5 << 20),
+    d = d // 2
+    n = len(turns)
+    added = sent is not None
+    in_hbm = pl.BlockSpec(memory_space=pltpu.HBM)
+    outs = [jax.ShapeDtypeStruct((n, d, 256), F32)]
+    if added:
+        outs += [jax.ShapeDtypeStruct((d // 2, 256), F32)] * (2 * n)
+    result = pl.pallas_call(
+        functools.partial(merge_kernel, turns, added),
+        out_shape=tuple(outs),
+        in_specs=[SMEM] + [in_hbm] * 3 + [VMEM] * added,
+        out_specs=(VMEM,) * len(outs),
+        scratch_shapes=[
+            pltpu.VMEM((tok, d), BF16),
+            pltpu.VMEM((n, tok, 256), BF16),
+            pltpu.VMEM((n, d, 256), BF16),
+            pltpu.SemaphoreType.DMA((1 + 2 * n,)),
+        ],
+        compiler_params=params(58),
+        cost_estimate=cost(2 * tok * d * 256 * n, (1 + 2 * n) << 19),
         name="merge",
-    )(half.reshape(1), inputs, key_grads, error)
-
-
-def sum_turn_kernel(x_ref, out_ref):
-    out_ref[...] = (x_ref[0] + x_ref[1] + x_ref[2] + x_ref[3]).T
-
-
-def sum_turn(x):
-    _, d, k = x.shape
+    )(jnp.stack([half, y]), inputs, key_grads, error, *([sent] if added else []))
+    return result[0], list(result[1:])
+
+
+def sum_turn_kernel(pos_ref, top, end, on, second, first, back, *refs):
+    outs, own_ref, turned = refs[:6], refs[6], refs[7]
+    turned[:, :256] = (top[...] + (on[...] + first[...])).T
+    turned[:, 256:] = (end[...] + (second[...] + back[...])).T
+    z = pos_ref[2]
+    for n, turn in enumerate((2, 1, 3)):
+        at = (z + turn) % 4 * 64
+        for h in range(2):
+            outs[2 * n + h][...] = turned[pl.ds(pl.multiple_of(at + 32 * h, 32), 32), :]
+    own_ref[...] = turned[pl.ds(pl.multiple_of(z * 64, 64), 64), :]
+
+
+def sum_turn(pos, top, end, came):
+    half = jax.ShapeDtypeStruct((32, 512), F32)
     return pl.pallas_call(
         sum_turn_kernel,
-        out_shape=jax.ShapeDtypeStruct((k, d), F32),
-        grid=(d // 128,),
-        in_specs=[pl.BlockSpec((4, 128, k), lambda i: (0, i, 0))],
-        out_specs=pl.BlockSpec((k, 128), lambda i: (0, i)),
+        out_shape=(half,) * 6 + (jax.ShapeDtypeStruct((64, 512), F32),),
+        in_specs=[SMEM] + [VMEM] * 6,
+        out_specs=(VMEM,) * 7,
+        scratch_shapes=[pltpu.VMEM((256, 512), F32)],
         compiler_params=params(24),
-        cost_estimate=cost(4 * d * k, 20 * d * k),
+        cost_estimate=cost(4 << 17, 3 << 20),
         name="sum_turn",
-    )(x)
+    )(pos, top, end, *came)
+
+
+def unit_kernel(own, on, second, first, back, unit_ref, copies_ref):
+    for h, (a, b) in enumerate(((on, first), (second, back))):
+        rows = pl.ds(32 * h, 32)
+        total = own[rows, :] + (a[...] + b[...])
+        unit_ref[rows, :] = total
+        for z in range(4):
+            copies_ref[z, rows, :] = total
+
+
+def make_unit(own, came):
+    return pl.pallas_call(
+        unit_kernel,
+        out_shape=(jax.ShapeDtypeStruct((64, 512), F32), jax.ShapeDtypeStruct((4, 64, 512), F32)),
+        in_specs=[VMEM] * 5,
+        out_specs=(VMEM, VMEM),
+        compiler_params=params(24),
+        cost_estimate=cost(1 << 17, 1 << 20),
+        name="make_unit",
+    )(own, *came)
 
 
 def block_kernel(pos_ref, u0, u1, u2, of_y, sent_ref, mine_ref):
@@ -193,18 +258,28 @@
                 part[after, here] = part[here, after].T
         q = q_ref[...]
         n = q.shape[0]
+        def product(x, y_hi, y_mid, y_low, dims):
+            hi, mid, low = x
+            by_hi = lax.dot_general(jnp.concatenate([hi, mid, low], axis=0), y_hi, dims, preferred_element_type=F32)
+            by_mid = lax.dot_general(jnp.concatenate([hi, mid], axis=0), y_mid, dims, preferred_element_type=F32)
+            by_low = lax.dot_general(hi, y_low, dims, preferred_element_type=F32)
+            small = by_hi[2 * n:] + by_mid[n:] + by_low
+            return by_hi[:n] + (by_hi[n:2 * n] + by_mid[:n] + small)
+
+        def solve(inv, x):
+            hi, mid, low = split3(inv)
+            left_parts = jnp.concatenate([hi, hi, mid, mid, hi, low], axis=1)
+            right_parts = jnp.concatenate([x[0], x[1], x[0], x[1], x[2], x[0]], axis=0)
+            return jnp.dot(left_parts, right_parts, preferred_element_type=F32)
+
         for turn in range(ITERS):
-            hi, mid, low = split3(q)
-            by_hi = jnp.dot(jnp.concatenate([hi, mid, low], axis=0), hi_ref[...], preferred_element_type=F32)
-            by_mid = jnp.dot(jnp.concatenate([hi, mid], axis=0), mid_ref[...], preferred_element_type=F32)
-            by_low = jnp.dot(hi, low_ref[...], preferred_element_type=F32)
-            small = by_hi[2 * n:] + by_mid[n:] + by_low
-            u = by_hi[:n] + (by_hi[n:2 * n] + by_mid[:n] + small)
-            gram = lax.dot_general(q, u, LANES, precision=HIGH, preferred_element_type=F32)
-            inv = inverse_factor(gram)
+            q_parts = split3(q)
+            u = product(q_parts, hi_ref[...], mid_ref[...], low_ref[...], (((1,), (0,)), ((), ())))
+            u_parts = split3(u)
+            inv = inverse_factor(product(u_parts, *q_parts, LANES))
             if turn == ITERS - 1:
-                w_out[...] = jnp.dot(inv, q, precision=HIGH, preferred_element_type=F32)
-            q = jnp.dot(inv, u, precision=HIGH, preferred_element_type=F32) * (1.0 / 32)
+                w_out[...] = solve(inv, q_parts)
+            q = solve(inv, u_parts) * (1.0 / 32)
         q_out[...] = q
 
 
@@ -225,12 +300,12 @@
     )(pos, own, away, q)
 
 
-def left_kernel(pos_ref, w_ref, m0, m1, m2, m3, out_ref):
+def left_kernel(pos_ref, w_ref, m0, m1, m3, m2_top, m2_end, out_ref):
     total = None
     n = w_ref.shape[0]
-    for turn, ref in enumerate((m0, m1, m2, m3)):
-        at = pl.multiple_of(((pos_ref[1] + 4 - turn) % 4) * 256, 256)
-        whi, wlow = split2(w_ref[:, pl.ds(at, 256)])
+    for turn, start, ref in ((0, 0, m0), (3, 0, m1), (1, 0, m3), (2, 0, m2_top), (2, 128, m2_end)):
+        at = pl.multiple_of((pos_ref[1] + turn) % 4 * 256 + start, 128)
+        whi, wlow = split2(w_ref[:, pl.ds(at, ref.shape[0])])
         mhi, mlow = split2(ref[...])
         both = jnp.dot(jnp.concatenate([whi, wlow], axis=0), mhi, preferred_element_type=F32)
         part = both[:n] + (both[n:] + jnp.dot(whi, mlow, preferred_element_type=F32))
@@ -243,7 +318,7 @@
     return pl.pallas_call(
         left_kernel,
         out_shape=jax.ShapeDtypeStruct((n, d), F32),
-        in_specs=[SMEM] + [VMEM] * 5,
+        in_specs=[SMEM] + [VMEM] * 6,
         out_specs=VMEM,
         compiler_params=params(24),
         cost_estimate=cost(6 * n * d * 1024, 2 << 20),
@@ -251,7 +326,10 @@
     )(pos, w, *blocks)
 
 
-def finish_kernel(pos_ref, mine, other, mom, own, away, q, err_out, mom_out, q_parts):
+TURNS = (2, 1, 3, 0)
+
+
+def finish_kernel(pos_ref, mine_opp, mine, other_opp, other, mom, own, away, q, err_out, mom_out, q_parts):
     i = pl.program_id(0)
 
     @pl.when(i == 0)
@@ -259,27 +337,28 @@
         hi, low = split2(q[...])
         q_parts[...] = jnp.concatenate([hi, hi, low, low], axis=0)
 
-    def step(merged, p_t):
+    def step(opp, rest, p_t):
         hi, low = split2(p_t[...])
         p_parts = jnp.concatenate([hi, low, hi, low], axis=0)
-        for n in range(4):
-            cols = pl.ds(256 * n, 256)
+        for n, turn in enumerate(TURNS):
+            cols = pl.ds(pl.multiple_of((pos_ref[1] + turn) % 4 * 256, 256), 256)
+            merged = opp[0] if n == 0 else rest[n - 1]
             approx = lax.dot_general(p_parts, q_parts[:, cols], ROWS, preferred_element_type=F32)
-            err_out[0, :, cols] = (merged[n] - approx).astype(BF16)
+            err_out[0, :, cols] = (merged - approx).astype(BF16)
             mom_out[:, cols] = (0.9 * mom[:, cols].astype(F32) + approx).astype(BF16)
 
     first = i < pl.num_programs(0) // 2
 
     @pl.when(first)
     def _():
-        step(mine, own)
+        step(mine_opp, mine, own)
 
     @pl.when(jnp.logical_not(first))
     def _():
-        step(other, away)
-
-
-def finish(pos, mine, other, error, momentum, own, away, q):
+        step(other_opp, other, away)
+
+
+def finish(pos, pieces, error, momentum, own, away, q):
     n, k = q.shape
     d = momentum.shape[0]
     rows = 256
@@ -293,6 +372,9 @@
 
     def late(i):
         return jnp.maximum(i - half, 0)
+
+    def pieces_at(count, when):
+        return pl.BlockSpec((count, rows, 256), lambda i, pos: (0, when(i), 0))
 
     return pl.pallas_call(
         finish_kernel,
@@ -301,8 +383,10 @@
             num_scalar_prefetch=1,
             grid=(d // rows,),
             in_specs=[
-                pl.BlockSpec((4, rows, k // 4), lambda i, pos: (0, early(i), 0)),
-                pl.BlockSpec((4, rows, k // 4), lambda i, pos: (0, late(i), 0)),
+                pieces_at(1, early),
+                pieces_at(3, early),
+                pieces_at(1, late),
+                pieces_at(3, late),
                 pl.BlockSpec((rows, k), lambda i, pos: (row(i, pos), 0)),
                 pl.BlockSpec((n, rows), lambda i, pos: (0, early(i))),
                 pl.BlockSpec((n, rows), lambda i, pos: (0, late(i))),
@@ -317,35 +401,48 @@
         compiler_params=params(24),
         cost_estimate=cost(8 * n * d * k, 10 << 20),
         name="finish",
-    )(pos, mine, other, momentum, own, away, q)
+    )(pos, *pieces, momentum, own, away, q)
 
 
 def shards(inputs, key_grads, error, momentum, q_start):
     i = lax.axis_index("dp")
-    y, c = (i // 2) % 4, i % 2
-    pos = jnp.stack([c, y])
-
-    other = merge(1 - c, inputs, key_grads, error)
-    sent = dp_shift(other, 0, 1)
-    mine = merge(c, inputs, key_grads, error)
-    pieces = exchange(mine + sent, Y_GROUPS)
-    unit = exchange(sum_turn(pieces).reshape(4, 64, 512), Z_GROUPS).sum(axis=0)
-    units = [unit] + [dp_shift(unit, dy, 0) for dy in (1, 2)]
-    of_y = gather(unit, 4, Z_GROUPS).reshape(256, 512)
+    z, y, c = i // 8, (i // 2) % 4, i % 2
+    pos = jnp.stack([c, y, z])
+
+    args = (inputs, key_grads, error)
+    other_opp, _ = merge(1 - c, y, TURNS[:1], *args)
+    other_opp, away_core = lax.optimization_barrier((other_opp, 1 - c))
+    sent_opp = dp_shift(other_opp, dc=1)
+    other, _ = merge(away_core, y, TURNS[1:], *args)
+    sent = dp_shift(other, dc=1)
+    mine_opp, opposite = merge(c, y, TURNS[:1], *args, sent_opp)
+    mine, sums = merge(c, y, TURNS[1:], *args, sent)
+    came = ring_sum(opposite, sums[0:2], sums[2:4], lambda x, d: dp_shift(x, dy=d))
+    *cut, own = sum_turn(pos, *sums[4:6], came)
+    came = ring_sum(cut[0:2], cut[2:4], cut[4:6], lambda x, d: dp_shift(x, dz=d))
+    unit, copies = make_unit(own, came)
+    units = [unit] + [dp_shift(unit, dy=dy) for dy in (1, 2)]
+    of_y = exchange(copies, Z_GROUPS).reshape(256, 512)
+    of_y, *units = lax.optimization_barrier((of_y, *units))
 
     to_core, part = g_block(pos, units, of_y)
-    part = part + dp_shift(to_core, 0, 1)
+    part = part + dp_shift(to_core, dc=1)
+    m1, m3 = dp_shift(of_y, dy=1), dp_shift(of_y, dy=-1)
     part = exchange(part, None, "shard").sum(axis=0)
+    part, m1, m3 = lax.optimization_barrier((part, m1, m3))
     part = gather(part, 16, ZY_GROUPS)
-    part, of_y = lax.optimization_barrier((part, of_y))
-    blocks = [of_y] + [dp_shift(of_y, dy, 0) for dy in (1, 2, 3)]
+    part, m1, m3 = lax.optimization_barrier((part, m1, m3))
+    m2_top, m2_end = dp_shift(m1[:128], dy=1), dp_shift(m3[128:], dy=-1)
     part = gather(part, 8, None, "shard")
-    part, blocks = lax.optimization_barrier((part, blocks))
-    q_t, w = iterate(pos, part, dp_shift(part, 0, 1), q_start.T)
-
+    part, m2_top, m2_end = lax.optimization_barrier((part, m2_top, m2_end))
+    q_t, w = iterate(pos, part, dp_shift(part, dc=1), q_start.T)
+
+    blocks = [of_y, m1, m3, m2_top, m2_end]
     own = left(pos, w, blocks)
-    away = dp_shift(own, 0, 1)
-    new_error, new_momentum = finish(pos, mine, other, error, momentum, own, away, q_t)
+    away = dp_shift(own, dc=1)
+    new_error, new_momentum = finish(
+        pos, (mine_opp, mine, other_opp, other), error, momentum, own, away, q_t
+    )
     return (new_error, new_momentum, q_t.T)
 
 

time: 172 us -> 173 us (level)
  blocking collectives: 74.7 us -> 25.2 us
  starting transfers between devices: 22 us -> 50.8 us
  waiting for transfers between devices: 38.1 us -> 47.2 us
  Pallas kernels: 30.6 us -> 38.7 us
  local copies, waits for them, and re-layouts: 2.99 us -> 5.87 us
  other arithmetic: 2 us -> 3.89 us
    all_to_all x4 -> x2, blocking collectives: 74.7 us -> 25.2 us  [exchange(): return lax.all_to_all(x, axis, 0, 0, axis_index_groups=groups)]
    ppermute x9 -> x23, starting transfers between devices: 13.5 us -> 43.7 us  [dp_shift(): return lax.ppermute(x, 'dp', pairs)]
    pallas_call x3 -> x6, Pallas kernels: 9.85 us -> 18.3 us  [the longest x4 16.7 us: merge(): pl.pallas_call(functools.partial(merge_kernel, turns, added), out_shape=t...]
    all_to_all x2, waiting for transfers between devices: 3.11 us -> 11.1 us  [exchange(): return lax.all_to_all(x, axis, 0, 0, axis_index_groups=groups)]
    unnamed x14 -> x30, local copies, waits for them, and re-layouts: 0.84 us -> 3.62 us
    another operation x1 -> x4, other arithmetic: 0.07 us -> 1.87 us  [the longest x3 1.8 us: merge(): jnp.stack([half, y])]
    ppermute x9 -> x23, waiting for transfers between devices: 35 us -> 36.1 us  [dp_shift(): return lax.ppermute(x, 'dp', pairs)]
  transfers between devices with their start and end apart: 11 -> 25, of which waited for: 9 -> 16; matrix products, arithmetic and copies ran while one was open for 0% -> 2% of each run, Pallas kernels for 3% -> 6%
where the time goes in v2:
time: 173 us
  starting transfers between devices  50.8 us (29%)
  waiting for transfers between devices  47.2 us (27%)
  Pallas kernels  38.7 us (22%)
  blocking collectives  25.2 us (15%)
  local copies, waits for them, and re-layouts  5.87 us (3%)
  other arithmetic  3.89 us (2%)
    ppermute x23, starting transfers between devices, dp_shift(): return lax.ppermute(x, 'dp', pairs)  43.7 us
    ppermute x23, waiting for transfers between devices, dp_shift(): return lax.ppermute(x, 'dp', pairs)  36.1 us
    all_to_all x2, blocking collectives, exchange(): return lax.all_to_all(x, axis, 0, 0, axis_index_groups=groups)  25.2 us
    pallas_call x4, Pallas kernels, merge(): pl.pallas_call(functools.partial(merge_kernel, turns, added), out_shape=t...  16.7 us
    pallas_call x1, Pallas kernels, iterate(): pl.pallas_call(iterate_kernel, out_shape=(jax.ShapeDtypeStruct(q.shape, F...  13.8 us
    all_to_all x2, waiting for transfers between devices, exchange(): return lax.all_to_all(x, axis, 0, 0, axis_index_groups=groups)  11.1 us
    all_to_all x2, starting transfers between devices, exchange(): return lax.all_to_all(x, axis, 0, 0, axis_index_groups=groups)  7.05 us
    pallas_call x1, Pallas kernels, finish(): pl.pallas_call(finish_kernel, out_shape=(jax.ShapeDtypeStruct(error.shape...  4.18 us
  transfers between devices with their start and end apart: 25, of which 16 were waited for; matrix products, arithmetic and copies ran while one was open for 2% of the time, Pallas kernels for 6%

profile of v2, /device:TPU:1, one launch (start us, length us, event | category | flops | bytes accessed | tf_op | source)
XLA Modules:
  0.0 172.6 jit_solution(506113757306765508)
XLA Ops:
  1.3 3.0 %merge.4.other_opp = f32[1,512,256]{2,1,0:T(8,128)} custom-call(s32[2]{0:T(128)} %pad_add_fusion.2.pos_ref, bf16[512,1024]{1,0:T(8,128)(2,1)} %acts.7, bf16[512,1024]{1,0:T(8,128)(2,1)} %grads.7, bf16[1,1024,1024]{2,1,0:T(8,128)(2,1)} %err.7), custom_call_target="tpu_custom_call" | custom-call | flops 134217728 | bytes 1572864 | tf_op jit(solution)/shard_map/merge/pallas_call | solution.py:106
  4.8 4.5 %merge.6.other = f32[3,512,256]{2,1,0:T(8,128)} custom-call(s32[2]{0:T(128)} %pad_add_fusion.3.pos_ref, bf16[512,1024]{1,0:T(8,128)(2,1)} %acts.7, bf16[512,1024]{1,0:T(8,128)(2,1)} %grads.7, bf16[1,1024,1024]{2,1,0:T(8,128)(2,1)} %err.7), custom_call_target="tpu_custom_call" | custom-call | flops 402653184 | bytes 3670016 | tf_op jit(solution)/shard_map/merge/pallas_call | solution.py:106
  9.3 3.3 %collective-permute-start.1 = (f32[3,512,256]{2,1,0:T(8,128)}, f32[3,512,256]{2,1,0:T(8,128)S(1)}, u32[]{:S(2)}, u32[]{:S(2)}) collective-permute-start(f32[3,512,256]{2,1,0:T(8,128)} %merge.6.other), channel_id=1, source_target_pairs={{0,8},{8,0},{16,24},{24,16},{32,40},{40,32},{48,56},{56,48},{64,72... | collective-permute-start | bytes 4718600 | tf_op jit(solution)/shard_map/ppermute | solution.py:29
  13.4 2.9 %collective-permute-done.refs_0_ = f32[1,512,256]{2,1,0:T(8,128)S(1)} collective-permute-done((f32[1,512,256]{2,1,0:T(8,128)S(1)}, f32[1,512,256]{2,1,0:T(8,128)S(1)}, u32[]{:S(2)}, u32[]{:S(2)}) %collective-permute-start) | collective-permute-done | bytes 524320 | tf_op jit(solution)/shard_map/ppermute | solution.py:29
  17.1 3.5 %merge.5 = (f32[1,512,256]{2,1,0:T(8,128)}, f32[256,256]{1,0:T(8,128)}, f32[256,256]{1,0:T(8,128)}) custom-call(s32[2]{0:T(128)} %pad_add_fusion.1.pos_ref, bf16[512,1024]{1,0:T(8,128)(2,1)} %acts.7, bf16[512,1024]{1,0:T(8,128)(2,1)} %grads.7, bf16[1,1024,1024]{2,1,0:T(8,128)(2,1)} %err.7, f32[1,512,256]{2,1,0:T(8,128)} %copy-done.14), custom_call_target="tpu_custom_call" | custom-call | flops 134217728 | bytes 1572864 | tf_op jit(solution)/shard_map/merge/pallas_call | solution.py:106
  20.7 2.7 %collective-permute-start.3 = (f32[256,256]{1,0:T(8,128)}, f32[256,256]{1,0:T(8,128)S(1)}, u32[]{:S(2)}, u32[]{:S(2)}) collective-permute-start(f32[256,256]{1,0:T(8,128)} %get-tuple-element.59), channel_id=1, source_target_pairs={{0,48},{8,56},{16,0},{24,8},{32,16},{40,24},{48,32},{56,40},{64,11... | collective-permute-start | bytes 786440 | tf_op jit(solution)/shard_map/ppermute | solution.py:29
  24.5 5.7 %merge.7 = (f32[3,512,256]{2,1,0:T(8,128)}, f32[256,256]{1,0:T(8,128)}, f32[256,256]{1,0:T(8,128)}, f32[256,256]{1,0:T(8,128)}, f32[256,256]{1,0:T(8,128)}, /*index=5*/f32[256,256]{1,0:T(8,128)}, f32[256,256]{1,0:T(8,128)}) custom-call(s32[2]{0:T(128)} %pad_add_fusion.1.pos_ref, bf16[512,1024]{1,0:T(8,128)(2,1)} %acts.7, bf16[512,1024]{1,0:T(8,128)(2,1)} %grads.7, ...), custom_call_target="tpu_custom_call" | custom-call | flops 402653184 | bytes 3670016 | tf_op jit(solution)/shard_map/merge/pallas_call | solution.py:106
  30.4 2.7 %collective-permute-start.5 = (f32[256,256]{1,0:T(8,128)}, f32[256,256]{1,0:T(8,128)S(1)}, u32[]{:S(2)}, u32[]{:S(2)}) collective-permute-start(f32[256,256]{1,0:T(8,128)} %get-tuple-element.61), channel_id=1, source_target_pairs={{0,48},{8,56},{16,0},{24,8},{32,16},{40,24},{48,32},{56,40},{64,11... | collective-permute-start | bytes 786440 | tf_op jit(solution)/shard_map/ppermute | solution.py:29
  33.0 5.9 %collective-permute-done.4.second = f32[256,256]{1,0:T(8,128)S(1)} collective-permute-done((f32[256,256]{1,0:T(8,128)}, f32[256,256]{1,0:T(8,128)S(1)}, u32[]{:S(2)}, u32[]{:S(2)}) %collective-permute-start.4) | collective-permute-done | bytes 262176 | tf_op jit(solution)/shard_map/ppermute | solution.py:29
  41.0 2.7 %collective-permute-start.7 = (f32[256,256]{1,0:T(8,128)S(1)}, f32[256,256]{1,0:T(8,128)S(1)}, u32[]{:S(2)}, u32[]{:S(2)}) collective-permute-start(f32[256,256]{1,0:T(8,128)S(1)} %add.27), channel_id=1, source_target_pairs={{0,48},{8,56},{16,0},{24,8},{32,16},{40,24},{48,32},{56,40},{64,11... | collective-permute-start | bytes 786440 | tf_op jit(solution)/shard_map/ppermute | solution.py:29
  43.8 3.6 %collective-permute-done.6.on = f32[256,256]{1,0:T(8,128)S(1)} collective-permute-done((f32[256,256]{1,0:T(8,128)S(1)}, f32[256,256]{1,0:T(8,128)S(1)}, u32[]{:S(2)}, u32[]{:S(2)}) %collective-permute-start.6) | collective-permute-done | bytes 262176 | tf_op jit(solution)/shard_map/ppermute | solution.py:29
  50.0 3.1 %collective-permute-start.9 = (f32[32,512]{1,0:T(8,128)S(1)}, f32[32,512]{1,0:T(8,128)S(1)}, u32[]{:S(2)}, u32[]{:S(2)}) collective-permute-start(f32[32,512]{1,0:T(8,128)S(1)} %get-tuple-element.70), channel_id=1, source_target_pairs={{0,192},{8,200},{16,208},{24,216},{32,224},{40,232},{48,240},{56,2... | collective-permute-start | bytes 196616 | tf_op jit(solution)/shard_map/ppermute | solution.py:29
  54.3 2.5 %collective-permute-start.11 = (f32[32,512]{1,0:T(8,128)S(1)}, f32[32,512]{1,0:T(8,128)S(1)}, u32[]{:S(2)}, u32[]{:S(2)}) collective-permute-start(f32[32,512]{1,0:T(8,128)S(1)} %get-tuple-element.72), channel_id=1, source_target_pairs={{0,192},{8,200},{16,208},{24,216},{32,224},{40,232},{48,240},{56,2... | collective-permute-start | bytes 196616 | tf_op jit(solution)/shard_map/ppermute | solution.py:29
  56.8 2.2 %collective-permute-done.10.second = f32[32,512]{1,0:T(8,128)S(1)} collective-permute-done((f32[32,512]{1,0:T(8,128)S(1)}, f32[32,512]{1,0:T(8,128)S(1)}, u32[]{:S(2)}, u32[]{:S(2)}) %collective-permute-start.10) | collective-permute-done | bytes 65568 | tf_op jit(solution)/shard_map/ppermute | solution.py:29
  59.0 2.4 %collective-permute-done.11.first = f32[32,512]{1,0:T(8,128)S(1)} collective-permute-done((f32[32,512]{1,0:T(8,128)S(1)}, f32[32,512]{1,0:T(8,128)S(1)}, u32[]{:S(2)}, u32[]{:S(2)}) %collective-permute-start.11) | collective-permute-done | bytes 65568 | tf_op jit(solution)/shard_map/ppermute | solution.py:29
  61.4 3.7 %collective-permute-start.12 = (f32[32,512]{1,0:T(8,128)S(1)}, f32[32,512]{1,0:T(8,128)S(1)}, u32[]{:S(2)}, u32[]{:S(2)}) collective-permute-start(f32[32,512]{1,0:T(8,128)S(1)} %add.28), channel_id=1, source_target_pairs={{0,64},{8,72},{16,80},{24,88},{32,96},{40,104},{48,112},{56,120},{... | collective-permute-start | bytes 196616 | tf_op jit(solution)/shard_map/ppermute | solution.py:29
  67.2 2.8 %collective-permute-done.13.back = f32[32,512]{1,0:T(8,128)S(1)} collective-permute-done((f32[32,512]{1,0:T(8,128)S(1)}, f32[32,512]{1,0:T(8,128)S(1)}, u32[]{:S(2)}, u32[]{:S(2)}) %collective-permute-start.13) | collective-permute-done | bytes 65568 | tf_op jit(solution)/shard_map/ppermute | solution.py:29
  70.8 3.5 %all-to-all-start = ((f32[4,64,512]{2,1,0:T(8,128)}), f32[4,64,512]{2,1,0:T(8,128)S(1)}, u32[]{:S(2)}, u32[]{:S(2)}) async-start(f32[4,64,512]{2,1,0:T(8,128)} %get-tuple-element.78), calls=%async_computation | async-start | bytes 1048576 | tf_op jit(solution)/shard_map/all_to_all | solution.py:41
  74.3 2.4 %collective-permute-start.15 = (f32[64,512]{1,0:T(8,128)S(1)}, f32[64,512]{1,0:T(8,128)S(1)}, u32[]{:S(2)}, u32[]{:S(2)}) collective-permute-start(f32[64,512]{1,0:T(8,128)S(1)} %get-tuple-element.80.u0), channel_id=1, source_target_pairs={{0,32},{8,40},{16,48},{24,56},{32,0},{40,8},{48,16},{56,24},{64,96... | collective-permute-start | bytes 393224 | tf_op jit(solution)/shard_map/ppermute | solution.py:29
  81.7 3.3 %all-to-all-done = f32[4,64,512]{2,1,0:T(8,128)S(1)} async-done(((f32[4,64,512]{2,1,0:T(8,128)}), f32[4,64,512]{2,1,0:T(8,128)S(1)}, u32[]{:S(2)}, u32[]{:S(2)}) %all-to-all-start) | async-done | bytes 524320 | tf_op jit(solution)/shard_map/all_to_all | solution.py:41
  85.0 3.4 %collective-permute-start.18 = (f32[256,512]{1,0:T(8,128)S(1)}, f32[256,512]{1,0:T(8,128)S(1)}, u32[]{:S(2)}, u32[]{:S(2)}) collective-permute-start(f32[256,512]{1,0:T(8,128)S(1)} %bitcast.8), channel_id=1, source_target_pairs={{0,48},{8,56},{16,0},{24,8},{32,16},{40,24},{48,32},{56,40},{64,11... | collective-permute-start | bytes 1572872 | tf_op jit(solution)/shard_map/ppermute | solution.py:29
  89.7 5.9 %collective-permute-start.16 = (f32[8,3,8,128]{3,2,1,0:T(8,128)S(1)}, f32[8,3,8,128]{3,2,1,0:T(8,128)S(1)}, u32[]{:S(2)}, u32[]{:S(2)}) collective-permute-start(f32[8,3,8,128]{3,2,1,0:T(8,128)S(1)} %get-tuple-element.85), channel_id=1, source_target_pairs={{0,8},{8,0},{16,24},{24,16},{32,40},{40,32},{48,56},{56,48},{64,72... | collective-permute-start | bytes 294920 | tf_op jit(solution)/shard_map/ppermute | solution.py:29
  96.6 9.1 %all_to_all.20 = f32[8,3,8,128]{3,2,1,0:T(8,128)S(1)} all-to-all(f32[8,3,8,128]{3,2,1,0:T(8,128)S(1)} %add.30), channel_id=1, replica_groups=mesh['dp'=32,'shard'=8] {'shard'}, dimensions={0} | all-to-all | bytes 196608 | tf_op jit(solution)/shard_map/all_to_all | solution.py:41
  105.8 16.1 %all_to_all.21 = f32[16,3,8,128]{3,2,1,0:T(8,128)S(1)} all-to-all(f32[16,3,8,128]{3,2,1,0:T(8,128)S(1)} %broadcast_in_dim.4), channel_id=1, replica_groups={{0,16,32,48,64,80,96,112,128,144,160,176,192,208,224,240},{8,24,40,56,7..., dimensions={0} | all-to-all | bytes 393216 | tf_op jit(solution)/shard_map/all_to_all | solution.py:41
  123.1 3.6 %all-to-all-start.3 = ((f32[8,16,3,8,128]{4,3,2,1,0:T(8,128)}), f32[8,16,3,8,128]{4,3,2,1,0:T(8,128)S(1)}, u32[]{:S(2)}, u32[]{:S(2)}) async-start(f32[8,16,3,8,128]{4,3,2,1,0:T(8,128)} %broadcast_in_dim.5), calls=%async_computation.3 | async-start | bytes 3145728 | tf_op jit(solution)/shard_map/all_to_all | solution.py:41
  129.2 3.8 %collective-permute-done.20.m2_end = f32[128,512]{1,0:T(8,128)S(1)} collective-permute-done((f32[128,512]{1,0:T(8,128)S(1)}, f32[128,512]{1,0:T(8,128)S(1)}, u32[]{:S(2)}, u32[]{:S(2)}) %collective-permute-start.20) | collective-permute-done | bytes 262176 | tf_op jit(solution)/shard_map/ppermute | solution.py:29
  133.0 2.2 %collective-permute-done.19.m2_top = f32[128,512]{1,0:T(8,128)S(1)} collective-permute-done((f32[128,512]{1,0:T(8,128)S(1)}, f32[128,512]{1,0:T(8,128)S(1)}, u32[]{:S(2)}, u32[]{:S(2)}) %collective-permute-start.19) | collective-permute-done | bytes 262176 | tf_op jit(solution)/shard_map/ppermute | solution.py:29
  135.9 7.8 %all-to-all-done.3.own_ref = f32[8,16,3,8,128]{4,3,2,1,0:T(8,128)S(1)} async-done(((f32[8,16,3,8,128]{4,3,2,1,0:T(8,128)}), f32[8,16,3,8,128]{4,3,2,1,0:T(8,128)S(1)}, u32[]{:S(2)}, u32[]{:S(2)}) %all-to-all-start.3) | async-done | bytes 1572896 | tf_op jit(solution)/shard_map/all_to_all | solution.py:41
  143.7 4.3 %collective-permute-start.21 = (f32[8,16,3,8,128]{4,3,2,1,0:T(8,128)S(1)}, f32[8,16,3,8,128]{4,3,2,1,0:T(8,128)S(1)}, u32[]{:S(2)}, u32[]{:S(2)}) collective-permute-start(f32[8,16,3,8,128]{4,3,2,1,0:T(8,128)S(1)} %all-to-all-done.3.own_ref), channel_id=1, source_target_pairs={{0,8},{8,0},{16,24},{24,16},{32,40},{40,32},{48,56},{56,48},{64,72... | collective-permute-start | bytes 4718600 | tf_op jit(solution)/shard_map/ppermute | solution.py:29
  148.0 3.0 %collective-permute-done.21.away_ref = f32[8,16,3,8,128]{4,3,2,1,0:T(8,128)S(1)} collective-permute-done((f32[8,16,3,8,128]{4,3,2,1,0:T(8,128)S(1)}, f32[8,16,3,8,128]{4,3,2,1,0:T(8,128)S(1)}, u32[]{:S(2)}, u32[]{:S(2)}) %collective-permute-start.21) | collective-permute-done | bytes 1572896 | tf_op jit(solution)/shard_map/ppermute | solution.py:29
  152.0 13.8 %iterations.1 = (f32[64,1024]{1,0:T(8,128)}, f32[64,1024]{1,0:T(8,128)S(1)}) custom-call(s32[3]{0:T(128)S(1)} %pad_add_fusion.pos_ref, f32[8,16,3,8,128]{4,3,2,1,0:T(8,128)S(1)} %all-to-all-done.3.own_ref, f32[8,16,3,8,128]{4,3,2,1,0:T(8,128)S(1)} %collective-permute-done.21.away_ref, f32[64,1024]{1,0:T(8,128)S(1)} %bitcast.13), custom_call_target="tpu_custom_call" | custom-call | flops 2415919104 | bytes 4194304 | tf_op jit(solution)/shard_map/iterations/pallas_call | solution.py:290
  168.4 4.2 %finish.1 = (bf16[1,1024,1024]{2,1,0:T(8,128)(2,1)}, bf16[1024,1024]{1,0:T(8,128)(2,1)}) custom-call(s32[3]{0:T(128)S(1)} %pad_add_fusion.pos_ref, f32[1,512,256]{2,1,0:T(8,128)S(1)} %copy-done.6, f32[3,512,256]{2,1,0:T(8,128)S(1)} %copy-done.3, f32[1,512,256]{2,1,0:T(8,128)S(1)} %copy-done.2, f32[3,512,256]{2,1,0:T(8,128)S(1)} %copy-done, ...), custom_call_target="tpu_custom_call" | custom-call | flops 536870912 | bytes 10485760 | tf_op jit(solution)/shard_map/finish/pallas_call | solution.py:379
  (74 shorter events, 28.1 us)
Async XLA Ops:
  9.3 14.1 %collective-permute-start.1 = (f32[3,512,256]{2,1,0:T(8,128)}, f32[3,512,256]{2,1,0:T(8,128)S(1)}, u32[]{:S(2)}, u32[]{:S(2)}) collective-permute-start(f32[3,512,256]{2,1,0:T(8,128)} %merge.6.other), channel_id=1, source_target_pairs={{0,8},{8,0},{16,24},{24,16},{32,40},{40,32},{48,56},{56,48},{64,72... | collective-permute-start | bytes 4718600 | tf_op jit(solution)/shard_map/ppermute | solution.py:29
  12.7 3.7 %collective-permute-start = (f32[1,512,256]{2,1,0:T(8,128)S(1)}, f32[1,512,256]{2,1,0:T(8,128)S(1)}, u32[]{:S(2)}, u32[]{:S(2)}) collective-permute-start(f32[1,512,256]{2,1,0:T(8,128)S(1)} %copy-done.2), channel_id=1, source_target_pairs={{0,8},{8,0},{16,24},{24,16},{32,40},{40,32},{48,56},{56,48},{64,72... | collective-permute-start | bytes 1572872 | tf_op jit(solution)/shard_map/ppermute | solution.py:29
  20.6 12.4 %collective-permute-start.2 = (f32[256,256]{1,0:T(8,128)}, f32[256,256]{1,0:T(8,128)S(1)}, u32[]{:S(2)}, u32[]{:S(2)}) collective-permute-start(f32[256,256]{1,0:T(8,128)} %get-tuple-element.58), channel_id=1, source_target_pairs={{0,16},{8,24},{16,32},{24,40},{32,48},{40,56},{48,0},{56,8},{64,80... | collective-permute-start | bytes 786440 | tf_op jit(solution)/shard_map/ppermute | solution.py:29
  20.7 12.3 %collective-permute-start.3 = (f32[256,256]{1,0:T(8,128)}, f32[256,256]{1,0:T(8,128)S(1)}, u32[]{:S(2)}, u32[]{:S(2)}) collective-permute-start(f32[256,256]{1,0:T(8,128)} %get-tuple-element.59), channel_id=1, source_target_pairs={{0,48},{8,56},{16,0},{24,8},{32,16},{40,24},{48,32},{56,40},{64,11... | collective-permute-start | bytes 786440 | tf_op jit(solution)/shard_map/ppermute | solution.py:29
  30.3 17.2 %copy-start.8 = (f32[256,256]{1,0:T(8,128)S(1)}, f32[256,256]{1,0:T(8,128)}, u32[]{:S(2)}) copy-start(f32[256,256]{1,0:T(8,128)} %get-tuple-element.55.top) | copy-start | bytes 786436
  30.3 17.2 %copy-start.9 = (f32[256,256]{1,0:T(8,128)S(1)}, f32[256,256]{1,0:T(8,128)}, u32[]{:S(2)}) copy-start(f32[256,256]{1,0:T(8,128)} %get-tuple-element.56.end) | copy-start | bytes 786436
  30.3 8.6 %collective-permute-start.4 = (f32[256,256]{1,0:T(8,128)}, f32[256,256]{1,0:T(8,128)S(1)}, u32[]{:S(2)}, u32[]{:S(2)}) collective-permute-start(f32[256,256]{1,0:T(8,128)} %get-tuple-element.60), channel_id=1, source_target_pairs={{0,16},{8,24},{16,32},{24,40},{32,48},{40,56},{48,0},{56,8},{64,80... | collective-permute-start | bytes 786440 | tf_op jit(solution)/shard_map/ppermute | solution.py:29
  30.4 8.5 %collective-permute-start.5 = (f32[256,256]{1,0:T(8,128)}, f32[256,256]{1,0:T(8,128)S(1)}, u32[]{:S(2)}, u32[]{:S(2)}) collective-permute-start(f32[256,256]{1,0:T(8,128)} %get-tuple-element.61), channel_id=1, source_target_pairs={{0,48},{8,56},{16,0},{24,8},{32,16},{40,24},{48,32},{56,40},{64,11... | collective-permute-start | bytes 786440 | tf_op jit(solution)/shard_map/ppermute | solution.py:29
  39.9 7.5 %collective-permute-start.6 = (f32[256,256]{1,0:T(8,128)S(1)}, f32[256,256]{1,0:T(8,128)S(1)}, u32[]{:S(2)}, u32[]{:S(2)}) collective-permute-start(f32[256,256]{1,0:T(8,128)S(1)} %add.26), channel_id=1, source_target_pairs={{0,16},{8,24},{16,32},{24,40},{32,48},{40,56},{48,0},{56,8},{64,80... | collective-permute-start | bytes 786440 | tf_op jit(solution)/shard_map/ppermute | solution.py:29
  41.0 6.5 %collective-permute-start.7 = (f32[256,256]{1,0:T(8,128)S(1)}, f32[256,256]{1,0:T(8,128)S(1)}, u32[]{:S(2)}, u32[]{:S(2)}) collective-permute-start(f32[256,256]{1,0:T(8,128)S(1)} %add.27), channel_id=1, source_target_pairs={{0,48},{8,56},{16,0},{24,8},{32,16},{40,24},{48,32},{56,40},{64,11... | collective-permute-start | bytes 786440 | tf_op jit(solution)/shard_map/ppermute | solution.py:29
  48.2 8.5 %collective-permute-start.8 = (f32[32,512]{1,0:T(8,128)S(1)}, f32[32,512]{1,0:T(8,128)S(1)}, u32[]{:S(2)}, u32[]{:S(2)}) collective-permute-start(f32[32,512]{1,0:T(8,128)S(1)} %get-tuple-element.69), channel_id=1, source_target_pairs={{0,64},{8,72},{16,80},{24,88},{32,96},{40,104},{48,112},{56,120},{... | collective-permute-start | bytes 196616 | tf_op jit(solution)/shard_map/ppermute | solution.py:29
  50.0 6.7 %collective-permute-start.9 = (f32[32,512]{1,0:T(8,128)S(1)}, f32[32,512]{1,0:T(8,128)S(1)}, u32[]{:S(2)}, u32[]{:S(2)}) collective-permute-start(f32[32,512]{1,0:T(8,128)S(1)} %get-tuple-element.70), channel_id=1, source_target_pairs={{0,192},{8,200},{16,208},{24,216},{32,224},{40,232},{48,240},{56,2... | collective-permute-start | bytes 196616 | tf_op jit(solution)/shard_map/ppermute | solution.py:29
  53.2 5.8 %collective-permute-start.10 = (f32[32,512]{1,0:T(8,128)S(1)}, f32[32,512]{1,0:T(8,128)S(1)}, u32[]{:S(2)}, u32[]{:S(2)}) collective-permute-start(f32[32,512]{1,0:T(8,128)S(1)} %get-tuple-element.71), channel_id=1, source_target_pairs={{0,64},{8,72},{16,80},{24,88},{32,96},{40,104},{48,112},{56,120},{... | collective-permute-start | bytes 196616 | tf_op jit(solution)/shard_map/ppermute | solution.py:29
  54.3 7.1 %collective-permute-start.11 = (f32[32,512]{1,0:T(8,128)S(1)}, f32[32,512]{1,0:T(8,128)S(1)}, u32[]{:S(2)}, u32[]{:S(2)}) collective-permute-start(f32[32,512]{1,0:T(8,128)S(1)} %get-tuple-element.72), channel_id=1, source_target_pairs={{0,192},{8,200},{16,208},{24,216},{32,224},{40,232},{48,240},{56,2... | collective-permute-start | bytes 196616 | tf_op jit(solution)/shard_map/ppermute | solution.py:29
  61.4 5.8 %collective-permute-start.12 = (f32[32,512]{1,0:T(8,128)S(1)}, f32[32,512]{1,0:T(8,128)S(1)}, u32[]{:S(2)}, u32[]{:S(2)}) collective-permute-start(f32[32,512]{1,0:T(8,128)S(1)} %add.28), channel_id=1, source_target_pairs={{0,64},{8,72},{16,80},{24,88},{32,96},{40,104},{48,112},{56,120},{... | collective-permute-start | bytes 196616 | tf_op jit(solution)/shard_map/ppermute | solution.py:29
  65.1 4.8 %collective-permute-start.13 = (f32[32,512]{1,0:T(8,128)S(1)}, f32[32,512]{1,0:T(8,128)S(1)}, u32[]{:S(2)}, u32[]{:S(2)}) collective-permute-start(f32[32,512]{1,0:T(8,128)S(1)} %add.29), channel_id=1, source_target_pairs={{0,192},{8,200},{16,208},{24,216},{32,224},{40,232},{48,240},{56,2... | collective-permute-start | bytes 196616 | tf_op jit(solution)/shard_map/ppermute | solution.py:29
  70.8 14.2 %all-to-all-start = ((f32[4,64,512]{2,1,0:T(8,128)}), f32[4,64,512]{2,1,0:T(8,128)S(1)}, u32[]{:S(2)}, u32[]{:S(2)}) async-start(f32[4,64,512]{2,1,0:T(8,128)} %get-tuple-element.78), calls=%async_computation | async-start | bytes 1048576 | tf_op jit(solution)/shard_map/all_to_all | solution.py:41
  74.3 5.4 %collective-permute-start.15 = (f32[64,512]{1,0:T(8,128)S(1)}, f32[64,512]{1,0:T(8,128)S(1)}, u32[]{:S(2)}, u32[]{:S(2)}) collective-permute-start(f32[64,512]{1,0:T(8,128)S(1)} %get-tuple-element.80.u0), channel_id=1, source_target_pairs={{0,32},{8,40},{16,48},{24,56},{32,0},{40,8},{48,16},{56,24},{64,96... | collective-permute-start | bytes 393224 | tf_op jit(solution)/shard_map/ppermute | solution.py:29
  76.7 5.0 %collective-permute-start.14 = (f32[64,512]{1,0:T(8,128)S(1)}, f32[64,512]{1,0:T(8,128)S(1)}, u32[]{:S(2)}, u32[]{:S(2)}) collective-permute-start(f32[64,512]{1,0:T(8,128)S(1)} %get-tuple-element.80.u0), channel_id=1, source_target_pairs={{0,16},{8,24},{16,32},{24,40},{32,48},{40,56},{48,0},{56,8},{64,80... | collective-permute-start | bytes 393224 | tf_op jit(solution)/shard_map/ppermute | solution.py:29
  85.0 20.7 %collective-permute-start.18 = (f32[256,512]{1,0:T(8,128)S(1)}, f32[256,512]{1,0:T(8,128)S(1)}, u32[]{:S(2)}, u32[]{:S(2)}) collective-permute-start(f32[256,512]{1,0:T(8,128)S(1)} %bitcast.8), channel_id=1, source_target_pairs={{0,48},{8,56},{16,0},{24,8},{32,16},{40,24},{48,32},{56,40},{64,11... | collective-permute-start | bytes 1572872 | tf_op jit(solution)/shard_map/ppermute | solution.py:29
  88.5 17.3 %collective-permute-start.17 = (f32[256,512]{1,0:T(8,128)S(1)}, f32[256,512]{1,0:T(8,128)S(1)}, u32[]{:S(2)}, u32[]{:S(2)}) collective-permute-start(f32[256,512]{1,0:T(8,128)S(1)} %bitcast.9), channel_id=1, source_target_pairs={{0,16},{8,24},{16,32},{24,40},{32,48},{40,56},{48,0},{56,8},{64,80... | collective-permute-start | bytes 1572872 | tf_op jit(solution)/shard_map/ppermute | solution.py:29
  89.7 6.8 %collective-permute-start.16 = (f32[8,3,8,128]{3,2,1,0:T(8,128)S(1)}, f32[8,3,8,128]{3,2,1,0:T(8,128)S(1)}, u32[]{:S(2)}, u32[]{:S(2)}) collective-permute-start(f32[8,3,8,128]{3,2,1,0:T(8,128)S(1)} %get-tuple-element.85), channel_id=1, source_target_pairs={{0,8},{8,0},{16,24},{24,16},{32,40},{40,32},{48,56},{56,48},{64,72... | collective-permute-start | bytes 294920 | tf_op jit(solution)/shard_map/ppermute | solution.py:29
  105.8 17.4 %copy-start.4 = (f32[256,512]{1,0:T(8,128)}, f32[256,512]{1,0:T(8,128)S(1)}, u32[]{:S(2)}) copy-start(f32[256,512]{1,0:T(8,128)S(1)} %collective-permute-done.17.m1) | copy-start | bytes 1572868
  123.1 20.6 %all-to-all-start.3 = ((f32[8,16,3,8,128]{4,3,2,1,0:T(8,128)}), f32[8,16,3,8,128]{4,3,2,1,0:T(8,128)S(1)}, u32[]{:S(2)}, u32[]{:S(2)}) async-start(f32[8,16,3,8,128]{4,3,2,1,0:T(8,128)} %broadcast_in_dim.5), calls=%async_computation.3 | async-start | bytes 3145728 | tf_op jit(solution)/shard_map/all_to_all | solution.py:41
  127.7 5.3 %collective-permute-start.20 = (f32[128,512]{1,0:T(8,128)S(1)}, f32[128,512]{1,0:T(8,128)S(1)}, u32[]{:S(2)}, u32[]{:S(2)}) collective-permute-start(f32[128,512]{1,0:T(8,128)S(1)} %slice.7), channel_id=1, source_target_pairs={{0,48},{8,56},{16,0},{24,8},{32,16},{40,24},{48,32},{56,40},{64,11... | collective-permute-start | bytes 786440 | tf_op jit(solution)/shard_map/ppermute | solution.py:29
  128.6 6.6 %collective-permute-start.19 = (f32[128,512]{1,0:T(8,128)S(1)}, f32[128,512]{1,0:T(8,128)S(1)}, u32[]{:S(2)}, u32[]{:S(2)}) collective-permute-start(f32[128,512]{1,0:T(8,128)S(1)} %slice.6), channel_id=1, source_target_pairs={{0,16},{8,24},{16,32},{24,40},{32,48},{40,56},{48,0},{56,8},{64,80... | collective-permute-start | bytes 786440 | tf_op jit(solution)/shard_map/ppermute | solution.py:29
  143.7 7.3 %collective-permute-start.21 = (f32[8,16,3,8,128]{4,3,2,1,0:T(8,128)S(1)}, f32[8,16,3,8,128]{4,3,2,1,0:T(8,128)S(1)}, u32[]{:S(2)}, u32[]{:S(2)}) collective-permute-start(f32[8,16,3,8,128]{4,3,2,1,0:T(8,128)S(1)} %all-to-all-done.3.own_ref), channel_id=1, source_target_pairs={{0,8},{8,0},{16,24},{24,16},{32,40},{40,32},{48,56},{56,48},{64,72... | collective-permute-start | bytes 4718600 | tf_op jit(solution)/shard_map/ppermute | solution.py:29
  152.0 13.9 %copy-start.5 = (f32[256,512]{1,0:T(8,128)S(1)}, f32[256,512]{1,0:T(8,128)}, u32[]{:S(2)}) copy-start(f32[256,512]{1,0:T(8,128)} %copy-done.4) | copy-start | bytes 1572868
  152.0 13.9 %copy-start.11 = (f32[128,512]{1,0:T(8,128)S(1)}, f32[128,512]{1,0:T(8,128)}, u32[]{:S(2)}) copy-start(f32[128,512]{1,0:T(8,128)} %copy-done.10) | copy-start | bytes 786436
  152.0 16.4 %copy-start.1 = (bf16[1024,1024]{1,0:T(8,128)(2,1)S(1)}, bf16[1024,1024]{1,0:T(8,128)(2,1)}, u32[]{:S(2)}) copy-start(bf16[1024,1024]{1,0:T(8,128)(2,1)} %mom.1) | copy-start | bytes 6291460
  152.0 16.4 %copy-start.3 = (f32[3,512,256]{2,1,0:T(8,128)S(1)}, f32[3,512,256]{2,1,0:T(8,128)}, u32[]{:S(2)}) copy-start(f32[3,512,256]{2,1,0:T(8,128)} %get-tuple-element.54.mine) | copy-start | bytes 4718596
  167.0 1.4 collective-permute-start.22
  (8 other events, 19.2 us)

commit v3 on v2

--- a/solution.py
+++ b/solution.py
@@ -37,12 +37,16 @@
     return on, second, first, back
 
 
+def small_ring_sum(opposite, following, before, step):
+    n = opposite[0].shape[0]
+    relay_on, relay_back = step(opposite[0], 1), step(opposite[1], -1)
+    on = step(following + jnp.pad(relay_on, ((0, n), (0, 0))), 1)
+    back = step(before + jnp.pad(relay_back, ((n, 0), (0, 0))), -1)
+    return on, back
+
+
 def exchange(x, groups, axis="dp"):
     return lax.all_to_all(x, axis, 0, 0, axis_index_groups=groups)
-
-
-def gather(x, n, groups, axis="dp"):
-    return exchange(jnp.broadcast_to(x[None], (n,) + x.shape), groups, axis)
 
 
 def params(mib, **more):
@@ -65,28 +69,18 @@
     return hi, mid, (rest - mid.astype(F32)).astype(BF16)
 
 
-def merge_kernel(turns, added, pos_ref, acts, grads, err, *refs):
+def merge_kernel(turns, own, added, pos_ref, acts, grads, err, *refs):
     sent, refs = (refs[0], refs[1:]) if added else (None, refs)
-    out_ref, refs = refs[0], refs[1:]
-    sums, refs = (refs[:2 * len(turns)], refs[2 * len(turns):]) if added else ((), refs)
-    x_buf, k_buf, e_buf, sems = refs
-    half, y = pos_ref[0], pos_ref[1]
-    tok, d = x_buf.shape
-    at_d = pl.ds(pl.multiple_of(half * d, 128), d)
-    copies = [pltpu.make_async_copy(acts.at[:, at_d], x_buf, sems.at[0])]
+    out_ref, sums = refs[0], refs[1:]
+    half = pos_ref[0] if own else 1 - pos_ref[0]
+    d = acts.shape[1] // 2
+    at_d = pl.ds(pl.multiple_of(half * d, 512), d)
+    factor = 1.0 / math.sqrt(acts.shape[0])
+    x = acts[:, at_d]
     for n, turn in enumerate(turns):
-        cols = pl.ds(pl.multiple_of((y + turn) % 4 * 256, 128), 256)
-        copies.append(pltpu.make_async_copy(grads.at[:, cols], k_buf.at[n], sems.at[1 + 2 * n]))
-        copies.append(pltpu.make_async_copy(err.at[0, at_d, cols], e_buf.at[n], sems.at[2 + 2 * n]))
-    for copy in copies:
-        copy.start()
-    copies[0].wait()
-    factor = 1.0 / math.sqrt(tok)
-    for n in range(len(turns)):
-        copies[1 + 2 * n].wait()
-        product = lax.dot_general(x_buf[...], k_buf[n], ROWS, preferred_element_type=F32)
-        copies[2 + 2 * n].wait()
-        merged = product * factor + e_buf[n].astype(F32)
+        cols = pl.ds(pl.multiple_of((pos_ref[1] + turn) % 4 * 256, 256), 256)
+        product = lax.dot_general(x, grads[:, cols], ROWS, preferred_element_type=F32)
+        merged = product * factor + err[0, at_d, cols].astype(F32)
         out_ref[n] = merged
         if added:
             total = merged + sent[n]
@@ -94,52 +88,48 @@
             sums[2 * n + 1][...] = total[d // 2:]
 
 
-def merge(half, y, turns, inputs, key_grads, error, sent=None):
+def merge(pos, own, turns, inputs, key_grads, error, sent=None):
     tok, d = inputs.shape
     d = d // 2
     n = len(turns)
     added = sent is not None
-    in_hbm = pl.BlockSpec(memory_space=pltpu.HBM)
     outs = [jax.ShapeDtypeStruct((n, d, 256), F32)]
     if added:
         outs += [jax.ShapeDtypeStruct((d // 2, 256), F32)] * (2 * n)
     result = pl.pallas_call(
-        functools.partial(merge_kernel, turns, added),
+        functools.partial(merge_kernel, turns, own, added),
         out_shape=tuple(outs),
-        in_specs=[SMEM] + [in_hbm] * 3 + [VMEM] * added,
+        in_specs=[SMEM] + [VMEM] * (3 + added),
         out_specs=(VMEM,) * len(outs),
-        scratch_shapes=[
-            pltpu.VMEM((tok, d), BF16),
-            pltpu.VMEM((n, tok, 256), BF16),
-            pltpu.VMEM((n, d, 256), BF16),
-            pltpu.SemaphoreType.DMA((1 + 2 * n,)),
-        ],
-        compiler_params=params(58),
+        compiler_params=params(24),
         cost_estimate=cost(2 * tok * d * 256 * n, (1 + 2 * n) << 19),
         name="merge",
-    )(jnp.stack([half, y]), inputs, key_grads, error, *([sent] if added else []))
+    )(pos, inputs, key_grads, error, *([sent] if added else []))
     return result[0], list(result[1:])
 
 
-def sum_turn_kernel(pos_ref, top, end, on, second, first, back, *refs):
-    outs, own_ref, turned = refs[:6], refs[6], refs[7]
+def sum_turn_kernel(pos_ref, top, end, on, second, first, back, opp_top, opp_end, after, before, own, turned):
     turned[:, :256] = (top[...] + (on[...] + first[...])).T
     turned[:, 256:] = (end[...] + (second[...] + back[...])).T
     z = pos_ref[2]
-    for n, turn in enumerate((2, 1, 3)):
-        at = (z + turn) % 4 * 64
-        for h in range(2):
-            outs[2 * n + h][...] = turned[pl.ds(pl.multiple_of(at + 32 * h, 32), 32), :]
-    own_ref[...] = turned[pl.ds(pl.multiple_of(z * 64, 64), 64), :]
+
+    def rows(turn, start, size):
+        return turned[pl.ds(pl.multiple_of((z + turn) % 4 * 64 + start, 32), size), :]
+
+    opp_top[...] = rows(2, 0, 32)
+    opp_end[...] = rows(2, 32, 32)
+    after[...] = rows(1, 0, 64)
+    before[...] = rows(3, 0, 64)
+    own[...] = rows(0, 0, 64)
 
 
 def sum_turn(pos, top, end, came):
-    half = jax.ShapeDtypeStruct((32, 512), F32)
+    outs = tuple(jax.ShapeDtypeStruct((n, 512), F32) for n in (32, 32, 64, 64, 64))
     return pl.pallas_call(
         sum_turn_kernel,
-        out_shape=(half,) * 6 + (jax.ShapeDtypeStruct((64, 512), F32),),
+        out_shape=outs,
         in_specs=[SMEM] + [VMEM] * 6,
-        out_specs=(VMEM,) * 7,
+        out_specs=(VMEM,) * 5,
         scratch_shapes=[pltpu.VMEM((256, 512), F32)],
         compiler_params=params(24),
         cost_estimate=cost(4 << 17, 3 << 20),
@@ -147,25 +137,31 @@
     )(pos, top, end, *came)
 
 
-def unit_kernel(own, on, second, first, back, unit_ref, copies_ref):
-    for h, (a, b) in enumerate(((on, first), (second, back))):
-        rows = pl.ds(32 * h, 32)
-        total = own[rows, :] + (a[...] + b[...])
-        unit_ref[rows, :] = total
-        for z in range(4):
-            copies_ref[z, rows, :] = total
-
-
-def make_unit(own, came):
-    return pl.pallas_call(
-        unit_kernel,
-        out_shape=(jax.ShapeDtypeStruct((64, 512), F32), jax.ShapeDtypeStruct((4, 64, 512), F32)),
-        in_specs=[VMEM] * 5,
-        out_specs=(VMEM, VMEM),
+def spread_kernel(leading, keep, *refs):
+    refs, outs = refs[:-1 - keep], refs[-1 - keep:]
+    terms = [refs[0][i] for i in range(refs[0].shape[0])] if leading else [ref[...] for ref in refs]
+    total = terms[0]
+    for term in terms[1:]:
+        total = total + term
+    copies_ref = outs[0]
+    for i in range(copies_ref.shape[0]):
+        copies_ref[i] = total
+    if keep:
+        outs[1][...] = total
+
+
+def spread(parts, copies, leading=False, keep=False):
+    shape = parts[0].shape[1:] if leading else parts[0].shape
+    outs = (jax.ShapeDtypeStruct((copies,) + shape, F32), jax.ShapeDtypeStruct(shape, F32))[:1 + keep]
+    return pl.pallas_call(
+        functools.partial(spread_kernel, leading, keep),
+        out_shape=outs,
+        in_specs=[VMEM] * len(parts),
+        out_specs=(VMEM,) * len(outs),
         compiler_params=params(24),
         cost_estimate=cost(1 << 17, 1 << 20),
-        name="make_unit",
-    )(own, *came)
+        name="spread",
+    )(*parts)
 
 
 def block_kernel(pos_ref, u0, u1, u2, of_y, sent_ref, mine_ref):
@@ -222,16 +218,18 @@
         for k in range(8):
             pivot = jnp.broadcast_to(c[t, k][k:k + 1], (8, 2 * n))
             pivots = jnp.where(sub == k, pivot, pivots)
-            turn = 1.0 / pivot
+            turn = pl.reciprocal(pivot, approx=True)
+            turn = turn + turn * (1.0 - pivot * turn)
+            turn = turn + turn * (1.0 - pivot * turn)
             lead = jnp.broadcast_to(b[t][k:k + 1], (8, 2 * n))
             heads = {l: jnp.broadcast_to(c[t, l][k:k + 1], (8, 2 * n)) for l in range(k + 1, 8)}
             for r in range(t, tiles):
                 m = c[r, k] * turn
+                for l in range(k + 1, 8):
+                    c[r, l] = c[r, l] - m * heads[l]
                 if r == t:
                     m = jnp.where(sub > k, m, 0.0)
                 b[r] = b[r] - m * lead
-                for l in range(k + 1, 8):
-                    c[r, l] = c[r, l] - m * heads[l]
         out.append(b[t] / jnp.sqrt(pivots))
     return jnp.concatenate(out, axis=0)[:, n:]
 
@@ -410,17 +408,17 @@
     pos = jnp.stack([c, y, z])
 
     args = (inputs, key_grads, error)
-    other_opp, _ = merge(1 - c, y, TURNS[:1], *args)
-    other_opp, away_core = lax.optimization_barrier((other_opp, 1 - c))
+    other_opp, _ = merge(pos, False, TURNS[:1], *args)
+    other_opp, pos = lax.optimization_barrier((other_opp, pos))
     sent_opp = dp_shift(other_opp, dc=1)
-    other, _ = merge(away_core, y, TURNS[1:], *args)
+    other, _ = merge(pos, False, TURNS[1:], *args)
     sent = dp_shift(other, dc=1)
-    mine_opp, opposite = merge(c, y, TURNS[:1], *args, sent_opp)
-    mine, sums = merge(c, y, TURNS[1:], *args, sent)
+    mine_opp, opposite = merge(pos, True, TURNS[:1], *args, sent_opp)
+    mine, sums = merge(pos, True, TURNS[1:], *args, sent)
     came = ring_sum(opposite, sums[0:2], sums[2:4], lambda x, d: dp_shift(x, dy=d))
-    *cut, own = sum_turn(pos, *sums[4:6], came)
-    came = ring_sum(cut[0:2], cut[2:4], cut[4:6], lambda x, d: dp_shift(x, dz=d))
-    unit, copies = make_unit(own, came)
+    *opposite, after, before, own = sum_turn(pos, *sums[4:6], came)
+    came = small_ring_sum(opposite, after, before, lambda x, d: dp_shift(x, dz=d))
+    copies, unit = spread([own, *came], 4, keep=True)
     units = [unit] + [dp_shift(unit, dy=dy) for dy in (1, 2)]
     of_y = exchange(copies, Z_GROUPS).reshape(256, 512)
     of_y, *units = lax.optimization_barrier((of_y, *units))
@@ -428,12 +426,12 @@
     to_core, part = g_block(pos, units, of_y)
     part = part + dp_shift(to_core, dc=1)
     m1, m3 = dp_shift(of_y, dy=1), dp_shift(of_y, dy=-1)
-    part = exchange(part, None, "shard").sum(axis=0)
-    part, m1, m3 = lax.optimization_barrier((part, m1, m3))
-    part = gather(part, 16, ZY_GROUPS)
+    (copies,) = spread([exchange(part, None, "shard")], 16, leading=True)
+    copies, m1, m3 = lax.optimization_barrier((copies, m1, m3))
+    part = exchange(copies, ZY_GROUPS)
     part, m1, m3 = lax.optimization_barrier((part, m1, m3))
     m2_top, m2_end = dp_shift(m1[:128], dy=1), dp_shift(m3[128:], dy=-1)
-    part = gather(part, 8, None, "shard")
+    part = exchange(spread([part], 8)[0], None, "shard")
     part, m2_top, m2_end = lax.optimization_barrier((part, m2_top, m2_end))
     q_t, w = iterate(pos, part, dp_shift(part, dc=1), q_start.T)
 

time: 173 us -> 164 us (0.948)
  Pallas kernels: 38.7 us -> 30.6 us
  starting transfers between devices: 50.8 us -> 46.5 us
  waiting for transfers between devices: 47.2 us -> 51.5 us
  other arithmetic: 3.89 us -> 0.19 us
  local copies, waits for them, and re-layouts: 5.87 us -> 8.3 us
    pallas_call x6 -> x8, Pallas kernels: 18.3 us -> 7.16 us  [the longest x4 4.28 us: merge(): pl.pallas_call(functools.partial(merge_kernel, turns, own, added), out_sh...]
    ppermute x23 -> x21, starting transfers between devices: 43.7 us -> 38.7 us  [dp_shift(): return lax.ppermute(x, 'dp', pairs)]
    unnamed x30 -> x28, local copies, waits for them, and re-layouts: 3.62 us -> 7.31 us
    ppermute x23 -> x21, waiting for transfers between devices: 36.1 us -> 39.7 us  [dp_shift(): return lax.ppermute(x, 'dp', pairs)]
    pallas_call x1, Pallas kernels: 13.8 us -> 16.9 us  [iterate(): pl.pallas_call(iterate_kernel, out_shape=(jax.ShapeDtypeStruct(q.shape, F...]
    another operation x3 -> x0, other arithmetic: 1.8 us -> none  [merge(): jnp.stack([half, y])]
  transfers between devices with their start and end apart: 25 -> 23, of which waited for: 16 -> 16; matrix products, arithmetic and copies ran while one was open for 2% -> 1% of each run, Pallas kernels for 6% -> 2%
where the time goes in v3:
time: 164 us
  waiting for transfers between devices  51.5 us (31%)
  starting transfers between devices  46.5 us (28%)
  Pallas kernels  30.6 us (19%)
  blocking collectives  25.8 us (16%)
  local copies, waits for them, and re-layouts  8.3 us (5%)
    ppermute x21, waiting for transfers between devices, dp_shift(): return lax.ppermute(x, 'dp', pairs)  39.7 us
    ppermute x21, starting transfers between devices, dp_shift(): return lax.ppermute(x, 'dp', pairs)  38.7 us
    all_to_all x2, blocking collectives, exchange(): return lax.all_to_all(x, axis, 0, 0, axis_index_groups=groups)  25.8 us
    pallas_call x1, Pallas kernels, iterate(): pl.pallas_call(iterate_kernel, out_shape=(jax.ShapeDtypeStruct(q.shape, F...  16.9 us
    all_to_all x2, waiting for transfers between devices, exchange(): return lax.all_to_all(x, axis, 0, 0, axis_index_groups=groups)  11.8 us
    all_to_all x2, starting transfers between devices, exchange(): return lax.all_to_all(x, axis, 0, 0, axis_index_groups=groups)  7.77 us
    unnamed x28, local copies, waits for them, and re-layouts  7.31 us
    pallas_call x4, Pallas kernels, merge(): pl.pallas_call(functools.partial(merge_kernel, turns, own, added), out_sh...  4.28 us
  transfers between devices with their start and end apart: 23, of which 16 were waited for; matrix products, arithmetic and copies ran while one was open for 1% of the time, Pallas kernels for 2%

profile of v3, /device:TPU:1, one launch (start us, length us, event | category | flops | bytes accessed | tf_op | source)
XLA Modules:
  0.0 163.8 jit_solution(3125151703596429188)
XLA Ops:
  0.7 1.6 copy-done
  6.9 3.3 %collective-permute-start.1 = (f32[3,512,256]{2,1,0:T(8,128)S(1)}, f32[3,512,256]{2,1,0:T(8,128)S(1)}, u32[]{:S(2)}, u32[]{:S(2)}) collective-permute-start(f32[3,512,256]{2,1,0:T(8,128)S(1)} %merge.6.other), channel_id=1, source_target_pairs={{0,8},{8,0},{16,24},{24,16},{32,40},{40,32},{48,56},{56,48},{64,72... | collective-permute-start | bytes 4718600 | tf_op jit(solution)/shard_map/ppermute | solution.py:29
  10.4 3.7 %collective-permute-done.refs_0_ = f32[1,512,256]{2,1,0:T(8,128)S(1)} collective-permute-done((f32[1,512,256]{2,1,0:T(8,128)S(1)}, f32[1,512,256]{2,1,0:T(8,128)S(1)}, u32[]{:S(2)}, u32[]{:S(2)}) %collective-permute-start) | collective-permute-done | bytes 524320 | tf_op jit(solution)/shard_map/ppermute | solution.py:29
  15.8 2.7 %collective-permute-start.3 = (f32[256,256]{1,0:T(8,128)S(1)}, f32[256,256]{1,0:T(8,128)S(1)}, u32[]{:S(2)}, u32[]{:S(2)}) collective-permute-start(f32[256,256]{1,0:T(8,128)S(1)} %get-tuple-element.53), channel_id=1, source_target_pairs={{0,48},{8,56},{16,0},{24,8},{32,16},{40,24},{48,32},{56,40},{64,11... | collective-permute-start | bytes 786440 | tf_op jit(solution)/shard_map/ppermute | solution.py:29
  19.8 2.7 %collective-permute-start.5 = (f32[256,256]{1,0:T(8,128)S(1)}, f32[256,256]{1,0:T(8,128)S(1)}, u32[]{:S(2)}, u32[]{:S(2)}) collective-permute-start(f32[256,256]{1,0:T(8,128)S(1)} %get-tuple-element.55), channel_id=1, source_target_pairs={{0,48},{8,56},{16,0},{24,8},{32,16},{40,24},{48,32},{56,40},{64,11... | collective-permute-start | bytes 786440 | tf_op jit(solution)/shard_map/ppermute | solution.py:29
  22.5 2.1 %collective-permute-done.2 = f32[256,256]{1,0:T(8,128)S(1)} collective-permute-done((f32[256,256]{1,0:T(8,128)S(1)}, f32[256,256]{1,0:T(8,128)S(1)}, u32[]{:S(2)}, u32[]{:S(2)}) %collective-permute-start.2) | collective-permute-done | bytes 262176 | tf_op jit(solution)/shard_map/ppermute | solution.py:29
  24.5 5.6 %collective-permute-done.4.second = f32[256,256]{1,0:T(8,128)S(1)} collective-permute-done((f32[256,256]{1,0:T(8,128)S(1)}, f32[256,256]{1,0:T(8,128)S(1)}, u32[]{:S(2)}, u32[]{:S(2)}) %collective-permute-start.4) | collective-permute-done | bytes 262176 | tf_op jit(solution)/shard_map/ppermute | solution.py:29
  30.3 2.7 %collective-permute-start.7 = (f32[256,256]{1,0:T(8,128)S(1)}, f32[256,256]{1,0:T(8,128)S(1)}, u32[]{:S(2)}, u32[]{:S(2)}) collective-permute-start(f32[256,256]{1,0:T(8,128)S(1)} %add.31), channel_id=1, source_target_pairs={{0,48},{8,56},{16,0},{24,8},{32,16},{40,24},{48,32},{56,40},{64,11... | collective-permute-start | bytes 786440 | tf_op jit(solution)/shard_map/ppermute | solution.py:29
  33.1 5.0 %collective-permute-done.6.on = f32[256,256]{1,0:T(8,128)S(1)} collective-permute-done((f32[256,256]{1,0:T(8,128)S(1)}, f32[256,256]{1,0:T(8,128)S(1)}, u32[]{:S(2)}, u32[]{:S(2)}) %collective-permute-start.6) | collective-permute-done | bytes 262176 | tf_op jit(solution)/shard_map/ppermute | solution.py:29
  38.9 4.5 %collective-permute-start.10 = (f32[32,512]{1,0:T(8,128)S(1)}, f32[32,512]{1,0:T(8,128)S(1)}, u32[]{:S(2)}, u32[]{:S(2)}) collective-permute-start(f32[32,512]{1,0:T(8,128)S(1)} %get-tuple-element.65), channel_id=1, source_target_pairs={{0,192},{8,200},{16,208},{24,216},{32,224},{40,232},{48,240},{56,2... | collective-permute-start | bytes 196616 | tf_op jit(solution)/shard_map/ppermute | solution.py:29
  43.4 1.3 collective-permute-done.10
  44.7 4.5 %collective-permute-start.11 = (f32[64,512]{1,0:T(8,128)S(1)}, f32[64,512]{1,0:T(8,128)S(1)}, u32[]{:S(2)}, u32[]{:S(2)}) collective-permute-start(f32[64,512]{1,0:T(8,128)S(1)} %pad_add_fusion), channel_id=1, source_target_pairs={{0,192},{8,200},{16,208},{24,216},{32,224},{40,232},{48,240},{56,2... | collective-permute-start | bytes 393224 | tf_op jit(solution)/shard_map/ppermute | solution.py:29
  49.4 3.2 %collective-permute-done.11.refs_2_ = f32[64,512]{1,0:T(8,128)S(1)} collective-permute-done((f32[64,512]{1,0:T(8,128)S(1)}, f32[64,512]{1,0:T(8,128)S(1)}, u32[]{:S(2)}, u32[]{:S(2)}) %collective-permute-start.11) | collective-permute-done | bytes 131104 | tf_op jit(solution)/shard_map/ppermute | solution.py:29
  52.6 3.5 %collective-permute-done.9.refs_1_ = f32[64,512]{1,0:T(8,128)S(1)} collective-permute-done((f32[64,512]{1,0:T(8,128)S(1)}, f32[64,512]{1,0:T(8,128)S(1)}, u32[]{:S(2)}, u32[]{:S(2)}) %collective-permute-start.9) | collective-permute-done | bytes 131104 | tf_op jit(solution)/shard_map/ppermute | solution.py:29
  56.9 3.5 %all-to-all-start = ((f32[4,64,512]{2,1,0:T(8,128)}), f32[4,64,512]{2,1,0:T(8,128)S(1)}, u32[]{:S(2)}, u32[]{:S(2)}) async-start(f32[4,64,512]{2,1,0:T(8,128)} %get-tuple-element.66), calls=%async_computation | async-start | bytes 1048576 | tf_op jit(solution)/shard_map/all_to_all | solution.py:49
  60.4 1.5 collective-permute-start.13
  63.2 2.7 %collective-permute-done.13.u2 = f32[64,512]{1,0:T(8,128)S(1)} collective-permute-done((f32[64,512]{1,0:T(8,128)S(1)}, f32[64,512]{1,0:T(8,128)S(1)}, u32[]{:S(2)}, u32[]{:S(2)}) %collective-permute-start.13) | collective-permute-done | bytes 131104 | tf_op jit(solution)/shard_map/ppermute | solution.py:29
  65.8 1.4 collective-permute-done.12.u1
  67.2 4.0 %all-to-all-done = f32[4,64,512]{2,1,0:T(8,128)S(1)} async-done(((f32[4,64,512]{2,1,0:T(8,128)}), f32[4,64,512]{2,1,0:T(8,128)S(1)}, u32[]{:S(2)}, u32[]{:S(2)}) %all-to-all-start) | async-done | bytes 524320 | tf_op jit(solution)/shard_map/all_to_all | solution.py:49
  71.2 2.0 %collective-permute-start.16 = (f32[256,512]{1,0:T(8,128)S(1)}, f32[256,512]{1,0:T(8,128)S(1)}, u32[]{:S(2)}, u32[]{:S(2)}) collective-permute-start(f32[256,512]{1,0:T(8,128)S(1)} %bitcast.6), channel_id=1, source_target_pairs={{0,48},{8,56},{16,0},{24,8},{32,16},{40,24},{48,32},{56,40},{64,11... | collective-permute-start | bytes 1572872 | tf_op jit(solution)/shard_map/ppermute | solution.py:29
  74.5 6.9 %collective-permute-start.14 = (f32[8,3,8,128]{3,2,1,0:T(8,128)S(1)}, f32[8,3,8,128]{3,2,1,0:T(8,128)S(1)}, u32[]{:S(2)}, u32[]{:S(2)}) collective-permute-start(f32[8,3,8,128]{3,2,1,0:T(8,128)S(1)} %get-tuple-element.73), channel_id=1, source_target_pairs={{0,8},{8,0},{16,24},{24,16},{32,40},{40,32},{48,56},{56,48},{64,72... | collective-permute-start | bytes 294920 | tf_op jit(solution)/shard_map/ppermute | solution.py:29
  82.3 10.3 %all_to_all.20.refs_0_ = f32[8,3,8,128]{3,2,1,0:T(8,128)S(1)} all-to-all(f32[8,3,8,128]{3,2,1,0:T(8,128)S(1)} %add.34), channel_id=1, replica_groups=mesh['dp'=32,'shard'=8] {'shard'}, dimensions={0} | all-to-all | bytes 196608 | tf_op jit(solution)/shard_map/all_to_all | solution.py:49
  93.4 15.6 %all_to_all.21.refs_0_ = f32[16,3,8,128]{3,2,1,0:T(8,128)S(1)} all-to-all(f32[16,3,8,128]{3,2,1,0:T(8,128)S(1)} %spread.4), channel_id=1, replica_groups={{0,16,32,48,64,80,96,112,128,144,160,176,192,208,224,240},{8,24,40,56,7..., dimensions={0} | all-to-all | bytes 393216 | tf_op jit(solution)/shard_map/all_to_all | solution.py:49
  109.0 1.2 spread.5
  110.3 4.3 %all-to-all-start.3 = ((f32[8,16,3,8,128]{4,3,2,1,0:T(8,128)}), f32[8,16,3,8,128]{4,3,2,1,0:T(8,128)}, u32[]{:S(2)}, u32[]{:S(2)}) async-start(f32[8,16,3,8,128]{4,3,2,1,0:T(8,128)} %spread.5), calls=%async_computation.3 | async-start | bytes 3145728 | tf_op jit(solution)/shard_map/all_to_all | solution.py:49
  117.1 3.8 %collective-permute-done.18.m2_end = f32[128,512]{1,0:T(8,128)S(1)} collective-permute-done((f32[128,512]{1,0:T(8,128)S(1)}, f32[128,512]{1,0:T(8,128)S(1)}, u32[]{:S(2)}, u32[]{:S(2)}) %collective-permute-start.18) | collective-permute-done | bytes 262176 | tf_op jit(solution)/shard_map/ppermute | solution.py:29
  120.9 2.3 %collective-permute-done.17.m2_top = f32[128,512]{1,0:T(8,128)S(1)} collective-permute-done((f32[128,512]{1,0:T(8,128)S(1)}, f32[128,512]{1,0:T(8,128)S(1)}, u32[]{:S(2)}, u32[]{:S(2)}) %collective-permute-start.17) | collective-permute-done | bytes 262176 | tf_op jit(solution)/shard_map/ppermute | solution.py:29
  123.8 7.8 %all-to-all-done.3.own_ref = f32[8,16,3,8,128]{4,3,2,1,0:T(8,128)} async-done(((f32[8,16,3,8,128]{4,3,2,1,0:T(8,128)}), f32[8,16,3,8,128]{4,3,2,1,0:T(8,128)}, u32[]{:S(2)}, u32[]{:S(2)}) %all-to-all-start.3) | async-done | bytes 1572896 | tf_op jit(solution)/shard_map/all_to_all | solution.py:49
  131.6 4.3 %collective-permute-start.19 = (f32[8,16,3,8,128]{4,3,2,1,0:T(8,128)}, f32[8,16,3,8,128]{4,3,2,1,0:T(8,128)S(1)}, u32[]{:S(2)}, u32[]{:S(2)}) collective-permute-start(f32[8,16,3,8,128]{4,3,2,1,0:T(8,128)} %all-to-all-done.3.own_ref), channel_id=1, source_target_pairs={{0,8},{8,0},{16,24},{24,16},{32,40},{40,32},{48,56},{56,48},{64,72... | collective-permute-start | bytes 4718600 | tf_op jit(solution)/shard_map/ppermute | solution.py:29
  135.9 3.2 %collective-permute-done.19.away_ref = f32[8,16,3,8,128]{4,3,2,1,0:T(8,128)S(1)} collective-permute-done((f32[8,16,3,8,128]{4,3,2,1,0:T(8,128)}, f32[8,16,3,8,128]{4,3,2,1,0:T(8,128)S(1)}, u32[]{:S(2)}, u32[]{:S(2)}) %collective-permute-start.19) | collective-permute-done | bytes 1572896 | tf_op jit(solution)/shard_map/ppermute | solution.py:29
  140.1 16.9 %iterations.1 = (f32[64,1024]{1,0:T(8,128)}, f32[64,1024]{1,0:T(8,128)S(1)}) custom-call(s32[3]{0:T(128)S(1)} %pad_add_fusion.2.pos_ref, f32[8,16,3,8,128]{4,3,2,1,0:T(8,128)} %all-to-all-done.3.own_ref, f32[8,16,3,8,128]{4,3,2,1,0:T(8,128)S(1)} %collective-permute-done.19.away_ref, f32[64,1024]{1,0:T(8,128)S(1)} %bitcast.11), custom_call_target="tpu_custom_call" | custom-call | flops 2415919104 | bytes 4194304 | tf_op jit(solution)/shard_map/iterations/pallas_call | solution.py:288
  159.6 4.2 %finish.1 = (bf16[1,1024,1024]{2,1,0:T(8,128)(2,1)}, bf16[1024,1024]{1,0:T(8,128)(2,1)}) custom-call(s32[3]{0:T(128)S(1)} %pad_add_fusion.2.pos_ref, f32[1,512,256]{2,1,0:T(8,128)S(1)} %copy-done.9, f32[3,512,256]{2,1,0:T(8,128)S(1)} %copy-done.5, f32[1,512,256]{2,1,0:T(8,128)S(1)} %merge.4.other_opp, f32[3,512,256]{2,1,0:T(8,128)S(1)} %merge.6.other, ...), custom_call_target="tpu_custom_call" | custom-call | flops 536870912 | bytes 10485760 | tf_op jit(solution)/shard_map/finish/pallas_call | solution.py:377
  (64 shorter events, 20.7 us)
Async XLA Ops:
  0.7 1.6 copy-start
  2.3 1.2 copy-start.1
  6.9 11.5 %collective-permute-start.1 = (f32[3,512,256]{2,1,0:T(8,128)S(1)}, f32[3,512,256]{2,1,0:T(8,128)S(1)}, u32[]{:S(2)}, u32[]{:S(2)}) collective-permute-start(f32[3,512,256]{2,1,0:T(8,128)S(1)} %merge.6.other), channel_id=1, source_target_pairs={{0,8},{8,0},{16,24},{24,16},{32,40},{40,32},{48,56},{56,48},{64,72... | collective-permute-start | bytes 4718600 | tf_op jit(solution)/shard_map/ppermute | solution.py:29
  10.3 3.8 %collective-permute-start = (f32[1,512,256]{2,1,0:T(8,128)S(1)}, f32[1,512,256]{2,1,0:T(8,128)S(1)}, u32[]{:S(2)}, u32[]{:S(2)}) collective-permute-start(f32[1,512,256]{2,1,0:T(8,128)S(1)} %merge.4.other_opp), channel_id=1, source_target_pairs={{0,8},{8,0},{16,24},{24,16},{32,40},{40,32},{48,56},{56,48},{64,72... | collective-permute-start | bytes 1572872 | tf_op jit(solution)/shard_map/ppermute | solution.py:29
  15.8 8.7 %collective-permute-start.2 = (f32[256,256]{1,0:T(8,128)S(1)}, f32[256,256]{1,0:T(8,128)S(1)}, u32[]{:S(2)}, u32[]{:S(2)}) collective-permute-start(f32[256,256]{1,0:T(8,128)S(1)} %get-tuple-element.52), channel_id=1, source_target_pairs={{0,16},{8,24},{16,32},{24,40},{32,48},{40,56},{48,0},{56,8},{64,80... | collective-permute-start | bytes 786440 | tf_op jit(solution)/shard_map/ppermute | solution.py:29
  15.8 8.7 %collective-permute-start.3 = (f32[256,256]{1,0:T(8,128)S(1)}, f32[256,256]{1,0:T(8,128)S(1)}, u32[]{:S(2)}, u32[]{:S(2)}) collective-permute-start(f32[256,256]{1,0:T(8,128)S(1)} %get-tuple-element.53), channel_id=1, source_target_pairs={{0,48},{8,56},{16,0},{24,8},{32,16},{40,24},{48,32},{56,40},{64,11... | collective-permute-start | bytes 786440 | tf_op jit(solution)/shard_map/ppermute | solution.py:29
  19.7 19.2 %copy-start.4 = (f32[3,512,256]{2,1,0:T(8,128)}, f32[3,512,256]{2,1,0:T(8,128)S(1)}, u32[]{:S(2)}) copy-start(f32[3,512,256]{2,1,0:T(8,128)S(1)} %get-tuple-element.48.mine) | copy-start | bytes 4718596
  19.7 10.4 %collective-permute-start.4 = (f32[256,256]{1,0:T(8,128)S(1)}, f32[256,256]{1,0:T(8,128)S(1)}, u32[]{:S(2)}, u32[]{:S(2)}) collective-permute-start(f32[256,256]{1,0:T(8,128)S(1)} %get-tuple-element.54), channel_id=1, source_target_pairs={{0,16},{8,24},{16,32},{24,40},{32,48},{40,56},{48,0},{56,8},{64,80... | collective-permute-start | bytes 786440 | tf_op jit(solution)/shard_map/ppermute | solution.py:29
  19.8 10.3 %collective-permute-start.5 = (f32[256,256]{1,0:T(8,128)S(1)}, f32[256,256]{1,0:T(8,128)S(1)}, u32[]{:S(2)}, u32[]{:S(2)}) collective-permute-start(f32[256,256]{1,0:T(8,128)S(1)} %get-tuple-element.55), channel_id=1, source_target_pairs={{0,48},{8,56},{16,0},{24,8},{32,16},{40,24},{48,32},{56,40},{64,11... | collective-permute-start | bytes 786440 | tf_op jit(solution)/shard_map/ppermute | solution.py:29
  30.2 7.9 %collective-permute-start.6 = (f32[256,256]{1,0:T(8,128)S(1)}, f32[256,256]{1,0:T(8,128)S(1)}, u32[]{:S(2)}, u32[]{:S(2)}) collective-permute-start(f32[256,256]{1,0:T(8,128)S(1)} %add.30), channel_id=1, source_target_pairs={{0,16},{8,24},{16,32},{24,40},{32,48},{40,56},{48,0},{56,8},{64,80... | collective-permute-start | bytes 786440 | tf_op jit(solution)/shard_map/ppermute | solution.py:29
  30.3 7.8 %collective-permute-start.7 = (f32[256,256]{1,0:T(8,128)S(1)}, f32[256,256]{1,0:T(8,128)S(1)}, u32[]{:S(2)}, u32[]{:S(2)}) collective-permute-start(f32[256,256]{1,0:T(8,128)S(1)} %add.31), channel_id=1, source_target_pairs={{0,48},{8,56},{16,0},{24,8},{32,16},{40,24},{48,32},{56,40},{64,11... | collective-permute-start | bytes 786440 | tf_op jit(solution)/shard_map/ppermute | solution.py:29
  38.9 5.8 %collective-permute-start.10 = (f32[32,512]{1,0:T(8,128)S(1)}, f32[32,512]{1,0:T(8,128)S(1)}, u32[]{:S(2)}, u32[]{:S(2)}) collective-permute-start(f32[32,512]{1,0:T(8,128)S(1)} %get-tuple-element.65), channel_id=1, source_target_pairs={{0,192},{8,200},{16,208},{24,216},{32,224},{40,232},{48,240},{56,2... | collective-permute-start | bytes 196616 | tf_op jit(solution)/shard_map/ppermute | solution.py:29
  43.4 5.9 %collective-permute-start.8 = (f32[32,512]{1,0:T(8,128)S(1)}, f32[32,512]{1,0:T(8,128)S(1)}, u32[]{:S(2)}, u32[]{:S(2)}) collective-permute-start(f32[32,512]{1,0:T(8,128)S(1)} %get-tuple-element.63), channel_id=1, source_target_pairs={{0,64},{8,72},{16,80},{24,88},{32,96},{40,104},{48,112},{56,120},{... | collective-permute-start | bytes 196616 | tf_op jit(solution)/shard_map/ppermute | solution.py:29
  44.7 7.8 %collective-permute-start.11 = (f32[64,512]{1,0:T(8,128)S(1)}, f32[64,512]{1,0:T(8,128)S(1)}, u32[]{:S(2)}, u32[]{:S(2)}) collective-permute-start(f32[64,512]{1,0:T(8,128)S(1)} %pad_add_fusion), channel_id=1, source_target_pairs={{0,192},{8,200},{16,208},{24,216},{32,224},{40,232},{48,240},{56,2... | collective-permute-start | bytes 393224 | tf_op jit(solution)/shard_map/ppermute | solution.py:29
  49.3 6.8 %collective-permute-start.9 = (f32[64,512]{1,0:T(8,128)S(1)}, f32[64,512]{1,0:T(8,128)S(1)}, u32[]{:S(2)}, u32[]{:S(2)}) collective-permute-start(f32[64,512]{1,0:T(8,128)S(1)} %pad_add_fusion.1), channel_id=1, source_target_pairs={{0,64},{8,72},{16,80},{24,88},{32,96},{40,104},{48,112},{56,120},{... | collective-permute-start | bytes 393224 | tf_op jit(solution)/shard_map/ppermute | solution.py:29
  56.9 14.3 %all-to-all-start = ((f32[4,64,512]{2,1,0:T(8,128)}), f32[4,64,512]{2,1,0:T(8,128)S(1)}, u32[]{:S(2)}, u32[]{:S(2)}) async-start(f32[4,64,512]{2,1,0:T(8,128)} %get-tuple-element.66), calls=%async_computation | async-start | bytes 1048576 | tf_op jit(solution)/shard_map/all_to_all | solution.py:49
  60.4 5.4 %collective-permute-start.13 = (f32[64,512]{1,0:T(8,128)S(1)}, f32[64,512]{1,0:T(8,128)S(1)}, u32[]{:S(2)}, u32[]{:S(2)}) collective-permute-start(f32[64,512]{1,0:T(8,128)S(1)} %get-tuple-element.68.u0), channel_id=1, source_target_pairs={{0,32},{8,40},{16,48},{24,56},{32,0},{40,8},{48,16},{56,24},{64,96... | collective-permute-start | bytes 393224 | tf_op jit(solution)/shard_map/ppermute | solution.py:29
  61.9 5.3 %collective-permute-start.12 = (f32[64,512]{1,0:T(8,128)S(1)}, f32[64,512]{1,0:T(8,128)S(1)}, u32[]{:S(2)}, u32[]{:S(2)}) collective-permute-start(f32[64,512]{1,0:T(8,128)S(1)} %get-tuple-element.68.u0), channel_id=1, source_target_pairs={{0,16},{8,24},{16,32},{24,40},{32,48},{40,56},{48,0},{56,8},{64,80... | collective-permute-start | bytes 393224 | tf_op jit(solution)/shard_map/ppermute | solution.py:29
  71.2 21.4 %collective-permute-start.16 = (f32[256,512]{1,0:T(8,128)S(1)}, f32[256,512]{1,0:T(8,128)S(1)}, u32[]{:S(2)}, u32[]{:S(2)}) collective-permute-start(f32[256,512]{1,0:T(8,128)S(1)} %bitcast.6), channel_id=1, source_target_pairs={{0,48},{8,56},{16,0},{24,8},{32,16},{40,24},{48,32},{56,40},{64,11... | collective-permute-start | bytes 1572872 | tf_op jit(solution)/shard_map/ppermute | solution.py:29
  73.2 19.4 %collective-permute-start.15 = (f32[256,512]{1,0:T(8,128)S(1)}, f32[256,512]{1,0:T(8,128)S(1)}, u32[]{:S(2)}, u32[]{:S(2)}) collective-permute-start(f32[256,512]{1,0:T(8,128)S(1)} %bitcast.7), channel_id=1, source_target_pairs={{0,16},{8,24},{16,32},{24,40},{32,48},{40,56},{48,0},{56,8},{64,80... | collective-permute-start | bytes 1572872 | tf_op jit(solution)/shard_map/ppermute | solution.py:29
  74.5 7.8 %collective-permute-start.14 = (f32[8,3,8,128]{3,2,1,0:T(8,128)S(1)}, f32[8,3,8,128]{3,2,1,0:T(8,128)S(1)}, u32[]{:S(2)}, u32[]{:S(2)}) collective-permute-start(f32[8,3,8,128]{3,2,1,0:T(8,128)S(1)} %get-tuple-element.73), channel_id=1, source_target_pairs={{0,8},{8,0},{16,24},{24,16},{32,40},{40,32},{48,56},{56,48},{64,72... | collective-permute-start | bytes 294920 | tf_op jit(solution)/shard_map/ppermute | solution.py:29
  110.3 21.4 %all-to-all-start.3 = ((f32[8,16,3,8,128]{4,3,2,1,0:T(8,128)}), f32[8,16,3,8,128]{4,3,2,1,0:T(8,128)}, u32[]{:S(2)}, u32[]{:S(2)}) async-start(f32[8,16,3,8,128]{4,3,2,1,0:T(8,128)} %spread.5), calls=%async_computation.3 | async-start | bytes 3145728 | tf_op jit(solution)/shard_map/all_to_all | solution.py:49
  115.6 5.3 %collective-permute-start.18 = (f32[128,512]{1,0:T(8,128)S(1)}, f32[128,512]{1,0:T(8,128)S(1)}, u32[]{:S(2)}, u32[]{:S(2)}) collective-permute-start(f32[128,512]{1,0:T(8,128)S(1)} %slice.7), channel_id=1, source_target_pairs={{0,48},{8,56},{16,0},{24,8},{32,16},{40,24},{48,32},{56,40},{64,11... | collective-permute-start | bytes 786440 | tf_op jit(solution)/shard_map/ppermute | solution.py:29
  116.5 6.7 %collective-permute-start.17 = (f32[128,512]{1,0:T(8,128)S(1)}, f32[128,512]{1,0:T(8,128)S(1)}, u32[]{:S(2)}, u32[]{:S(2)}) collective-permute-start(f32[128,512]{1,0:T(8,128)S(1)} %slice.6), channel_id=1, source_target_pairs={{0,16},{8,24},{16,32},{24,40},{32,48},{40,56},{48,0},{56,8},{64,80... | collective-permute-start | bytes 786440 | tf_op jit(solution)/shard_map/ppermute | solution.py:29
  131.6 7.5 %collective-permute-start.19 = (f32[8,16,3,8,128]{4,3,2,1,0:T(8,128)}, f32[8,16,3,8,128]{4,3,2,1,0:T(8,128)S(1)}, u32[]{:S(2)}, u32[]{:S(2)}) collective-permute-start(f32[8,16,3,8,128]{4,3,2,1,0:T(8,128)} %all-to-all-done.3.own_ref), channel_id=1, source_target_pairs={{0,8},{8,0},{16,24},{24,16},{32,40},{40,32},{48,56},{56,48},{64,72... | collective-permute-start | bytes 4718600 | tf_op jit(solution)/shard_map/ppermute | solution.py:29
  140.1 16.9 %copy-start.7 = (f32[256,512]{1,0:T(8,128)S(1)}, f32[256,512]{1,0:T(8,128)}, u32[]{:S(2)}) copy-start(f32[256,512]{1,0:T(8,128)} %copy-done.6) | copy-start | bytes 1572868
  140.1 16.9 %copy-start.12 = (f32[128,512]{1,0:T(8,128)S(1)}, f32[128,512]{1,0:T(8,128)}, u32[]{:S(2)}) copy-start(f32[128,512]{1,0:T(8,128)} %copy-done.11) | copy-start | bytes 786436
  140.1 19.5 %copy-start.5 = (f32[3,512,256]{2,1,0:T(8,128)S(1)}, f32[3,512,256]{2,1,0:T(8,128)}, u32[]{:S(2)}) copy-start(f32[3,512,256]{2,1,0:T(8,128)} %copy-done.4) | copy-start | bytes 4718596
  140.1 19.5 %copy-start.9 = (f32[1,512,256]{2,1,0:T(8,128)S(1)}, f32[1,512,256]{2,1,0:T(8,128)}, u32[]{:S(2)}) copy-start(f32[1,512,256]{2,1,0:T(8,128)} %copy-done.8) | copy-start | bytes 1572868
  157.0 2.6 %copy-start.3 = (bf16[1024,1024]{1,0:T(8,128)(2,1)S(1)}, bf16[1024,1024]{1,0:T(8,128)(2,1)}, u32[]{:S(2)}) copy-start(bf16[1024,1024]{1,0:T(8,128)(2,1)} %mom.1) | copy-start | bytes 6291460
  157.0 2.6 %copy-start.10 = (f32[64,1024]{1,0:T(8,128)S(1)}, f32[64,1024]{1,0:T(8,128)}, u32[]{:S(2)}) copy-start(f32[64,1024]{1,0:T(8,128)} %get-tuple-element.84.q) | copy-start | bytes 786436
  158.2 1.4 collective-permute-start.20
  (5 other events, 4.5 us)

commit v4 on v3

--- a/solution.py
+++ b/solution.py
@@ -101,7 +101,7 @@
         out_shape=tuple(outs),
         in_specs=[SMEM] + [VMEM] * (3 + added),
         out_specs=(VMEM,) * len(outs),
-        compiler_params=params(24),
+        compiler_params=params(16),
         cost_estimate=cost(2 * tok * d * 256 * n, (1 + 2 * n) << 19),
         name="merge",
     )(pos, inputs, key_grads, error, *([sent] if added else []))
@@ -131,7 +131,7 @@
         in_specs=[SMEM] + [VMEM] * 6,
         out_specs=(VMEM,) * 5,
         scratch_shapes=[pltpu.VMEM((256, 512), F32)],
-        compiler_params=params(24),
+        compiler_params=params(16),
         cost_estimate=cost(4 << 17, 3 << 20),
         name="sum_turn",
     )(pos, top, end, *came)
@@ -158,7 +158,7 @@
         out_shape=outs,
         in_specs=[VMEM] * len(parts),
         out_specs=(VMEM,) * len(outs),
-        compiler_params=params(24),
+        compiler_params=params(16),
         cost_estimate=cost(1 << 17, 1 << 20),
         name="spread",
     )(*parts)
@@ -192,7 +192,7 @@
         out_shape=(jax.ShapeDtypeStruct((8, 3, 8, 128), F32),) * 2,
         in_specs=[SMEM] + [VMEM] * 4,
         out_specs=(VMEM, VMEM),
-        compiler_params=params(24),
+        compiler_params=params(16),
         cost_estimate=cost(2 * 6 * 192 * k * d, 2 << 20),
         name="g_block",
     )(pos, *units, of_y)
@@ -218,9 +218,7 @@
         for k in range(8):
             pivot = jnp.broadcast_to(c[t, k][k:k + 1], (8, 2 * n))
             pivots = jnp.where(sub == k, pivot, pivots)
-            turn = pl.reciprocal(pivot, approx=True)
-            turn = turn + turn * (1.0 - pivot * turn)
-            turn = turn + turn * (1.0 - pivot * turn)
+            turn = 1.0 / pivot
             lead = jnp.broadcast_to(b[t][k:k + 1], (8, 2 * n))
             heads = {l: jnp.broadcast_to(c[t, l][k:k + 1], (8, 2 * n)) for l in range(k + 1, 8)}
             for r in range(t, tiles):
@@ -270,14 +268,23 @@
             right_parts = jnp.concatenate([x[0], x[1], x[0], x[1], x[2], x[0]], axis=0)
             return jnp.dot(left_parts, right_parts, preferred_element_type=F32)
 
+        def times_g(x):
+            return product(x, hi_ref[...], mid_ref[...], low_ref[...], (((1,), (0,)), ((), ())))
+
+        q_parts = split3(q)
+        u = times_g(q_parts)
         for turn in range(ITERS):
-            q_parts = split3(q)
-            u = product(q_parts, hi_ref[...], mid_ref[...], low_ref[...], (((1,), (0,)), ((), ())))
             u_parts = split3(u)
-            inv = inverse_factor(product(u_parts, *q_parts, LANES))
-            if turn == ITERS - 1:
+            gram = product(u_parts, *q_parts, LANES)
+            last = turn == ITERS - 1
+            v_parts = None if last else split3(times_g(u_parts))
+            inv = inverse_factor(gram)
+            if last:
                 w_out[...] = solve(inv, q_parts)
             q = solve(inv, u_parts) * (1.0 / 32)
+            if not last:
+                q_parts = split3(q)
+                u = solve(inv, v_parts) * (1.0 / 32)
         q_out[...] = q
 
 
@@ -292,7 +299,7 @@
         in_specs=[SMEM, part, part, whole],
         out_specs=(whole, whole),
         scratch_shapes=[pltpu.VMEM((k, k), BF16)] * 3,
-        compiler_params=params(40),
+        compiler_params=params(20),
         cost_estimate=cost(36 * n * k * k, 4 * k * k),
         name="iterations",
     )(pos, own, away, q)
@@ -318,7 +325,7 @@
         out_shape=jax.ShapeDtypeStruct((n, d), F32),
         in_specs=[SMEM] + [VMEM] * 6,
         out_specs=VMEM,
-        compiler_params=params(24),
+        compiler_params=params(16),
         cost_estimate=cost(6 * n * d * 1024, 2 << 20),
         name="left",
     )(pos, w, *blocks)
@@ -396,7 +403,7 @@
             ),
             scratch_shapes=[pltpu.VMEM((4 * n, k), BF16)],
         ),
-        compiler_params=params(24),
+        compiler_params=params(16),
         cost_estimate=cost(8 * n * d * k, 10 << 20),
         name="finish",
     )(pos, *pieces, momentum, own, away, q)
@@ -412,6 +419,7 @@
     other_opp, pos = lax.optimization_barrier((other_opp, pos))
     sent_opp = dp_shift(other_opp, dc=1)
     other, _ = merge(pos, False, TURNS[1:], *args)
+    other, sent_opp = lax.optimization_barrier((other, sent_opp))
     sent = dp_shift(other, dc=1)
     mine_opp, opposite = merge(pos, True, TURNS[:1], *args, sent_opp)
     mine, sums = merge(pos, True, TURNS[1:], *args, sent)

time: 164 us -> 158 us (0.963)
  Pallas kernels: 30.6 us -> 27.1 us
    pallas_call x1, Pallas kernels: 16.9 us -> 13.4 us  [iterate(): pl.pallas_call(iterate_kernel, out_shape=(jax.ShapeDtypeStruct(q.shape, F...]
  transfers between devices with their start and end apart: 23 -> 23, of which waited for: 16 -> 16; matrix products, arithmetic and copies ran while one was open for 1% -> 1% of each run, Pallas kernels for 2% -> 3%
where the time goes in v4:
time: 158 us; the launch traced here: 157 us
  waiting for transfers between devices  50.9 us (32%)
  starting transfers between devices  45 us (28%)
  Pallas kernels  27.1 us (17%)
  blocking collectives  25 us (16%)
  local copies, waits for them, and re-layouts  8.3 us (5%)
    ppermute x21, waiting for transfers between devices, dp_shift(): return lax.ppermute(x, 'dp', pairs)  38.7 us
    ppermute x21, starting transfers between devices, dp_shift(): return lax.ppermute(x, 'dp', pairs)  37.2 us
    all_to_all x2, blocking collectives, exchange(): return lax.all_to_all(x, axis, 0, 0, axis_index_groups=groups)  25 us
    pallas_call x1, Pallas kernels, iterate(): pl.pallas_call(iterate_kernel, out_shape=(jax.ShapeDtypeStruct(q.shape, F...  13.4 us
    all_to_all x2, waiting for transfers between devices, exchange(): return lax.all_to_all(x, axis, 0, 0, axis_index_groups=groups)  12.2 us
    all_to_all x2, starting transfers between devices, exchange(): return lax.all_to_all(x, axis, 0, 0, axis_index_groups=groups)  7.77 us
    unnamed x28, local copies, waits for them, and re-layouts  7.31 us
    pallas_call x4, Pallas kernels, merge(): pl.pallas_call(functools.partial(merge_kernel, turns, own, added), out_sh...  4.29 us
  transfers between devices with their start and end apart: 23, of which 16 were waited for; matrix products, arithmetic and copies ran while one was open for 1% of the time, Pallas kernels for 3%

profile of v4, /device:TPU:1, one launch (start us, length us, event | category | flops | bytes accessed | tf_op | source)
XLA Modules:
  0.0 157.4 jit_solution(13909418260870223027)
XLA Ops:
  0.7 1.6 %copy-done = bf16[1,1024,1024]{2,1,0:T(8,128)(2,1)S(1)} copy-done((bf16[1,1024,1024]{2,1,0:T(8,128)(2,1)S(1)}, bf16[1,1024,1024]{2,1,0:T(8,128)(2,1)}, u32[]{:S(2)}) %copy-start) | copy-done | bytes 2097176
  2.3 1.2 copy-done.1
  5.7 3.3 %collective-permute-start = (f32[1,512,256]{2,1,0:T(8,128)S(1)}, f32[1,512,256]{2,1,0:T(8,128)S(1)}, u32[]{:S(2)}, u32[]{:S(2)}) collective-permute-start(f32[1,512,256]{2,1,0:T(8,128)S(1)} %merge.4.other_opp), channel_id=1, source_target_pairs={{0,8},{8,0},{16,24},{24,16},{32,40},{40,32},{48,56},{56,48},{64,72... | collective-permute-start | bytes 1572872 | tf_op jit(solution)/shard_map/ppermute | solution.py:29
  12.7 2.7 %collective-permute-start.3 = (f32[256,256]{1,0:T(8,128)S(1)}, f32[256,256]{1,0:T(8,128)S(1)}, u32[]{:S(2)}, u32[]{:S(2)}) collective-permute-start(f32[256,256]{1,0:T(8,128)S(1)} %get-tuple-element.57), channel_id=1, source_target_pairs={{0,48},{8,56},{16,0},{24,8},{32,16},{40,24},{48,32},{56,40},{64,11... | collective-permute-start | bytes 786440 | tf_op jit(solution)/shard_map/ppermute | solution.py:29
  16.7 2.7 %collective-permute-start.5 = (f32[256,256]{1,0:T(8,128)S(1)}, f32[256,256]{1,0:T(8,128)S(1)}, u32[]{:S(2)}, u32[]{:S(2)}) collective-permute-start(f32[256,256]{1,0:T(8,128)S(1)} %get-tuple-element.59), channel_id=1, source_target_pairs={{0,48},{8,56},{16,0},{24,8},{32,16},{40,24},{48,32},{56,40},{64,11... | collective-permute-start | bytes 786440 | tf_op jit(solution)/shard_map/ppermute | solution.py:29
  19.4 2.3 %collective-permute-done.2 = f32[256,256]{1,0:T(8,128)S(1)} collective-permute-done((f32[256,256]{1,0:T(8,128)S(1)}, f32[256,256]{1,0:T(8,128)S(1)}, u32[]{:S(2)}, u32[]{:S(2)}) %collective-permute-start.2) | collective-permute-done | bytes 262176 | tf_op jit(solution)/shard_map/ppermute | solution.py:29
  21.7 5.6 %collective-permute-done.4.second = f32[256,256]{1,0:T(8,128)S(1)} collective-permute-done((f32[256,256]{1,0:T(8,128)S(1)}, f32[256,256]{1,0:T(8,128)S(1)}, u32[]{:S(2)}, u32[]{:S(2)}) %collective-permute-start.4) | collective-permute-done | bytes 262176 | tf_op jit(solution)/shard_map/ppermute | solution.py:29
  27.5 2.7 %collective-permute-start.7 = (f32[256,256]{1,0:T(8,128)S(1)}, f32[256,256]{1,0:T(8,128)S(1)}, u32[]{:S(2)}, u32[]{:S(2)}) collective-permute-start(f32[256,256]{1,0:T(8,128)S(1)} %add.31), channel_id=1, source_target_pairs={{0,48},{8,56},{16,0},{24,8},{32,16},{40,24},{48,32},{56,40},{64,11... | collective-permute-start | bytes 786440 | tf_op jit(solution)/shard_map/ppermute | solution.py:29
  30.2 5.3 %collective-permute-done.6.on = f32[256,256]{1,0:T(8,128)S(1)} collective-permute-done((f32[256,256]{1,0:T(8,128)S(1)}, f32[256,256]{1,0:T(8,128)S(1)}, u32[]{:S(2)}, u32[]{:S(2)}) %collective-permute-start.6) | collective-permute-done | bytes 262176 | tf_op jit(solution)/shard_map/ppermute | solution.py:29
  36.3 4.5 %collective-permute-start.10 = (f32[32,512]{1,0:T(8,128)S(1)}, f32[32,512]{1,0:T(8,128)S(1)}, u32[]{:S(2)}, u32[]{:S(2)}) collective-permute-start(f32[32,512]{1,0:T(8,128)S(1)} %get-tuple-element.69), channel_id=1, source_target_pairs={{0,192},{8,200},{16,208},{24,216},{32,224},{40,232},{48,240},{56,2... | collective-permute-start | bytes 196616 | tf_op jit(solution)/shard_map/ppermute | solution.py:29
  40.8 1.3 collective-permute-done.10
  42.2 4.5 %collective-permute-start.11 = (f32[64,512]{1,0:T(8,128)S(1)}, f32[64,512]{1,0:T(8,128)S(1)}, u32[]{:S(2)}, u32[]{:S(2)}) collective-permute-start(f32[64,512]{1,0:T(8,128)S(1)} %pad_add_fusion), channel_id=1, source_target_pairs={{0,192},{8,200},{16,208},{24,216},{32,224},{40,232},{48,240},{56,2... | collective-permute-start | bytes 393224 | tf_op jit(solution)/shard_map/ppermute | solution.py:29
  46.8 3.2 %collective-permute-done.11.refs_2_ = f32[64,512]{1,0:T(8,128)S(1)} collective-permute-done((f32[64,512]{1,0:T(8,128)S(1)}, f32[64,512]{1,0:T(8,128)S(1)}, u32[]{:S(2)}, u32[]{:S(2)}) %collective-permute-start.11) | collective-permute-done | bytes 131104 | tf_op jit(solution)/shard_map/ppermute | solution.py:29
  50.0 4.6 %collective-permute-done.9.refs_1_ = f32[64,512]{1,0:T(8,128)S(1)} collective-permute-done((f32[64,512]{1,0:T(8,128)S(1)}, f32[64,512]{1,0:T(8,128)S(1)}, u32[]{:S(2)}, u32[]{:S(2)}) %collective-permute-start.9) | collective-permute-done | bytes 131104 | tf_op jit(solution)/shard_map/ppermute | solution.py:29
  55.5 3.5 %all-to-all-start = ((f32[4,64,512]{2,1,0:T(8,128)}), f32[4,64,512]{2,1,0:T(8,128)S(1)}, u32[]{:S(2)}, u32[]{:S(2)}) async-start(f32[4,64,512]{2,1,0:T(8,128)} %get-tuple-element.70), calls=%async_computation | async-start | bytes 1048576 | tf_op jit(solution)/shard_map/all_to_all | solution.py:49
  59.4 1.6 collective-permute-start.12
  60.9 3.5 %collective-permute-done.13.u2 = f32[64,512]{1,0:T(8,128)S(1)} collective-permute-done((f32[64,512]{1,0:T(8,128)S(1)}, f32[64,512]{1,0:T(8,128)S(1)}, u32[]{:S(2)}, u32[]{:S(2)}) %collective-permute-start.13) | collective-permute-done | bytes 131104 | tf_op jit(solution)/shard_map/ppermute | solution.py:29
  64.4 1.3 collective-permute-done.12.u1
  65.7 4.4 %all-to-all-done = f32[4,64,512]{2,1,0:T(8,128)S(1)} async-done(((f32[4,64,512]{2,1,0:T(8,128)}), f32[4,64,512]{2,1,0:T(8,128)S(1)}, u32[]{:S(2)}, u32[]{:S(2)}) %all-to-all-start) | async-done | bytes 524320 | tf_op jit(solution)/shard_map/all_to_all | solution.py:49
  71.6 1.2 g_block.1
  72.9 6.4 %collective-permute-start.14 = (f32[8,3,8,128]{3,2,1,0:T(8,128)S(1)}, f32[8,3,8,128]{3,2,1,0:T(8,128)S(1)}, u32[]{:S(2)}, u32[]{:S(2)}) collective-permute-start(f32[8,3,8,128]{3,2,1,0:T(8,128)S(1)} %get-tuple-element.77), channel_id=1, source_target_pairs={{0,8},{8,0},{16,24},{24,16},{32,40},{40,32},{48,56},{56,48},{64,72... | collective-permute-start | bytes 294920 | tf_op jit(solution)/shard_map/ppermute | solution.py:29
  80.3 9.4 %all_to_all.20.refs_0_ = f32[8,3,8,128]{3,2,1,0:T(8,128)S(1)} all-to-all(f32[8,3,8,128]{3,2,1,0:T(8,128)S(1)} %add.34), channel_id=1, replica_groups=mesh['dp'=32,'shard'=8] {'shard'}, dimensions={0} | all-to-all | bytes 196608 | tf_op jit(solution)/shard_map/all_to_all | solution.py:49
  90.6 15.5 %all_to_all.21.refs_0_ = f32[16,3,8,128]{3,2,1,0:T(8,128)S(1)} all-to-all(f32[16,3,8,128]{3,2,1,0:T(8,128)S(1)} %spread.4), channel_id=1, replica_groups={{0,16,32,48,64,80,96,112,128,144,160,176,192,208,224,240},{8,24,40,56,7..., dimensions={0} | all-to-all | bytes 393216 | tf_op jit(solution)/shard_map/all_to_all | solution.py:49
  106.1 1.2 spread.5
  107.3 4.3 %all-to-all-start.3 = ((f32[8,16,3,8,128]{4,3,2,1,0:T(8,128)}), f32[8,16,3,8,128]{4,3,2,1,0:T(8,128)}, u32[]{:S(2)}, u32[]{:S(2)}) async-start(f32[8,16,3,8,128]{4,3,2,1,0:T(8,128)} %spread.5), calls=%async_computation.3 | async-start | bytes 3145728 | tf_op jit(solution)/shard_map/all_to_all | solution.py:49
  114.2 3.8 %collective-permute-done.18.m2_end = f32[128,512]{1,0:T(8,128)S(1)} collective-permute-done((f32[128,512]{1,0:T(8,128)S(1)}, f32[128,512]{1,0:T(8,128)S(1)}, u32[]{:S(2)}, u32[]{:S(2)}) %collective-permute-start.18) | collective-permute-done | bytes 262176 | tf_op jit(solution)/shard_map/ppermute | solution.py:29
  118.0 2.3 %collective-permute-done.17.m2_top = f32[128,512]{1,0:T(8,128)S(1)} collective-permute-done((f32[128,512]{1,0:T(8,128)S(1)}, f32[128,512]{1,0:T(8,128)S(1)}, u32[]{:S(2)}, u32[]{:S(2)}) %collective-permute-start.17) | collective-permute-done | bytes 262176 | tf_op jit(solution)/shard_map/ppermute | solution.py:29
  120.9 7.8 %all-to-all-done.3.own_ref = f32[8,16,3,8,128]{4,3,2,1,0:T(8,128)} async-done(((f32[8,16,3,8,128]{4,3,2,1,0:T(8,128)}), f32[8,16,3,8,128]{4,3,2,1,0:T(8,128)}, u32[]{:S(2)}, u32[]{:S(2)}) %all-to-all-start.3) | async-done | bytes 1572896 | tf_op jit(solution)/shard_map/all_to_all | solution.py:49
  128.7 4.3 %collective-permute-start.19 = (f32[8,16,3,8,128]{4,3,2,1,0:T(8,128)}, f32[8,16,3,8,128]{4,3,2,1,0:T(8,128)S(1)}, u32[]{:S(2)}, u32[]{:S(2)}) collective-permute-start(f32[8,16,3,8,128]{4,3,2,1,0:T(8,128)} %all-to-all-done.3.own_ref), channel_id=1, source_target_pairs={{0,8},{8,0},{16,24},{24,16},{32,40},{40,32},{48,56},{56,48},{64,72... | collective-permute-start | bytes 4718600 | tf_op jit(solution)/shard_map/ppermute | solution.py:29
  133.0 3.2 %collective-permute-done.19.away_ref = f32[8,16,3,8,128]{4,3,2,1,0:T(8,128)S(1)} collective-permute-done((f32[8,16,3,8,128]{4,3,2,1,0:T(8,128)}, f32[8,16,3,8,128]{4,3,2,1,0:T(8,128)S(1)}, u32[]{:S(2)}, u32[]{:S(2)}) %collective-permute-start.19) | collective-permute-done | bytes 1572896 | tf_op jit(solution)/shard_map/ppermute | solution.py:29
  137.2 13.4 %iterations.1 = (f32[64,1024]{1,0:T(8,128)}, f32[64,1024]{1,0:T(8,128)S(1)}) custom-call(s32[3]{0:T(128)S(1)} %pad_add_fusion.2.pos_ref, f32[8,16,3,8,128]{4,3,2,1,0:T(8,128)} %all-to-all-done.3.own_ref, f32[8,16,3,8,128]{4,3,2,1,0:T(8,128)S(1)} %collective-permute-done.19.away_ref, f32[64,1024]{1,0:T(8,128)S(1)} %bitcast.11), custom_call_target="tpu_custom_call" | custom-call | flops 2415919104 | bytes 4194304 | tf_op jit(solution)/shard_map/iterations/pallas_call | solution.py:295
  153.2 4.2 %finish.1 = (bf16[1,1024,1024]{2,1,0:T(8,128)(2,1)}, bf16[1024,1024]{1,0:T(8,128)(2,1)}) custom-call(s32[3]{0:T(128)S(1)} %pad_add_fusion.2.pos_ref, f32[1,512,256]{2,1,0:T(8,128)S(1)} %copy-done.9, f32[3,512,256]{2,1,0:T(8,128)S(1)} %copy-done.5, f32[1,512,256]{2,1,0:T(8,128)S(1)} %merge.4.other_opp, f32[3,512,256]{2,1,0:T(8,128)S(1)} %merge.5.other, ...), custom_call_target="tpu_custom_call" | custom-call | flops 536870912 | bytes 10485760 | tf_op jit(solution)/shard_map/finish/pallas_call | solution.py:384
  (64 shorter events, 19.5 us)
Async XLA Ops:
  0.7 1.6 %copy-start = (bf16[1,1024,1024]{2,1,0:T(8,128)(2,1)S(1)}, bf16[1,1024,1024]{2,1,0:T(8,128)(2,1)}, u32[]{:S(2)}) copy-start(bf16[1,1024,1024]{2,1,0:T(8,128)(2,1)} %err.7) | copy-start | bytes 6291460
  2.3 1.2 copy-start.1
  5.7 4.9 %collective-permute-start = (f32[1,512,256]{2,1,0:T(8,128)S(1)}, f32[1,512,256]{2,1,0:T(8,128)S(1)}, u32[]{:S(2)}, u32[]{:S(2)}) collective-permute-start(f32[1,512,256]{2,1,0:T(8,128)S(1)} %merge.4.other_opp), channel_id=1, source_target_pairs={{0,8},{8,0},{16,24},{24,16},{32,40},{40,32},{48,56},{56,48},{64,72... | collective-permute-start | bytes 1572872 | tf_op jit(solution)/shard_map/ppermute | solution.py:29
  10.6 4.8 %collective-permute-start.1 = (f32[3,512,256]{2,1,0:T(8,128)S(1)}, f32[3,512,256]{2,1,0:T(8,128)S(1)}, u32[]{:S(2)}, u32[]{:S(2)}) collective-permute-start(f32[3,512,256]{2,1,0:T(8,128)S(1)} %merge.5.other), channel_id=1, source_target_pairs={{0,8},{8,0},{16,24},{24,16},{32,40},{40,32},{48,56},{56,48},{64,72... | collective-permute-start | bytes 4718600 | tf_op jit(solution)/shard_map/ppermute | solution.py:29
  12.7 9.0 %collective-permute-start.2 = (f32[256,256]{1,0:T(8,128)S(1)}, f32[256,256]{1,0:T(8,128)S(1)}, u32[]{:S(2)}, u32[]{:S(2)}) collective-permute-start(f32[256,256]{1,0:T(8,128)S(1)} %get-tuple-element.56), channel_id=1, source_target_pairs={{0,16},{8,24},{16,32},{24,40},{32,48},{40,56},{48,0},{56,8},{64,80... | collective-permute-start | bytes 786440 | tf_op jit(solution)/shard_map/ppermute | solution.py:29
  12.7 9.0 %collective-permute-start.3 = (f32[256,256]{1,0:T(8,128)S(1)}, f32[256,256]{1,0:T(8,128)S(1)}, u32[]{:S(2)}, u32[]{:S(2)}) collective-permute-start(f32[256,256]{1,0:T(8,128)S(1)} %get-tuple-element.57), channel_id=1, source_target_pairs={{0,48},{8,56},{16,0},{24,8},{32,16},{40,24},{48,32},{56,40},{64,11... | collective-permute-start | bytes 786440 | tf_op jit(solution)/shard_map/ppermute | solution.py:29
  16.6 19.7 %copy-start.4 = (f32[3,512,256]{2,1,0:T(8,128)}, f32[3,512,256]{2,1,0:T(8,128)S(1)}, u32[]{:S(2)}) copy-start(f32[3,512,256]{2,1,0:T(8,128)S(1)} %get-tuple-element.52.mine) | copy-start | bytes 4718596
  16.6 10.7 %collective-permute-start.4 = (f32[256,256]{1,0:T(8,128)S(1)}, f32[256,256]{1,0:T(8,128)S(1)}, u32[]{:S(2)}, u32[]{:S(2)}) collective-permute-start(f32[256,256]{1,0:T(8,128)S(1)} %get-tuple-element.58), channel_id=1, source_target_pairs={{0,16},{8,24},{16,32},{24,40},{32,48},{40,56},{48,0},{56,8},{64,80... | collective-permute-start | bytes 786440 | tf_op jit(solution)/shard_map/ppermute | solution.py:29
  16.7 10.6 %collective-permute-start.5 = (f32[256,256]{1,0:T(8,128)S(1)}, f32[256,256]{1,0:T(8,128)S(1)}, u32[]{:S(2)}, u32[]{:S(2)}) collective-permute-start(f32[256,256]{1,0:T(8,128)S(1)} %get-tuple-element.59), channel_id=1, source_target_pairs={{0,48},{8,56},{16,0},{24,8},{32,16},{40,24},{48,32},{56,40},{64,11... | collective-permute-start | bytes 786440 | tf_op jit(solution)/shard_map/ppermute | solution.py:29
  27.3 8.1 %collective-permute-start.6 = (f32[256,256]{1,0:T(8,128)S(1)}, f32[256,256]{1,0:T(8,128)S(1)}, u32[]{:S(2)}, u32[]{:S(2)}) collective-permute-start(f32[256,256]{1,0:T(8,128)S(1)} %add.30), channel_id=1, source_target_pairs={{0,16},{8,24},{16,32},{24,40},{32,48},{40,56},{48,0},{56,8},{64,80... | collective-permute-start | bytes 786440 | tf_op jit(solution)/shard_map/ppermute | solution.py:29
  27.5 8.0 %collective-permute-start.7 = (f32[256,256]{1,0:T(8,128)S(1)}, f32[256,256]{1,0:T(8,128)S(1)}, u32[]{:S(2)}, u32[]{:S(2)}) collective-permute-start(f32[256,256]{1,0:T(8,128)S(1)} %add.31), channel_id=1, source_target_pairs={{0,48},{8,56},{16,0},{24,8},{32,16},{40,24},{48,32},{56,40},{64,11... | collective-permute-start | bytes 786440 | tf_op jit(solution)/shard_map/ppermute | solution.py:29
  36.3 5.8 %collective-permute-start.10 = (f32[32,512]{1,0:T(8,128)S(1)}, f32[32,512]{1,0:T(8,128)S(1)}, u32[]{:S(2)}, u32[]{:S(2)}) collective-permute-start(f32[32,512]{1,0:T(8,128)S(1)} %get-tuple-element.69), channel_id=1, source_target_pairs={{0,192},{8,200},{16,208},{24,216},{32,224},{40,232},{48,240},{56,2... | collective-permute-start | bytes 196616 | tf_op jit(solution)/shard_map/ppermute | solution.py:29
  40.8 5.9 %collective-permute-start.8 = (f32[32,512]{1,0:T(8,128)S(1)}, f32[32,512]{1,0:T(8,128)S(1)}, u32[]{:S(2)}, u32[]{:S(2)}) collective-permute-start(f32[32,512]{1,0:T(8,128)S(1)} %get-tuple-element.67), channel_id=1, source_target_pairs={{0,64},{8,72},{16,80},{24,88},{32,96},{40,104},{48,112},{56,120},{... | collective-permute-start | bytes 196616 | tf_op jit(solution)/shard_map/ppermute | solution.py:29
  42.2 7.8 %collective-permute-start.11 = (f32[64,512]{1,0:T(8,128)S(1)}, f32[64,512]{1,0:T(8,128)S(1)}, u32[]{:S(2)}, u32[]{:S(2)}) collective-permute-start(f32[64,512]{1,0:T(8,128)S(1)} %pad_add_fusion), channel_id=1, source_target_pairs={{0,192},{8,200},{16,208},{24,216},{32,224},{40,232},{48,240},{56,2... | collective-permute-start | bytes 393224 | tf_op jit(solution)/shard_map/ppermute | solution.py:29
  46.7 7.9 %collective-permute-start.9 = (f32[64,512]{1,0:T(8,128)S(1)}, f32[64,512]{1,0:T(8,128)S(1)}, u32[]{:S(2)}, u32[]{:S(2)}) collective-permute-start(f32[64,512]{1,0:T(8,128)S(1)} %pad_add_fusion.1), channel_id=1, source_target_pairs={{0,64},{8,72},{16,80},{24,88},{32,96},{40,104},{48,112},{56,120},{... | collective-permute-start | bytes 393224 | tf_op jit(solution)/shard_map/ppermute | solution.py:29
  55.5 14.7 %all-to-all-start = ((f32[4,64,512]{2,1,0:T(8,128)}), f32[4,64,512]{2,1,0:T(8,128)S(1)}, u32[]{:S(2)}, u32[]{:S(2)}) async-start(f32[4,64,512]{2,1,0:T(8,128)} %get-tuple-element.70), calls=%async_computation | async-start | bytes 1048576 | tf_op jit(solution)/shard_map/all_to_all | solution.py:49
  58.9 5.5 %collective-permute-start.13 = (f32[64,512]{1,0:T(8,128)S(1)}, f32[64,512]{1,0:T(8,128)S(1)}, u32[]{:S(2)}, u32[]{:S(2)}) collective-permute-start(f32[64,512]{1,0:T(8,128)S(1)} %get-tuple-element.72.u0), channel_id=1, source_target_pairs={{0,32},{8,40},{16,48},{24,56},{32,0},{40,8},{48,16},{56,24},{64,96... | collective-permute-start | bytes 393224 | tf_op jit(solution)/shard_map/ppermute | solution.py:29
  59.4 6.4 %collective-permute-start.12 = (f32[64,512]{1,0:T(8,128)S(1)}, f32[64,512]{1,0:T(8,128)S(1)}, u32[]{:S(2)}, u32[]{:S(2)}) collective-permute-start(f32[64,512]{1,0:T(8,128)S(1)} %get-tuple-element.72.u0), channel_id=1, source_target_pairs={{0,16},{8,24},{16,32},{24,40},{32,48},{40,56},{48,0},{56,8},{64,80... | collective-permute-start | bytes 393224 | tf_op jit(solution)/shard_map/ppermute | solution.py:29
  70.2 19.6 %collective-permute-start.16 = (f32[256,512]{1,0:T(8,128)S(1)}, f32[256,512]{1,0:T(8,128)S(1)}, u32[]{:S(2)}, u32[]{:S(2)}) collective-permute-start(f32[256,512]{1,0:T(8,128)S(1)} %bitcast.6), channel_id=1, source_target_pairs={{0,48},{8,56},{16,0},{24,8},{32,16},{40,24},{48,32},{56,40},{64,11... | collective-permute-start | bytes 1572872 | tf_op jit(solution)/shard_map/ppermute | solution.py:29
  71.1 18.7 %collective-permute-start.15 = (f32[256,512]{1,0:T(8,128)S(1)}, f32[256,512]{1,0:T(8,128)S(1)}, u32[]{:S(2)}, u32[]{:S(2)}) collective-permute-start(f32[256,512]{1,0:T(8,128)S(1)} %bitcast.7), channel_id=1, source_target_pairs={{0,16},{8,24},{16,32},{24,40},{32,48},{40,56},{48,0},{56,8},{64,80... | collective-permute-start | bytes 1572872 | tf_op jit(solution)/shard_map/ppermute | solution.py:29
  72.9 7.4 %collective-permute-start.14 = (f32[8,3,8,128]{3,2,1,0:T(8,128)S(1)}, f32[8,3,8,128]{3,2,1,0:T(8,128)S(1)}, u32[]{:S(2)}, u32[]{:S(2)}) collective-permute-start(f32[8,3,8,128]{3,2,1,0:T(8,128)S(1)} %get-tuple-element.77), channel_id=1, source_target_pairs={{0,8},{8,0},{16,24},{24,16},{32,40},{40,32},{48,56},{56,48},{64,72... | collective-permute-start | bytes 294920 | tf_op jit(solution)/shard_map/ppermute | solution.py:29
  107.3 21.4 %all-to-all-start.3 = ((f32[8,16,3,8,128]{4,3,2,1,0:T(8,128)}), f32[8,16,3,8,128]{4,3,2,1,0:T(8,128)}, u32[]{:S(2)}, u32[]{:S(2)}) async-start(f32[8,16,3,8,128]{4,3,2,1,0:T(8,128)} %spread.5), calls=%async_computation.3 | async-start | bytes 3145728 | tf_op jit(solution)/shard_map/all_to_all | solution.py:49
  112.7 5.3 %collective-permute-start.18 = (f32[128,512]{1,0:T(8,128)S(1)}, f32[128,512]{1,0:T(8,128)S(1)}, u32[]{:S(2)}, u32[]{:S(2)}) collective-permute-start(f32[128,512]{1,0:T(8,128)S(1)} %slice.7), channel_id=1, source_target_pairs={{0,48},{8,56},{16,0},{24,8},{32,16},{40,24},{48,32},{56,40},{64,11... | collective-permute-start | bytes 786440 | tf_op jit(solution)/shard_map/ppermute | solution.py:29
  113.5 6.7 %collective-permute-start.17 = (f32[128,512]{1,0:T(8,128)S(1)}, f32[128,512]{1,0:T(8,128)S(1)}, u32[]{:S(2)}, u32[]{:S(2)}) collective-permute-start(f32[128,512]{1,0:T(8,128)S(1)} %slice.6), channel_id=1, source_target_pairs={{0,16},{8,24},{16,32},{24,40},{32,48},{40,56},{48,0},{56,8},{64,80... | collective-permute-start | bytes 786440 | tf_op jit(solution)/shard_map/ppermute | solution.py:29
  128.7 7.5 %collective-permute-start.19 = (f32[8,16,3,8,128]{4,3,2,1,0:T(8,128)}, f32[8,16,3,8,128]{4,3,2,1,0:T(8,128)S(1)}, u32[]{:S(2)}, u32[]{:S(2)}) collective-permute-start(f32[8,16,3,8,128]{4,3,2,1,0:T(8,128)} %all-to-all-done.3.own_ref), channel_id=1, source_target_pairs={{0,8},{8,0},{16,24},{24,16},{32,40},{40,32},{48,56},{56,48},{64,72... | collective-permute-start | bytes 4718600 | tf_op jit(solution)/shard_map/ppermute | solution.py:29
  137.2 13.4 %copy-start.7 = (f32[256,512]{1,0:T(8,128)S(1)}, f32[256,512]{1,0:T(8,128)}, u32[]{:S(2)}) copy-start(f32[256,512]{1,0:T(8,128)} %copy-done.6) | copy-start | bytes 1572868
  137.2 13.4 %copy-start.12 = (f32[128,512]{1,0:T(8,128)S(1)}, f32[128,512]{1,0:T(8,128)}, u32[]{:S(2)}) copy-start(f32[128,512]{1,0:T(8,128)} %copy-done.11) | copy-start | bytes 786436
  137.2 16.0 %copy-start.5 = (f32[3,512,256]{2,1,0:T(8,128)S(1)}, f32[3,512,256]{2,1,0:T(8,128)}, u32[]{:S(2)}) copy-start(f32[3,512,256]{2,1,0:T(8,128)} %copy-done.4) | copy-start | bytes 4718596
  137.2 16.0 %copy-start.9 = (f32[1,512,256]{2,1,0:T(8,128)S(1)}, f32[1,512,256]{2,1,0:T(8,128)}, u32[]{:S(2)}) copy-start(f32[1,512,256]{2,1,0:T(8,128)} %copy-done.8) | copy-start | bytes 1572868
  150.7 2.6 %copy-start.3 = (bf16[1024,1024]{1,0:T(8,128)(2,1)S(1)}, bf16[1024,1024]{1,0:T(8,128)(2,1)}, u32[]{:S(2)}) copy-start(bf16[1024,1024]{1,0:T(8,128)(2,1)} %mom.1) | copy-start | bytes 6291460
  150.7 2.6 %copy-start.10 = (f32[64,1024]{1,0:T(8,128)S(1)}, f32[64,1024]{1,0:T(8,128)}, u32[]{:S(2)}) copy-start(f32[64,1024]{1,0:T(8,128)} %get-tuple-element.88.q) | copy-start | bytes 786436
  151.8 1.4 collective-permute-start.20
  (5 other events, 4.5 us)

commit v5 on v4

--- a/solution.py
+++ b/solution.py
@@ -69,9 +69,7 @@
     return hi, mid, (rest - mid.astype(F32)).astype(BF16)
 
 
-def merge_kernel(turns, own, added, pos_ref, acts, grads, err, *refs):
-    sent, refs = (refs[0], refs[1:]) if added else (None, refs)
-    out_ref, sums = refs[0], refs[1:]
+def merge_kernel(turns, own, pos_ref, acts, grads, err, *refs):
     half = pos_ref[0] if own else 1 - pos_ref[0]
     d = acts.shape[1] // 2
     at_d = pl.ds(pl.multiple_of(half * d, 512), d)
@@ -81,31 +79,64 @@
         cols = pl.ds(pl.multiple_of((pos_ref[1] + turn) % 4 * 256, 256), 256)
         product = lax.dot_general(x, grads[:, cols], ROWS, preferred_element_type=F32)
         merged = product * factor + err[0, at_d, cols].astype(F32)
-        out_ref[n] = merged
-        if added:
-            total = merged + sent[n]
-            sums[2 * n][...] = total[:d // 2]
-            sums[2 * n + 1][...] = total[d // 2:]
-
-
-def merge(pos, own, turns, inputs, key_grads, error, sent=None):
+        if own:
+            total = merged + refs[0][n]
+            refs[1 + 2 * n][...] = total[:d // 2]
+            refs[2 + 2 * n][...] = total[d // 2:]
+        else:
+            refs[0][n] = merged
+
+
+def merge(pos, turns, inputs, key_grads, error, sent=None):
     tok, d = inputs.shape
     d = d // 2
     n = len(turns)
-    added = sent is not None
-    outs = [jax.ShapeDtypeStruct((n, d, 256), F32)]
-    if added:
-        outs += [jax.ShapeDtypeStruct((d // 2, 256), F32)] * (2 * n)
-    result = pl.pallas_call(
-        functools.partial(merge_kernel, turns, own, added),
-        out_shape=tuple(outs),
-        in_specs=[SMEM] + [VMEM] * (3 + added),
-        out_specs=(VMEM,) * len(outs),
+    own = sent is not None
+    outs = (jax.ShapeDtypeStruct((d // 2, 256), F32),) * (2 * n) if own else jax.ShapeDtypeStruct((n, d, 256), F32)
+    return pl.pallas_call(
+        functools.partial(merge_kernel, turns, own),
+        out_shape=outs,
+        in_specs=[SMEM] + [VMEM] * (3 + own),
+        out_specs=(VMEM,) * (2 * n) if own else VMEM,
         compiler_params=params(16),
         cost_estimate=cost(2 * tok * d * 256 * n, (1 + 2 * n) << 19),
         name="merge",
-    )(pos, inputs, key_grads, error, *([sent] if added else []))
-    return result[0], list(result[1:])
+    )(pos, inputs, key_grads, error, *([sent] if own else []))
+
+
+def merge_all_kernel(acts, grads, err, q, out_ref, q_parts):
+    factor = 1.0 / math.sqrt(acts.shape[0])
+    product = lax.dot_general(acts[...], grads[...], ROWS, preferred_element_type=F32)
+    out_ref[...] = product * factor + err[0].astype(F32)
+
+    @pl.when(pl.program_id(0) == 0)
+    def _():
+        for n, part in enumerate(split3(q[...])):
+            q_parts[n] = part
+
+
+def merge_all(inputs, key_grads, error, q):
+    tok, d = inputs.shape
+    k = key_grads.shape[1]
+    rows = 256
+    return pl.pallas_call(
+        merge_all_kernel,
+        out_shape=(jax.ShapeDtypeStruct((d, k), F32), jax.ShapeDtypeStruct((3,) + q.shape, BF16)),
+        grid=(d // rows,),
+        in_specs=[
+            pl.BlockSpec((tok, rows), lambda i: (0, i)),
+            pl.BlockSpec((tok, k), lambda i: (0, 0)),
+            pl.BlockSpec((1, rows, k), lambda i: (0, i, 0)),
+            pl.BlockSpec(q.shape, lambda i: (0, 0)),
+        ],
+        out_specs=(
+            pl.BlockSpec((rows, k), lambda i: (i, 0)),
+            pl.BlockSpec((3,) + q.shape, lambda i: (0, 0, 0)),
+        ),
+        compiler_params=params(16),
+        cost_estimate=cost(2 * tok * d * k, 8 << 20),
+        name="merge_all",
+    )(inputs, key_grads, error, q)
 
 
 def sum_turn_kernel(pos_ref, top, end, on, second, first, back, opp_top, opp_end, after, before, own, turned):
@@ -201,12 +232,18 @@
 def inverse_factor(gram):
     n = gram.shape[0]
     tiles = n // 8
-    gram = 0.5 * (gram + gram.T)
     row = lax.broadcasted_iota(jnp.int32, (n, n), 0)
     col = lax.broadcasted_iota(jnp.int32, (n, n), 1)
+    diagonal = jnp.where(row == col, gram, 0.0)
+    scale = lax.rsqrt(jnp.sum(diagonal, axis=0, keepdims=True))
+    gram = gram * lax.rsqrt(jnp.sum(diagonal, axis=1, keepdims=True)) * scale
     both = jnp.concatenate([gram, jnp.where(row == col, 1.0, 0.0)], axis=1)
     b = [both[8 * r:8 * r + 8] for r in range(tiles)]
     sub = lax.broadcasted_iota(jnp.int32, (8, 2 * n), 0)
+
+    def spread_row(x, k):
+        return jnp.broadcast_to(x[k:k + 1], (8, 2 * n))
+
     out = []
     for t in range(tiles):
         c = {
@@ -215,21 +252,26 @@
             for k in range(8)
         }
         pivots = jnp.ones((8, 2 * n), F32)
-        for k in range(8):
-            pivot = jnp.broadcast_to(c[t, k][k:k + 1], (8, 2 * n))
-            pivots = jnp.where(sub == k, pivot, pivots)
-            turn = 1.0 / pivot
-            lead = jnp.broadcast_to(b[t][k:k + 1], (8, 2 * n))
-            heads = {l: jnp.broadcast_to(c[t, l][k:k + 1], (8, 2 * n)) for l in range(k + 1, 8)}
+        for k in range(0, 8, 2):
+            here, after = c[t, k], c[t, k + 1]
+            p11, p12 = spread_row(here, k), spread_row(after, k)
+            p21, p22 = spread_row(here, k + 1), spread_row(after, k + 1)
+            det = p11 * p22 - p12 * p21
+            turn, turn_one = 1.0 / det, 1.0 / p11
+            pivots = jnp.where(sub == k, p11, jnp.where(sub == k + 1, det * turn_one, pivots))
+            lead, lead_after = spread_row(b[t], k), spread_row(b[t], k + 1)
+            heads = {l: (spread_row(c[t, l], k), spread_row(c[t, l], k + 1)) for l in range(k + 2, 8)}
             for r in range(t, tiles):
-                m = c[r, k] * turn
-                for l in range(k + 1, 8):
-                    c[r, l] = c[r, l] - m * heads[l]
+                m = (c[r, k] * p22 - c[r, k + 1] * p21) * turn
+                m_after = (c[r, k + 1] * p11 - c[r, k] * p12) * turn
+                for l in range(k + 2, 8):
+                    c[r, l] = c[r, l] - (m * heads[l][0] + m_after * heads[l][1])
                 if r == t:
-                    m = jnp.where(sub > k, m, 0.0)
-                b[r] = b[r] - m * lead
+                    m = jnp.where(sub > k + 1, m, jnp.where(sub == k + 1, p21 * turn_one, 0.0))
+                    m_after = jnp.where(sub > k + 1, m_after, 0.0)
+                b[r] = b[r] - (m * lead + m_after * lead_after)
         out.append(b[t] / jnp.sqrt(pivots))
-    return jnp.concatenate(out, axis=0)[:, n:]
+    return jnp.concatenate(out, axis=0)[:, n:] * scale
 
 
 def iterate_kernel(pos_ref, own_ref, away_ref, q_ref, q_out, w_out, hi_ref, mid_ref, low_ref):
@@ -252,8 +294,7 @@
             here, after = pl.ds(y * 256, 256), pl.ds((y + 1) % 4 * 256, 256)
             for part in parts:
                 part[after, here] = part[here, after].T
-        q = q_ref[...]
-        n = q.shape[0]
+        n = q_out.shape[0]
         def product(x, y_hi, y_mid, y_low, dims):
             hi, mid, low = x
             by_hi = lax.dot_general(jnp.concatenate([hi, mid, low], axis=0), y_hi, dims, preferred_element_type=F32)
@@ -271,7 +312,7 @@
         def times_g(x):
             return product(x, hi_ref[...], mid_ref[...], low_ref[...], (((1,), (0,)), ((), ())))
 
-        q_parts = split3(q)
+        q_parts = [q_ref[i] for i in range(3)]
         u = times_g(q_parts)
         for turn in range(ITERS):
             u_parts = split3(u)
@@ -288,21 +329,21 @@
         q_out[...] = q
 
 
-def iterate(pos, own, away, q):
-    n, k = q.shape
+def iterate(pos, own, away, q_parts):
+    _, n, k = q_parts.shape
     part = pl.BlockSpec((2,) + own.shape[1:], lambda s: (s, 0, 0, 0, 0))
     whole = pl.BlockSpec((n, k), lambda s: (0, 0))
     return pl.pallas_call(
         iterate_kernel,
-        out_shape=(jax.ShapeDtypeStruct(q.shape, F32),) * 2,
+        out_shape=(jax.ShapeDtypeStruct((n, k), F32),) * 2,
         grid=(own.shape[0] // 2,),
-        in_specs=[SMEM, part, part, whole],
+        in_specs=[SMEM, part, part, pl.BlockSpec((3, n, k), lambda s: (0, 0, 0))],
         out_specs=(whole, whole),
         scratch_shapes=[pltpu.VMEM((k, k), BF16)] * 3,
         compiler_params=params(20),
         cost_estimate=cost(36 * n * k * k, 4 * k * k),
         name="iterations",
-    )(pos, own, away, q)
+    )(pos, own, away, q_parts)
 
 
 def left_kernel(pos_ref, w_ref, m0, m1, m3, m2_top, m2_end, out_ref):
@@ -331,10 +372,7 @@
     )(pos, w, *blocks)
 
 
-TURNS = (2, 1, 3, 0)
-
-
-def finish_kernel(pos_ref, mine_opp, mine, other_opp, other, mom, own, away, q, err_out, mom_out, q_parts):
+def finish_kernel(pos_ref, merged, mom, own, away, q, err_out, mom_out, q_parts):
     i = pl.program_id(0)
 
     @pl.when(i == 0)
@@ -342,28 +380,17 @@
         hi, low = split2(q[...])
         q_parts[...] = jnp.concatenate([hi, hi, low, low], axis=0)
 
-    def step(opp, rest, p_t):
-        hi, low = split2(p_t[...])
-        p_parts = jnp.concatenate([hi, low, hi, low], axis=0)
-        for n, turn in enumerate(TURNS):
-            cols = pl.ds(pl.multiple_of((pos_ref[1] + turn) % 4 * 256, 256), 256)
-            merged = opp[0] if n == 0 else rest[n - 1]
-            approx = lax.dot_general(p_parts, q_parts[:, cols], ROWS, preferred_element_type=F32)
-            err_out[0, :, cols] = (merged - approx).astype(BF16)
-            mom_out[:, cols] = (0.9 * mom[:, cols].astype(F32) + approx).astype(BF16)
-
     first = i < pl.num_programs(0) // 2
-
-    @pl.when(first)
-    def _():
-        step(mine_opp, mine, own)
-
-    @pl.when(jnp.logical_not(first))
-    def _():
-        step(other_opp, other, away)
-
-
-def finish(pos, pieces, error, momentum, own, away, q):
+    hi, low = split2(jnp.where(first, own[...], away[...]))
+    p_parts = jnp.concatenate([hi, low, hi, low], axis=0)
+    for n in range(4):
+        cols = pl.ds(256 * n, 256)
+        approx = lax.dot_general(p_parts, q_parts[:, cols], ROWS, preferred_element_type=F32)
+        err_out[0, :, cols] = (merged[:, cols] - approx).astype(BF16)
+        mom_out[:, cols] = (0.9 * mom[:, cols].astype(F32) + approx).astype(BF16)
+
+
+def finish(pos, merged, momentum, own, away, q):
     n, k = q.shape
     d = momentum.shape[0]
     rows = 256
@@ -372,41 +399,30 @@
     def row(i, pos):
         return jnp.where(i < half, pos[0], 1 - pos[0]) * half + i % half
 
-    def early(i):
-        return jnp.minimum(i, half - 1)
-
-    def late(i):
-        return jnp.maximum(i - half, 0)
-
-    def pieces_at(count, when):
-        return pl.BlockSpec((count, rows, 256), lambda i, pos: (0, when(i), 0))
-
+    block = pl.BlockSpec((rows, k), lambda i, pos: (row(i, pos), 0))
     return pl.pallas_call(
         finish_kernel,
-        out_shape=(jax.ShapeDtypeStruct(error.shape, BF16), jax.ShapeDtypeStruct(momentum.shape, BF16)),
+        out_shape=(jax.ShapeDtypeStruct((1, d, k), BF16), jax.ShapeDtypeStruct(momentum.shape, BF16)),
         grid_spec=pltpu.PrefetchScalarGridSpec(
             num_scalar_prefetch=1,
             grid=(d // rows,),
             in_specs=[
-                pieces_at(1, early),
-                pieces_at(3, early),
-                pieces_at(1, late),
-                pieces_at(3, late),
-                pl.BlockSpec((rows, k), lambda i, pos: (row(i, pos), 0)),
-                pl.BlockSpec((n, rows), lambda i, pos: (0, early(i))),
-                pl.BlockSpec((n, rows), lambda i, pos: (0, late(i))),
+                block,
+                block,
+                pl.BlockSpec((n, rows), lambda i, pos: (0, jnp.minimum(i, half - 1))),
+                pl.BlockSpec((n, rows), lambda i, pos: (0, jnp.maximum(i - half, 0))),
                 pl.BlockSpec((n, k), lambda i, pos: (0, 0)),
             ],
-            out_specs=(
-                pl.BlockSpec((1, rows, k), lambda i, pos: (0, row(i, pos), 0)),
-                pl.BlockSpec((rows, k), lambda i, pos: (row(i, pos), 0)),
-            ),
+            out_specs=(pl.BlockSpec((1, rows, k), lambda i, pos: (0, row(i, pos), 0)), block),
             scratch_shapes=[pltpu.VMEM((4 * n, k), BF16)],
         ),
         compiler_params=params(16),
-        cost_estimate=cost(8 * n * d * k, 10 << 20),
+        cost_estimate=cost(8 * n * d * k, 12 << 20),
         name="finish",
-    )(pos, *pieces, momentum, own, away, q)
+    )(pos, merged, momentum, own, away, q)
+
+
+TURNS = (2, 1, 3, 0)
 
 
 def shards(inputs, key_grads, error, momentum, q_start):
@@ -415,14 +431,12 @@
     pos = jnp.stack([c, y, z])
 
     args = (inputs, key_grads, error)
-    other_opp, _ = merge(pos, False, TURNS[:1], *args)
-    other_opp, pos = lax.optimization_barrier((other_opp, pos))
-    sent_opp = dp_shift(other_opp, dc=1)
-    other, _ = merge(pos, False, TURNS[1:], *args)
-    other, sent_opp = lax.optimization_barrier((other, sent_opp))
+    other, pos = lax.optimization_barrier((merge(pos, TURNS[:1], *args), pos))
+    sent_opp = dp_shift(other, dc=1)
+    other, sent_opp = lax.optimization_barrier((merge(pos, TURNS[1:], *args), sent_opp))
     sent = dp_shift(other, dc=1)
-    mine_opp, opposite = merge(pos, True, TURNS[:1], *args, sent_opp)
-    mine, sums = merge(pos, True, TURNS[1:], *args, sent)
+    opposite = merge(pos, TURNS[:1], *args, sent_opp)
+    sums = merge(pos, TURNS[1:], *args, sent)
     came = ring_sum(opposite, sums[0:2], sums[2:4], lambda x, d: dp_shift(x, dy=d))
     *opposite, after, before, own = sum_turn(pos, *sums[4:6], came)
     came = small_ring_sum(opposite, after, before, lambda x, d: dp_shift(x, dz=d))
@@ -432,23 +446,24 @@
     of_y, *units = lax.optimization_barrier((of_y, *units))
 
     to_core, part = g_block(pos, units, of_y)
+    to_core, of_y = lax.optimization_barrier((to_core, of_y))
     part = part + dp_shift(to_core, dc=1)
     m1, m3 = dp_shift(of_y, dy=1), dp_shift(of_y, dy=-1)
     (copies,) = spread([exchange(part, None, "shard")], 16, leading=True)
     copies, m1, m3 = lax.optimization_barrier((copies, m1, m3))
     part = exchange(copies, ZY_GROUPS)
-    part, m1, m3 = lax.optimization_barrier((part, m1, m3))
+    part, m1, m3, args, q_t = lax.optimization_barrier((part, m1, m3, args, q_start.T))
     m2_top, m2_end = dp_shift(m1[:128], dy=1), dp_shift(m3[128:], dy=-1)
     part = exchange(spread([part], 8)[0], None, "shard")
-    part, m2_top, m2_end = lax.optimization_barrier((part, m2_top, m2_end))
-    q_t, w = iterate(pos, part, dp_shift(part, dc=1), q_start.T)
+    part, m2_top, m2_end, merged, q_parts = lax.optimization_barrier(
+        (part, m2_top, m2_end, *merge_all(*args, q_t))
+    )
+    q_t, w = iterate(pos, part, dp_shift(part, dc=1), q_parts)
 
     blocks = [of_y, m1, m3, m2_top, m2_end]
     own = left(pos, w, blocks)
     away = dp_shift(own, dc=1)
-    new_error, new_momentum = finish(
-        pos, (mine_opp, mine, other_opp, other), error, momentum, own, away, q_t
-    )
+    new_error, new_momentum = finish(pos, merged, momentum, own, away, q_t)
     return (new_error, new_momentum, q_t.T)
 
 

time: 158 us -> 157 us (level)
  waiting for transfers between devices: 50.9 us -> 43.4 us
  local copies, waits for them, and re-layouts: 8.3 us -> 13.6 us
    ppermute x21, waiting for transfers between devices: 38.7 us -> 32.9 us  [dp_shift(): return lax.ppermute(x, 'dp', pairs)]
    unnamed x28 -> x48, local copies, waits for them, and re-layouts: 7.31 us -> 11.6 us
    pallas_call x6 -> x7, Pallas kernels: 21.9 us -> 23.7 us  [the longest x1 13.6 us: iterate(): pl.pallas_call(iterate_kernel, out_shape=(jax.ShapeDtypeStruct((n, k), F3...]
    all_to_all x2, waiting for transfers between devices: 12.2 us -> 10.5 us  [exchange(): return lax.all_to_all(x, axis, 0, 0, axis_index_groups=groups)]
  transfers between devices with their start and end apart: 23 -> 23, of which waited for: 16 -> 14; matrix products, arithmetic and copies ran while one was open for 1% -> 1% of each run, Pallas kernels for 3% -> 4%
where the time goes in v5:
time: 157 us; the launch traced here: 156 us
  starting transfers between devices  45.1 us (29%)
  waiting for transfers between devices  43.4 us (28%)
  Pallas kernels  27.8 us (18%)
  blocking collectives  25.3 us (16%)
  local copies, waits for them, and re-layouts  13.6 us (9%)
    ppermute x21, starting transfers between devices, dp_shift(): return lax.ppermute(x, 'dp', pairs)  37.1 us
    ppermute x21, waiting for transfers between devices, dp_shift(): return lax.ppermute(x, 'dp', pairs)  32.9 us
    all_to_all x2, blocking collectives, exchange(): return lax.all_to_all(x, axis, 0, 0, axis_index_groups=groups)  25.3 us
    pallas_call x1, Pallas kernels, iterate(): pl.pallas_call(iterate_kernel, out_shape=(jax.ShapeDtypeStruct((n, k), F3...  13.6 us
    unnamed x48, local copies, waits for them, and re-layouts  11.6 us
    all_to_all x2, waiting for transfers between devices, exchange(): return lax.all_to_all(x, axis, 0, 0, axis_index_groups=groups)  10.5 us
    all_to_all x2, starting transfers between devices, exchange(): return lax.all_to_all(x, axis, 0, 0, axis_index_groups=groups)  8.05 us
    pallas_call x4, Pallas kernels, merge(): pl.pallas_call(functools.partial(merge_kernel, turns, own), out_shape=out...  4.3 us
  transfers between devices with their start and end apart: 23, of which 14 were waited for; matrix products, arithmetic and copies ran while one was open for 1% of the time, Pallas kernels for 4%

profile of v5, /device:TPU:1, one launch (start us, length us, event | category | flops | bytes accessed | tf_op | source)
XLA Modules:
  0.0 156.3 jit_solution(3012123436549995097)
XLA Ops:
  0.7 1.6 %copy-done = bf16[1,1024,1024]{2,1,0:T(8,128)(2,1)S(1)} copy-done((bf16[1,1024,1024]{2,1,0:T(8,128)(2,1)S(1)}, bf16[1,1024,1024]{2,1,0:T(8,128)(2,1)}, u32[]{:S(2)}) %copy-start) | copy-done | bytes 2097176
  2.3 1.2 copy-done.2
  5.7 3.3 %collective-permute-start = (f32[1,512,256]{2,1,0:T(8,128)S(1)}, f32[1,512,256]{2,1,0:T(8,128)S(1)}, u32[]{:S(2)}, u32[]{:S(2)}) collective-permute-start(f32[1,512,256]{2,1,0:T(8,128)S(1)} %merge.4), channel_id=1, source_target_pairs={{0,8},{8,0},{16,24},{24,16},{32,40},{40,32},{48,56},{56,48},{64,72... | collective-permute-start | bytes 1572872 | tf_op jit(solution)/shard_map/ppermute | solution.py:29
  12.0 2.7 %collective-permute-start.3 = (f32[256,256]{1,0:T(8,128)S(1)}, f32[256,256]{1,0:T(8,128)S(1)}, u32[]{:S(2)}, u32[]{:S(2)}) collective-permute-start(f32[256,256]{1,0:T(8,128)S(1)} %get-tuple-element.63), channel_id=1, source_target_pairs={{0,48},{8,56},{16,0},{24,8},{32,16},{40,24},{48,32},{56,40},{64,11... | collective-permute-start | bytes 786440 | tf_op jit(solution)/shard_map/ppermute | solution.py:29
  14.7 1.2 merge.6
  16.0 2.7 %collective-permute-start.5 = (f32[256,256]{1,0:T(8,128)S(1)}, f32[256,256]{1,0:T(8,128)S(1)}, u32[]{:S(2)}, u32[]{:S(2)}) collective-permute-start(f32[256,256]{1,0:T(8,128)S(1)} %get-tuple-element.65), channel_id=1, source_target_pairs={{0,48},{8,56},{16,0},{24,8},{32,16},{40,24},{48,32},{56,40},{64,11... | collective-permute-start | bytes 786440 | tf_op jit(solution)/shard_map/ppermute | solution.py:29
  18.7 2.3 %collective-permute-done.2 = f32[256,256]{1,0:T(8,128)S(1)} collective-permute-done((f32[256,256]{1,0:T(8,128)S(1)}, f32[256,256]{1,0:T(8,128)S(1)}, u32[]{:S(2)}, u32[]{:S(2)}) %collective-permute-start.2) | collective-permute-done | bytes 262176 | tf_op jit(solution)/shard_map/ppermute | solution.py:29
  21.0 5.6 %collective-permute-done.4.second = f32[256,256]{1,0:T(8,128)S(1)} collective-permute-done((f32[256,256]{1,0:T(8,128)S(1)}, f32[256,256]{1,0:T(8,128)S(1)}, u32[]{:S(2)}, u32[]{:S(2)}) %collective-permute-start.4) | collective-permute-done | bytes 262176 | tf_op jit(solution)/shard_map/ppermute | solution.py:29
  26.8 2.7 %collective-permute-start.7 = (f32[256,256]{1,0:T(8,128)S(1)}, f32[256,256]{1,0:T(8,128)S(1)}, u32[]{:S(2)}, u32[]{:S(2)}) collective-permute-start(f32[256,256]{1,0:T(8,128)S(1)} %add.31), channel_id=1, source_target_pairs={{0,48},{8,56},{16,0},{24,8},{32,16},{40,24},{48,32},{56,40},{64,11... | collective-permute-start | bytes 786440 | tf_op jit(solution)/shard_map/ppermute | solution.py:29
  29.5 5.3 %collective-permute-done.6.on = f32[256,256]{1,0:T(8,128)S(1)} collective-permute-done((f32[256,256]{1,0:T(8,128)S(1)}, f32[256,256]{1,0:T(8,128)S(1)}, u32[]{:S(2)}, u32[]{:S(2)}) %collective-permute-start.6) | collective-permute-done | bytes 262176 | tf_op jit(solution)/shard_map/ppermute | solution.py:29
  35.6 4.5 %collective-permute-start.10 = (f32[32,512]{1,0:T(8,128)S(1)}, f32[32,512]{1,0:T(8,128)S(1)}, u32[]{:S(2)}, u32[]{:S(2)}) collective-permute-start(f32[32,512]{1,0:T(8,128)S(1)} %get-tuple-element.75), channel_id=1, source_target_pairs={{0,192},{8,200},{16,208},{24,216},{32,224},{40,232},{48,240},{56,2... | collective-permute-start | bytes 196616 | tf_op jit(solution)/shard_map/ppermute | solution.py:29
  40.1 1.3 collective-permute-done.10
  41.4 4.5 %collective-permute-start.11 = (f32[64,512]{1,0:T(8,128)S(1)}, f32[64,512]{1,0:T(8,128)S(1)}, u32[]{:S(2)}, u32[]{:S(2)}) collective-permute-start(f32[64,512]{1,0:T(8,128)S(1)} %pad_add_fusion), channel_id=1, source_target_pairs={{0,192},{8,200},{16,208},{24,216},{32,224},{40,232},{48,240},{56,2... | collective-permute-start | bytes 393224 | tf_op jit(solution)/shard_map/ppermute | solution.py:29
  46.1 3.2 %collective-permute-done.11.refs_2_ = f32[64,512]{1,0:T(8,128)S(1)} collective-permute-done((f32[64,512]{1,0:T(8,128)S(1)}, f32[64,512]{1,0:T(8,128)S(1)}, u32[]{:S(2)}, u32[]{:S(2)}) %collective-permute-start.11) | collective-permute-done | bytes 131104 | tf_op jit(solution)/shard_map/ppermute | solution.py:29
  49.3 4.6 %collective-permute-done.9.refs_1_ = f32[64,512]{1,0:T(8,128)S(1)} collective-permute-done((f32[64,512]{1,0:T(8,128)S(1)}, f32[64,512]{1,0:T(8,128)S(1)}, u32[]{:S(2)}, u32[]{:S(2)}) %collective-permute-start.9) | collective-permute-done | bytes 131104 | tf_op jit(solution)/shard_map/ppermute | solution.py:29
  54.7 3.5 %all-to-all-start = ((f32[4,64,512]{2,1,0:T(8,128)}), f32[4,64,512]{2,1,0:T(8,128)S(1)}, u32[]{:S(2)}, u32[]{:S(2)}) async-start(f32[4,64,512]{2,1,0:T(8,128)} %get-tuple-element.76), calls=%async_computation | async-start | bytes 1048576 | tf_op jit(solution)/shard_map/all_to_all | solution.py:49
  58.8 1.2 collective-permute-start.12
  60.0 3.7 %collective-permute-done.13.u2 = f32[64,512]{1,0:T(8,128)S(1)} collective-permute-done((f32[64,512]{1,0:T(8,128)S(1)}, f32[64,512]{1,0:T(8,128)S(1)}, u32[]{:S(2)}, u32[]{:S(2)}) %collective-permute-start.13) | collective-permute-done | bytes 131104 | tf_op jit(solution)/shard_map/ppermute | solution.py:29
  63.7 1.3 collective-permute-done.12.u1
  65.0 4.4 %all-to-all-done = f32[4,64,512]{2,1,0:T(8,128)S(1)} async-done(((f32[4,64,512]{2,1,0:T(8,128)}), f32[4,64,512]{2,1,0:T(8,128)S(1)}, u32[]{:S(2)}, u32[]{:S(2)}) %all-to-all-start) | async-done | bytes 524320 | tf_op jit(solution)/shard_map/all_to_all | solution.py:49
  69.5 1.2 g_block.1
  72.3 6.0 %collective-permute-start.14 = (f32[8,3,8,128]{3,2,1,0:T(8,128)S(1)}, f32[8,3,8,128]{3,2,1,0:T(8,128)S(1)}, u32[]{:S(2)}, u32[]{:S(2)}) collective-permute-start(f32[8,3,8,128]{3,2,1,0:T(8,128)S(1)} %get-tuple-element.84), channel_id=1, source_target_pairs={{0,8},{8,0},{16,24},{24,16},{32,40},{40,32},{48,56},{56,48},{64,72... | collective-permute-start | bytes 294920 | tf_op jit(solution)/shard_map/ppermute | solution.py:29
  79.2 9.8 %all_to_all.20.refs_0_ = f32[8,3,8,128]{3,2,1,0:T(8,128)S(1)} all-to-all(f32[8,3,8,128]{3,2,1,0:T(8,128)S(1)} %add.34), channel_id=1, replica_groups=mesh['dp'=32,'shard'=8] {'shard'}, dimensions={0} | all-to-all | bytes 196608 | tf_op jit(solution)/shard_map/all_to_all | solution.py:49
  89.0 15.6 %all_to_all.21.refs_0_ = f32[16,3,8,128]{3,2,1,0:T(8,128)S(1)} all-to-all(f32[16,3,8,128]{3,2,1,0:T(8,128)S(1)} %spread.4), channel_id=1, replica_groups={{0,16,32,48,64,80,96,112,128,144,160,176,192,208,224,240},{8,24,40,56,7..., dimensions={0} | all-to-all | bytes 393216 | tf_op jit(solution)/shard_map/all_to_all | solution.py:49
  105.9 4.6 %all-to-all-start.3 = ((f32[8,16,3,8,128]{4,3,2,1,0:T(8,128)}), f32[8,16,3,8,128]{4,3,2,1,0:T(8,128)}, u32[]{:S(2)}, u32[]{:S(2)}) async-start(f32[8,16,3,8,128]{4,3,2,1,0:T(8,128)} %copy-done.6), calls=%async_computation.3 | async-start | bytes 3145728 | tf_op jit(solution)/shard_map/all_to_all | solution.py:49
  115.2 2.1 %merge_all.1 = (f32[1024,1024]{1,0:T(8,128)S(1)}, bf16[3,64,1024]{2,1,0:T(8,128)(2,1)S(1)}) custom-call(bf16[512,1024]{1,0:T(8,128)(2,1)S(1)} %copy-done.3, bf16[512,1024]{1,0:T(8,128)(2,1)S(1)} %copy-done.5, bf16[1,1024,1024]{2,1,0:T(8,128)(2,1)S(1)} %copy-done.1, f32[64,1024]{1,0:T(8,128)S(1)} %bitcast.10), custom_call_target="tpu_custom_call" | custom-call | flops 1073741824 | bytes 8388608 | tf_op jit(solution)/shard_map/merge_all/pallas_call | solution.py:122
  117.3 2.0 %copy-done.7 = f32[1024,1024]{1,0:T(8,128)} copy-done((f32[1024,1024]{1,0:T(8,128)}, f32[1024,1024]{1,0:T(8,128)S(1)}, u32[]{:S(2)}) %copy-start.7) | copy-done | bytes 4194328
  121.5 6.0 %all-to-all-done.3.own_ref = f32[8,16,3,8,128]{4,3,2,1,0:T(8,128)} async-done(((f32[8,16,3,8,128]{4,3,2,1,0:T(8,128)}), f32[8,16,3,8,128]{4,3,2,1,0:T(8,128)}, u32[]{:S(2)}, u32[]{:S(2)}) %all-to-all-start.3) | async-done | bytes 1572896 | tf_op jit(solution)/shard_map/all_to_all | solution.py:49
  127.6 4.6 %collective-permute-start.19 = (f32[8,16,3,8,128]{4,3,2,1,0:T(8,128)}, f32[8,16,3,8,128]{4,3,2,1,0:T(8,128)S(1)}, u32[]{:S(2)}, u32[]{:S(2)}) collective-permute-start(f32[8,16,3,8,128]{4,3,2,1,0:T(8,128)} %all-to-all-done.3.own_ref), channel_id=1, source_target_pairs={{0,8},{8,0},{16,24},{24,16},{32,40},{40,32},{48,56},{56,48},{64,72... | collective-permute-start | bytes 4718600 | tf_op jit(solution)/shard_map/ppermute | solution.py:29
  132.2 3.2 %collective-permute-done.19.away_ref = f32[8,16,3,8,128]{4,3,2,1,0:T(8,128)S(1)} collective-permute-done((f32[8,16,3,8,128]{4,3,2,1,0:T(8,128)}, f32[8,16,3,8,128]{4,3,2,1,0:T(8,128)S(1)}, u32[]{:S(2)}, u32[]{:S(2)}) %collective-permute-start.19) | collective-permute-done | bytes 1572896 | tf_op jit(solution)/shard_map/ppermute | solution.py:29
  136.4 13.6 %iterations.1 = (f32[64,1024]{1,0:T(8,128)}, f32[64,1024]{1,0:T(8,128)S(1)}) custom-call(s32[3]{0:T(128)S(1)} %pad_add_fusion.2.pos_ref, f32[8,16,3,8,128]{4,3,2,1,0:T(8,128)} %all-to-all-done.3.own_ref, f32[8,16,3,8,128]{4,3,2,1,0:T(8,128)S(1)} %collective-permute-done.19.away_ref, bf16[3,64,1024]{2,1,0:T(8,128)(2,1)S(1)} %copy-done.23), custom_call_target="tpu_custom_call" | custom-call | flops 2415919104 | bytes 4194304 | tf_op jit(solution)/shard_map/iterations/pallas_call | solution.py:336
  152.7 3.7 %finish.1 = (bf16[1,1024,1024]{2,1,0:T(8,128)(2,1)}, bf16[1024,1024]{1,0:T(8,128)(2,1)}) custom-call(s32[3]{0:T(128)S(1)} %pad_add_fusion.2.pos_ref, f32[1024,1024]{1,0:T(8,128)S(1)} %copy-done.8, bf16[1024,1024]{1,0:T(8,128)(2,1)S(1)} %copy-done.9, f32[64,512]{1,0:T(8,128)S(1)} %left.1.own, f32[64,512]{1,0:T(8,128)S(1)} %collective-permute-done.20.away, ...), custom_call_target="tpu_custom_call" | custom-call | flops 536870912 | bytes 12582912 | tf_op jit(solution)/shard_map/finish/pallas_call | solution.py:403
  (85 shorter events, 22.0 us)
Async XLA Ops:
  5.7 4.9 %collective-permute-start = (f32[1,512,256]{2,1,0:T(8,128)S(1)}, f32[1,512,256]{2,1,0:T(8,128)S(1)}, u32[]{:S(2)}, u32[]{:S(2)}) collective-permute-start(f32[1,512,256]{2,1,0:T(8,128)S(1)} %merge.4), channel_id=1, source_target_pairs={{0,8},{8,0},{16,24},{24,16},{32,40},{40,32},{48,56},{56,48},{64,72... | collective-permute-start | bytes 1572872 | tf_op jit(solution)/shard_map/ppermute | solution.py:29
  10.6 4.1 %collective-permute-start.1 = (f32[3,512,256]{2,1,0:T(8,128)S(1)}, f32[3,512,256]{2,1,0:T(8,128)S(1)}, u32[]{:S(2)}, u32[]{:S(2)}) collective-permute-start(f32[3,512,256]{2,1,0:T(8,128)S(1)} %merge.5), channel_id=1, source_target_pairs={{0,8},{8,0},{16,24},{24,16},{32,40},{40,32},{48,56},{56,48},{64,72... | collective-permute-start | bytes 4718600 | tf_op jit(solution)/shard_map/ppermute | solution.py:29
  11.9 9.1 %collective-permute-start.2 = (f32[256,256]{1,0:T(8,128)S(1)}, f32[256,256]{1,0:T(8,128)S(1)}, u32[]{:S(2)}, u32[]{:S(2)}) collective-permute-start(f32[256,256]{1,0:T(8,128)S(1)} %get-tuple-element.62), channel_id=1, source_target_pairs={{0,16},{8,24},{16,32},{24,40},{32,48},{40,56},{48,0},{56,8},{64,80... | collective-permute-start | bytes 786440 | tf_op jit(solution)/shard_map/ppermute | solution.py:29
  12.0 9.0 %collective-permute-start.3 = (f32[256,256]{1,0:T(8,128)S(1)}, f32[256,256]{1,0:T(8,128)S(1)}, u32[]{:S(2)}, u32[]{:S(2)}) collective-permute-start(f32[256,256]{1,0:T(8,128)S(1)} %get-tuple-element.63), channel_id=1, source_target_pairs={{0,48},{8,56},{16,0},{24,8},{32,16},{40,24},{48,32},{56,40},{64,11... | collective-permute-start | bytes 786440 | tf_op jit(solution)/shard_map/ppermute | solution.py:29
  15.9 10.7 %collective-permute-start.4 = (f32[256,256]{1,0:T(8,128)S(1)}, f32[256,256]{1,0:T(8,128)S(1)}, u32[]{:S(2)}, u32[]{:S(2)}) collective-permute-start(f32[256,256]{1,0:T(8,128)S(1)} %get-tuple-element.64), channel_id=1, source_target_pairs={{0,16},{8,24},{16,32},{24,40},{32,48},{40,56},{48,0},{56,8},{64,80... | collective-permute-start | bytes 786440 | tf_op jit(solution)/shard_map/ppermute | solution.py:29
  16.0 10.6 %collective-permute-start.5 = (f32[256,256]{1,0:T(8,128)S(1)}, f32[256,256]{1,0:T(8,128)S(1)}, u32[]{:S(2)}, u32[]{:S(2)}) collective-permute-start(f32[256,256]{1,0:T(8,128)S(1)} %get-tuple-element.65), channel_id=1, source_target_pairs={{0,48},{8,56},{16,0},{24,8},{32,16},{40,24},{48,32},{56,40},{64,11... | collective-permute-start | bytes 786440 | tf_op jit(solution)/shard_map/ppermute | solution.py:29
  26.6 8.1 %collective-permute-start.6 = (f32[256,256]{1,0:T(8,128)S(1)}, f32[256,256]{1,0:T(8,128)S(1)}, u32[]{:S(2)}, u32[]{:S(2)}) collective-permute-start(f32[256,256]{1,0:T(8,128)S(1)} %add.30), channel_id=1, source_target_pairs={{0,16},{8,24},{16,32},{24,40},{32,48},{40,56},{48,0},{56,8},{64,80... | collective-permute-start | bytes 786440 | tf_op jit(solution)/shard_map/ppermute | solution.py:29
  26.8 8.0 %collective-permute-start.7 = (f32[256,256]{1,0:T(8,128)S(1)}, f32[256,256]{1,0:T(8,128)S(1)}, u32[]{:S(2)}, u32[]{:S(2)}) collective-permute-start(f32[256,256]{1,0:T(8,128)S(1)} %add.31), channel_id=1, source_target_pairs={{0,48},{8,56},{16,0},{24,8},{32,16},{40,24},{48,32},{56,40},{64,11... | collective-permute-start | bytes 786440 | tf_op jit(solution)/shard_map/ppermute | solution.py:29
  35.6 5.8 %collective-permute-start.10 = (f32[32,512]{1,0:T(8,128)S(1)}, f32[32,512]{1,0:T(8,128)S(1)}, u32[]{:S(2)}, u32[]{:S(2)}) collective-permute-start(f32[32,512]{1,0:T(8,128)S(1)} %get-tuple-element.75), channel_id=1, source_target_pairs={{0,192},{8,200},{16,208},{24,216},{32,224},{40,232},{48,240},{56,2... | collective-permute-start | bytes 196616 | tf_op jit(solution)/shard_map/ppermute | solution.py:29
  40.1 5.9 %collective-permute-start.8 = (f32[32,512]{1,0:T(8,128)S(1)}, f32[32,512]{1,0:T(8,128)S(1)}, u32[]{:S(2)}, u32[]{:S(2)}) collective-permute-start(f32[32,512]{1,0:T(8,128)S(1)} %get-tuple-element.73), channel_id=1, source_target_pairs={{0,64},{8,72},{16,80},{24,88},{32,96},{40,104},{48,112},{56,120},{... | collective-permute-start | bytes 196616 | tf_op jit(solution)/shard_map/ppermute | solution.py:29
  41.4 7.8 %collective-permute-start.11 = (f32[64,512]{1,0:T(8,128)S(1)}, f32[64,512]{1,0:T(8,128)S(1)}, u32[]{:S(2)}, u32[]{:S(2)}) collective-permute-start(f32[64,512]{1,0:T(8,128)S(1)} %pad_add_fusion), channel_id=1, source_target_pairs={{0,192},{8,200},{16,208},{24,216},{32,224},{40,232},{48,240},{56,2... | collective-permute-start | bytes 393224 | tf_op jit(solution)/shard_map/ppermute | solution.py:29
  46.0 7.9 %collective-permute-start.9 = (f32[64,512]{1,0:T(8,128)S(1)}, f32[64,512]{1,0:T(8,128)S(1)}, u32[]{:S(2)}, u32[]{:S(2)}) collective-permute-start(f32[64,512]{1,0:T(8,128)S(1)} %pad_add_fusion.1), channel_id=1, source_target_pairs={{0,64},{8,72},{16,80},{24,88},{32,96},{40,104},{48,112},{56,120},{... | collective-permute-start | bytes 393224 | tf_op jit(solution)/shard_map/ppermute | solution.py:29
  54.7 14.7 %all-to-all-start = ((f32[4,64,512]{2,1,0:T(8,128)}), f32[4,64,512]{2,1,0:T(8,128)S(1)}, u32[]{:S(2)}, u32[]{:S(2)}) async-start(f32[4,64,512]{2,1,0:T(8,128)} %get-tuple-element.76), calls=%async_computation | async-start | bytes 1048576 | tf_op jit(solution)/shard_map/all_to_all | solution.py:49
  58.2 5.5 %collective-permute-start.13 = (f32[64,512]{1,0:T(8,128)S(1)}, f32[64,512]{1,0:T(8,128)S(1)}, u32[]{:S(2)}, u32[]{:S(2)}) collective-permute-start(f32[64,512]{1,0:T(8,128)S(1)} %get-tuple-element.78.u0), channel_id=1, source_target_pairs={{0,32},{8,40},{16,48},{24,56},{32,0},{40,8},{48,16},{56,24},{64,96... | collective-permute-start | bytes 393224 | tf_op jit(solution)/shard_map/ppermute | solution.py:29
  58.8 6.2 %collective-permute-start.12 = (f32[64,512]{1,0:T(8,128)S(1)}, f32[64,512]{1,0:T(8,128)S(1)}, u32[]{:S(2)}, u32[]{:S(2)}) collective-permute-start(f32[64,512]{1,0:T(8,128)S(1)} %get-tuple-element.78.u0), channel_id=1, source_target_pairs={{0,16},{8,24},{16,32},{24,40},{32,48},{40,56},{48,0},{56,8},{64,80... | collective-permute-start | bytes 393224 | tf_op jit(solution)/shard_map/ppermute | solution.py:29
  69.5 35.2 %copy-start.10 = (f32[4,64,512]{2,1,0:T(8,128)}, f32[4,64,512]{2,1,0:T(8,128)S(1)}, u32[]{:S(2)}) copy-start(f32[4,64,512]{2,1,0:T(8,128)S(1)} %all-to-all-done) | copy-start | bytes 1572868
  70.7 18.3 %collective-permute-start.16 = (f32[256,512]{1,0:T(8,128)S(1)}, f32[256,512]{1,0:T(8,128)S(1)}, u32[]{:S(2)}, u32[]{:S(2)}) collective-permute-start(f32[256,512]{1,0:T(8,128)S(1)} %bitcast.7), channel_id=1, source_target_pairs={{0,48},{8,56},{16,0},{24,8},{32,16},{40,24},{48,32},{56,40},{64,11... | collective-permute-start | bytes 1572872 | tf_op jit(solution)/shard_map/ppermute | solution.py:29
  71.5 17.5 %collective-permute-start.15 = (f32[256,512]{1,0:T(8,128)S(1)}, f32[256,512]{1,0:T(8,128)S(1)}, u32[]{:S(2)}, u32[]{:S(2)}) collective-permute-start(f32[256,512]{1,0:T(8,128)S(1)} %bitcast.8), channel_id=1, source_target_pairs={{0,16},{8,24},{16,32},{24,40},{32,48},{40,56},{48,0},{56,8},{64,80... | collective-permute-start | bytes 1572872 | tf_op jit(solution)/shard_map/ppermute | solution.py:29
  72.3 6.9 %collective-permute-start.14 = (f32[8,3,8,128]{3,2,1,0:T(8,128)S(1)}, f32[8,3,8,128]{3,2,1,0:T(8,128)S(1)}, u32[]{:S(2)}, u32[]{:S(2)}) collective-permute-start(f32[8,3,8,128]{3,2,1,0:T(8,128)S(1)} %get-tuple-element.84), channel_id=1, source_target_pairs={{0,8},{8,0},{16,24},{24,16},{32,40},{40,32},{48,56},{56,48},{64,72... | collective-permute-start | bytes 294920 | tf_op jit(solution)/shard_map/ppermute | solution.py:29
  89.0 15.6 %copy-start.12 = (f32[256,512]{1,0:T(8,128)}, f32[256,512]{1,0:T(8,128)S(1)}, u32[]{:S(2)}) copy-start(f32[256,512]{1,0:T(8,128)S(1)} %collective-permute-done.16.m3) | copy-start | bytes 1572868
  89.0 15.6 %copy-start.14 = (f32[256,512]{1,0:T(8,128)}, f32[256,512]{1,0:T(8,128)S(1)}, u32[]{:S(2)}) copy-start(f32[256,512]{1,0:T(8,128)S(1)} %collective-permute-done.15.m1) | copy-start | bytes 1572868
  105.9 21.7 %all-to-all-start.3 = ((f32[8,16,3,8,128]{4,3,2,1,0:T(8,128)}), f32[8,16,3,8,128]{4,3,2,1,0:T(8,128)}, u32[]{:S(2)}, u32[]{:S(2)}) async-start(f32[8,16,3,8,128]{4,3,2,1,0:T(8,128)} %copy-done.6), calls=%async_computation.3 | async-start | bytes 3145728 | tf_op jit(solution)/shard_map/all_to_all | solution.py:49
  112.4 7.6 %collective-permute-start.18 = (f32[128,512]{1,0:T(8,128)S(1)}, f32[128,512]{1,0:T(8,128)S(1)}, u32[]{:S(2)}, u32[]{:S(2)}) collective-permute-start(f32[128,512]{1,0:T(8,128)S(1)} %slice.7), channel_id=1, source_target_pairs={{0,48},{8,56},{16,0},{24,8},{32,16},{40,24},{48,32},{56,40},{64,11... | collective-permute-start | bytes 786440 | tf_op jit(solution)/shard_map/ppermute | solution.py:29
  113.3 7.5 %collective-permute-start.17 = (f32[128,512]{1,0:T(8,128)S(1)}, f32[128,512]{1,0:T(8,128)S(1)}, u32[]{:S(2)}, u32[]{:S(2)}) collective-permute-start(f32[128,512]{1,0:T(8,128)S(1)} %slice.6), channel_id=1, source_target_pairs={{0,16},{8,24},{16,32},{24,40},{32,48},{40,56},{48,0},{56,8},{64,80... | collective-permute-start | bytes 786440 | tf_op jit(solution)/shard_map/ppermute | solution.py:29
  127.6 22.5 %copy-start.11 = (f32[4,64,512]{2,1,0:T(8,128)S(1)}, f32[4,64,512]{2,1,0:T(8,128)}, u32[]{:S(2)}) copy-start(f32[4,64,512]{2,1,0:T(8,128)} %copy-done.10) | copy-start | bytes 1572868
  127.6 22.5 %copy-start.13 = (f32[256,512]{1,0:T(8,128)S(1)}, f32[256,512]{1,0:T(8,128)}, u32[]{:S(2)}) copy-start(f32[256,512]{1,0:T(8,128)} %copy-done.12) | copy-start | bytes 1572868
  127.6 22.5 %copy-start.15 = (f32[256,512]{1,0:T(8,128)S(1)}, f32[256,512]{1,0:T(8,128)}, u32[]{:S(2)}) copy-start(f32[256,512]{1,0:T(8,128)} %copy-done.14) | copy-start | bytes 1572868
  127.6 22.5 %copy-start.19 = (f32[128,512]{1,0:T(8,128)S(1)}, f32[128,512]{1,0:T(8,128)}, u32[]{:S(2)}) copy-start(f32[128,512]{1,0:T(8,128)} %copy-done.18) | copy-start | bytes 786436
  127.6 22.5 %copy-start.21 = (f32[128,512]{1,0:T(8,128)S(1)}, f32[128,512]{1,0:T(8,128)}, u32[]{:S(2)}) copy-start(f32[128,512]{1,0:T(8,128)} %copy-done.20) | copy-start | bytes 786436
  127.6 7.8 %collective-permute-start.19 = (f32[8,16,3,8,128]{4,3,2,1,0:T(8,128)}, f32[8,16,3,8,128]{4,3,2,1,0:T(8,128)S(1)}, u32[]{:S(2)}, u32[]{:S(2)}) collective-permute-start(f32[8,16,3,8,128]{4,3,2,1,0:T(8,128)} %all-to-all-done.3.own_ref), channel_id=1, source_target_pairs={{0,8},{8,0},{16,24},{24,16},{32,40},{40,32},{48,56},{56,48},{64,72... | collective-permute-start | bytes 4718600 | tf_op jit(solution)/shard_map/ppermute | solution.py:29
  136.4 16.2 %copy-start.8 = (f32[1024,1024]{1,0:T(8,128)S(1)}, f32[1024,1024]{1,0:T(8,128)}, u32[]{:S(2)}) copy-start(f32[1024,1024]{1,0:T(8,128)} %copy-done.7) | copy-start | bytes 12582916
  151.2 1.5 collective-permute-start.20
  (15 other events, 41.1 us)

commit v6 on v5

--- a/solution.py
+++ b/solution.py
@@ -29,12 +29,11 @@
     return lax.ppermute(x, "dp", pairs)
 
 
-def ring_sum(opposite, following, before, step):
+def ring_sum(opposite, following, before, own, step):
     relay_on, relay_back = step(opposite[0], 1), step(opposite[1], -1)
     second, first = step(following[1], 1), step(before[0], -1)
-    relay_on, relay_back, second, first = lax.optimization_barrier((relay_on, relay_back, second, first))
     on, back = step(following[0] + relay_on, 1), step(before[1] + relay_back, -1)
-    return on, second, first, back
+    return own[0] + first, own[1] + second, on, back
 
 
 def small_ring_sum(opposite, following, before, step):
@@ -139,9 +138,9 @@
     )(inputs, key_grads, error, q)
 
 
-def sum_turn_kernel(pos_ref, top, end, on, second, first, back, opp_top, opp_end, after, before, own, turned):
-    turned[:, :256] = (top[...] + (on[...] + first[...])).T
-    turned[:, 256:] = (end[...] + (second[...] + back[...])).T
+def sum_turn_kernel(pos_ref, top, end, on, back, opp_top, opp_end, after, before, own, turned):
+    turned[:, :256] = (top[...] + on[...]).T
+    turned[:, 256:] = (end[...] + back[...]).T
     z = pos_ref[2]
 
     def rows(turn, start, size):
@@ -154,18 +153,18 @@
     own[...] = rows(0, 0, 64)
 
 
-def sum_turn(pos, top, end, came):
+def sum_turn(pos, parts):
     outs = tuple(jax.ShapeDtypeStruct((n, 512), F32) for n in (32, 32, 64, 64, 64))
     return pl.pallas_call(
         sum_turn_kernel,
         out_shape=outs,
-        in_specs=[SMEM] + [VMEM] * 6,
+        in_specs=[SMEM] + [VMEM] * 4,
         out_specs=(VMEM,) * 5,
         scratch_shapes=[pltpu.VMEM((256, 512), F32)],
-        compiler_params=params(16),
+        compiler_params=params(12),
         cost_estimate=cost(4 << 17, 3 << 20),
         name="sum_turn",
-    )(pos, top, end, *came)
+    )(pos, *parts)
 
 
 def spread_kernel(leading, keep, *refs):
@@ -189,7 +188,7 @@
         out_shape=outs,
         in_specs=[VMEM] * len(parts),
         out_specs=(VMEM,) * len(outs),
-        compiler_params=params(16),
+        compiler_params=params(10),
         cost_estimate=cost(1 << 17, 1 << 20),
         name="spread",
     )(*parts)
@@ -223,7 +222,7 @@
         out_shape=(jax.ShapeDtypeStruct((8, 3, 8, 128), F32),) * 2,
         in_specs=[SMEM] + [VMEM] * 4,
         out_specs=(VMEM, VMEM),
-        compiler_params=params(16),
+        compiler_params=params(12),
         cost_estimate=cost(2 * 6 * 192 * k * d, 2 << 20),
         name="g_block",
     )(pos, *units, of_y)
@@ -279,14 +278,16 @@
     parts = (hi_ref, mid_ref, low_ref)
     for ref, core in ((own_ref, pos_ref[0]), (away_ref, 1 - pos_ref[0])):
         for z in range(4):
+            ready = []
             for y in range(4):
+                for e in range(3):
+                    both = jnp.concatenate([ref[0, z * 4 + y, e], ref[1, z * 4 + y, e]], axis=0)
+                    ready.append((y, e, split3(both)))
+            for y, e, values in ready:
                 to = pl.ds(pl.multiple_of(y * 256 + core * 128, 128), 128)
-                for e in range(3):
-                    start = (y - e) % 4 * 256 + z * 64 + s * 16
-                    at = pl.ds(pl.multiple_of(start, 16), 16)
-                    both = jnp.concatenate([ref[0, z * 4 + y, e], ref[1, z * 4 + y, e]], axis=0)
-                    for part, value in zip(parts, split3(both)):
-                        part[at, to] = value
+                at = pl.ds(pl.multiple_of((y - e) % 4 * 256 + z * 64 + s * 16, 16), 16)
+                for part, value in zip(parts, values):
+                    part[at, to] = value
 
     @pl.when(s == pl.num_programs(0) - 1)
     def _():
@@ -366,7 +367,7 @@
         out_shape=jax.ShapeDtypeStruct((n, d), F32),
         in_specs=[SMEM] + [VMEM] * 6,
         out_specs=VMEM,
-        compiler_params=params(16),
+        compiler_params=params(12),
         cost_estimate=cost(6 * n * d * 1024, 2 << 20),
         name="left",
     )(pos, w, *blocks)
@@ -437,8 +438,8 @@
     sent = dp_shift(other, dc=1)
     opposite = merge(pos, TURNS[:1], *args, sent_opp)
     sums = merge(pos, TURNS[1:], *args, sent)
-    came = ring_sum(opposite, sums[0:2], sums[2:4], lambda x, d: dp_shift(x, dy=d))
-    *opposite, after, before, own = sum_turn(pos, *sums[4:6], came)
+    parts = ring_sum(opposite, sums[0:2], sums[2:4], sums[4:6], lambda x, d: dp_shift(x, dy=d))
+    *opposite, after, before, own = sum_turn(pos, parts)
     came = small_ring_sum(opposite, after, before, lambda x, d: dp_shift(x, dz=d))
     copies, unit = spread([own, *came], 4, keep=True)
     units = [unit] + [dp_shift(unit, dy=dy) for dy in (1, 2)]

time: 157 us -> 155 us (0.987)
  waiting for transfers between devices: 43.4 us -> 39 us
  starting transfers between devices: 45.1 us -> 46.8 us
    all_to_all x2, waiting for transfers between devices: 10.5 us -> 7.91 us  [exchange(): return lax.all_to_all(x, axis, 0, 0, axis_index_groups=groups)]
    ppermute x21, waiting for transfers between devices: 32.9 us -> 31.1 us  [dp_shift(): return lax.ppermute(x, 'dp', pairs)]
    ppermute x21, starting transfers between devices: 37.1 us -> 38.8 us  [dp_shift(): return lax.ppermute(x, 'dp', pairs)]
  transfers between devices with their start and end apart: 23 -> 23, of which waited for: 14 -> 15; matrix products, arithmetic and copies ran while one was open for 1% -> 1% of each run, Pallas kernels for 4% -> 4%
where the time goes in v6:
time: 155 us; the launch traced here: 154 us
  starting transfers between devices  46.8 us (30%)
  waiting for transfers between devices  39 us (25%)
  Pallas kernels  27.8 us (18%)
  blocking collectives  25.8 us (17%)
  local copies, waits for them, and re-layouts  13.6 us (9%)
    ppermute x21, starting transfers between devices, dp_shift(): return lax.ppermute(x, 'dp', pairs)  38.8 us
    ppermute x21, waiting for transfers between devices, dp_shift(): return lax.ppermute(x, 'dp', pairs)  31.1 us
    all_to_all x2, blocking collectives, exchange(): return lax.all_to_all(x, axis, 0, 0, axis_index_groups=groups)  25.8 us
    pallas_call x1, Pallas kernels, iterate(): pl.pallas_call(iterate_kernel, out_shape=(jax.ShapeDtypeStruct((n, k), F3...  13.6 us
    unnamed x48, local copies, waits for them, and re-layouts  11.6 us
    all_to_all x2, starting transfers between devices, exchange(): return lax.all_to_all(x, axis, 0, 0, axis_index_groups=groups)  8.05 us
    all_to_all x2, waiting for transfers between devices, exchange(): return lax.all_to_all(x, axis, 0, 0, axis_index_groups=groups)  7.91 us
    pallas_call x4, Pallas kernels, merge(): pl.pallas_call(functools.partial(merge_kernel, turns, own), out_shape=out...  4.3 us
  transfers between devices with their start and end apart: 23, of which 15 were waited for; matrix products, arithmetic and copies ran while one was open for 1% of the time, Pallas kernels for 4%

profile of v6, /device:TPU:1, one launch (start us, length us, event | category | flops | bytes accessed | tf_op | source)
XLA Modules:
  0.0 154.2 jit_solution(58148369324077638)
XLA Ops:
  0.7 1.6 %copy-done = bf16[1,1024,1024]{2,1,0:T(8,128)(2,1)S(1)} copy-done((bf16[1,1024,1024]{2,1,0:T(8,128)(2,1)S(1)}, bf16[1,1024,1024]{2,1,0:T(8,128)(2,1)}, u32[]{:S(2)}) %copy-start) | copy-done | bytes 2097176
  2.3 1.2 copy-done.2
  5.7 3.3 %collective-permute-start = (f32[1,512,256]{2,1,0:T(8,128)S(1)}, f32[1,512,256]{2,1,0:T(8,128)S(1)}, u32[]{:S(2)}, u32[]{:S(2)}) collective-permute-start(f32[1,512,256]{2,1,0:T(8,128)S(1)} %merge.4), channel_id=1, source_target_pairs={{0,8},{8,0},{16,24},{24,16},{32,40},{40,32},{48,56},{56,48},{64,72... | collective-permute-start | bytes 1572872 | tf_op jit(solution)/shard_map/ppermute | solution.py:29
  12.0 2.7 %collective-permute-start.6 = (f32[256,256]{1,0:T(8,128)S(1)}, f32[256,256]{1,0:T(8,128)S(1)}, u32[]{:S(2)}, u32[]{:S(2)}) collective-permute-start(f32[256,256]{1,0:T(8,128)S(1)} %get-tuple-element.62), channel_id=1, source_target_pairs={{0,48},{8,56},{16,0},{24,8},{32,16},{40,24},{48,32},{56,40},{64,11... | collective-permute-start | bytes 786440 | tf_op jit(solution)/shard_map/ppermute | solution.py:29
  14.7 1.2 merge.6
  17.4 3.5 %collective-permute-done.4 = f32[256,256]{1,0:T(8,128)S(1)} collective-permute-done((f32[256,256]{1,0:T(8,128)S(1)}, f32[256,256]{1,0:T(8,128)S(1)}, u32[]{:S(2)}, u32[]{:S(2)}) %collective-permute-start.4) | collective-permute-done | bytes 262176 | tf_op jit(solution)/shard_map/ppermute | solution.py:29
  21.1 2.7 %collective-permute-start.7 = (f32[256,256]{1,0:T(8,128)S(1)}, f32[256,256]{1,0:T(8,128)S(1)}, u32[]{:S(2)}, u32[]{:S(2)}) collective-permute-start(f32[256,256]{1,0:T(8,128)S(1)} %add.39), channel_id=1, source_target_pairs={{0,48},{8,56},{16,0},{24,8},{32,16},{40,24},{48,32},{56,40},{64,11... | collective-permute-start | bytes 786440 | tf_op jit(solution)/shard_map/ppermute | solution.py:29
  23.9 1.7 %collective-permute-done.2 = f32[256,256]{1,0:T(8,128)S(1)} collective-permute-done((f32[256,256]{1,0:T(8,128)S(1)}, f32[256,256]{1,0:T(8,128)S(1)}, u32[]{:S(2)}, u32[]{:S(2)}) %collective-permute-start.2) | collective-permute-done | bytes 262176 | tf_op jit(solution)/shard_map/ppermute | solution.py:29
  26.6 5.6 %collective-permute-done.5.on = f32[256,256]{1,0:T(8,128)S(1)} collective-permute-done((f32[256,256]{1,0:T(8,128)S(1)}, f32[256,256]{1,0:T(8,128)S(1)}, u32[]{:S(2)}, u32[]{:S(2)}) %collective-permute-start.5) | collective-permute-done | bytes 262176 | tf_op jit(solution)/shard_map/ppermute | solution.py:29
  33.0 4.2 %collective-permute-start.10 = (f32[32,512]{1,0:T(8,128)S(1)}, f32[32,512]{1,0:T(8,128)S(1)}, u32[]{:S(2)}, u32[]{:S(2)}) collective-permute-start(f32[32,512]{1,0:T(8,128)S(1)} %get-tuple-element.67), channel_id=1, source_target_pairs={{0,192},{8,200},{16,208},{24,216},{32,224},{40,232},{48,240},{56,2... | collective-permute-start | bytes 196616 | tf_op jit(solution)/shard_map/ppermute | solution.py:29
  37.2 1.3 collective-permute-done.10
  38.6 4.7 %collective-permute-start.11 = (f32[64,512]{1,0:T(8,128)S(1)}, f32[64,512]{1,0:T(8,128)S(1)}, u32[]{:S(2)}, u32[]{:S(2)}) collective-permute-start(f32[64,512]{1,0:T(8,128)S(1)} %pad_add_fusion), channel_id=1, source_target_pairs={{0,192},{8,200},{16,208},{24,216},{32,224},{40,232},{48,240},{56,2... | collective-permute-start | bytes 393224 | tf_op jit(solution)/shard_map/ppermute | solution.py:29
  43.4 3.2 %collective-permute-done.11.refs_2_ = f32[64,512]{1,0:T(8,128)S(1)} collective-permute-done((f32[64,512]{1,0:T(8,128)S(1)}, f32[64,512]{1,0:T(8,128)S(1)}, u32[]{:S(2)}, u32[]{:S(2)}) %collective-permute-start.11) | collective-permute-done | bytes 131104 | tf_op jit(solution)/shard_map/ppermute | solution.py:29
  46.6 3.9 %collective-permute-done.9.refs_1_ = f32[64,512]{1,0:T(8,128)S(1)} collective-permute-done((f32[64,512]{1,0:T(8,128)S(1)}, f32[64,512]{1,0:T(8,128)S(1)}, u32[]{:S(2)}, u32[]{:S(2)}) %collective-permute-start.9) | collective-permute-done | bytes 131104 | tf_op jit(solution)/shard_map/ppermute | solution.py:29
  51.3 3.5 %all-to-all-start = ((f32[4,64,512]{2,1,0:T(8,128)}), f32[4,64,512]{2,1,0:T(8,128)S(1)}, u32[]{:S(2)}, u32[]{:S(2)}) async-start(f32[4,64,512]{2,1,0:T(8,128)} %get-tuple-element.68), calls=%async_computation | async-start | bytes 1048576 | tf_op jit(solution)/shard_map/all_to_all | solution.py:48
  54.8 3.1 %collective-permute-start.13 = (f32[64,512]{1,0:T(8,128)S(1)}, f32[64,512]{1,0:T(8,128)S(1)}, u32[]{:S(2)}, u32[]{:S(2)}) collective-permute-start(f32[64,512]{1,0:T(8,128)S(1)} %get-tuple-element.70.u0), channel_id=1, source_target_pairs={{0,32},{8,40},{16,48},{24,56},{32,0},{40,8},{48,16},{56,24},{64,96... | collective-permute-start | bytes 393224 | tf_op jit(solution)/shard_map/ppermute | solution.py:29
  57.9 2.4 %collective-permute-done.13.u2 = f32[64,512]{1,0:T(8,128)S(1)} collective-permute-done((f32[64,512]{1,0:T(8,128)S(1)}, f32[64,512]{1,0:T(8,128)S(1)}, u32[]{:S(2)}, u32[]{:S(2)}) %collective-permute-start.13) | collective-permute-done | bytes 131104 | tf_op jit(solution)/shard_map/ppermute | solution.py:29
  60.3 3.0 %collective-permute-done.12.u1 = f32[64,512]{1,0:T(8,128)S(1)} collective-permute-done((f32[64,512]{1,0:T(8,128)S(1)}, f32[64,512]{1,0:T(8,128)S(1)}, u32[]{:S(2)}, u32[]{:S(2)}) %collective-permute-start.12) | collective-permute-done | bytes 131104 | tf_op jit(solution)/shard_map/ppermute | solution.py:29
  63.3 1.9 %all-to-all-done = f32[4,64,512]{2,1,0:T(8,128)S(1)} async-done(((f32[4,64,512]{2,1,0:T(8,128)}), f32[4,64,512]{2,1,0:T(8,128)S(1)}, u32[]{:S(2)}, u32[]{:S(2)}) %all-to-all-start) | async-done | bytes 524320 | tf_op jit(solution)/shard_map/all_to_all | solution.py:48
  65.1 1.2 g_block.1
  66.4 2.4 %collective-permute-start.16 = (f32[256,512]{1,0:T(8,128)S(1)}, f32[256,512]{1,0:T(8,128)S(1)}, u32[]{:S(2)}, u32[]{:S(2)}) collective-permute-start(f32[256,512]{1,0:T(8,128)S(1)} %bitcast.7), channel_id=1, source_target_pairs={{0,48},{8,56},{16,0},{24,8},{32,16},{40,24},{48,32},{56,40},{64,11... | collective-permute-start | bytes 1572872 | tf_op jit(solution)/shard_map/ppermute | solution.py:29
  69.8 5.9 %collective-permute-start.14 = (f32[8,3,8,128]{3,2,1,0:T(8,128)S(1)}, f32[8,3,8,128]{3,2,1,0:T(8,128)S(1)}, u32[]{:S(2)}, u32[]{:S(2)}) collective-permute-start(f32[8,3,8,128]{3,2,1,0:T(8,128)S(1)} %get-tuple-element.76), channel_id=1, source_target_pairs={{0,8},{8,0},{16,24},{24,16},{32,40},{40,32},{48,56},{56,48},{64,72... | collective-permute-start | bytes 294920 | tf_op jit(solution)/shard_map/ppermute | solution.py:29
  76.6 10.3 %all_to_all.20.refs_0_ = f32[8,3,8,128]{3,2,1,0:T(8,128)S(1)} all-to-all(f32[8,3,8,128]{3,2,1,0:T(8,128)S(1)} %add.42), channel_id=1, replica_groups=mesh['dp'=32,'shard'=8] {'shard'}, dimensions={0} | all-to-all | bytes 196608 | tf_op jit(solution)/shard_map/all_to_all | solution.py:48
  87.0 15.5 %all_to_all.21.refs_0_ = f32[16,3,8,128]{3,2,1,0:T(8,128)S(1)} all-to-all(f32[16,3,8,128]{3,2,1,0:T(8,128)S(1)} %spread.4), channel_id=1, replica_groups={{0,16,32,48,64,80,96,112,128,144,160,176,192,208,224,240},{8,24,40,56,7..., dimensions={0} | all-to-all | bytes 393216 | tf_op jit(solution)/shard_map/all_to_all | solution.py:48
  103.8 4.6 %all-to-all-start.3 = ((f32[8,16,3,8,128]{4,3,2,1,0:T(8,128)}), f32[8,16,3,8,128]{4,3,2,1,0:T(8,128)}, u32[]{:S(2)}, u32[]{:S(2)}) async-start(f32[8,16,3,8,128]{4,3,2,1,0:T(8,128)} %copy-done.6), calls=%async_computation.3 | async-start | bytes 3145728 | tf_op jit(solution)/shard_map/all_to_all | solution.py:48
  113.1 2.1 %merge_all.1 = (f32[1024,1024]{1,0:T(8,128)S(1)}, bf16[3,64,1024]{2,1,0:T(8,128)(2,1)S(1)}) custom-call(bf16[512,1024]{1,0:T(8,128)(2,1)S(1)} %copy-done.3, bf16[512,1024]{1,0:T(8,128)(2,1)S(1)} %copy-done.5, bf16[1,1024,1024]{2,1,0:T(8,128)(2,1)S(1)} %copy-done.1, f32[64,1024]{1,0:T(8,128)S(1)} %bitcast.10), custom_call_target="tpu_custom_call" | custom-call | flops 1073741824 | bytes 8388608 | tf_op jit(solution)/shard_map/merge_all/pallas_call | solution.py:121
  115.2 2.0 %copy-done.7 = f32[1024,1024]{1,0:T(8,128)} copy-done((f32[1024,1024]{1,0:T(8,128)}, f32[1024,1024]{1,0:T(8,128)S(1)}, u32[]{:S(2)}) %copy-start.7) | copy-done | bytes 4194328
  119.4 6.0 %all-to-all-done.3.own_ref = f32[8,16,3,8,128]{4,3,2,1,0:T(8,128)} async-done(((f32[8,16,3,8,128]{4,3,2,1,0:T(8,128)}), f32[8,16,3,8,128]{4,3,2,1,0:T(8,128)}, u32[]{:S(2)}, u32[]{:S(2)}) %all-to-all-start.3) | async-done | bytes 1572896 | tf_op jit(solution)/shard_map/all_to_all | solution.py:48
  125.5 4.6 %collective-permute-start.19 = (f32[8,16,3,8,128]{4,3,2,1,0:T(8,128)}, f32[8,16,3,8,128]{4,3,2,1,0:T(8,128)S(1)}, u32[]{:S(2)}, u32[]{:S(2)}) collective-permute-start(f32[8,16,3,8,128]{4,3,2,1,0:T(8,128)} %all-to-all-done.3.own_ref), channel_id=1, source_target_pairs={{0,8},{8,0},{16,24},{24,16},{32,40},{40,32},{48,56},{56,48},{64,72... | collective-permute-start | bytes 4718600 | tf_op jit(solution)/shard_map/ppermute | solution.py:29
  130.0 3.2 %collective-permute-done.19.away_ref = f32[8,16,3,8,128]{4,3,2,1,0:T(8,128)S(1)} collective-permute-done((f32[8,16,3,8,128]{4,3,2,1,0:T(8,128)}, f32[8,16,3,8,128]{4,3,2,1,0:T(8,128)S(1)}, u32[]{:S(2)}, u32[]{:S(2)}) %collective-permute-start.19) | collective-permute-done | bytes 1572896 | tf_op jit(solution)/shard_map/ppermute | solution.py:29
  134.3 13.6 %iterations.1 = (f32[64,1024]{1,0:T(8,128)}, f32[64,1024]{1,0:T(8,128)S(1)}) custom-call(s32[3]{0:T(128)S(1)} %pad_add_fusion.2.pos_ref, f32[8,16,3,8,128]{4,3,2,1,0:T(8,128)} %all-to-all-done.3.own_ref, f32[8,16,3,8,128]{4,3,2,1,0:T(8,128)S(1)} %collective-permute-done.19.away_ref, bf16[3,64,1024]{2,1,0:T(8,128)(2,1)S(1)} %copy-done.23), custom_call_target="tpu_custom_call" | custom-call | flops 2415919104 | bytes 4194304 | tf_op jit(solution)/shard_map/iterations/pallas_call | solution.py:337
  150.5 3.7 %finish.1 = (bf16[1,1024,1024]{2,1,0:T(8,128)(2,1)}, bf16[1024,1024]{1,0:T(8,128)(2,1)}) custom-call(s32[3]{0:T(128)S(1)} %pad_add_fusion.2.pos_ref, f32[1024,1024]{1,0:T(8,128)S(1)} %copy-done.8, bf16[1024,1024]{1,0:T(8,128)(2,1)S(1)} %copy-done.9, f32[64,512]{1,0:T(8,128)S(1)} %left.1.own, f32[64,512]{1,0:T(8,128)S(1)} %collective-permute-done.20.away, ...), custom_call_target="tpu_custom_call" | custom-call | flops 536870912 | bytes 12582912 | tf_op jit(solution)/shard_map/finish/pallas_call | solution.py:404
  (87 shorter events, 23.4 us)
Async XLA Ops:
  5.7 4.9 %collective-permute-start = (f32[1,512,256]{2,1,0:T(8,128)S(1)}, f32[1,512,256]{2,1,0:T(8,128)S(1)}, u32[]{:S(2)}, u32[]{:S(2)}) collective-permute-start(f32[1,512,256]{2,1,0:T(8,128)S(1)} %merge.4), channel_id=1, source_target_pairs={{0,8},{8,0},{16,24},{24,16},{32,40},{40,32},{48,56},{56,48},{64,72... | collective-permute-start | bytes 1572872 | tf_op jit(solution)/shard_map/ppermute | solution.py:29
  10.6 4.1 %collective-permute-start.1 = (f32[3,512,256]{2,1,0:T(8,128)S(1)}, f32[3,512,256]{2,1,0:T(8,128)S(1)}, u32[]{:S(2)}, u32[]{:S(2)}) collective-permute-start(f32[3,512,256]{2,1,0:T(8,128)S(1)} %merge.5), channel_id=1, source_target_pairs={{0,8},{8,0},{16,24},{24,16},{32,40},{40,32},{48,56},{56,48},{64,72... | collective-permute-start | bytes 4718600 | tf_op jit(solution)/shard_map/ppermute | solution.py:29
  11.9 9.1 %collective-permute-start.4 = (f32[256,256]{1,0:T(8,128)S(1)}, f32[256,256]{1,0:T(8,128)S(1)}, u32[]{:S(2)}, u32[]{:S(2)}) collective-permute-start(f32[256,256]{1,0:T(8,128)S(1)} %get-tuple-element.60), channel_id=1, source_target_pairs={{0,16},{8,24},{16,32},{24,40},{32,48},{40,56},{48,0},{56,8},{64,80... | collective-permute-start | bytes 786440 | tf_op jit(solution)/shard_map/ppermute | solution.py:29
  12.0 9.1 %collective-permute-start.6 = (f32[256,256]{1,0:T(8,128)S(1)}, f32[256,256]{1,0:T(8,128)S(1)}, u32[]{:S(2)}, u32[]{:S(2)}) collective-permute-start(f32[256,256]{1,0:T(8,128)S(1)} %get-tuple-element.62), channel_id=1, source_target_pairs={{0,48},{8,56},{16,0},{24,8},{32,16},{40,24},{48,32},{56,40},{64,11... | collective-permute-start | bytes 786440 | tf_op jit(solution)/shard_map/ppermute | solution.py:29
  15.9 9.6 %collective-permute-start.2 = (f32[256,256]{1,0:T(8,128)S(1)}, f32[256,256]{1,0:T(8,128)S(1)}, u32[]{:S(2)}, u32[]{:S(2)}) collective-permute-start(f32[256,256]{1,0:T(8,128)S(1)} %get-tuple-element.55), channel_id=1, source_target_pairs={{0,48},{8,56},{16,0},{24,8},{32,16},{40,24},{48,32},{56,40},{64,11... | collective-permute-start | bytes 786440 | tf_op jit(solution)/shard_map/ppermute | solution.py:29
  16.3 10.3 %collective-permute-start.3 = (f32[256,256]{1,0:T(8,128)S(1)}, f32[256,256]{1,0:T(8,128)S(1)}, u32[]{:S(2)}, u32[]{:S(2)}) collective-permute-start(f32[256,256]{1,0:T(8,128)S(1)} %get-tuple-element.57), channel_id=1, source_target_pairs={{0,16},{8,24},{16,32},{24,40},{32,48},{40,56},{48,0},{56,8},{64,80... | collective-permute-start | bytes 786440 | tf_op jit(solution)/shard_map/ppermute | solution.py:29
  21.0 11.2 %collective-permute-start.5 = (f32[256,256]{1,0:T(8,128)S(1)}, f32[256,256]{1,0:T(8,128)S(1)}, u32[]{:S(2)}, u32[]{:S(2)}) collective-permute-start(f32[256,256]{1,0:T(8,128)S(1)} %add.38), channel_id=1, source_target_pairs={{0,16},{8,24},{16,32},{24,40},{32,48},{40,56},{48,0},{56,8},{64,80... | collective-permute-start | bytes 786440 | tf_op jit(solution)/shard_map/ppermute | solution.py:29
  21.1 11.1 %collective-permute-start.7 = (f32[256,256]{1,0:T(8,128)S(1)}, f32[256,256]{1,0:T(8,128)S(1)}, u32[]{:S(2)}, u32[]{:S(2)}) collective-permute-start(f32[256,256]{1,0:T(8,128)S(1)} %add.39), channel_id=1, source_target_pairs={{0,48},{8,56},{16,0},{24,8},{32,16},{40,24},{48,32},{56,40},{64,11... | collective-permute-start | bytes 786440 | tf_op jit(solution)/shard_map/ppermute | solution.py:29
  33.0 5.6 %collective-permute-start.10 = (f32[32,512]{1,0:T(8,128)S(1)}, f32[32,512]{1,0:T(8,128)S(1)}, u32[]{:S(2)}, u32[]{:S(2)}) collective-permute-start(f32[32,512]{1,0:T(8,128)S(1)} %get-tuple-element.67), channel_id=1, source_target_pairs={{0,192},{8,200},{16,208},{24,216},{32,224},{40,232},{48,240},{56,2... | collective-permute-start | bytes 196616 | tf_op jit(solution)/shard_map/ppermute | solution.py:29
  37.2 6.0 %collective-permute-start.8 = (f32[32,512]{1,0:T(8,128)S(1)}, f32[32,512]{1,0:T(8,128)S(1)}, u32[]{:S(2)}, u32[]{:S(2)}) collective-permute-start(f32[32,512]{1,0:T(8,128)S(1)} %get-tuple-element.65), channel_id=1, source_target_pairs={{0,64},{8,72},{16,80},{24,88},{32,96},{40,104},{48,112},{56,120},{... | collective-permute-start | bytes 196616 | tf_op jit(solution)/shard_map/ppermute | solution.py:29
  38.6 8.0 %collective-permute-start.11 = (f32[64,512]{1,0:T(8,128)S(1)}, f32[64,512]{1,0:T(8,128)S(1)}, u32[]{:S(2)}, u32[]{:S(2)}) collective-permute-start(f32[64,512]{1,0:T(8,128)S(1)} %pad_add_fusion), channel_id=1, source_target_pairs={{0,192},{8,200},{16,208},{24,216},{32,224},{40,232},{48,240},{56,2... | collective-permute-start | bytes 393224 | tf_op jit(solution)/shard_map/ppermute | solution.py:29
  43.3 7.2 %collective-permute-start.9 = (f32[64,512]{1,0:T(8,128)S(1)}, f32[64,512]{1,0:T(8,128)S(1)}, u32[]{:S(2)}, u32[]{:S(2)}) collective-permute-start(f32[64,512]{1,0:T(8,128)S(1)} %pad_add_fusion.1), channel_id=1, source_target_pairs={{0,64},{8,72},{16,80},{24,88},{32,96},{40,104},{48,112},{56,120},{... | collective-permute-start | bytes 393224 | tf_op jit(solution)/shard_map/ppermute | solution.py:29
  51.3 13.8 %all-to-all-start = ((f32[4,64,512]{2,1,0:T(8,128)}), f32[4,64,512]{2,1,0:T(8,128)S(1)}, u32[]{:S(2)}, u32[]{:S(2)}) async-start(f32[4,64,512]{2,1,0:T(8,128)} %get-tuple-element.68), calls=%async_computation | async-start | bytes 1048576 | tf_op jit(solution)/shard_map/all_to_all | solution.py:48
  54.8 5.5 %collective-permute-start.13 = (f32[64,512]{1,0:T(8,128)S(1)}, f32[64,512]{1,0:T(8,128)S(1)}, u32[]{:S(2)}, u32[]{:S(2)}) collective-permute-start(f32[64,512]{1,0:T(8,128)S(1)} %get-tuple-element.70.u0), channel_id=1, source_target_pairs={{0,32},{8,40},{16,48},{24,56},{32,0},{40,8},{48,16},{56,24},{64,96... | collective-permute-start | bytes 393224 | tf_op jit(solution)/shard_map/ppermute | solution.py:29
  57.9 5.3 %collective-permute-start.12 = (f32[64,512]{1,0:T(8,128)S(1)}, f32[64,512]{1,0:T(8,128)S(1)}, u32[]{:S(2)}, u32[]{:S(2)}) collective-permute-start(f32[64,512]{1,0:T(8,128)S(1)} %get-tuple-element.70.u0), channel_id=1, source_target_pairs={{0,16},{8,24},{16,32},{24,40},{32,48},{40,56},{48,0},{56,8},{64,80... | collective-permute-start | bytes 393224 | tf_op jit(solution)/shard_map/ppermute | solution.py:29
  65.1 37.4 %copy-start.10 = (f32[4,64,512]{2,1,0:T(8,128)}, f32[4,64,512]{2,1,0:T(8,128)S(1)}, u32[]{:S(2)}) copy-start(f32[4,64,512]{2,1,0:T(8,128)S(1)} %all-to-all-done) | copy-start | bytes 1572868
  66.4 20.5 %collective-permute-start.16 = (f32[256,512]{1,0:T(8,128)S(1)}, f32[256,512]{1,0:T(8,128)S(1)}, u32[]{:S(2)}, u32[]{:S(2)}) collective-permute-start(f32[256,512]{1,0:T(8,128)S(1)} %bitcast.7), channel_id=1, source_target_pairs={{0,48},{8,56},{16,0},{24,8},{32,16},{40,24},{48,32},{56,40},{64,11... | collective-permute-start | bytes 1572872 | tf_op jit(solution)/shard_map/ppermute | solution.py:29
  68.8 18.1 %collective-permute-start.15 = (f32[256,512]{1,0:T(8,128)S(1)}, f32[256,512]{1,0:T(8,128)S(1)}, u32[]{:S(2)}, u32[]{:S(2)}) collective-permute-start(f32[256,512]{1,0:T(8,128)S(1)} %bitcast.8), channel_id=1, source_target_pairs={{0,16},{8,24},{16,32},{24,40},{32,48},{40,56},{48,0},{56,8},{64,80... | collective-permute-start | bytes 1572872 | tf_op jit(solution)/shard_map/ppermute | solution.py:29
  69.8 6.9 %collective-permute-start.14 = (f32[8,3,8,128]{3,2,1,0:T(8,128)S(1)}, f32[8,3,8,128]{3,2,1,0:T(8,128)S(1)}, u32[]{:S(2)}, u32[]{:S(2)}) collective-permute-start(f32[8,3,8,128]{3,2,1,0:T(8,128)S(1)} %get-tuple-element.76), channel_id=1, source_target_pairs={{0,8},{8,0},{16,24},{24,16},{32,40},{40,32},{48,56},{56,48},{64,72... | collective-permute-start | bytes 294920 | tf_op jit(solution)/shard_map/ppermute | solution.py:29
  86.9 15.6 %copy-start.12 = (f32[256,512]{1,0:T(8,128)}, f32[256,512]{1,0:T(8,128)S(1)}, u32[]{:S(2)}) copy-start(f32[256,512]{1,0:T(8,128)S(1)} %collective-permute-done.16.m3) | copy-start | bytes 1572868
  87.0 15.5 %copy-start.14 = (f32[256,512]{1,0:T(8,128)}, f32[256,512]{1,0:T(8,128)S(1)}, u32[]{:S(2)}) copy-start(f32[256,512]{1,0:T(8,128)S(1)} %collective-permute-done.15.m1) | copy-start | bytes 1572868
  103.8 21.7 %all-to-all-start.3 = ((f32[8,16,3,8,128]{4,3,2,1,0:T(8,128)}), f32[8,16,3,8,128]{4,3,2,1,0:T(8,128)}, u32[]{:S(2)}, u32[]{:S(2)}) async-start(f32[8,16,3,8,128]{4,3,2,1,0:T(8,128)} %copy-done.6), calls=%async_computation.3 | async-start | bytes 3145728 | tf_op jit(solution)/shard_map/all_to_all | solution.py:48
  110.3 7.6 %collective-permute-start.18 = (f32[128,512]{1,0:T(8,128)S(1)}, f32[128,512]{1,0:T(8,128)S(1)}, u32[]{:S(2)}, u32[]{:S(2)}) collective-permute-start(f32[128,512]{1,0:T(8,128)S(1)} %slice.7), channel_id=1, source_target_pairs={{0,48},{8,56},{16,0},{24,8},{32,16},{40,24},{48,32},{56,40},{64,11... | collective-permute-start | bytes 786440 | tf_op jit(solution)/shard_map/ppermute | solution.py:29
  111.2 7.5 %collective-permute-start.17 = (f32[128,512]{1,0:T(8,128)S(1)}, f32[128,512]{1,0:T(8,128)S(1)}, u32[]{:S(2)}, u32[]{:S(2)}) collective-permute-start(f32[128,512]{1,0:T(8,128)S(1)} %slice.6), channel_id=1, source_target_pairs={{0,16},{8,24},{16,32},{24,40},{32,48},{40,56},{48,0},{56,8},{64,80... | collective-permute-start | bytes 786440 | tf_op jit(solution)/shard_map/ppermute | solution.py:29
  125.4 22.5 %copy-start.11 = (f32[4,64,512]{2,1,0:T(8,128)S(1)}, f32[4,64,512]{2,1,0:T(8,128)}, u32[]{:S(2)}) copy-start(f32[4,64,512]{2,1,0:T(8,128)} %copy-done.10) | copy-start | bytes 1572868
  125.4 22.5 %copy-start.13 = (f32[256,512]{1,0:T(8,128)S(1)}, f32[256,512]{1,0:T(8,128)}, u32[]{:S(2)}) copy-start(f32[256,512]{1,0:T(8,128)} %copy-done.12) | copy-start | bytes 1572868
  125.4 22.5 %copy-start.15 = (f32[256,512]{1,0:T(8,128)S(1)}, f32[256,512]{1,0:T(8,128)}, u32[]{:S(2)}) copy-start(f32[256,512]{1,0:T(8,128)} %copy-done.14) | copy-start | bytes 1572868
  125.4 22.5 %copy-start.19 = (f32[128,512]{1,0:T(8,128)S(1)}, f32[128,512]{1,0:T(8,128)}, u32[]{:S(2)}) copy-start(f32[128,512]{1,0:T(8,128)} %copy-done.18) | copy-start | bytes 786436
  125.5 22.5 %copy-start.21 = (f32[128,512]{1,0:T(8,128)S(1)}, f32[128,512]{1,0:T(8,128)}, u32[]{:S(2)}) copy-start(f32[128,512]{1,0:T(8,128)} %copy-done.20) | copy-start | bytes 786436
  125.5 7.8 %collective-permute-start.19 = (f32[8,16,3,8,128]{4,3,2,1,0:T(8,128)}, f32[8,16,3,8,128]{4,3,2,1,0:T(8,128)S(1)}, u32[]{:S(2)}, u32[]{:S(2)}) collective-permute-start(f32[8,16,3,8,128]{4,3,2,1,0:T(8,128)} %all-to-all-done.3.own_ref), channel_id=1, source_target_pairs={{0,8},{8,0},{16,24},{24,16},{32,40},{40,32},{48,56},{56,48},{64,72... | collective-permute-start | bytes 4718600 | tf_op jit(solution)/shard_map/ppermute | solution.py:29
  134.3 16.2 %copy-start.8 = (f32[1024,1024]{1,0:T(8,128)S(1)}, f32[1024,1024]{1,0:T(8,128)}, u32[]{:S(2)}) copy-start(f32[1024,1024]{1,0:T(8,128)} %copy-done.7) | copy-start | bytes 12582916
  149.1 1.5 collective-permute-start.20
  (15 other events, 41.1 us)

commit v7 on v6

--- a/solution.py
+++ b/solution.py
@@ -17,7 +17,6 @@
 VMEM = pl.BlockSpec(memory_space=pltpu.VMEM)
 SMEM = pl.BlockSpec(memory_space=pltpu.SMEM)
 
-Z_GROUPS = [[z * 8 + y * 2 + c for z in range(4)] for y in range(4) for c in range(2)]
 ZY_GROUPS = [[z * 8 + y * 2 + c for z in range(4) for y in range(4)] for c in range(2)]
 
 
@@ -167,36 +166,31 @@
     )(pos, *parts)
 
 
-def spread_kernel(leading, keep, *refs):
-    refs, outs = refs[:-1 - keep], refs[-1 - keep:]
-    terms = [refs[0][i] for i in range(refs[0].shape[0])] if leading else [ref[...] for ref in refs]
-    total = terms[0]
-    for term in terms[1:]:
-        total = total + term
-    copies_ref = outs[0]
+def spread_kernel(leading, x_ref, copies_ref):
+    total = x_ref[0] if leading else x_ref[...]
+    for i in range(1, x_ref.shape[0] if leading else 1):
+        total = total + x_ref[i]
     for i in range(copies_ref.shape[0]):
         copies_ref[i] = total
-    if keep:
-        outs[1][...] = total
-
-
-def spread(parts, copies, leading=False, keep=False):
-    shape = parts[0].shape[1:] if leading else parts[0].shape
-    outs = (jax.ShapeDtypeStruct((copies,) + shape, F32), jax.ShapeDtypeStruct(shape, F32))[:1 + keep]
-    return pl.pallas_call(
-        functools.partial(spread_kernel, leading, keep),
-        out_shape=outs,
-        in_specs=[VMEM] * len(parts),
-        out_specs=(VMEM,) * len(outs),
-        compiler_params=params(10),
+
+
+def spread(x, copies, leading=False, grant=10):
+    return pl.pallas_call(
+        functools.partial(spread_kernel, leading),
+        out_shape=jax.ShapeDtypeStruct((copies,) + x.shape[leading:], F32),
+        in_specs=[VMEM],
+        out_specs=VMEM,
+        compiler_params=params(grant),
         cost_estimate=cost(1 << 17, 1 << 20),
         name="spread",
-    )(*parts)
-
-
-def block_kernel(pos_ref, u0, u1, u2, of_y, sent_ref, mine_ref):
-    core = pos_ref[0]
-    rows = jnp.concatenate([u0[...], u1[...], u2[...]], axis=0)
+    )(x)
+
+
+def block_kernel(pos_ref, unit, u1, u2, z1, z3, z2, sent_ref, mine_ref, of_y):
+    core, z = pos_ref[0], pos_ref[2]
+    for turn, ref in ((0, unit), (3, z1), (1, z3), (2, z2)):
+        of_y[pl.ds(pl.multiple_of((z + turn) % 4 * 64, 64), 64), :] = ref[...]
+    rows = jnp.concatenate([unit[...], u1[...], u2[...]], axis=0)
     block = lax.dot_general(rows, of_y[...], LANES, precision=HIGH, preferred_element_type=F32)
 
     def put(ref, part):
@@ -215,17 +209,17 @@
         put(sent_ref, block[:, :128])
 
 
-def g_block(pos, units, of_y):
-    k, d = of_y.shape
+def g_block(pos, units):
+    k, d = units[0].shape
     return pl.pallas_call(
         block_kernel,
-        out_shape=(jax.ShapeDtypeStruct((8, 3, 8, 128), F32),) * 2,
-        in_specs=[SMEM] + [VMEM] * 4,
-        out_specs=(VMEM, VMEM),
+        out_shape=(jax.ShapeDtypeStruct((8, 3, 8, 128), F32),) * 2 + (jax.ShapeDtypeStruct((4 * k, d), F32),),
+        in_specs=[SMEM] + [VMEM] * 6,
+        out_specs=(VMEM,) * 3,
         compiler_params=params(12),
-        cost_estimate=cost(2 * 6 * 192 * k * d, 2 << 20),
+        cost_estimate=cost(2 * 6 * 192 * 4 * k * d, 2 << 20),
         name="g_block",
-    )(pos, *units, of_y)
+    )(pos, *units)
 
 
 def inverse_factor(gram):
@@ -441,21 +435,21 @@
     parts = ring_sum(opposite, sums[0:2], sums[2:4], sums[4:6], lambda x, d: dp_shift(x, dy=d))
     *opposite, after, before, own = sum_turn(pos, parts)
     came = small_ring_sum(opposite, after, before, lambda x, d: dp_shift(x, dz=d))
-    copies, unit = spread([own, *came], 4, keep=True)
-    units = [unit] + [dp_shift(unit, dy=dy) for dy in (1, 2)]
-    of_y = exchange(copies, Z_GROUPS).reshape(256, 512)
-    of_y, *units = lax.optimization_barrier((of_y, *units))
-
-    to_core, part = g_block(pos, units, of_y)
+    unit = own + (came[0] + came[1])
+    z1, z3 = dp_shift(unit, dz=1), dp_shift(unit, dz=-1)
+    u1, u2 = dp_shift(unit, dy=1), dp_shift(unit, dy=2)
+    units = [unit, u1, u2, z1, z3, dp_shift(z1, dz=1)]
+
+    to_core, part, of_y = g_block(pos, units)
     to_core, of_y = lax.optimization_barrier((to_core, of_y))
     part = part + dp_shift(to_core, dc=1)
     m1, m3 = dp_shift(of_y, dy=1), dp_shift(of_y, dy=-1)
-    (copies,) = spread([exchange(part, None, "shard")], 16, leading=True)
+    copies = spread(exchange(part, None, "shard"), 16, leading=True)
     copies, m1, m3 = lax.optimization_barrier((copies, m1, m3))
     part = exchange(copies, ZY_GROUPS)
     part, m1, m3, args, q_t = lax.optimization_barrier((part, m1, m3, args, q_start.T))
     m2_top, m2_end = dp_shift(m1[:128], dy=1), dp_shift(m3[128:], dy=-1)
-    part = exchange(spread([part], 8)[0], None, "shard")
+    part = exchange(spread(part, 8, grant=58), None, "shard")
     part, m2_top, m2_end, merged, q_parts = lax.optimization_barrier(
         (part, m2_top, m2_end, *merge_all(*args, q_t))
     )

time: 155 us -> 155 us (level)
  Pallas kernels: 27.8 us -> 30 us
    all_to_all x2 -> x1, starting transfers between devices: 8.05 us -> 4.57 us  [exchange(): return lax.all_to_all(x, axis, 0, 0, axis_index_groups=groups)]
    ppermute x21 -> x24, starting transfers between devices: 38.8 us -> 41.3 us  [dp_shift(): return lax.ppermute(x, 'dp', pairs)]
    ppermute x21 -> x24, waiting for transfers between devices: 31.1 us -> 33.3 us  [dp_shift(): return lax.ppermute(x, 'dp', pairs)]
    all_to_all x2 -> x1, waiting for transfers between devices: 7.91 us -> 6.05 us  [exchange(): return lax.all_to_all(x, axis, 0, 0, axis_index_groups=groups)]
    unnamed x48 -> x38, local copies, waits for them, and re-layouts: 11.6 us -> 10.4 us
  transfers between devices with their start and end apart: 23 -> 25, of which waited for: 15 -> 15; matrix products, arithmetic and copies ran while one was open for 1% -> 1% of each run, Pallas kernels for 4% -> 4%
where the time goes in v7:
time: 155 us; the launch traced here: 154 us
  starting transfers between devices  45.9 us (30%)
  waiting for transfers between devices  39.4 us (25%)
  Pallas kernels  30 us (19%)
  blocking collectives  25.6 us (17%)
  local copies, waits for them, and re-layouts  12.4 us (8%)
    ppermute x24, starting transfers between devices, dp_shift(): return lax.ppermute(x, 'dp', pairs)  41.3 us
    ppermute x24, waiting for transfers between devices, dp_shift(): return lax.ppermute(x, 'dp', pairs)  33.3 us
    all_to_all x2, blocking collectives, exchange(): return lax.all_to_all(x, axis, 0, 0, axis_index_groups=groups)  25.6 us
    pallas_call x1, Pallas kernels, iterate(): pl.pallas_call(iterate_kernel, out_shape=(jax.ShapeDtypeStruct((n, k), F3...  13.6 us
    unnamed x38, local copies, waits for them, and re-layouts  10.4 us
    all_to_all x1, waiting for transfers between devices, exchange(): return lax.all_to_all(x, axis, 0, 0, axis_index_groups=groups)  6.05 us
    all_to_all x1, starting transfers between devices, exchange(): return lax.all_to_all(x, axis, 0, 0, axis_index_groups=groups)  4.57 us
    pallas_call x4, Pallas kernels, merge(): pl.pallas_call(functools.partial(merge_kernel, turns, own), out_shape=out...  4.3 us
  transfers between devices with their start and end apart: 25, of which 15 were waited for; matrix products, arithmetic and copies ran while one was open for 1% of the time, Pallas kernels for 4%

profile of v7, /device:TPU:1, one launch (start us, length us, event | category | flops | bytes accessed | tf_op | source)
XLA Modules:
  0.0 154.4 jit_solution(11941686775213189264)
XLA Ops:
  0.7 1.6 %copy-done = bf16[1,1024,1024]{2,1,0:T(8,128)(2,1)S(1)} copy-done((bf16[1,1024,1024]{2,1,0:T(8,128)(2,1)S(1)}, bf16[1,1024,1024]{2,1,0:T(8,128)(2,1)}, u32[]{:S(2)}) %copy-start) | copy-done | bytes 2097176
  5.7 3.3 %collective-permute-start = (f32[1,512,256]{2,1,0:T(8,128)S(1)}, f32[1,512,256]{2,1,0:T(8,128)S(1)}, u32[]{:S(2)}, u32[]{:S(2)}) collective-permute-start(f32[1,512,256]{2,1,0:T(8,128)S(1)} %merge.4), channel_id=1, source_target_pairs={{0,8},{8,0},{16,24},{24,16},{32,40},{40,32},{48,56},{56,48},{64,72... | collective-permute-start | bytes 1572872 | tf_op jit(solution)/shard_map/ppermute | solution.py:28
  12.0 2.7 %collective-permute-start.6 = (f32[256,256]{1,0:T(8,128)S(1)}, f32[256,256]{1,0:T(8,128)S(1)}, u32[]{:S(2)}, u32[]{:S(2)}) collective-permute-start(f32[256,256]{1,0:T(8,128)S(1)} %get-tuple-element.57), channel_id=1, source_target_pairs={{0,48},{8,56},{16,0},{24,8},{32,16},{40,24},{48,32},{56,40},{64,11... | collective-permute-start | bytes 786440 | tf_op jit(solution)/shard_map/ppermute | solution.py:28
  17.5 3.5 %collective-permute-done.4 = f32[256,256]{1,0:T(8,128)S(1)} collective-permute-done((f32[256,256]{1,0:T(8,128)S(1)}, f32[256,256]{1,0:T(8,128)S(1)}, u32[]{:S(2)}, u32[]{:S(2)}) %collective-permute-start.4) | collective-permute-done | bytes 262176 | tf_op jit(solution)/shard_map/ppermute | solution.py:28
  21.2 2.7 %collective-permute-start.7 = (f32[256,256]{1,0:T(8,128)S(1)}, f32[256,256]{1,0:T(8,128)S(1)}, u32[]{:S(2)}, u32[]{:S(2)}) collective-permute-start(f32[256,256]{1,0:T(8,128)S(1)} %add.45), channel_id=1, source_target_pairs={{0,48},{8,56},{16,0},{24,8},{32,16},{40,24},{48,32},{56,40},{64,11... | collective-permute-start | bytes 786440 | tf_op jit(solution)/shard_map/ppermute | solution.py:28
  23.9 1.7 %collective-permute-done.2 = f32[256,256]{1,0:T(8,128)S(1)} collective-permute-done((f32[256,256]{1,0:T(8,128)S(1)}, f32[256,256]{1,0:T(8,128)S(1)}, u32[]{:S(2)}, u32[]{:S(2)}) %collective-permute-start.2) | collective-permute-done | bytes 262176 | tf_op jit(solution)/shard_map/ppermute | solution.py:28
  26.6 5.6 %collective-permute-done.5.on = f32[256,256]{1,0:T(8,128)S(1)} collective-permute-done((f32[256,256]{1,0:T(8,128)S(1)}, f32[256,256]{1,0:T(8,128)S(1)}, u32[]{:S(2)}, u32[]{:S(2)}) %collective-permute-start.5) | collective-permute-done | bytes 262176 | tf_op jit(solution)/shard_map/ppermute | solution.py:28
  33.0 4.2 %collective-permute-start.10 = (f32[32,512]{1,0:T(8,128)S(1)}, f32[32,512]{1,0:T(8,128)S(1)}, u32[]{:S(2)}, u32[]{:S(2)}) collective-permute-start(f32[32,512]{1,0:T(8,128)S(1)} %get-tuple-element.62), channel_id=1, source_target_pairs={{0,192},{8,200},{16,208},{24,216},{32,224},{40,232},{48,240},{56,2... | collective-permute-start | bytes 196616 | tf_op jit(solution)/shard_map/ppermute | solution.py:28
  37.2 1.3 collective-permute-done.10
  38.6 4.7 %collective-permute-start.11 = (f32[64,512]{1,0:T(8,128)S(1)}, f32[64,512]{1,0:T(8,128)S(1)}, u32[]{:S(2)}, u32[]{:S(2)}) collective-permute-start(f32[64,512]{1,0:T(8,128)S(1)} %pad_add_fusion), channel_id=1, source_target_pairs={{0,192},{8,200},{16,208},{24,216},{32,224},{40,232},{48,240},{56,2... | collective-permute-start | bytes 393224 | tf_op jit(solution)/shard_map/ppermute | solution.py:28
  43.4 3.2 %collective-permute-done.11 = f32[64,512]{1,0:T(8,128)S(1)} collective-permute-done((f32[64,512]{1,0:T(8,128)S(1)}, f32[64,512]{1,0:T(8,128)S(1)}, u32[]{:S(2)}, u32[]{:S(2)}) %collective-permute-start.11) | collective-permute-done | bytes 131104 | tf_op jit(solution)/shard_map/ppermute | solution.py:28
  46.6 3.9 %collective-permute-done.9 = f32[64,512]{1,0:T(8,128)S(1)} collective-permute-done((f32[64,512]{1,0:T(8,128)S(1)}, f32[64,512]{1,0:T(8,128)S(1)}, u32[]{:S(2)}, u32[]{:S(2)}) %collective-permute-start.9) | collective-permute-done | bytes 131104 | tf_op jit(solution)/shard_map/ppermute | solution.py:28
  50.6 3.6 %collective-permute-start.15 = (f32[64,512]{1,0:T(8,128)S(1)}, f32[64,512]{1,0:T(8,128)S(1)}, u32[]{:S(2)}, u32[]{:S(2)}) collective-permute-start(f32[64,512]{1,0:T(8,128)S(1)} %add_add_fusion.unit), channel_id=1, source_target_pairs={{0,192},{8,200},{16,208},{24,216},{32,224},{40,232},{48,240},{56,2... | collective-permute-start | bytes 393224 | tf_op jit(solution)/shard_map/ppermute | solution.py:28
  54.2 3.0 %collective-permute-start.13 = (f32[64,512]{1,0:T(8,128)S(1)}, f32[64,512]{1,0:T(8,128)S(1)}, u32[]{:S(2)}, u32[]{:S(2)}) collective-permute-start(f32[64,512]{1,0:T(8,128)S(1)} %add_add_fusion.unit), channel_id=1, source_target_pairs={{0,32},{8,40},{16,48},{24,56},{32,0},{40,8},{48,16},{56,24},{64,96... | collective-permute-start | bytes 393224 | tf_op jit(solution)/shard_map/ppermute | solution.py:28
  57.2 2.3 %collective-permute-done.13.u2 = f32[64,512]{1,0:T(8,128)S(1)} collective-permute-done((f32[64,512]{1,0:T(8,128)S(1)}, f32[64,512]{1,0:T(8,128)S(1)}, u32[]{:S(2)}, u32[]{:S(2)}) %collective-permute-start.13) | collective-permute-done | bytes 131104 | tf_op jit(solution)/shard_map/ppermute | solution.py:28
  59.6 3.0 %collective-permute-done.12.u1 = f32[64,512]{1,0:T(8,128)S(1)} collective-permute-done((f32[64,512]{1,0:T(8,128)S(1)}, f32[64,512]{1,0:T(8,128)S(1)}, u32[]{:S(2)}, u32[]{:S(2)}) %collective-permute-start.12) | collective-permute-done | bytes 131104 | tf_op jit(solution)/shard_map/ppermute | solution.py:28
  62.5 2.3 %collective-permute-done.16.z2 = f32[64,512]{1,0:T(8,128)S(1)} collective-permute-done((f32[64,512]{1,0:T(8,128)S(1)}, f32[64,512]{1,0:T(8,128)S(1)}, u32[]{:S(2)}, u32[]{:S(2)}) %collective-permute-start.16) | collective-permute-done | bytes 131104 | tf_op jit(solution)/shard_map/ppermute | solution.py:28
  64.8 1.3 g_block.1
  66.1 2.2 %collective-permute-start.19 = (f32[256,512]{1,0:T(8,128)S(1)}, f32[256,512]{1,0:T(8,128)}, u32[]{:S(2)}, u32[]{:S(2)}) collective-permute-start(f32[256,512]{1,0:T(8,128)S(1)} %get-tuple-element.67.m0), channel_id=1, source_target_pairs={{0,48},{8,56},{16,0},{24,8},{32,16},{40,24},{48,32},{56,40},{64,11... | collective-permute-start | bytes 1572872 | tf_op jit(solution)/shard_map/ppermute | solution.py:28
  68.5 6.2 %collective-permute-start.17 = (f32[8,3,8,128]{3,2,1,0:T(8,128)S(1)}, f32[8,3,8,128]{3,2,1,0:T(8,128)S(1)}, u32[]{:S(2)}, u32[]{:S(2)}) collective-permute-start(f32[8,3,8,128]{3,2,1,0:T(8,128)S(1)} %get-tuple-element.66), channel_id=1, source_target_pairs={{0,8},{8,0},{16,24},{24,16},{32,40},{40,32},{48,56},{56,48},{64,72... | collective-permute-start | bytes 294920 | tf_op jit(solution)/shard_map/ppermute | solution.py:28
  75.6 11.7 %all_to_all.15.x_ref = f32[8,3,8,128]{3,2,1,0:T(8,128)S(1)} all-to-all(f32[8,3,8,128]{3,2,1,0:T(8,128)S(1)} %add.50), channel_id=1, replica_groups=mesh['dp'=32,'shard'=8] {'shard'}, dimensions={0} | all-to-all | bytes 196608 | tf_op jit(solution)/shard_map/all_to_all | solution.py:47
  87.4 13.8 %all_to_all.16.x_ref = f32[16,3,8,128]{3,2,1,0:T(8,128)} all-to-all(f32[16,3,8,128]{3,2,1,0:T(8,128)S(1)} %spread.2), channel_id=1, replica_groups={{0,16,32,48,64,80,96,112,128,144,160,176,192,208,224,240},{8,24,40,56,7..., dimensions={0} | all-to-all | bytes 393216 | tf_op jit(solution)/shard_map/all_to_all | solution.py:47
  101.2 2.2 %spread.3 = f32[8,16,3,8,128]{4,3,2,1,0:T(8,128)} custom-call(f32[16,3,8,128]{3,2,1,0:T(8,128)} %all_to_all.16.x_ref), custom_call_target="tpu_custom_call" | custom-call | flops 131072 | bytes 1048576 | tf_op jit(solution)/shard_map/spread/pallas_call | solution.py:178
  103.4 4.6 %all-to-all-start.2 = ((f32[8,16,3,8,128]{4,3,2,1,0:T(8,128)}), f32[8,16,3,8,128]{4,3,2,1,0:T(8,128)}, u32[]{:S(2)}, u32[]{:S(2)}) async-start(f32[8,16,3,8,128]{4,3,2,1,0:T(8,128)} %spread.3), calls=%async_computation.2 | async-start | bytes 3145728 | tf_op jit(solution)/shard_map/all_to_all | solution.py:47
  112.7 2.1 %merge_all.1 = (f32[1024,1024]{1,0:T(8,128)S(1)}, bf16[3,64,1024]{2,1,0:T(8,128)(2,1)S(1)}) custom-call(bf16[512,1024]{1,0:T(8,128)(2,1)S(1)} %copy-done.3, bf16[512,1024]{1,0:T(8,128)(2,1)S(1)} %copy-done.5, bf16[1,1024,1024]{2,1,0:T(8,128)(2,1)S(1)} %copy-done.1, f32[64,1024]{1,0:T(8,128)S(1)} %bitcast.5), custom_call_target="tpu_custom_call" | custom-call | flops 1073741824 | bytes 8388608 | tf_op jit(solution)/shard_map/merge_all/pallas_call | solution.py:120
  114.9 2.0 %copy-done.6 = f32[1024,1024]{1,0:T(8,128)} copy-done((f32[1024,1024]{1,0:T(8,128)}, f32[1024,1024]{1,0:T(8,128)S(1)}, u32[]{:S(2)}) %copy-start.6) | copy-done | bytes 4194328
  119.0 6.0 %all-to-all-done.2.own_ref = f32[8,16,3,8,128]{4,3,2,1,0:T(8,128)} async-done(((f32[8,16,3,8,128]{4,3,2,1,0:T(8,128)}), f32[8,16,3,8,128]{4,3,2,1,0:T(8,128)}, u32[]{:S(2)}, u32[]{:S(2)}) %all-to-all-start.2) | async-done | bytes 1572896 | tf_op jit(solution)/shard_map/all_to_all | solution.py:47
  125.1 4.3 %collective-permute-start.22 = (f32[8,16,3,8,128]{4,3,2,1,0:T(8,128)}, f32[8,16,3,8,128]{4,3,2,1,0:T(8,128)S(1)}, u32[]{:S(2)}, u32[]{:S(2)}) collective-permute-start(f32[8,16,3,8,128]{4,3,2,1,0:T(8,128)} %all-to-all-done.2.own_ref), channel_id=1, source_target_pairs={{0,8},{8,0},{16,24},{24,16},{32,40},{40,32},{48,56},{56,48},{64,72... | collective-permute-start | bytes 4718600 | tf_op jit(solution)/shard_map/ppermute | solution.py:28
  129.4 3.2 %collective-permute-done.22.away_ref = f32[8,16,3,8,128]{4,3,2,1,0:T(8,128)S(1)} collective-permute-done((f32[8,16,3,8,128]{4,3,2,1,0:T(8,128)}, f32[8,16,3,8,128]{4,3,2,1,0:T(8,128)S(1)}, u32[]{:S(2)}, u32[]{:S(2)}) %collective-permute-start.22) | collective-permute-done | bytes 1572896 | tf_op jit(solution)/shard_map/ppermute | solution.py:28
  133.6 13.6 %iterations.1 = (f32[64,1024]{1,0:T(8,128)}, f32[64,1024]{1,0:T(8,128)S(1)}) custom-call(s32[3]{0:T(128)S(1)} %pad_add_fusion.2.pos_ref, f32[8,16,3,8,128]{4,3,2,1,0:T(8,128)} %all-to-all-done.2.own_ref, f32[8,16,3,8,128]{4,3,2,1,0:T(8,128)S(1)} %collective-permute-done.22.away_ref, bf16[3,64,1024]{2,1,0:T(8,128)(2,1)S(1)} %copy-done.18), custom_call_target="tpu_custom_call" | custom-call | flops 2415919104 | bytes 4194304 | tf_op jit(solution)/shard_map/iterations/pallas_call | solution.py:331
  147.3 1.9 %left.1.own = f32[64,512]{1,0:T(8,128)S(1)} custom-call(s32[3]{0:T(128)S(1)} %pad_add_fusion.2.pos_ref, f32[64,1024]{1,0:T(8,128)S(1)} %get-tuple-element.83.w_ref, f32[256,512]{1,0:T(8,128)S(1)} %copy-done.10, f32[256,512]{1,0:T(8,128)} %collective-permute-done.18.m1, f32[256,512]{1,0:T(8,128)} %collective-permute-done.19.m3, f32[128,512]{1,0:T(8,128)S(1)} %copy-done.16, ...), custom_call_target="tpu_custom_call" | custom-call | flops 201326592 | bytes 2097152 | tf_op jit(solution)/shard_map/left/pallas_call | solution.py:359
  150.7 3.7 %finish.1 = (bf16[1,1024,1024]{2,1,0:T(8,128)(2,1)}, bf16[1024,1024]{1,0:T(8,128)(2,1)}) custom-call(s32[3]{0:T(128)S(1)} %pad_add_fusion.2.pos_ref, f32[1024,1024]{1,0:T(8,128)S(1)} %copy-done.7, bf16[1024,1024]{1,0:T(8,128)(2,1)S(1)} %copy-done.8, f32[64,512]{1,0:T(8,128)S(1)} %left.1.own, f32[64,512]{1,0:T(8,128)S(1)} %collective-permute-done.23.away, ...), custom_call_target="tpu_custom_call" | custom-call | flops 536870912 | bytes 12582912 | tf_op jit(solution)/shard_map/finish/pallas_call | solution.py:398
  (81 shorter events, 22.0 us)
Async XLA Ops:
  5.7 4.9 %collective-permute-start = (f32[1,512,256]{2,1,0:T(8,128)S(1)}, f32[1,512,256]{2,1,0:T(8,128)S(1)}, u32[]{:S(2)}, u32[]{:S(2)}) collective-permute-start(f32[1,512,256]{2,1,0:T(8,128)S(1)} %merge.4), channel_id=1, source_target_pairs={{0,8},{8,0},{16,24},{24,16},{32,40},{40,32},{48,56},{56,48},{64,72... | collective-permute-start | bytes 1572872 | tf_op jit(solution)/shard_map/ppermute | solution.py:28
  10.6 4.1 %collective-permute-start.1 = (f32[3,512,256]{2,1,0:T(8,128)S(1)}, f32[3,512,256]{2,1,0:T(8,128)S(1)}, u32[]{:S(2)}, u32[]{:S(2)}) collective-permute-start(f32[3,512,256]{2,1,0:T(8,128)S(1)} %merge.5), channel_id=1, source_target_pairs={{0,8},{8,0},{16,24},{24,16},{32,40},{40,32},{48,56},{56,48},{64,72... | collective-permute-start | bytes 4718600 | tf_op jit(solution)/shard_map/ppermute | solution.py:28
  11.9 9.1 %collective-permute-start.4 = (f32[256,256]{1,0:T(8,128)S(1)}, f32[256,256]{1,0:T(8,128)S(1)}, u32[]{:S(2)}, u32[]{:S(2)}) collective-permute-start(f32[256,256]{1,0:T(8,128)S(1)} %get-tuple-element.55), channel_id=1, source_target_pairs={{0,16},{8,24},{16,32},{24,40},{32,48},{40,56},{48,0},{56,8},{64,80... | collective-permute-start | bytes 786440 | tf_op jit(solution)/shard_map/ppermute | solution.py:28
  12.0 9.1 %collective-permute-start.6 = (f32[256,256]{1,0:T(8,128)S(1)}, f32[256,256]{1,0:T(8,128)S(1)}, u32[]{:S(2)}, u32[]{:S(2)}) collective-permute-start(f32[256,256]{1,0:T(8,128)S(1)} %get-tuple-element.57), channel_id=1, source_target_pairs={{0,48},{8,56},{16,0},{24,8},{32,16},{40,24},{48,32},{56,40},{64,11... | collective-permute-start | bytes 786440 | tf_op jit(solution)/shard_map/ppermute | solution.py:28
  15.9 9.6 %collective-permute-start.2 = (f32[256,256]{1,0:T(8,128)S(1)}, f32[256,256]{1,0:T(8,128)S(1)}, u32[]{:S(2)}, u32[]{:S(2)}) collective-permute-start(f32[256,256]{1,0:T(8,128)S(1)} %get-tuple-element.50), channel_id=1, source_target_pairs={{0,48},{8,56},{16,0},{24,8},{32,16},{40,24},{48,32},{56,40},{64,11... | collective-permute-start | bytes 786440 | tf_op jit(solution)/shard_map/ppermute | solution.py:28
  16.3 10.3 %collective-permute-start.3 = (f32[256,256]{1,0:T(8,128)S(1)}, f32[256,256]{1,0:T(8,128)S(1)}, u32[]{:S(2)}, u32[]{:S(2)}) collective-permute-start(f32[256,256]{1,0:T(8,128)S(1)} %get-tuple-element.52), channel_id=1, source_target_pairs={{0,16},{8,24},{16,32},{24,40},{32,48},{40,56},{48,0},{56,8},{64,80... | collective-permute-start | bytes 786440 | tf_op jit(solution)/shard_map/ppermute | solution.py:28
  21.0 11.2 %collective-permute-start.5 = (f32[256,256]{1,0:T(8,128)S(1)}, f32[256,256]{1,0:T(8,128)S(1)}, u32[]{:S(2)}, u32[]{:S(2)}) collective-permute-start(f32[256,256]{1,0:T(8,128)S(1)} %add.44), channel_id=1, source_target_pairs={{0,16},{8,24},{16,32},{24,40},{32,48},{40,56},{48,0},{56,8},{64,80... | collective-permute-start | bytes 786440 | tf_op jit(solution)/shard_map/ppermute | solution.py:28
  21.2 11.1 %collective-permute-start.7 = (f32[256,256]{1,0:T(8,128)S(1)}, f32[256,256]{1,0:T(8,128)S(1)}, u32[]{:S(2)}, u32[]{:S(2)}) collective-permute-start(f32[256,256]{1,0:T(8,128)S(1)} %add.45), channel_id=1, source_target_pairs={{0,48},{8,56},{16,0},{24,8},{32,16},{40,24},{48,32},{56,40},{64,11... | collective-permute-start | bytes 786440 | tf_op jit(solution)/shard_map/ppermute | solution.py:28
  33.0 5.6 %collective-permute-start.10 = (f32[32,512]{1,0:T(8,128)S(1)}, f32[32,512]{1,0:T(8,128)S(1)}, u32[]{:S(2)}, u32[]{:S(2)}) collective-permute-start(f32[32,512]{1,0:T(8,128)S(1)} %get-tuple-element.62), channel_id=1, source_target_pairs={{0,192},{8,200},{16,208},{24,216},{32,224},{40,232},{48,240},{56,2... | collective-permute-start | bytes 196616 | tf_op jit(solution)/shard_map/ppermute | solution.py:28
  37.2 6.0 %collective-permute-start.8 = (f32[32,512]{1,0:T(8,128)S(1)}, f32[32,512]{1,0:T(8,128)S(1)}, u32[]{:S(2)}, u32[]{:S(2)}) collective-permute-start(f32[32,512]{1,0:T(8,128)S(1)} %get-tuple-element.60), channel_id=1, source_target_pairs={{0,64},{8,72},{16,80},{24,88},{32,96},{40,104},{48,112},{56,120},{... | collective-permute-start | bytes 196616 | tf_op jit(solution)/shard_map/ppermute | solution.py:28
  38.6 8.0 %collective-permute-start.11 = (f32[64,512]{1,0:T(8,128)S(1)}, f32[64,512]{1,0:T(8,128)S(1)}, u32[]{:S(2)}, u32[]{:S(2)}) collective-permute-start(f32[64,512]{1,0:T(8,128)S(1)} %pad_add_fusion), channel_id=1, source_target_pairs={{0,192},{8,200},{16,208},{24,216},{32,224},{40,232},{48,240},{56,2... | collective-permute-start | bytes 393224 | tf_op jit(solution)/shard_map/ppermute | solution.py:28
  43.3 7.2 %collective-permute-start.9 = (f32[64,512]{1,0:T(8,128)S(1)}, f32[64,512]{1,0:T(8,128)S(1)}, u32[]{:S(2)}, u32[]{:S(2)}) collective-permute-start(f32[64,512]{1,0:T(8,128)S(1)} %pad_add_fusion.1), channel_id=1, source_target_pairs={{0,64},{8,72},{16,80},{24,88},{32,96},{40,104},{48,112},{56,120},{... | collective-permute-start | bytes 393224 | tf_op jit(solution)/shard_map/ppermute | solution.py:28
  50.5 6.7 %collective-permute-start.14 = (f32[64,512]{1,0:T(8,128)S(1)}, f32[64,512]{1,0:T(8,128)S(1)}, u32[]{:S(2)}, u32[]{:S(2)}) collective-permute-start(f32[64,512]{1,0:T(8,128)S(1)} %add_add_fusion.unit), channel_id=1, source_target_pairs={{0,64},{8,72},{16,80},{24,88},{32,96},{40,104},{48,112},{56,120},{... | collective-permute-start | bytes 393224 | tf_op jit(solution)/shard_map/ppermute | solution.py:28
  50.6 6.6 %collective-permute-start.15 = (f32[64,512]{1,0:T(8,128)S(1)}, f32[64,512]{1,0:T(8,128)S(1)}, u32[]{:S(2)}, u32[]{:S(2)}) collective-permute-start(f32[64,512]{1,0:T(8,128)S(1)} %add_add_fusion.unit), channel_id=1, source_target_pairs={{0,192},{8,200},{16,208},{24,216},{32,224},{40,232},{48,240},{56,2... | collective-permute-start | bytes 393224 | tf_op jit(solution)/shard_map/ppermute | solution.py:28
  54.2 5.4 %collective-permute-start.13 = (f32[64,512]{1,0:T(8,128)S(1)}, f32[64,512]{1,0:T(8,128)S(1)}, u32[]{:S(2)}, u32[]{:S(2)}) collective-permute-start(f32[64,512]{1,0:T(8,128)S(1)} %add_add_fusion.unit), channel_id=1, source_target_pairs={{0,32},{8,40},{16,48},{24,56},{32,0},{40,8},{48,16},{56,24},{64,96... | collective-permute-start | bytes 393224 | tf_op jit(solution)/shard_map/ppermute | solution.py:28
  57.2 5.3 %collective-permute-start.12 = (f32[64,512]{1,0:T(8,128)S(1)}, f32[64,512]{1,0:T(8,128)S(1)}, u32[]{:S(2)}, u32[]{:S(2)}) collective-permute-start(f32[64,512]{1,0:T(8,128)S(1)} %add_add_fusion.unit), channel_id=1, source_target_pairs={{0,16},{8,24},{16,32},{24,40},{32,48},{40,56},{48,0},{56,8},{64,80... | collective-permute-start | bytes 393224 | tf_op jit(solution)/shard_map/ppermute | solution.py:28
  57.2 7.6 %collective-permute-start.16 = (f32[64,512]{1,0:T(8,128)S(1)}, f32[64,512]{1,0:T(8,128)S(1)}, u32[]{:S(2)}, u32[]{:S(2)}) collective-permute-start(f32[64,512]{1,0:T(8,128)S(1)} %collective-permute-done.14.z1), channel_id=1, source_target_pairs={{0,64},{8,72},{16,80},{24,88},{32,96},{40,104},{48,112},{56,120},{... | collective-permute-start | bytes 393224 | tf_op jit(solution)/shard_map/ppermute | solution.py:28
  66.1 35.1 %copy-start.9 = (f32[256,512]{1,0:T(8,128)}, f32[256,512]{1,0:T(8,128)S(1)}, u32[]{:S(2)}) copy-start(f32[256,512]{1,0:T(8,128)S(1)} %get-tuple-element.67.m0) | copy-start | bytes 1572868
  66.1 21.3 %collective-permute-start.19 = (f32[256,512]{1,0:T(8,128)S(1)}, f32[256,512]{1,0:T(8,128)}, u32[]{:S(2)}, u32[]{:S(2)}) collective-permute-start(f32[256,512]{1,0:T(8,128)S(1)} %get-tuple-element.67.m0), channel_id=1, source_target_pairs={{0,48},{8,56},{16,0},{24,8},{32,16},{40,24},{48,32},{56,40},{64,11... | collective-permute-start | bytes 1572872 | tf_op jit(solution)/shard_map/ppermute | solution.py:28
  68.3 19.1 %collective-permute-start.18 = (f32[256,512]{1,0:T(8,128)S(1)}, f32[256,512]{1,0:T(8,128)}, u32[]{:S(2)}, u32[]{:S(2)}) collective-permute-start(f32[256,512]{1,0:T(8,128)S(1)} %get-tuple-element.67.m0), channel_id=1, source_target_pairs={{0,16},{8,24},{16,32},{24,40},{32,48},{40,56},{48,0},{56,8},{64,80... | collective-permute-start | bytes 1572872 | tf_op jit(solution)/shard_map/ppermute | solution.py:28
  68.5 7.1 %collective-permute-start.17 = (f32[8,3,8,128]{3,2,1,0:T(8,128)S(1)}, f32[8,3,8,128]{3,2,1,0:T(8,128)S(1)}, u32[]{:S(2)}, u32[]{:S(2)}) collective-permute-start(f32[8,3,8,128]{3,2,1,0:T(8,128)S(1)} %get-tuple-element.66), channel_id=1, source_target_pairs={{0,8},{8,0},{16,24},{24,16},{32,40},{40,32},{48,56},{56,48},{64,72... | collective-permute-start | bytes 294920 | tf_op jit(solution)/shard_map/ppermute | solution.py:28
  103.4 8.1 %copy-start.3 = (bf16[512,1024]{1,0:T(8,128)(2,1)S(1)}, bf16[512,1024]{1,0:T(8,128)(2,1)}, u32[]{:S(2)}) copy-start(bf16[512,1024]{1,0:T(8,128)(2,1)} %acts.8) | copy-start | bytes 3145732
  103.4 8.1 %copy-start.11 = (f32[1024,64]{0,1:T(8,128)S(1)}, f32[1024,64]{0,1:T(8,128)}, u32[]{:S(2)}) copy-start(f32[1024,64]{0,1:T(8,128)} %param.9) | copy-start | bytes 786436
  103.4 21.7 %all-to-all-start.2 = ((f32[8,16,3,8,128]{4,3,2,1,0:T(8,128)}), f32[8,16,3,8,128]{4,3,2,1,0:T(8,128)}, u32[]{:S(2)}, u32[]{:S(2)}) async-start(f32[8,16,3,8,128]{4,3,2,1,0:T(8,128)} %spread.3), calls=%async_computation.2 | async-start | bytes 3145728 | tf_op jit(solution)/shard_map/all_to_all | solution.py:47
  109.9 7.7 %collective-permute-start.21 = (f32[128,512]{1,0:T(8,128)S(1)}, f32[128,512]{1,0:T(8,128)S(1)}, u32[]{:S(2)}, u32[]{:S(2)}) collective-permute-start(f32[128,512]{1,0:T(8,128)S(1)} %slice.7), channel_id=1, source_target_pairs={{0,48},{8,56},{16,0},{24,8},{32,16},{40,24},{48,32},{56,40},{64,11... | collective-permute-start | bytes 786440 | tf_op jit(solution)/shard_map/ppermute | solution.py:28
  110.8 7.5 %collective-permute-start.20 = (f32[128,512]{1,0:T(8,128)S(1)}, f32[128,512]{1,0:T(8,128)S(1)}, u32[]{:S(2)}, u32[]{:S(2)}) collective-permute-start(f32[128,512]{1,0:T(8,128)S(1)} %slice.6), channel_id=1, source_target_pairs={{0,16},{8,24},{16,32},{24,40},{32,48},{40,56},{48,0},{56,8},{64,80... | collective-permute-start | bytes 786440 | tf_op jit(solution)/shard_map/ppermute | solution.py:28
  125.1 22.2 %copy-start.10 = (f32[256,512]{1,0:T(8,128)S(1)}, f32[256,512]{1,0:T(8,128)}, u32[]{:S(2)}) copy-start(f32[256,512]{1,0:T(8,128)} %copy-done.9) | copy-start | bytes 1572868
  125.1 22.2 %copy-start.14 = (f32[128,512]{1,0:T(8,128)S(1)}, f32[128,512]{1,0:T(8,128)}, u32[]{:S(2)}) copy-start(f32[128,512]{1,0:T(8,128)} %copy-done.13) | copy-start | bytes 786436
  125.1 22.2 %copy-start.16 = (f32[128,512]{1,0:T(8,128)S(1)}, f32[128,512]{1,0:T(8,128)}, u32[]{:S(2)}) copy-start(f32[128,512]{1,0:T(8,128)} %copy-done.15) | copy-start | bytes 786436
  125.1 7.5 %collective-permute-start.22 = (f32[8,16,3,8,128]{4,3,2,1,0:T(8,128)}, f32[8,16,3,8,128]{4,3,2,1,0:T(8,128)S(1)}, u32[]{:S(2)}, u32[]{:S(2)}) collective-permute-start(f32[8,16,3,8,128]{4,3,2,1,0:T(8,128)} %all-to-all-done.2.own_ref), channel_id=1, source_target_pairs={{0,8},{8,0},{16,24},{24,16},{32,40},{40,32},{48,56},{56,48},{64,72... | collective-permute-start | bytes 4718600 | tf_op jit(solution)/shard_map/ppermute | solution.py:28
  133.6 17.0 %copy-start.7 = (f32[1024,1024]{1,0:T(8,128)S(1)}, f32[1024,1024]{1,0:T(8,128)}, u32[]{:S(2)}) copy-start(f32[1024,1024]{1,0:T(8,128)} %copy-done.6) | copy-start | bytes 12582916
  149.2 1.4 collective-permute-start.23
  (12 other events, 25.3 us)

commit v8 on v7

--- a/solution.py
+++ b/solution.py
@@ -267,8 +267,22 @@
     return jnp.concatenate(out, axis=0)[:, n:] * scale
 
 
-def iterate_kernel(pos_ref, own_ref, away_ref, q_ref, q_out, w_out, hi_ref, mid_ref, low_ref):
+BLOCKS = ((0, 0, 256), (3, 0, 256), (1, 0, 256), (2, 0, 128), (2, 128, 128))
+
+
+def iterate_kernel(pos_ref, own_ref, away_ref, q_hbm, m0, m1, m3, m2_top, m2_end,
+                   q_out, p_out, hi_ref, mid_ref, low_ref, q_ref, m_ref, sems):
     s = pl.program_id(0)
+    copies = [pltpu.make_async_copy(q_hbm, q_ref, sems.at[0])]
+    for n, ((turn, start, size), ref) in enumerate(zip(BLOCKS, (m0, m1, m3, m2_top, m2_end))):
+        at = pl.ds(pl.multiple_of((pos_ref[1] + turn) % 4 * 256 + start, 128), size)
+        copies.append(pltpu.make_async_copy(ref, m_ref.at[at, :], sems.at[1 + n]))
+
+    @pl.when(s == 0)
+    def _():
+        for copy in copies:
+            copy.start()
+
     parts = (hi_ref, mid_ref, low_ref)
     for ref, core in ((own_ref, pos_ref[0]), (away_ref, 1 - pos_ref[0])):
         for z in range(4):
@@ -289,6 +303,7 @@
             here, after = pl.ds(y * 256, 256), pl.ds((y + 1) % 4 * 256, 256)
             for part in parts:
                 part[after, here] = part[here, after].T
+        copies[0].wait()
         n = q_out.shape[0]
         def product(x, y_hi, y_mid, y_low, dims):
             hi, mid, low = x
@@ -316,55 +331,40 @@
             v_parts = None if last else split3(times_g(u_parts))
             inv = inverse_factor(gram)
             if last:
-                w_out[...] = solve(inv, q_parts)
+                w = solve(inv, q_parts)
             q = solve(inv, u_parts) * (1.0 / 32)
             if not last:
                 q_parts = split3(q)
                 u = solve(inv, v_parts) * (1.0 / 32)
         q_out[...] = q
-
-
-def iterate(pos, own, away, q_parts):
+        w_hi, w_low = split2(w)
+        for copy in copies[1:]:
+            copy.wait()
+        m_hi, m_low = split2(m_ref[...])
+        both = jnp.dot(jnp.concatenate([w_hi, w_low], axis=0), m_hi, preferred_element_type=F32)
+        p_out[...] = both[:n] + (both[n:] + jnp.dot(w_hi, m_low, preferred_element_type=F32))
+
+
+def iterate(pos, own, away, q_parts, blocks):
     _, n, k = q_parts.shape
+    d = blocks[0].shape[1]
     part = pl.BlockSpec((2,) + own.shape[1:], lambda s: (s, 0, 0, 0, 0))
-    whole = pl.BlockSpec((n, k), lambda s: (0, 0))
+    anywhere = pl.BlockSpec(memory_space=pl.ANY)
     return pl.pallas_call(
         iterate_kernel,
-        out_shape=(jax.ShapeDtypeStruct((n, k), F32),) * 2,
+        out_shape=(jax.ShapeDtypeStruct((n, k), F32), jax.ShapeDtypeStruct((n, d), F32)),
         grid=(own.shape[0] // 2,),
-        in_specs=[SMEM, part, part, pl.BlockSpec((3, n, k), lambda s: (0, 0, 0))],
-        out_specs=(whole, whole),
-        scratch_shapes=[pltpu.VMEM((k, k), BF16)] * 3,
-        compiler_params=params(20),
+        in_specs=[SMEM, part, part] + [anywhere] * 6,
+        out_specs=(pl.BlockSpec((n, k), lambda s: (0, 0)), pl.BlockSpec((n, d), lambda s: (0, 0))),
+        scratch_shapes=[pltpu.VMEM((k, k), BF16)] * 3 + [
+            pltpu.VMEM((3, n, k), BF16),
+            pltpu.VMEM((k, d), F32),
+            pltpu.SemaphoreType.DMA((6,)),
+        ],
+        compiler_params=params(26),
         cost_estimate=cost(36 * n * k * k, 4 * k * k),
         name="iterations",
-    )(pos, own, away, q_parts)
-
-
-def left_kernel(pos_ref, w_ref, m0, m1, m3, m2_top, m2_end, out_ref):
-    total = None
-    n = w_ref.shape[0]
-    for turn, start, ref in ((0, 0, m0), (3, 0, m1), (1, 0, m3), (2, 0, m2_top), (2, 128, m2_end)):
-        at = pl.multiple_of((pos_ref[1] + turn) % 4 * 256 + start, 128)
-        whi, wlow = split2(w_ref[:, pl.ds(at, ref.shape[0])])
-        mhi, mlow = split2(ref[...])
-        both = jnp.dot(jnp.concatenate([whi, wlow], axis=0), mhi, preferred_element_type=F32)
-        part = both[:n] + (both[n:] + jnp.dot(whi, mlow, preferred_element_type=F32))
-        total = part if total is None else total + part
-    out_ref[...] = total
-
-
-def left(pos, w, blocks):
-    n, d = w.shape[0], blocks[0].shape[1]
-    return pl.pallas_call(
-        left_kernel,
-        out_shape=jax.ShapeDtypeStruct((n, d), F32),
-        in_specs=[SMEM] + [VMEM] * 6,
-        out_specs=VMEM,
-        compiler_params=params(12),
-        cost_estimate=cost(6 * n * d * 1024, 2 << 20),
-        name="left",
-    )(pos, w, *blocks)
+    )(pos, own, away, q_parts, *blocks)
 
 
 def finish_kernel(pos_ref, merged, mom, own, away, q, err_out, mom_out, q_parts):
@@ -445,7 +445,6 @@
     part = part + dp_shift(to_core, dc=1)
     m1, m3 = dp_shift(of_y, dy=1), dp_shift(of_y, dy=-1)
     copies = spread(exchange(part, None, "shard"), 16, leading=True)
-    copies, m1, m3 = lax.optimization_barrier((copies, m1, m3))
     part = exchange(copies, ZY_GROUPS)
     part, m1, m3, args, q_t = lax.optimization_barrier((part, m1, m3, args, q_start.T))
     m2_top, m2_end = dp_shift(m1[:128], dy=1), dp_shift(m3[128:], dy=-1)
@@ -453,10 +452,9 @@
     part, m2_top, m2_end, merged, q_parts = lax.optimization_barrier(
         (part, m2_top, m2_end, *merge_all(*args, q_t))
     )
-    q_t, w = iterate(pos, part, dp_shift(part, dc=1), q_parts)
-
     blocks = [of_y, m1, m3, m2_top, m2_end]
-    own = left(pos, w, blocks)
+    q_t, own = iterate(pos, part, dp_shift(part, dc=1), q_parts, blocks)
+
     away = dp_shift(own, dc=1)
     new_error, new_momentum = finish(pos, merged, momentum, own, away, q_t)
     return (new_error, new_momentum, q_t.T)

time: 155 us -> 160 us (1.032)
  blocking collectives: 25.6 us -> 0 us
  starting transfers between devices: 45.9 us -> 58.3 us
  waiting for transfers between devices: 39.4 us -> 49.5 us
  local copies, waits for them, and re-layouts: 12.4 us -> 19.1 us
    all_to_all x2 -> x0, blocking collectives: 25.6 us -> none  [exchange(): return lax.all_to_all(x, axis, 0, 0, axis_index_groups=groups)]
    all_to_all x1 -> x3, starting transfers between devices: 4.57 us -> 14.9 us  [exchange(): return lax.all_to_all(x, axis, 0, 0, axis_index_groups=groups)]
    unnamed x38 -> x48, local copies, waits for them, and re-layouts: 10.4 us -> 17.1 us
    ppermute x24, waiting for transfers between devices: 33.3 us -> 39.9 us  [dp_shift(): return lax.ppermute(x, 'dp', pairs)]
    all_to_all x1 -> x3, waiting for transfers between devices: 6.05 us -> 9.63 us  [exchange(): return lax.all_to_all(x, axis, 0, 0, axis_index_groups=groups)]
    ppermute x24, starting transfers between devices: 41.3 us -> 43.4 us  [dp_shift(): return lax.ppermute(x, 'dp', pairs)]
    pallas_call x1 -> x0, Pallas kernels: 1.92 us -> none  [left(): pl.pallas_call(left_kernel, out_shape=jax.ShapeDtypeStruct((n, d), F32),...]
  transfers between devices with their start and end apart: 25 -> 27, of which waited for: 15 -> 19; matrix products, arithmetic and copies ran while one was open for 1% -> 1% of each run, Pallas kernels for 4% -> 4%
where the time goes in v8:
time: 160 us; the launch traced here: 159 us
  starting transfers between devices  58.3 us (36%)
  waiting for transfers between devices  49.5 us (31%)
  Pallas kernels  30.2 us (19%)
  local copies, waits for them, and re-layouts  19.1 us (12%)
    ppermute x24, starting transfers between devices, dp_shift(): return lax.ppermute(x, 'dp', pairs)  43.4 us
    ppermute x24, waiting for transfers between devices, dp_shift(): return lax.ppermute(x, 'dp', pairs)  39.9 us
    unnamed x48, local copies, waits for them, and re-layouts  17.1 us
    pallas_call x1, Pallas kernels, iterate(): pl.pallas_call(iterate_kernel, out_shape=(jax.ShapeDtypeStruct((n, k), F3...  15.1 us
    all_to_all x3, starting transfers between devices, exchange(): return lax.all_to_all(x, axis, 0, 0, axis_index_groups=groups)  14.9 us
    all_to_all x3, waiting for transfers between devices, exchange(): return lax.all_to_all(x, axis, 0, 0, axis_index_groups=groups)  9.63 us
    pallas_call x4, Pallas kernels, merge(): pl.pallas_call(functools.partial(merge_kernel, turns, own), out_shape=out...  4.3 us
    pallas_call x1, Pallas kernels, finish(): pl.pallas_call(finish_kernel, out_shape=(jax.ShapeDtypeStruct((1, d, k),...  3.74 us
  transfers between devices with their start and end apart: 27, of which 19 were waited for; matrix products, arithmetic and copies ran while one was open for 1% of the time, Pallas kernels for 4%

profile of v8, /device:TPU:1, one launch (start us, length us, event | category | flops | bytes accessed | tf_op | source)
XLA Modules:
  0.0 158.9 jit_solution(17940756664086975655)
XLA Ops:
  0.7 1.6 %copy-done = bf16[1,1024,1024]{2,1,0:T(8,128)(2,1)S(1)} copy-done((bf16[1,1024,1024]{2,1,0:T(8,128)(2,1)S(1)}, bf16[1,1024,1024]{2,1,0:T(8,128)(2,1)}, u32[]{:S(2)}) %copy-start) | copy-done | bytes 2097176
  5.7 3.3 %collective-permute-start = (f32[1,512,256]{2,1,0:T(8,128)S(1)}, f32[1,512,256]{2,1,0:T(8,128)S(1)}, u32[]{:S(2)}, u32[]{:S(2)}) collective-permute-start(f32[1,512,256]{2,1,0:T(8,128)S(1)} %merge.4), channel_id=1, source_target_pairs={{0,8},{8,0},{16,24},{24,16},{32,40},{40,32},{48,56},{56,48},{64,72... | collective-permute-start | bytes 1572872 | tf_op jit(solution)/shard_map/ppermute | solution.py:28
  12.0 2.7 %collective-permute-start.6 = (f32[256,256]{1,0:T(8,128)S(1)}, f32[256,256]{1,0:T(8,128)S(1)}, u32[]{:S(2)}, u32[]{:S(2)}) collective-permute-start(f32[256,256]{1,0:T(8,128)S(1)} %get-tuple-element.54), channel_id=1, source_target_pairs={{0,48},{8,56},{16,0},{24,8},{32,16},{40,24},{48,32},{56,40},{64,11... | collective-permute-start | bytes 786440 | tf_op jit(solution)/shard_map/ppermute | solution.py:28
  17.5 3.5 %collective-permute-done.4 = f32[256,256]{1,0:T(8,128)S(1)} collective-permute-done((f32[256,256]{1,0:T(8,128)S(1)}, f32[256,256]{1,0:T(8,128)S(1)}, u32[]{:S(2)}, u32[]{:S(2)}) %collective-permute-start.4) | collective-permute-done | bytes 262176 | tf_op jit(solution)/shard_map/ppermute | solution.py:28
  21.2 2.7 %collective-permute-start.7 = (f32[256,256]{1,0:T(8,128)S(1)}, f32[256,256]{1,0:T(8,128)S(1)}, u32[]{:S(2)}, u32[]{:S(2)}) collective-permute-start(f32[256,256]{1,0:T(8,128)S(1)} %add.45), channel_id=1, source_target_pairs={{0,48},{8,56},{16,0},{24,8},{32,16},{40,24},{48,32},{56,40},{64,11... | collective-permute-start | bytes 786440 | tf_op jit(solution)/shard_map/ppermute | solution.py:28
  23.9 1.7 %collective-permute-done.2 = f32[256,256]{1,0:T(8,128)S(1)} collective-permute-done((f32[256,256]{1,0:T(8,128)S(1)}, f32[256,256]{1,0:T(8,128)S(1)}, u32[]{:S(2)}, u32[]{:S(2)}) %collective-permute-start.2) | collective-permute-done | bytes 262176 | tf_op jit(solution)/shard_map/ppermute | solution.py:28
  26.6 5.6 %collective-permute-done.5.on = f32[256,256]{1,0:T(8,128)S(1)} collective-permute-done((f32[256,256]{1,0:T(8,128)S(1)}, f32[256,256]{1,0:T(8,128)S(1)}, u32[]{:S(2)}, u32[]{:S(2)}) %collective-permute-start.5) | collective-permute-done | bytes 262176 | tf_op jit(solution)/shard_map/ppermute | solution.py:28
  33.0 4.2 %collective-permute-start.10 = (f32[32,512]{1,0:T(8,128)S(1)}, f32[32,512]{1,0:T(8,128)S(1)}, u32[]{:S(2)}, u32[]{:S(2)}) collective-permute-start(f32[32,512]{1,0:T(8,128)S(1)} %get-tuple-element.59), channel_id=1, source_target_pairs={{0,192},{8,200},{16,208},{24,216},{32,224},{40,232},{48,240},{56,2... | collective-permute-start | bytes 196616 | tf_op jit(solution)/shard_map/ppermute | solution.py:28
  38.6 4.7 %collective-permute-start.11 = (f32[64,512]{1,0:T(8,128)S(1)}, f32[64,512]{1,0:T(8,128)S(1)}, u32[]{:S(2)}, u32[]{:S(2)}) collective-permute-start(f32[64,512]{1,0:T(8,128)S(1)} %pad_add_fusion), channel_id=1, source_target_pairs={{0,192},{8,200},{16,208},{24,216},{32,224},{40,232},{48,240},{56,2... | collective-permute-start | bytes 393224 | tf_op jit(solution)/shard_map/ppermute | solution.py:28
  43.4 3.2 %collective-permute-done.11 = f32[64,512]{1,0:T(8,128)S(1)} collective-permute-done((f32[64,512]{1,0:T(8,128)S(1)}, f32[64,512]{1,0:T(8,128)S(1)}, u32[]{:S(2)}, u32[]{:S(2)}) %collective-permute-start.11) | collective-permute-done | bytes 131104 | tf_op jit(solution)/shard_map/ppermute | solution.py:28
  46.6 3.9 %collective-permute-done.9 = f32[64,512]{1,0:T(8,128)S(1)} collective-permute-done((f32[64,512]{1,0:T(8,128)S(1)}, f32[64,512]{1,0:T(8,128)S(1)}, u32[]{:S(2)}, u32[]{:S(2)}) %collective-permute-start.9) | collective-permute-done | bytes 131104 | tf_op jit(solution)/shard_map/ppermute | solution.py:28
  50.6 3.6 %collective-permute-start.15 = (f32[64,512]{1,0:T(8,128)S(1)}, f32[64,512]{1,0:T(8,128)S(1)}, u32[]{:S(2)}, u32[]{:S(2)}) collective-permute-start(f32[64,512]{1,0:T(8,128)S(1)} %add_add_fusion.unit), channel_id=1, source_target_pairs={{0,192},{8,200},{16,208},{24,216},{32,224},{40,232},{48,240},{56,2... | collective-permute-start | bytes 393224 | tf_op jit(solution)/shard_map/ppermute | solution.py:28
  54.2 3.0 %collective-permute-start.13 = (f32[64,512]{1,0:T(8,128)S(1)}, f32[64,512]{1,0:T(8,128)S(1)}, u32[]{:S(2)}, u32[]{:S(2)}) collective-permute-start(f32[64,512]{1,0:T(8,128)S(1)} %add_add_fusion.unit), channel_id=1, source_target_pairs={{0,32},{8,40},{16,48},{24,56},{32,0},{40,8},{48,16},{56,24},{64,96... | collective-permute-start | bytes 393224 | tf_op jit(solution)/shard_map/ppermute | solution.py:28
  57.2 2.3 %collective-permute-done.13.u2 = f32[64,512]{1,0:T(8,128)S(1)} collective-permute-done((f32[64,512]{1,0:T(8,128)S(1)}, f32[64,512]{1,0:T(8,128)S(1)}, u32[]{:S(2)}, u32[]{:S(2)}) %collective-permute-start.13) | collective-permute-done | bytes 131104 | tf_op jit(solution)/shard_map/ppermute | solution.py:28
  59.6 3.0 %collective-permute-done.12.u1 = f32[64,512]{1,0:T(8,128)S(1)} collective-permute-done((f32[64,512]{1,0:T(8,128)S(1)}, f32[64,512]{1,0:T(8,128)S(1)}, u32[]{:S(2)}, u32[]{:S(2)}) %collective-permute-start.12) | collective-permute-done | bytes 131104 | tf_op jit(solution)/shard_map/ppermute | solution.py:28
  62.5 2.3 %collective-permute-done.16.z2 = f32[64,512]{1,0:T(8,128)S(1)} collective-permute-done((f32[64,512]{1,0:T(8,128)S(1)}, f32[64,512]{1,0:T(8,128)S(1)}, u32[]{:S(2)}, u32[]{:S(2)}) %collective-permute-start.16) | collective-permute-done | bytes 131104 | tf_op jit(solution)/shard_map/ppermute | solution.py:28
  66.1 6.0 %collective-permute-start.17 = (f32[8,3,8,128]{3,2,1,0:T(8,128)S(1)}, f32[8,3,8,128]{3,2,1,0:T(8,128)S(1)}, u32[]{:S(2)}, u32[]{:S(2)}) collective-permute-start(f32[8,3,8,128]{3,2,1,0:T(8,128)S(1)} %get-tuple-element.63), channel_id=1, source_target_pairs={{0,8},{8,0},{16,24},{24,16},{32,40},{40,32},{48,56},{56,48},{64,72... | collective-permute-start | bytes 294920 | tf_op jit(solution)/shard_map/ppermute | solution.py:28
  73.7 4.2 %all-to-all-start = ((f32[8,3,8,128]{3,2,1,0:T(8,128)}), f32[8,3,8,128]{3,2,1,0:T(8,128)S(1)}, u32[]{:S(2)}, u32[]{:S(2)}) async-start(f32[8,3,8,128]{3,2,1,0:T(8,128)} %add.50), calls=%async_computation | async-start | bytes 196608 | tf_op jit(solution)/shard_map/all_to_all | solution.py:47
  77.9 4.7 %collective-permute-start.19 = (f32[256,512]{1,0:T(8,128)S(1)}, f32[256,512]{1,0:T(8,128)S(1)}, u32[]{:S(2)}, u32[]{:S(2)}) collective-permute-start(f32[256,512]{1,0:T(8,128)S(1)} %get-tuple-element.64.m0), channel_id=1, source_target_pairs={{0,48},{8,56},{16,0},{24,8},{32,16},{40,24},{48,32},{56,40},{64,11... | collective-permute-start | bytes 1572872 | tf_op jit(solution)/shard_map/ppermute | solution.py:28
  83.9 6.1 %all-to-all-start.1 = ((f32[16,3,8,128]{3,2,1,0:T(8,128)}), f32[16,3,8,128]{3,2,1,0:T(8,128)S(1)}, u32[]{:S(2)}, u32[]{:S(2)}) async-start(f32[16,3,8,128]{3,2,1,0:T(8,128)} %spread.2), calls=%async_computation.1 | async-start | bytes 393216 | tf_op jit(solution)/shard_map/all_to_all | solution.py:47
  90.0 3.2 %collective-permute-done.19.m3 = f32[256,512]{1,0:T(8,128)S(1)} collective-permute-done((f32[256,512]{1,0:T(8,128)S(1)}, f32[256,512]{1,0:T(8,128)S(1)}, u32[]{:S(2)}, u32[]{:S(2)}) %collective-permute-start.19) | collective-permute-done | bytes 524320 | tf_op jit(solution)/shard_map/ppermute | solution.py:28
  93.2 3.4 %collective-permute-done.18.m1 = f32[256,512]{1,0:T(8,128)S(1)} collective-permute-done((f32[256,512]{1,0:T(8,128)S(1)}, f32[256,512]{1,0:T(8,128)S(1)}, u32[]{:S(2)}, u32[]{:S(2)}) %collective-permute-start.18) | collective-permute-done | bytes 524320 | tf_op jit(solution)/shard_map/ppermute | solution.py:28
  96.6 3.0 %all-to-all-done.1.x_ref = f32[16,3,8,128]{3,2,1,0:T(8,128)S(1)} async-done(((f32[16,3,8,128]{3,2,1,0:T(8,128)}), f32[16,3,8,128]{3,2,1,0:T(8,128)S(1)}, u32[]{:S(2)}, u32[]{:S(2)}) %all-to-all-start.1) | async-done | bytes 196640 | tf_op jit(solution)/shard_map/all_to_all | solution.py:47
  100.3 2.2 %spread.3 = f32[8,16,3,8,128]{4,3,2,1,0:T(8,128)} custom-call(f32[16,3,8,128]{3,2,1,0:T(8,128)} %copy-done.23), custom_call_target="tpu_custom_call" | custom-call | flops 131072 | bytes 1048576 | tf_op jit(solution)/shard_map/spread/pallas_call | solution.py:178
  102.4 4.6 %all-to-all-start.2 = ((f32[8,16,3,8,128]{4,3,2,1,0:T(8,128)}), f32[8,16,3,8,128]{4,3,2,1,0:T(8,128)}, u32[]{:S(2)}, u32[]{:S(2)}) async-start(f32[8,16,3,8,128]{4,3,2,1,0:T(8,128)} %spread.3), calls=%async_computation.2 | async-start | bytes 3145728 | tf_op jit(solution)/shard_map/all_to_all | solution.py:47
  111.7 2.1 %merge_all.1 = (f32[1024,1024]{1,0:T(8,128)S(1)}, bf16[3,64,1024]{2,1,0:T(8,128)(2,1)S(1)}) custom-call(bf16[512,1024]{1,0:T(8,128)(2,1)S(1)} %copy-done.3, bf16[512,1024]{1,0:T(8,128)(2,1)S(1)} %copy-done.5, bf16[1,1024,1024]{2,1,0:T(8,128)(2,1)S(1)} %copy-done.1, f32[64,1024]{1,0:T(8,128)S(1)} %bitcast.5), custom_call_target="tpu_custom_call" | custom-call | flops 1073741824 | bytes 8388608 | tf_op jit(solution)/shard_map/merge_all/pallas_call | solution.py:120
  113.9 2.0 %copy-done.6 = f32[1024,1024]{1,0:T(8,128)} copy-done((f32[1024,1024]{1,0:T(8,128)}, f32[1024,1024]{1,0:T(8,128)S(1)}, u32[]{:S(2)}) %copy-start.6) | copy-done | bytes 4194328
  118.1 6.0 %all-to-all-done.2.own_ref = f32[8,16,3,8,128]{4,3,2,1,0:T(8,128)} async-done(((f32[8,16,3,8,128]{4,3,2,1,0:T(8,128)}), f32[8,16,3,8,128]{4,3,2,1,0:T(8,128)}, u32[]{:S(2)}, u32[]{:S(2)}) %all-to-all-start.2) | async-done | bytes 1572896 | tf_op jit(solution)/shard_map/all_to_all | solution.py:47
  124.1 4.3 %collective-permute-start.22 = (f32[8,16,3,8,128]{4,3,2,1,0:T(8,128)}, f32[8,16,3,8,128]{4,3,2,1,0:T(8,128)S(1)}, u32[]{:S(2)}, u32[]{:S(2)}) collective-permute-start(f32[8,16,3,8,128]{4,3,2,1,0:T(8,128)} %all-to-all-done.2.own_ref), channel_id=1, source_target_pairs={{0,8},{8,0},{16,24},{24,16},{32,40},{40,32},{48,56},{56,48},{64,72... | collective-permute-start | bytes 4718600 | tf_op jit(solution)/shard_map/ppermute | solution.py:28
  128.4 3.2 %collective-permute-done.22.away_ref = f32[8,16,3,8,128]{4,3,2,1,0:T(8,128)S(1)} collective-permute-done((f32[8,16,3,8,128]{4,3,2,1,0:T(8,128)}, f32[8,16,3,8,128]{4,3,2,1,0:T(8,128)S(1)}, u32[]{:S(2)}, u32[]{:S(2)}) %collective-permute-start.22) | collective-permute-done | bytes 1572896 | tf_op jit(solution)/shard_map/ppermute | solution.py:28
  137.7 15.1 %iterations.1 = (f32[64,1024]{1,0:T(8,128)}, f32[64,512]{1,0:T(8,128)S(1)}) custom-call(s32[3]{0:T(128)S(1)} %pad_add_fusion.2.pos_ref, f32[8,16,3,8,128]{4,3,2,1,0:T(8,128)} %all-to-all-done.2.own_ref, f32[8,16,3,8,128]{4,3,2,1,0:T(8,128)S(1)} %collective-permute-done.22.away_ref, bf16[3,64,1024]{2,1,0:T(8,128)(2,1)S(1)} %copy-done.18, ...), custom_call_target="tpu_custom_call" | custom-call | flops 2415919104 | bytes 4194304 | tf_op jit(solution)/shard_map/iterations/pallas_call | solution.py:353
  155.1 3.7 %finish.1 = (bf16[1,1024,1024]{2,1,0:T(8,128)(2,1)}, bf16[1024,1024]{1,0:T(8,128)(2,1)}) custom-call(s32[3]{0:T(128)S(1)} %pad_add_fusion.2.pos_ref, f32[1024,1024]{1,0:T(8,128)S(1)} %copy-done.7, bf16[1024,1024]{1,0:T(8,128)(2,1)S(1)} %copy-done.8, f32[64,512]{1,0:T(8,128)S(1)} %get-tuple-element.79.own, f32[64,512]{1,0:T(8,128)S(1)} %collective-permute-done.23.away, ...), custom_call_target="tpu_custom_call" | custom-call | flops 536870912 | bytes 12582912 | tf_op jit(solution)/shard_map/finish/pallas_call | solution.py:398
  (92 shorter events, 32.9 us)
Async XLA Ops:
  5.7 4.9 %collective-permute-start = (f32[1,512,256]{2,1,0:T(8,128)S(1)}, f32[1,512,256]{2,1,0:T(8,128)S(1)}, u32[]{:S(2)}, u32[]{:S(2)}) collective-permute-start(f32[1,512,256]{2,1,0:T(8,128)S(1)} %merge.4), channel_id=1, source_target_pairs={{0,8},{8,0},{16,24},{24,16},{32,40},{40,32},{48,56},{56,48},{64,72... | collective-permute-start | bytes 1572872 | tf_op jit(solution)/shard_map/ppermute | solution.py:28
  10.6 4.1 %collective-permute-start.1 = (f32[3,512,256]{2,1,0:T(8,128)S(1)}, f32[3,512,256]{2,1,0:T(8,128)S(1)}, u32[]{:S(2)}, u32[]{:S(2)}) collective-permute-start(f32[3,512,256]{2,1,0:T(8,128)S(1)} %merge.5), channel_id=1, source_target_pairs={{0,8},{8,0},{16,24},{24,16},{32,40},{40,32},{48,56},{56,48},{64,72... | collective-permute-start | bytes 4718600 | tf_op jit(solution)/shard_map/ppermute | solution.py:28
  11.9 9.1 %collective-permute-start.4 = (f32[256,256]{1,0:T(8,128)S(1)}, f32[256,256]{1,0:T(8,128)S(1)}, u32[]{:S(2)}, u32[]{:S(2)}) collective-permute-start(f32[256,256]{1,0:T(8,128)S(1)} %get-tuple-element.52), channel_id=1, source_target_pairs={{0,16},{8,24},{16,32},{24,40},{32,48},{40,56},{48,0},{56,8},{64,80... | collective-permute-start | bytes 786440 | tf_op jit(solution)/shard_map/ppermute | solution.py:28
  12.0 9.1 %collective-permute-start.6 = (f32[256,256]{1,0:T(8,128)S(1)}, f32[256,256]{1,0:T(8,128)S(1)}, u32[]{:S(2)}, u32[]{:S(2)}) collective-permute-start(f32[256,256]{1,0:T(8,128)S(1)} %get-tuple-element.54), channel_id=1, source_target_pairs={{0,48},{8,56},{16,0},{24,8},{32,16},{40,24},{48,32},{56,40},{64,11... | collective-permute-start | bytes 786440 | tf_op jit(solution)/shard_map/ppermute | solution.py:28
  15.9 9.6 %collective-permute-start.2 = (f32[256,256]{1,0:T(8,128)S(1)}, f32[256,256]{1,0:T(8,128)S(1)}, u32[]{:S(2)}, u32[]{:S(2)}) collective-permute-start(f32[256,256]{1,0:T(8,128)S(1)} %get-tuple-element.47), channel_id=1, source_target_pairs={{0,48},{8,56},{16,0},{24,8},{32,16},{40,24},{48,32},{56,40},{64,11... | collective-permute-start | bytes 786440 | tf_op jit(solution)/shard_map/ppermute | solution.py:28
  16.3 10.3 %collective-permute-start.3 = (f32[256,256]{1,0:T(8,128)S(1)}, f32[256,256]{1,0:T(8,128)S(1)}, u32[]{:S(2)}, u32[]{:S(2)}) collective-permute-start(f32[256,256]{1,0:T(8,128)S(1)} %get-tuple-element.49), channel_id=1, source_target_pairs={{0,16},{8,24},{16,32},{24,40},{32,48},{40,56},{48,0},{56,8},{64,80... | collective-permute-start | bytes 786440 | tf_op jit(solution)/shard_map/ppermute | solution.py:28
  21.0 11.2 %collective-permute-start.5 = (f32[256,256]{1,0:T(8,128)S(1)}, f32[256,256]{1,0:T(8,128)S(1)}, u32[]{:S(2)}, u32[]{:S(2)}) collective-permute-start(f32[256,256]{1,0:T(8,128)S(1)} %add.44), channel_id=1, source_target_pairs={{0,16},{8,24},{16,32},{24,40},{32,48},{40,56},{48,0},{56,8},{64,80... | collective-permute-start | bytes 786440 | tf_op jit(solution)/shard_map/ppermute | solution.py:28
  21.2 11.1 %collective-permute-start.7 = (f32[256,256]{1,0:T(8,128)S(1)}, f32[256,256]{1,0:T(8,128)S(1)}, u32[]{:S(2)}, u32[]{:S(2)}) collective-permute-start(f32[256,256]{1,0:T(8,128)S(1)} %add.45), channel_id=1, source_target_pairs={{0,48},{8,56},{16,0},{24,8},{32,16},{40,24},{48,32},{56,40},{64,11... | collective-permute-start | bytes 786440 | tf_op jit(solution)/shard_map/ppermute | solution.py:28
  33.0 5.6 %collective-permute-start.10 = (f32[32,512]{1,0:T(8,128)S(1)}, f32[32,512]{1,0:T(8,128)S(1)}, u32[]{:S(2)}, u32[]{:S(2)}) collective-permute-start(f32[32,512]{1,0:T(8,128)S(1)} %get-tuple-element.59), channel_id=1, source_target_pairs={{0,192},{8,200},{16,208},{24,216},{32,224},{40,232},{48,240},{56,2... | collective-permute-start | bytes 196616 | tf_op jit(solution)/shard_map/ppermute | solution.py:28
  37.2 6.0 %collective-permute-start.8 = (f32[32,512]{1,0:T(8,128)S(1)}, f32[32,512]{1,0:T(8,128)S(1)}, u32[]{:S(2)}, u32[]{:S(2)}) collective-permute-start(f32[32,512]{1,0:T(8,128)S(1)} %get-tuple-element.57), channel_id=1, source_target_pairs={{0,64},{8,72},{16,80},{24,88},{32,96},{40,104},{48,112},{56,120},{... | collective-permute-start | bytes 196616 | tf_op jit(solution)/shard_map/ppermute | solution.py:28
  38.6 8.0 %collective-permute-start.11 = (f32[64,512]{1,0:T(8,128)S(1)}, f32[64,512]{1,0:T(8,128)S(1)}, u32[]{:S(2)}, u32[]{:S(2)}) collective-permute-start(f32[64,512]{1,0:T(8,128)S(1)} %pad_add_fusion), channel_id=1, source_target_pairs={{0,192},{8,200},{16,208},{24,216},{32,224},{40,232},{48,240},{56,2... | collective-permute-start | bytes 393224 | tf_op jit(solution)/shard_map/ppermute | solution.py:28
  43.3 7.2 %collective-permute-start.9 = (f32[64,512]{1,0:T(8,128)S(1)}, f32[64,512]{1,0:T(8,128)S(1)}, u32[]{:S(2)}, u32[]{:S(2)}) collective-permute-start(f32[64,512]{1,0:T(8,128)S(1)} %pad_add_fusion.1), channel_id=1, source_target_pairs={{0,64},{8,72},{16,80},{24,88},{32,96},{40,104},{48,112},{56,120},{... | collective-permute-start | bytes 393224 | tf_op jit(solution)/shard_map/ppermute | solution.py:28
  50.5 6.7 %collective-permute-start.14 = (f32[64,512]{1,0:T(8,128)S(1)}, f32[64,512]{1,0:T(8,128)S(1)}, u32[]{:S(2)}, u32[]{:S(2)}) collective-permute-start(f32[64,512]{1,0:T(8,128)S(1)} %add_add_fusion.unit), channel_id=1, source_target_pairs={{0,64},{8,72},{16,80},{24,88},{32,96},{40,104},{48,112},{56,120},{... | collective-permute-start | bytes 393224 | tf_op jit(solution)/shard_map/ppermute | solution.py:28
  50.6 6.6 %collective-permute-start.15 = (f32[64,512]{1,0:T(8,128)S(1)}, f32[64,512]{1,0:T(8,128)S(1)}, u32[]{:S(2)}, u32[]{:S(2)}) collective-permute-start(f32[64,512]{1,0:T(8,128)S(1)} %add_add_fusion.unit), channel_id=1, source_target_pairs={{0,192},{8,200},{16,208},{24,216},{32,224},{40,232},{48,240},{56,2... | collective-permute-start | bytes 393224 | tf_op jit(solution)/shard_map/ppermute | solution.py:28
  54.2 5.4 %collective-permute-start.13 = (f32[64,512]{1,0:T(8,128)S(1)}, f32[64,512]{1,0:T(8,128)S(1)}, u32[]{:S(2)}, u32[]{:S(2)}) collective-permute-start(f32[64,512]{1,0:T(8,128)S(1)} %add_add_fusion.unit), channel_id=1, source_target_pairs={{0,32},{8,40},{16,48},{24,56},{32,0},{40,8},{48,16},{56,24},{64,96... | collective-permute-start | bytes 393224 | tf_op jit(solution)/shard_map/ppermute | solution.py:28
  57.2 5.3 %collective-permute-start.12 = (f32[64,512]{1,0:T(8,128)S(1)}, f32[64,512]{1,0:T(8,128)S(1)}, u32[]{:S(2)}, u32[]{:S(2)}) collective-permute-start(f32[64,512]{1,0:T(8,128)S(1)} %add_add_fusion.unit), channel_id=1, source_target_pairs={{0,16},{8,24},{16,32},{24,40},{32,48},{40,56},{48,0},{56,8},{64,80... | collective-permute-start | bytes 393224 | tf_op jit(solution)/shard_map/ppermute | solution.py:28
  57.2 7.6 %collective-permute-start.16 = (f32[64,512]{1,0:T(8,128)S(1)}, f32[64,512]{1,0:T(8,128)S(1)}, u32[]{:S(2)}, u32[]{:S(2)}) collective-permute-start(f32[64,512]{1,0:T(8,128)S(1)} %collective-permute-done.14.z1), channel_id=1, source_target_pairs={{0,64},{8,72},{16,80},{24,88},{32,96},{40,104},{48,112},{56,120},{... | collective-permute-start | bytes 393224 | tf_op jit(solution)/shard_map/ppermute | solution.py:28
  66.1 33.5 %copy-start.15 = (f32[256,512]{1,0:T(8,128)}, f32[256,512]{1,0:T(8,128)S(1)}, u32[]{:S(2)}) copy-start(f32[256,512]{1,0:T(8,128)S(1)} %get-tuple-element.64.m0) | copy-start | bytes 1572868
  66.1 6.9 %collective-permute-start.17 = (f32[8,3,8,128]{3,2,1,0:T(8,128)S(1)}, f32[8,3,8,128]{3,2,1,0:T(8,128)S(1)}, u32[]{:S(2)}, u32[]{:S(2)}) collective-permute-start(f32[8,3,8,128]{3,2,1,0:T(8,128)S(1)} %get-tuple-element.63), channel_id=1, source_target_pairs={{0,8},{8,0},{16,24},{24,16},{32,40},{40,32},{48,56},{56,48},{64,72... | collective-permute-start | bytes 294920 | tf_op jit(solution)/shard_map/ppermute | solution.py:28
  73.7 9.5 %all-to-all-start = ((f32[8,3,8,128]{3,2,1,0:T(8,128)}), f32[8,3,8,128]{3,2,1,0:T(8,128)S(1)}, u32[]{:S(2)}, u32[]{:S(2)}) async-start(f32[8,3,8,128]{3,2,1,0:T(8,128)} %add.50), calls=%async_computation | async-start | bytes 196608 | tf_op jit(solution)/shard_map/all_to_all | solution.py:47
  77.9 15.3 %collective-permute-start.19 = (f32[256,512]{1,0:T(8,128)S(1)}, f32[256,512]{1,0:T(8,128)S(1)}, u32[]{:S(2)}, u32[]{:S(2)}) collective-permute-start(f32[256,512]{1,0:T(8,128)S(1)} %get-tuple-element.64.m0), channel_id=1, source_target_pairs={{0,48},{8,56},{16,0},{24,8},{32,16},{40,24},{48,32},{56,40},{64,11... | collective-permute-start | bytes 1572872 | tf_op jit(solution)/shard_map/ppermute | solution.py:28
  82.6 14.0 %collective-permute-start.18 = (f32[256,512]{1,0:T(8,128)S(1)}, f32[256,512]{1,0:T(8,128)S(1)}, u32[]{:S(2)}, u32[]{:S(2)}) collective-permute-start(f32[256,512]{1,0:T(8,128)S(1)} %get-tuple-element.64.m0), channel_id=1, source_target_pairs={{0,16},{8,24},{16,32},{24,40},{32,48},{40,56},{48,0},{56,8},{64,80... | collective-permute-start | bytes 1572872 | tf_op jit(solution)/shard_map/ppermute | solution.py:28
  83.9 15.7 %all-to-all-start.1 = ((f32[16,3,8,128]{3,2,1,0:T(8,128)}), f32[16,3,8,128]{3,2,1,0:T(8,128)S(1)}, u32[]{:S(2)}, u32[]{:S(2)}) async-start(f32[16,3,8,128]{3,2,1,0:T(8,128)} %spread.2), calls=%async_computation.1 | async-start | bytes 393216 | tf_op jit(solution)/shard_map/all_to_all | solution.py:47
  102.4 8.1 %copy-start.3 = (bf16[512,1024]{1,0:T(8,128)(2,1)S(1)}, bf16[512,1024]{1,0:T(8,128)(2,1)}, u32[]{:S(2)}) copy-start(bf16[512,1024]{1,0:T(8,128)(2,1)} %acts.8) | copy-start | bytes 3145732
  102.4 8.1 %copy-start.9 = (f32[1024,64]{0,1:T(8,128)S(1)}, f32[1024,64]{0,1:T(8,128)}, u32[]{:S(2)}) copy-start(f32[1024,64]{0,1:T(8,128)} %param.9) | copy-start | bytes 786436
  102.4 21.7 %all-to-all-start.2 = ((f32[8,16,3,8,128]{4,3,2,1,0:T(8,128)}), f32[8,16,3,8,128]{4,3,2,1,0:T(8,128)}, u32[]{:S(2)}, u32[]{:S(2)}) async-start(f32[8,16,3,8,128]{4,3,2,1,0:T(8,128)} %spread.3), calls=%async_computation.2 | async-start | bytes 3145728 | tf_op jit(solution)/shard_map/all_to_all | solution.py:47
  109.0 7.7 %collective-permute-start.21 = (f32[128,512]{1,0:T(8,128)S(1)}, f32[128,512]{1,0:T(8,128)S(1)}, u32[]{:S(2)}, u32[]{:S(2)}) collective-permute-start(f32[128,512]{1,0:T(8,128)S(1)} %slice.7), channel_id=1, source_target_pairs={{0,48},{8,56},{16,0},{24,8},{32,16},{40,24},{48,32},{56,40},{64,11... | collective-permute-start | bytes 786440 | tf_op jit(solution)/shard_map/ppermute | solution.py:28
  109.9 7.5 %collective-permute-start.20 = (f32[128,512]{1,0:T(8,128)S(1)}, f32[128,512]{1,0:T(8,128)S(1)}, u32[]{:S(2)}, u32[]{:S(2)}) collective-permute-start(f32[128,512]{1,0:T(8,128)S(1)} %slice.6), channel_id=1, source_target_pairs={{0,16},{8,24},{16,32},{24,40},{32,48},{40,56},{48,0},{56,8},{64,80... | collective-permute-start | bytes 786440 | tf_op jit(solution)/shard_map/ppermute | solution.py:28
  124.1 30.1 %copy-start.8 = (bf16[1024,1024]{1,0:T(8,128)(2,1)S(1)}, bf16[1024,1024]{1,0:T(8,128)(2,1)}, u32[]{:S(2)}) copy-start(bf16[1024,1024]{1,0:T(8,128)(2,1)} %mom.1) | copy-start | bytes 6291460
  124.1 7.5 %collective-permute-start.22 = (f32[8,16,3,8,128]{4,3,2,1,0:T(8,128)}, f32[8,16,3,8,128]{4,3,2,1,0:T(8,128)S(1)}, u32[]{:S(2)}, u32[]{:S(2)}) collective-permute-start(f32[8,16,3,8,128]{4,3,2,1,0:T(8,128)} %all-to-all-done.2.own_ref), channel_id=1, source_target_pairs={{0,8},{8,0},{16,24},{24,16},{32,40},{40,32},{48,56},{56,48},{64,72... | collective-permute-start | bytes 4718600 | tf_op jit(solution)/shard_map/ppermute | solution.py:28
  137.7 16.5 %copy-start.7 = (f32[1024,1024]{1,0:T(8,128)S(1)}, f32[1024,1024]{1,0:T(8,128)}, u32[]{:S(2)}) copy-start(f32[1024,1024]{1,0:T(8,128)} %copy-done.6) | copy-start | bytes 12582916
  152.7 1.4 collective-permute-start.23
  (19 other events, 34.6 us)

commit v9 on v7

--- a/solution.py
+++ b/solution.py
@@ -17,8 +17,6 @@
 VMEM = pl.BlockSpec(memory_space=pltpu.VMEM)
 SMEM = pl.BlockSpec(memory_space=pltpu.SMEM)
 
-ZY_GROUPS = [[z * 8 + y * 2 + c for z in range(4) for y in range(4)] for c in range(2)]
-
 
 def dp_shift(x, dz=0, dy=0, dc=0):
     pairs = []
@@ -43,8 +41,8 @@
     return on, back
 
 
-def exchange(x, groups, axis="dp"):
-    return lax.all_to_all(x, axis, 0, 0, axis_index_groups=groups)
+def exchange(x, axis):
+    return lax.all_to_all(x, axis, 0, 0)
 
 
 def params(mib, **more):
@@ -166,24 +164,49 @@
     )(pos, *parts)
 
 
-def spread_kernel(leading, x_ref, copies_ref):
-    total = x_ref[0] if leading else x_ref[...]
-    for i in range(1, x_ref.shape[0] if leading else 1):
-        total = total + x_ref[i]
-    for i in range(copies_ref.shape[0]):
-        copies_ref[i] = total
-
-
-def spread(x, copies, leading=False, grant=10):
-    return pl.pallas_call(
-        functools.partial(spread_kernel, leading),
-        out_shape=jax.ShapeDtypeStruct((copies,) + x.shape[leading:], F32),
-        in_specs=[VMEM],
+RING = (0, 3, 1, 2)
+
+
+def order_kernel(pos_ref, *refs):
+    for turn, ref in zip(RING, refs):
+        refs[-1][(pos_ref[2] + turn) % 4] = ref[...]
+
+
+def order(pos, pieces):
+    return pl.pallas_call(
+        order_kernel,
+        out_shape=jax.ShapeDtypeStruct((4,) + pieces[0].shape, F32),
+        in_specs=[SMEM] + [VMEM] * 4,
         out_specs=VMEM,
-        compiler_params=params(grant),
-        cost_estimate=cost(1 << 17, 1 << 20),
+        compiler_params=params(10),
+        cost_estimate=cost(1 << 14, 1 << 17),
+        name="order",
+    )(pos, *pieces)
+
+
+def spread_kernel(pos_ref, a, b, c, d, out, whole, sems):
+    for turn, ref in zip(RING, (a, b, c, d)):
+        for z in range(4):
+            whole[z, (pos_ref[1] + turn) % 4] = ref[z]
+    copies = [pltpu.make_async_copy(whole, out.at[i], sems.at[i]) for i in range(8)]
+    for copy in copies:
+        copy.start()
+    for copy in copies:
+        copy.wait()
+
+
+def spread(pos, pieces):
+    shape = (4,) + pieces[0].shape
+    return pl.pallas_call(
+        spread_kernel,
+        out_shape=jax.ShapeDtypeStruct((8,) + shape, F32),
+        in_specs=[SMEM] + [VMEM] * 4,
+        out_specs=pl.BlockSpec(memory_space=pl.ANY),
+        scratch_shapes=[pltpu.VMEM(shape, F32), pltpu.SemaphoreType.DMA((8,))],
+        compiler_params=params(10),
+        cost_estimate=cost(1 << 17, 2 << 20),
         name="spread",
-    )(x)
+    )(pos, *pieces)
 
 
 def block_kernel(pos_ref, unit, u1, u2, z1, z3, z2, sent_ref, mine_ref, of_y):
@@ -444,12 +467,12 @@
     to_core, of_y = lax.optimization_barrier((to_core, of_y))
     part = part + dp_shift(to_core, dc=1)
     m1, m3 = dp_shift(of_y, dy=1), dp_shift(of_y, dy=-1)
-    copies = spread(exchange(part, None, "shard"), 16, leading=True)
-    copies, m1, m3 = lax.optimization_barrier((copies, m1, m3))
-    part = exchange(copies, ZY_GROUPS)
-    part, m1, m3, args, q_t = lax.optimization_barrier((part, m1, m3, args, q_start.T))
+    part = exchange(part, "shard").sum(axis=0)
+    part = order(pos, [part] + [dp_shift(part, dz=d) for d in (1, -1, 2)])
+    near = [part] + [dp_shift(part, dy=d) for d in (1, -1, 2)]
+    near, m1, m3, args, q_t = lax.optimization_barrier((near, m1, m3, args, q_start.T))
     m2_top, m2_end = dp_shift(m1[:128], dy=1), dp_shift(m3[128:], dy=-1)
-    part = exchange(spread(part, 8, grant=58), None, "shard")
+    part = exchange(spread(pos, near).reshape(8, 16, 3, 8, 128), "shard")
     part, m2_top, m2_end, merged, q_parts = lax.optimization_barrier(
         (part, m2_top, m2_end, *merge_all(*args, q_t))
     )

time: 155 us -> 157 us (1.013)
  blocking collectives: 25.6 us -> 11.7 us
  starting transfers between devices: 45.9 us -> 53.7 us
  waiting for transfers between devices: 39.4 us -> 46 us
    all_to_all x2 -> x1, blocking collectives: 25.6 us -> 11.7 us  [exchange(): return lax.all_to_all(x, axis, 0, 0)]
    ppermute x24 -> x30, waiting for transfers between devices: 33.3 us -> 41.2 us  [dp_shift(): return lax.ppermute(x, 'dp', pairs)]
    ppermute x24 -> x30, starting transfers between devices: 41.3 us -> 49.1 us  [dp_shift(): return lax.ppermute(x, 'dp', pairs)]
    unnamed x38 -> x48, local copies, waits for them, and re-layouts: 10.4 us -> 11.7 us
  transfers between devices with their start and end apart: 25 -> 31, of which waited for: 15 -> 20; matrix products, arithmetic and copies ran while one was open for 1% -> 1% of each run, Pallas kernels for 4% -> 4%
where the time goes in v9:
time: 157 us; the launch traced here: 156 us
  starting transfers between devices  53.7 us (34%)
  waiting for transfers between devices  46 us (29%)
  Pallas kernels  30.1 us (19%)
  local copies, waits for them, and re-layouts  13.6 us (9%)
  blocking collectives  11.7 us (7%)
    ppermute x30, starting transfers between devices, dp_shift(): return lax.ppermute(x, 'dp', pairs)  49.1 us
    ppermute x30, waiting for transfers between devices, dp_shift(): return lax.ppermute(x, 'dp', pairs)  41.2 us
    pallas_call x1, Pallas kernels, iterate(): pl.pallas_call(iterate_kernel, out_shape=(jax.ShapeDtypeStruct((n, k), F3...  13.6 us
    all_to_all x1, blocking collectives, exchange(): return lax.all_to_all(x, axis, 0, 0)  11.7 us
    unnamed x48, local copies, waits for them, and re-layouts  11.7 us
    all_to_all x1, waiting for transfers between devices, exchange(): return lax.all_to_all(x, axis, 0, 0)  4.83 us
    all_to_all x1, starting transfers between devices, exchange(): return lax.all_to_all(x, axis, 0, 0)  4.56 us
    pallas_call x4, Pallas kernels, merge(): pl.pallas_call(functools.partial(merge_kernel, turns, own), out_shape=out...  4.3 us
  transfers between devices with their start and end apart: 31, of which 20 were waited for; matrix products, arithmetic and copies ran while one was open for 1% of the time, Pallas kernels for 4%

profile of v9, /device:TPU:1, one launch (start us, length us, event | category | flops | bytes accessed | tf_op | source)
XLA Modules:
  0.0 156.4 jit_solution(11140439744293895045)
XLA Ops:
  0.7 1.6 %copy-done = bf16[1,1024,1024]{2,1,0:T(8,128)(2,1)S(1)} copy-done((bf16[1,1024,1024]{2,1,0:T(8,128)(2,1)S(1)}, bf16[1,1024,1024]{2,1,0:T(8,128)(2,1)}, u32[]{:S(2)}) %copy-start) | copy-done | bytes 2097176
  5.7 3.3 %collective-permute-start = (f32[1,512,256]{2,1,0:T(8,128)S(1)}, f32[1,512,256]{2,1,0:T(8,128)S(1)}, u32[]{:S(2)}, u32[]{:S(2)}) collective-permute-start(f32[1,512,256]{2,1,0:T(8,128)S(1)} %merge.4), channel_id=1, source_target_pairs={{0,8},{8,0},{16,24},{24,16},{32,40},{40,32},{48,56},{56,48},{64,72... | collective-permute-start | bytes 1572872 | tf_op jit(solution)/shard_map/ppermute | solution.py:26
  12.0 2.7 %collective-permute-start.6 = (f32[256,256]{1,0:T(8,128)S(1)}, f32[256,256]{1,0:T(8,128)S(1)}, u32[]{:S(2)}, u32[]{:S(2)}) collective-permute-start(f32[256,256]{1,0:T(8,128)S(1)} %get-tuple-element.57), channel_id=1, source_target_pairs={{0,48},{8,56},{16,0},{24,8},{32,16},{40,24},{48,32},{56,40},{64,11... | collective-permute-start | bytes 786440 | tf_op jit(solution)/shard_map/ppermute | solution.py:26
  17.4 3.5 %collective-permute-done.4 = f32[256,256]{1,0:T(8,128)S(1)} collective-permute-done((f32[256,256]{1,0:T(8,128)S(1)}, f32[256,256]{1,0:T(8,128)S(1)}, u32[]{:S(2)}, u32[]{:S(2)}) %collective-permute-start.4) | collective-permute-done | bytes 262176 | tf_op jit(solution)/shard_map/ppermute | solution.py:26
  21.1 2.7 %collective-permute-start.7 = (f32[256,256]{1,0:T(8,128)S(1)}, f32[256,256]{1,0:T(8,128)S(1)}, u32[]{:S(2)}, u32[]{:S(2)}) collective-permute-start(f32[256,256]{1,0:T(8,128)S(1)} %add.45), channel_id=1, source_target_pairs={{0,48},{8,56},{16,0},{24,8},{32,16},{40,24},{48,32},{56,40},{64,11... | collective-permute-start | bytes 786440 | tf_op jit(solution)/shard_map/ppermute | solution.py:26
  23.9 1.7 %collective-permute-done.2 = f32[256,256]{1,0:T(8,128)S(1)} collective-permute-done((f32[256,256]{1,0:T(8,128)S(1)}, f32[256,256]{1,0:T(8,128)S(1)}, u32[]{:S(2)}, u32[]{:S(2)}) %collective-permute-start.2) | collective-permute-done | bytes 262176 | tf_op jit(solution)/shard_map/ppermute | solution.py:26
  26.6 5.6 %collective-permute-done.5.on = f32[256,256]{1,0:T(8,128)S(1)} collective-permute-done((f32[256,256]{1,0:T(8,128)S(1)}, f32[256,256]{1,0:T(8,128)S(1)}, u32[]{:S(2)}, u32[]{:S(2)}) %collective-permute-start.5) | collective-permute-done | bytes 262176 | tf_op jit(solution)/shard_map/ppermute | solution.py:26
  33.0 4.2 %collective-permute-start.10 = (f32[32,512]{1,0:T(8,128)S(1)}, f32[32,512]{1,0:T(8,128)S(1)}, u32[]{:S(2)}, u32[]{:S(2)}) collective-permute-start(f32[32,512]{1,0:T(8,128)S(1)} %get-tuple-element.62), channel_id=1, source_target_pairs={{0,192},{8,200},{16,208},{24,216},{32,224},{40,232},{48,240},{56,2... | collective-permute-start | bytes 196616 | tf_op jit(solution)/shard_map/ppermute | solution.py:26
  38.6 4.7 %collective-permute-start.11 = (f32[64,512]{1,0:T(8,128)S(1)}, f32[64,512]{1,0:T(8,128)S(1)}, u32[]{:S(2)}, u32[]{:S(2)}) collective-permute-start(f32[64,512]{1,0:T(8,128)S(1)} %pad_add_fusion), channel_id=1, source_target_pairs={{0,192},{8,200},{16,208},{24,216},{32,224},{40,232},{48,240},{56,2... | collective-permute-start | bytes 393224 | tf_op jit(solution)/shard_map/ppermute | solution.py:26
  43.4 3.2 %collective-permute-done.11 = f32[64,512]{1,0:T(8,128)S(1)} collective-permute-done((f32[64,512]{1,0:T(8,128)S(1)}, f32[64,512]{1,0:T(8,128)S(1)}, u32[]{:S(2)}, u32[]{:S(2)}) %collective-permute-start.11) | collective-permute-done | bytes 131104 | tf_op jit(solution)/shard_map/ppermute | solution.py:26
  46.6 3.9 %collective-permute-done.9 = f32[64,512]{1,0:T(8,128)S(1)} collective-permute-done((f32[64,512]{1,0:T(8,128)S(1)}, f32[64,512]{1,0:T(8,128)S(1)}, u32[]{:S(2)}, u32[]{:S(2)}) %collective-permute-start.9) | collective-permute-done | bytes 131104 | tf_op jit(solution)/shard_map/ppermute | solution.py:26
  50.6 3.6 %collective-permute-start.15 = (f32[64,512]{1,0:T(8,128)S(1)}, f32[64,512]{1,0:T(8,128)S(1)}, u32[]{:S(2)}, u32[]{:S(2)}) collective-permute-start(f32[64,512]{1,0:T(8,128)S(1)} %add_add_fusion.unit), channel_id=1, source_target_pairs={{0,192},{8,200},{16,208},{24,216},{32,224},{40,232},{48,240},{56,2... | collective-permute-start | bytes 393224 | tf_op jit(solution)/shard_map/ppermute | solution.py:26
  54.2 3.0 %collective-permute-start.13 = (f32[64,512]{1,0:T(8,128)S(1)}, f32[64,512]{1,0:T(8,128)S(1)}, u32[]{:S(2)}, u32[]{:S(2)}) collective-permute-start(f32[64,512]{1,0:T(8,128)S(1)} %add_add_fusion.unit), channel_id=1, source_target_pairs={{0,32},{8,40},{16,48},{24,56},{32,0},{40,8},{48,16},{56,24},{64,96... | collective-permute-start | bytes 393224 | tf_op jit(solution)/shard_map/ppermute | solution.py:26
  57.2 2.3 %collective-permute-done.13.u2 = f32[64,512]{1,0:T(8,128)S(1)} collective-permute-done((f32[64,512]{1,0:T(8,128)S(1)}, f32[64,512]{1,0:T(8,128)S(1)}, u32[]{:S(2)}, u32[]{:S(2)}) %collective-permute-start.13) | collective-permute-done | bytes 131104 | tf_op jit(solution)/shard_map/ppermute | solution.py:26
  59.6 3.0 %collective-permute-done.12.u1 = f32[64,512]{1,0:T(8,128)S(1)} collective-permute-done((f32[64,512]{1,0:T(8,128)S(1)}, f32[64,512]{1,0:T(8,128)S(1)}, u32[]{:S(2)}, u32[]{:S(2)}) %collective-permute-start.12) | collective-permute-done | bytes 131104 | tf_op jit(solution)/shard_map/ppermute | solution.py:26
  62.5 2.2 %collective-permute-done.16.z2 = f32[64,512]{1,0:T(8,128)S(1)} collective-permute-done((f32[64,512]{1,0:T(8,128)S(1)}, f32[64,512]{1,0:T(8,128)S(1)}, u32[]{:S(2)}, u32[]{:S(2)}) %collective-permute-start.16) | collective-permute-done | bytes 131104 | tf_op jit(solution)/shard_map/ppermute | solution.py:26
  66.1 2.4 %collective-permute-start.25 = (f32[256,512]{1,0:T(8,128)S(1)}, f32[256,512]{1,0:T(8,128)S(1)}, u32[]{:S(2)}, u32[]{:S(2)}) collective-permute-start(f32[256,512]{1,0:T(8,128)S(1)} %get-tuple-element.67.m0), channel_id=1, source_target_pairs={{0,48},{8,56},{16,0},{24,8},{32,16},{40,24},{48,32},{56,40},{64,11... | collective-permute-start | bytes 1572872 | tf_op jit(solution)/shard_map/ppermute | solution.py:26
  68.5 6.3 %collective-permute-start.17 = (f32[8,3,8,128]{3,2,1,0:T(8,128)S(1)}, f32[8,3,8,128]{3,2,1,0:T(8,128)S(1)}, u32[]{:S(2)}, u32[]{:S(2)}) collective-permute-start(f32[8,3,8,128]{3,2,1,0:T(8,128)S(1)} %get-tuple-element.66), channel_id=1, source_target_pairs={{0,8},{8,0},{16,24},{24,16},{32,40},{40,32},{48,56},{56,48},{64,72... | collective-permute-start | bytes 294920 | tf_op jit(solution)/shard_map/ppermute | solution.py:26
  75.7 11.7 %all_to_all.10 = f32[8,3,8,128]{3,2,1,0:T(8,128)S(1)} all-to-all(f32[8,3,8,128]{3,2,1,0:T(8,128)S(1)} %add.50), channel_id=1, replica_groups=mesh['dp'=32,'shard'=8] {'shard'}, dimensions={0} | all-to-all | bytes 196608 | tf_op jit(solution)/shard_map/all_to_all | solution.py:45
  87.5 1.6 %collective-permute-start.19 = (f32[3,8,128]{2,1,0:T(8,128)S(1)}, f32[3,8,128]{2,1,0:T(8,128)S(1)}, u32[]{:S(2)}, u32[]{:S(2)}) collective-permute-start(f32[3,8,128]{2,1,0:T(8,128)S(1)} %reduce_sum.9.refs_0_), channel_id=1, source_target_pairs={{0,192},{8,200},{16,208},{24,216},{32,224},{40,232},{48,240},{56,2... | collective-permute-start | bytes 36872 | tf_op jit(solution)/shard_map/ppermute | solution.py:26
  89.9 4.0 %collective-permute-done.20.refs_3_ = f32[3,8,128]{2,1,0:T(8,128)S(1)} collective-permute-done((f32[3,8,128]{2,1,0:T(8,128)S(1)}, f32[3,8,128]{2,1,0:T(8,128)S(1)}, u32[]{:S(2)}, u32[]{:S(2)}) %collective-permute-start.20) | collective-permute-done | bytes 12320 | tf_op jit(solution)/shard_map/ppermute | solution.py:26
  96.1 1.8 %collective-permute-start.22 = (f32[4,3,8,128]{3,2,1,0:T(8,128)S(1)}, f32[4,3,8,128]{3,2,1,0:T(8,128)S(1)}, u32[]{:S(2)}, u32[]{:S(2)}) collective-permute-start(f32[4,3,8,128]{3,2,1,0:T(8,128)S(1)} %order.1.a), channel_id=1, source_target_pairs={{0,48},{8,56},{16,0},{24,8},{32,16},{40,24},{48,32},{56,40},{64,11... | collective-permute-start | bytes 147464 | tf_op jit(solution)/shard_map/ppermute | solution.py:26
  100.4 1.7 %collective-permute-done.21.b = f32[4,3,8,128]{3,2,1,0:T(8,128)S(1)} collective-permute-done((f32[4,3,8,128]{3,2,1,0:T(8,128)S(1)}, f32[4,3,8,128]{3,2,1,0:T(8,128)S(1)}, u32[]{:S(2)}, u32[]{:S(2)}) %collective-permute-start.21) | collective-permute-done | bytes 49184 | tf_op jit(solution)/shard_map/ppermute | solution.py:26
  102.1 2.7 %spread.1 = f32[8,4,4,3,8,128]{5,4,3,2,1,0:T(8,128)S(1)} custom-call(s32[3]{0:T(128)S(1)} %pad_add_fusion.2.pos_ref, f32[4,3,8,128]{3,2,1,0:T(8,128)S(1)} %order.1.a, f32[4,3,8,128]{3,2,1,0:T(8,128)S(1)} %collective-permute-done.21.b, f32[4,3,8,128]{3,2,1,0:T(8,128)S(1)} %collective-permute-done.22.c, f32[4,3,8,128]{3,2,1,0:T(8,128)S(1)} %collective-permute-done.23.d), custom_call_target="tpu_custom_call" | custom-call | flops 131072 | bytes 2097152 | tf_op jit(solution)/shard_map/spread/pallas_call | solution.py:200
  106.0 4.6 %all-to-all-start.1 = ((f32[8,16,3,8,128]{4,3,2,1,0:T(8,128)}), f32[8,16,3,8,128]{4,3,2,1,0:T(8,128)}, u32[]{:S(2)}, u32[]{:S(2)}) async-start(f32[8,16,3,8,128]{4,3,2,1,0:T(8,128)} %bitcast.6), calls=%async_computation.1 | async-start | bytes 3145728 | tf_op jit(solution)/shard_map/all_to_all | solution.py:45
  115.2 2.1 %merge_all.1 = (f32[1024,1024]{1,0:T(8,128)S(1)}, bf16[3,64,1024]{2,1,0:T(8,128)(2,1)S(1)}) custom-call(bf16[512,1024]{1,0:T(8,128)(2,1)S(1)} %copy-done.3, bf16[512,1024]{1,0:T(8,128)(2,1)S(1)} %copy-done.5, bf16[1,1024,1024]{2,1,0:T(8,128)(2,1)S(1)} %copy-done.1, f32[64,1024]{1,0:T(8,128)S(1)} %bitcast.7), custom_call_target="tpu_custom_call" | custom-call | flops 1073741824 | bytes 8388608 | tf_op jit(solution)/shard_map/merge_all/pallas_call | solution.py:118
  117.4 2.0 %copy-done.7 = f32[1024,1024]{1,0:T(8,128)} copy-done((f32[1024,1024]{1,0:T(8,128)}, f32[1024,1024]{1,0:T(8,128)S(1)}, u32[]{:S(2)}) %copy-start.7) | copy-done | bytes 4194328
  121.6 4.8 %all-to-all-done.1.own_ref = f32[8,16,3,8,128]{4,3,2,1,0:T(8,128)} async-done(((f32[8,16,3,8,128]{4,3,2,1,0:T(8,128)}), f32[8,16,3,8,128]{4,3,2,1,0:T(8,128)}, u32[]{:S(2)}, u32[]{:S(2)}) %all-to-all-start.1) | async-done | bytes 1572896 | tf_op jit(solution)/shard_map/all_to_all | solution.py:45
  126.4 5.8 %collective-permute-start.28 = (f32[8,16,3,8,128]{4,3,2,1,0:T(8,128)}, f32[8,16,3,8,128]{4,3,2,1,0:T(8,128)S(1)}, u32[]{:S(2)}, u32[]{:S(2)}) collective-permute-start(f32[8,16,3,8,128]{4,3,2,1,0:T(8,128)} %all-to-all-done.1.own_ref), channel_id=1, source_target_pairs={{0,8},{8,0},{16,24},{24,16},{32,40},{40,32},{48,56},{56,48},{64,72... | collective-permute-start | bytes 4718600 | tf_op jit(solution)/shard_map/ppermute | solution.py:26
  132.2 3.2 %collective-permute-done.28.away_ref = f32[8,16,3,8,128]{4,3,2,1,0:T(8,128)S(1)} collective-permute-done((f32[8,16,3,8,128]{4,3,2,1,0:T(8,128)}, f32[8,16,3,8,128]{4,3,2,1,0:T(8,128)S(1)}, u32[]{:S(2)}, u32[]{:S(2)}) %collective-permute-start.28) | collective-permute-done | bytes 1572896 | tf_op jit(solution)/shard_map/ppermute | solution.py:26
  136.5 13.6 %iterations.1 = (f32[64,1024]{1,0:T(8,128)}, f32[64,1024]{1,0:T(8,128)S(1)}) custom-call(s32[3]{0:T(128)S(1)} %pad_add_fusion.2.pos_ref, f32[8,16,3,8,128]{4,3,2,1,0:T(8,128)} %all-to-all-done.1.own_ref, f32[8,16,3,8,128]{4,3,2,1,0:T(8,128)S(1)} %collective-permute-done.28.away_ref, bf16[3,64,1024]{2,1,0:T(8,128)(2,1)S(1)} %copy-done.23), custom_call_target="tpu_custom_call" | custom-call | flops 2415919104 | bytes 4194304 | tf_op jit(solution)/shard_map/iterations/pallas_call | solution.py:354
  152.7 3.7 %finish.1 = (bf16[1,1024,1024]{2,1,0:T(8,128)(2,1)}, bf16[1024,1024]{1,0:T(8,128)(2,1)}) custom-call(s32[3]{0:T(128)S(1)} %pad_add_fusion.2.pos_ref, f32[1024,1024]{1,0:T(8,128)S(1)} %copy-done.8, bf16[1024,1024]{1,0:T(8,128)(2,1)S(1)} %copy-done.9, f32[64,512]{1,0:T(8,128)S(1)} %left.1.own, f32[64,512]{1,0:T(8,128)S(1)} %collective-permute-done.29.away, ...), custom_call_target="tpu_custom_call" | custom-call | flops 536870912 | bytes 12582912 | tf_op jit(solution)/shard_map/finish/pallas_call | solution.py:421
  (103 shorter events, 32.3 us)
Async XLA Ops:
  5.7 4.9 %collective-permute-start = (f32[1,512,256]{2,1,0:T(8,128)S(1)}, f32[1,512,256]{2,1,0:T(8,128)S(1)}, u32[]{:S(2)}, u32[]{:S(2)}) collective-permute-start(f32[1,512,256]{2,1,0:T(8,128)S(1)} %merge.4), channel_id=1, source_target_pairs={{0,8},{8,0},{16,24},{24,16},{32,40},{40,32},{48,56},{56,48},{64,72... | collective-permute-start | bytes 1572872 | tf_op jit(solution)/shard_map/ppermute | solution.py:26
  10.6 4.1 %collective-permute-start.1 = (f32[3,512,256]{2,1,0:T(8,128)S(1)}, f32[3,512,256]{2,1,0:T(8,128)S(1)}, u32[]{:S(2)}, u32[]{:S(2)}) collective-permute-start(f32[3,512,256]{2,1,0:T(8,128)S(1)} %merge.5), channel_id=1, source_target_pairs={{0,8},{8,0},{16,24},{24,16},{32,40},{40,32},{48,56},{56,48},{64,72... | collective-permute-start | bytes 4718600 | tf_op jit(solution)/shard_map/ppermute | solution.py:26
  11.9 9.1 %collective-permute-start.4 = (f32[256,256]{1,0:T(8,128)S(1)}, f32[256,256]{1,0:T(8,128)S(1)}, u32[]{:S(2)}, u32[]{:S(2)}) collective-permute-start(f32[256,256]{1,0:T(8,128)S(1)} %get-tuple-element.55), channel_id=1, source_target_pairs={{0,16},{8,24},{16,32},{24,40},{32,48},{40,56},{48,0},{56,8},{64,80... | collective-permute-start | bytes 786440 | tf_op jit(solution)/shard_map/ppermute | solution.py:26
  12.0 9.1 %collective-permute-start.6 = (f32[256,256]{1,0:T(8,128)S(1)}, f32[256,256]{1,0:T(8,128)S(1)}, u32[]{:S(2)}, u32[]{:S(2)}) collective-permute-start(f32[256,256]{1,0:T(8,128)S(1)} %get-tuple-element.57), channel_id=1, source_target_pairs={{0,48},{8,56},{16,0},{24,8},{32,16},{40,24},{48,32},{56,40},{64,11... | collective-permute-start | bytes 786440 | tf_op jit(solution)/shard_map/ppermute | solution.py:26
  15.9 9.6 %collective-permute-start.2 = (f32[256,256]{1,0:T(8,128)S(1)}, f32[256,256]{1,0:T(8,128)S(1)}, u32[]{:S(2)}, u32[]{:S(2)}) collective-permute-start(f32[256,256]{1,0:T(8,128)S(1)} %get-tuple-element.50), channel_id=1, source_target_pairs={{0,48},{8,56},{16,0},{24,8},{32,16},{40,24},{48,32},{56,40},{64,11... | collective-permute-start | bytes 786440 | tf_op jit(solution)/shard_map/ppermute | solution.py:26
  16.3 10.3 %collective-permute-start.3 = (f32[256,256]{1,0:T(8,128)S(1)}, f32[256,256]{1,0:T(8,128)S(1)}, u32[]{:S(2)}, u32[]{:S(2)}) collective-permute-start(f32[256,256]{1,0:T(8,128)S(1)} %get-tuple-element.52), channel_id=1, source_target_pairs={{0,16},{8,24},{16,32},{24,40},{32,48},{40,56},{48,0},{56,8},{64,80... | collective-permute-start | bytes 786440 | tf_op jit(solution)/shard_map/ppermute | solution.py:26
  21.0 11.2 %collective-permute-start.5 = (f32[256,256]{1,0:T(8,128)S(1)}, f32[256,256]{1,0:T(8,128)S(1)}, u32[]{:S(2)}, u32[]{:S(2)}) collective-permute-start(f32[256,256]{1,0:T(8,128)S(1)} %add.44), channel_id=1, source_target_pairs={{0,16},{8,24},{16,32},{24,40},{32,48},{40,56},{48,0},{56,8},{64,80... | collective-permute-start | bytes 786440 | tf_op jit(solution)/shard_map/ppermute | solution.py:26
  21.1 11.1 %collective-permute-start.7 = (f32[256,256]{1,0:T(8,128)S(1)}, f32[256,256]{1,0:T(8,128)S(1)}, u32[]{:S(2)}, u32[]{:S(2)}) collective-permute-start(f32[256,256]{1,0:T(8,128)S(1)} %add.45), channel_id=1, source_target_pairs={{0,48},{8,56},{16,0},{24,8},{32,16},{40,24},{48,32},{56,40},{64,11... | collective-permute-start | bytes 786440 | tf_op jit(solution)/shard_map/ppermute | solution.py:26
  33.0 5.6 %collective-permute-start.10 = (f32[32,512]{1,0:T(8,128)S(1)}, f32[32,512]{1,0:T(8,128)S(1)}, u32[]{:S(2)}, u32[]{:S(2)}) collective-permute-start(f32[32,512]{1,0:T(8,128)S(1)} %get-tuple-element.62), channel_id=1, source_target_pairs={{0,192},{8,200},{16,208},{24,216},{32,224},{40,232},{48,240},{56,2... | collective-permute-start | bytes 196616 | tf_op jit(solution)/shard_map/ppermute | solution.py:26
  37.2 6.0 %collective-permute-start.8 = (f32[32,512]{1,0:T(8,128)S(1)}, f32[32,512]{1,0:T(8,128)S(1)}, u32[]{:S(2)}, u32[]{:S(2)}) collective-permute-start(f32[32,512]{1,0:T(8,128)S(1)} %get-tuple-element.60), channel_id=1, source_target_pairs={{0,64},{8,72},{16,80},{24,88},{32,96},{40,104},{48,112},{56,120},{... | collective-permute-start | bytes 196616 | tf_op jit(solution)/shard_map/ppermute | solution.py:26
  38.6 8.0 %collective-permute-start.11 = (f32[64,512]{1,0:T(8,128)S(1)}, f32[64,512]{1,0:T(8,128)S(1)}, u32[]{:S(2)}, u32[]{:S(2)}) collective-permute-start(f32[64,512]{1,0:T(8,128)S(1)} %pad_add_fusion), channel_id=1, source_target_pairs={{0,192},{8,200},{16,208},{24,216},{32,224},{40,232},{48,240},{56,2... | collective-permute-start | bytes 393224 | tf_op jit(solution)/shard_map/ppermute | solution.py:26
  43.3 7.2 %collective-permute-start.9 = (f32[64,512]{1,0:T(8,128)S(1)}, f32[64,512]{1,0:T(8,128)S(1)}, u32[]{:S(2)}, u32[]{:S(2)}) collective-permute-start(f32[64,512]{1,0:T(8,128)S(1)} %pad_add_fusion.1), channel_id=1, source_target_pairs={{0,64},{8,72},{16,80},{24,88},{32,96},{40,104},{48,112},{56,120},{... | collective-permute-start | bytes 393224 | tf_op jit(solution)/shard_map/ppermute | solution.py:26
  50.5 6.7 %collective-permute-start.14 = (f32[64,512]{1,0:T(8,128)S(1)}, f32[64,512]{1,0:T(8,128)S(1)}, u32[]{:S(2)}, u32[]{:S(2)}) collective-permute-start(f32[64,512]{1,0:T(8,128)S(1)} %add_add_fusion.unit), channel_id=1, source_target_pairs={{0,64},{8,72},{16,80},{24,88},{32,96},{40,104},{48,112},{56,120},{... | collective-permute-start | bytes 393224 | tf_op jit(solution)/shard_map/ppermute | solution.py:26
  50.6 6.6 %collective-permute-start.15 = (f32[64,512]{1,0:T(8,128)S(1)}, f32[64,512]{1,0:T(8,128)S(1)}, u32[]{:S(2)}, u32[]{:S(2)}) collective-permute-start(f32[64,512]{1,0:T(8,128)S(1)} %add_add_fusion.unit), channel_id=1, source_target_pairs={{0,192},{8,200},{16,208},{24,216},{32,224},{40,232},{48,240},{56,2... | collective-permute-start | bytes 393224 | tf_op jit(solution)/shard_map/ppermute | solution.py:26
  54.2 5.4 %collective-permute-start.13 = (f32[64,512]{1,0:T(8,128)S(1)}, f32[64,512]{1,0:T(8,128)S(1)}, u32[]{:S(2)}, u32[]{:S(2)}) collective-permute-start(f32[64,512]{1,0:T(8,128)S(1)} %add_add_fusion.unit), channel_id=1, source_target_pairs={{0,32},{8,40},{16,48},{24,56},{32,0},{40,8},{48,16},{56,24},{64,96... | collective-permute-start | bytes 393224 | tf_op jit(solution)/shard_map/ppermute | solution.py:26
  57.2 5.3 %collective-permute-start.12 = (f32[64,512]{1,0:T(8,128)S(1)}, f32[64,512]{1,0:T(8,128)S(1)}, u32[]{:S(2)}, u32[]{:S(2)}) collective-permute-start(f32[64,512]{1,0:T(8,128)S(1)} %add_add_fusion.unit), channel_id=1, source_target_pairs={{0,16},{8,24},{16,32},{24,40},{32,48},{40,56},{48,0},{56,8},{64,80... | collective-permute-start | bytes 393224 | tf_op jit(solution)/shard_map/ppermute | solution.py:26
  57.2 7.5 %collective-permute-start.16 = (f32[64,512]{1,0:T(8,128)S(1)}, f32[64,512]{1,0:T(8,128)S(1)}, u32[]{:S(2)}, u32[]{:S(2)}) collective-permute-start(f32[64,512]{1,0:T(8,128)S(1)} %collective-permute-done.14.z1), channel_id=1, source_target_pairs={{0,64},{8,72},{16,80},{24,88},{32,96},{40,104},{48,112},{56,120},{... | collective-permute-start | bytes 393224 | tf_op jit(solution)/shard_map/ppermute | solution.py:26
  66.0 38.7 %copy-start.14 = (f32[256,512]{1,0:T(8,128)}, f32[256,512]{1,0:T(8,128)S(1)}, u32[]{:S(2)}) copy-start(f32[256,512]{1,0:T(8,128)S(1)} %get-tuple-element.67.m0) | copy-start | bytes 1572868
  66.1 36.0 %collective-permute-start.25 = (f32[256,512]{1,0:T(8,128)S(1)}, f32[256,512]{1,0:T(8,128)S(1)}, u32[]{:S(2)}, u32[]{:S(2)}) collective-permute-start(f32[256,512]{1,0:T(8,128)S(1)} %get-tuple-element.67.m0), channel_id=1, source_target_pairs={{0,48},{8,56},{16,0},{24,8},{32,16},{40,24},{48,32},{56,40},{64,11... | collective-permute-start | bytes 1572872 | tf_op jit(solution)/shard_map/ppermute | solution.py:26
  68.4 33.6 %collective-permute-start.24 = (f32[256,512]{1,0:T(8,128)S(1)}, f32[256,512]{1,0:T(8,128)S(1)}, u32[]{:S(2)}, u32[]{:S(2)}) collective-permute-start(f32[256,512]{1,0:T(8,128)S(1)} %get-tuple-element.67.m0), channel_id=1, source_target_pairs={{0,16},{8,24},{16,32},{24,40},{32,48},{40,56},{48,0},{56,8},{64,80... | collective-permute-start | bytes 1572872 | tf_op jit(solution)/shard_map/ppermute | solution.py:26
  68.5 7.2 %collective-permute-start.17 = (f32[8,3,8,128]{3,2,1,0:T(8,128)S(1)}, f32[8,3,8,128]{3,2,1,0:T(8,128)S(1)}, u32[]{:S(2)}, u32[]{:S(2)}) collective-permute-start(f32[8,3,8,128]{3,2,1,0:T(8,128)S(1)} %get-tuple-element.66), channel_id=1, source_target_pairs={{0,8},{8,0},{16,24},{24,16},{32,40},{40,32},{48,56},{56,48},{64,72... | collective-permute-start | bytes 294920 | tf_op jit(solution)/shard_map/ppermute | solution.py:26
  87.4 6.5 %collective-permute-start.20 = (f32[3,8,128]{2,1,0:T(8,128)S(1)}, f32[3,8,128]{2,1,0:T(8,128)S(1)}, u32[]{:S(2)}, u32[]{:S(2)}) collective-permute-start(f32[3,8,128]{2,1,0:T(8,128)S(1)} %reduce_sum.9.refs_0_), channel_id=1, source_target_pairs={{0,128},{8,136},{16,144},{24,152},{32,160},{40,168},{48,176},{56,1... | collective-permute-start | bytes 36872 | tf_op jit(solution)/shard_map/ppermute | solution.py:26
  87.5 6.4 %collective-permute-start.19 = (f32[3,8,128]{2,1,0:T(8,128)S(1)}, f32[3,8,128]{2,1,0:T(8,128)S(1)}, u32[]{:S(2)}, u32[]{:S(2)}) collective-permute-start(f32[3,8,128]{2,1,0:T(8,128)S(1)} %reduce_sum.9.refs_0_), channel_id=1, source_target_pairs={{0,192},{8,200},{16,208},{24,216},{32,224},{40,232},{48,240},{56,2... | collective-permute-start | bytes 36872 | tf_op jit(solution)/shard_map/ppermute | solution.py:26
  89.1 5.1 %collective-permute-start.18 = (f32[3,8,128]{2,1,0:T(8,128)S(1)}, f32[3,8,128]{2,1,0:T(8,128)S(1)}, u32[]{:S(2)}, u32[]{:S(2)}) collective-permute-start(f32[3,8,128]{2,1,0:T(8,128)S(1)} %reduce_sum.9.refs_0_), channel_id=1, source_target_pairs={{0,64},{8,72},{16,80},{24,88},{32,96},{40,104},{48,112},{56,120},{... | collective-permute-start | bytes 36872 | tf_op jit(solution)/shard_map/ppermute | solution.py:26
  94.8 4.5 %collective-permute-start.23 = (f32[4,3,8,128]{3,2,1,0:T(8,128)S(1)}, f32[4,3,8,128]{3,2,1,0:T(8,128)S(1)}, u32[]{:S(2)}, u32[]{:S(2)}) collective-permute-start(f32[4,3,8,128]{3,2,1,0:T(8,128)S(1)} %order.1.a), channel_id=1, source_target_pairs={{0,32},{8,40},{16,48},{24,56},{32,0},{40,8},{48,16},{56,24},{64,96... | collective-permute-start | bytes 147464 | tf_op jit(solution)/shard_map/ppermute | solution.py:26
  96.1 4.3 %collective-permute-start.22 = (f32[4,3,8,128]{3,2,1,0:T(8,128)S(1)}, f32[4,3,8,128]{3,2,1,0:T(8,128)S(1)}, u32[]{:S(2)}, u32[]{:S(2)}) collective-permute-start(f32[4,3,8,128]{3,2,1,0:T(8,128)S(1)} %order.1.a), channel_id=1, source_target_pairs={{0,48},{8,56},{16,0},{24,8},{32,16},{40,24},{48,32},{56,40},{64,11... | collective-permute-start | bytes 147464 | tf_op jit(solution)/shard_map/ppermute | solution.py:26
  97.9 4.2 %collective-permute-start.21 = (f32[4,3,8,128]{3,2,1,0:T(8,128)S(1)}, f32[4,3,8,128]{3,2,1,0:T(8,128)S(1)}, u32[]{:S(2)}, u32[]{:S(2)}) collective-permute-start(f32[4,3,8,128]{3,2,1,0:T(8,128)S(1)} %order.1.a), channel_id=1, source_target_pairs={{0,16},{8,24},{16,32},{24,40},{32,48},{40,56},{48,0},{56,8},{64,80... | collective-permute-start | bytes 147464 | tf_op jit(solution)/shard_map/ppermute | solution.py:26
  106.0 20.5 %all-to-all-start.1 = ((f32[8,16,3,8,128]{4,3,2,1,0:T(8,128)}), f32[8,16,3,8,128]{4,3,2,1,0:T(8,128)}, u32[]{:S(2)}, u32[]{:S(2)}) async-start(f32[8,16,3,8,128]{4,3,2,1,0:T(8,128)} %bitcast.6), calls=%async_computation.1 | async-start | bytes 3145728 | tf_op jit(solution)/shard_map/all_to_all | solution.py:45
  112.5 7.7 %collective-permute-start.27 = (f32[128,512]{1,0:T(8,128)S(1)}, f32[128,512]{1,0:T(8,128)S(1)}, u32[]{:S(2)}, u32[]{:S(2)}) collective-permute-start(f32[128,512]{1,0:T(8,128)S(1)} %slice.7), channel_id=1, source_target_pairs={{0,48},{8,56},{16,0},{24,8},{32,16},{40,24},{48,32},{56,40},{64,11... | collective-permute-start | bytes 786440 | tf_op jit(solution)/shard_map/ppermute | solution.py:26
  113.1 7.8 %collective-permute-start.26 = (f32[128,512]{1,0:T(8,128)S(1)}, f32[128,512]{1,0:T(8,128)S(1)}, u32[]{:S(2)}, u32[]{:S(2)}) collective-permute-start(f32[128,512]{1,0:T(8,128)S(1)} %slice.6), channel_id=1, source_target_pairs={{0,16},{8,24},{16,32},{24,40},{32,48},{40,56},{48,0},{56,8},{64,80... | collective-permute-start | bytes 786440 | tf_op jit(solution)/shard_map/ppermute | solution.py:26
  126.4 9.0 %collective-permute-start.28 = (f32[8,16,3,8,128]{4,3,2,1,0:T(8,128)}, f32[8,16,3,8,128]{4,3,2,1,0:T(8,128)S(1)}, u32[]{:S(2)}, u32[]{:S(2)}) collective-permute-start(f32[8,16,3,8,128]{4,3,2,1,0:T(8,128)} %all-to-all-done.1.own_ref), channel_id=1, source_target_pairs={{0,8},{8,0},{16,24},{24,16},{32,40},{40,32},{48,56},{56,48},{64,72... | collective-permute-start | bytes 4718600 | tf_op jit(solution)/shard_map/ppermute | solution.py:26
  151.2 1.5 collective-permute-start.29
  (23 other events, 181.1 us)

commit v10 on v7

--- a/solution.py
+++ b/solution.py
@@ -174,13 +174,13 @@
         copies_ref[i] = total
 
 
-def spread(x, copies, leading=False, grant=10):
+def spread(x, copies, leading=False):
     return pl.pallas_call(
         functools.partial(spread_kernel, leading),
         out_shape=jax.ShapeDtypeStruct((copies,) + x.shape[leading:], F32),
         in_specs=[VMEM],
         out_specs=VMEM,
-        compiler_params=params(grant),
+        compiler_params=params(10),
         cost_estimate=cost(1 << 17, 1 << 20),
         name="spread",
     )(x)
@@ -445,11 +445,10 @@
     part = part + dp_shift(to_core, dc=1)
     m1, m3 = dp_shift(of_y, dy=1), dp_shift(of_y, dy=-1)
     copies = spread(exchange(part, None, "shard"), 16, leading=True)
-    copies, m1, m3 = lax.optimization_barrier((copies, m1, m3))
     part = exchange(copies, ZY_GROUPS)
     part, m1, m3, args, q_t = lax.optimization_barrier((part, m1, m3, args, q_start.T))
     m2_top, m2_end = dp_shift(m1[:128], dy=1), dp_shift(m3[128:], dy=-1)
-    part = exchange(spread(part, 8, grant=58), None, "shard")
+    part = exchange(spread(part, 8), None, "shard")
     part, m2_top, m2_end, merged, q_parts = lax.optimization_barrier(
         (part, m2_top, m2_end, *merge_all(*args, q_t))
     )

time: 155 us -> 152 us (0.981)
  blocking collectives: 25.6 us -> 0 us
  starting transfers between devices: 45.9 us -> 58.7 us
  waiting for transfers between devices: 39.4 us -> 49.5 us
  Pallas kernels: 30 us -> 27.7 us
    all_to_all x2 -> x0, blocking collectives: 25.6 us -> none  [exchange(): return lax.all_to_all(x, axis, 0, 0, axis_index_groups=groups)]
    all_to_all x1 -> x3, starting transfers between devices: 4.57 us -> 14.2 us  [exchange(): return lax.all_to_all(x, axis, 0, 0, axis_index_groups=groups)]
    ppermute x24, waiting for transfers between devices: 33.3 us -> 39.8 us  [dp_shift(): return lax.ppermute(x, 'dp', pairs)]
    all_to_all x1 -> x3, waiting for transfers between devices: 6.05 us -> 9.66 us  [exchange(): return lax.all_to_all(x, axis, 0, 0, axis_index_groups=groups)]
    ppermute x24, starting transfers between devices: 41.3 us -> 44.4 us  [dp_shift(): return lax.ppermute(x, 'dp', pairs)]
    unnamed x38 -> x48, local copies, waits for them, and re-layouts: 10.4 us -> 11.7 us
  transfers between devices with their start and end apart: 25 -> 27, of which waited for: 15 -> 19; matrix products, arithmetic and copies ran while one was open for 1% -> 1% of each run, Pallas kernels for 4% -> 4%
where the time goes in v10:
time: 152 us; the launch traced here: 151 us
  starting transfers between devices  58.7 us (39%)
  waiting for transfers between devices  49.5 us (33%)
  Pallas kernels  27.7 us (18%)
  local copies, waits for them, and re-layouts  13.6 us (9%)
    ppermute x24, starting transfers between devices, dp_shift(): return lax.ppermute(x, 'dp', pairs)  44.4 us
    ppermute x24, waiting for transfers between devices, dp_shift(): return lax.ppermute(x, 'dp', pairs)  39.8 us
    all_to_all x3, starting transfers between devices, exchange(): return lax.all_to_all(x, axis, 0, 0, axis_index_groups=groups)  14.2 us
    pallas_call x1, Pallas kernels, iterate(): pl.pallas_call(iterate_kernel, out_shape=(jax.ShapeDtypeStruct((n, k), F3...  13.6 us
    unnamed x48, local copies, waits for them, and re-layouts  11.7 us
    all_to_all x3, waiting for transfers between devices, exchange(): return lax.all_to_all(x, axis, 0, 0, axis_index_groups=groups)  9.66 us
    pallas_call x4, Pallas kernels, merge(): pl.pallas_call(functools.partial(merge_kernel, turns, own), out_shape=out...  4.3 us
    pallas_call x1, Pallas kernels, finish(): pl.pallas_call(finish_kernel, out_shape=(jax.ShapeDtypeStruct((1, d, k),...  3.68 us
  transfers between devices with their start and end apart: 27, of which 19 were waited for; matrix products, arithmetic and copies ran while one was open for 1% of the time, Pallas kernels for 4%

profile of v10, /device:TPU:1, one launch (start us, length us, event | category | flops | bytes accessed | tf_op | source)
XLA Modules:
  0.0 151.3 jit_solution(7764799046754528105)
XLA Ops:
  0.7 1.6 %copy-done = bf16[1,1024,1024]{2,1,0:T(8,128)(2,1)S(1)} copy-done((bf16[1,1024,1024]{2,1,0:T(8,128)(2,1)S(1)}, bf16[1,1024,1024]{2,1,0:T(8,128)(2,1)}, u32[]{:S(2)}) %copy-start) | copy-done | bytes 2097176
  5.7 3.3 %collective-permute-start = (f32[1,512,256]{2,1,0:T(8,128)S(1)}, f32[1,512,256]{2,1,0:T(8,128)S(1)}, u32[]{:S(2)}, u32[]{:S(2)}) collective-permute-start(f32[1,512,256]{2,1,0:T(8,128)S(1)} %merge.4), channel_id=1, source_target_pairs={{0,8},{8,0},{16,24},{24,16},{32,40},{40,32},{48,56},{56,48},{64,72... | collective-permute-start | bytes 1572872 | tf_op jit(solution)/shard_map/ppermute | solution.py:28
  12.0 2.7 %collective-permute-start.6 = (f32[256,256]{1,0:T(8,128)S(1)}, f32[256,256]{1,0:T(8,128)S(1)}, u32[]{:S(2)}, u32[]{:S(2)}) collective-permute-start(f32[256,256]{1,0:T(8,128)S(1)} %get-tuple-element.54), channel_id=1, source_target_pairs={{0,48},{8,56},{16,0},{24,8},{32,16},{40,24},{48,32},{56,40},{64,11... | collective-permute-start | bytes 786440 | tf_op jit(solution)/shard_map/ppermute | solution.py:28
  17.4 3.5 %collective-permute-done.4 = f32[256,256]{1,0:T(8,128)S(1)} collective-permute-done((f32[256,256]{1,0:T(8,128)S(1)}, f32[256,256]{1,0:T(8,128)S(1)}, u32[]{:S(2)}, u32[]{:S(2)}) %collective-permute-start.4) | collective-permute-done | bytes 262176 | tf_op jit(solution)/shard_map/ppermute | solution.py:28
  21.1 2.7 %collective-permute-start.7 = (f32[256,256]{1,0:T(8,128)S(1)}, f32[256,256]{1,0:T(8,128)S(1)}, u32[]{:S(2)}, u32[]{:S(2)}) collective-permute-start(f32[256,256]{1,0:T(8,128)S(1)} %add.45), channel_id=1, source_target_pairs={{0,48},{8,56},{16,0},{24,8},{32,16},{40,24},{48,32},{56,40},{64,11... | collective-permute-start | bytes 786440 | tf_op jit(solution)/shard_map/ppermute | solution.py:28
  23.9 1.7 %collective-permute-done.2 = f32[256,256]{1,0:T(8,128)S(1)} collective-permute-done((f32[256,256]{1,0:T(8,128)S(1)}, f32[256,256]{1,0:T(8,128)S(1)}, u32[]{:S(2)}, u32[]{:S(2)}) %collective-permute-start.2) | collective-permute-done | bytes 262176 | tf_op jit(solution)/shard_map/ppermute | solution.py:28
  26.6 5.6 %collective-permute-done.5.on = f32[256,256]{1,0:T(8,128)S(1)} collective-permute-done((f32[256,256]{1,0:T(8,128)S(1)}, f32[256,256]{1,0:T(8,128)S(1)}, u32[]{:S(2)}, u32[]{:S(2)}) %collective-permute-start.5) | collective-permute-done | bytes 262176 | tf_op jit(solution)/shard_map/ppermute | solution.py:28
  33.0 4.2 %collective-permute-start.10 = (f32[32,512]{1,0:T(8,128)S(1)}, f32[32,512]{1,0:T(8,128)S(1)}, u32[]{:S(2)}, u32[]{:S(2)}) collective-permute-start(f32[32,512]{1,0:T(8,128)S(1)} %get-tuple-element.59), channel_id=1, source_target_pairs={{0,192},{8,200},{16,208},{24,216},{32,224},{40,232},{48,240},{56,2... | collective-permute-start | bytes 196616 | tf_op jit(solution)/shard_map/ppermute | solution.py:28
  37.2 1.3 collective-permute-done.10
  38.6 4.7 %collective-permute-start.11 = (f32[64,512]{1,0:T(8,128)S(1)}, f32[64,512]{1,0:T(8,128)S(1)}, u32[]{:S(2)}, u32[]{:S(2)}) collective-permute-start(f32[64,512]{1,0:T(8,128)S(1)} %pad_add_fusion), channel_id=1, source_target_pairs={{0,192},{8,200},{16,208},{24,216},{32,224},{40,232},{48,240},{56,2... | collective-permute-start | bytes 393224 | tf_op jit(solution)/shard_map/ppermute | solution.py:28
  43.4 3.2 %collective-permute-done.11 = f32[64,512]{1,0:T(8,128)S(1)} collective-permute-done((f32[64,512]{1,0:T(8,128)S(1)}, f32[64,512]{1,0:T(8,128)S(1)}, u32[]{:S(2)}, u32[]{:S(2)}) %collective-permute-start.11) | collective-permute-done | bytes 131104 | tf_op jit(solution)/shard_map/ppermute | solution.py:28
  46.6 3.9 %collective-permute-done.9 = f32[64,512]{1,0:T(8,128)S(1)} collective-permute-done((f32[64,512]{1,0:T(8,128)S(1)}, f32[64,512]{1,0:T(8,128)S(1)}, u32[]{:S(2)}, u32[]{:S(2)}) %collective-permute-start.9) | collective-permute-done | bytes 131104 | tf_op jit(solution)/shard_map/ppermute | solution.py:28
  50.6 3.6 %collective-permute-start.15 = (f32[64,512]{1,0:T(8,128)S(1)}, f32[64,512]{1,0:T(8,128)S(1)}, u32[]{:S(2)}, u32[]{:S(2)}) collective-permute-start(f32[64,512]{1,0:T(8,128)S(1)} %add_add_fusion.unit), channel_id=1, source_target_pairs={{0,192},{8,200},{16,208},{24,216},{32,224},{40,232},{48,240},{56,2... | collective-permute-start | bytes 393224 | tf_op jit(solution)/shard_map/ppermute | solution.py:28
  54.2 3.0 %collective-permute-start.13 = (f32[64,512]{1,0:T(8,128)S(1)}, f32[64,512]{1,0:T(8,128)S(1)}, u32[]{:S(2)}, u32[]{:S(2)}) collective-permute-start(f32[64,512]{1,0:T(8,128)S(1)} %add_add_fusion.unit), channel_id=1, source_target_pairs={{0,32},{8,40},{16,48},{24,56},{32,0},{40,8},{48,16},{56,24},{64,96... | collective-permute-start | bytes 393224 | tf_op jit(solution)/shard_map/ppermute | solution.py:28
  57.2 2.3 %collective-permute-done.13.u2 = f32[64,512]{1,0:T(8,128)S(1)} collective-permute-done((f32[64,512]{1,0:T(8,128)S(1)}, f32[64,512]{1,0:T(8,128)S(1)}, u32[]{:S(2)}, u32[]{:S(2)}) %collective-permute-start.13) | collective-permute-done | bytes 131104 | tf_op jit(solution)/shard_map/ppermute | solution.py:28
  59.6 3.0 %collective-permute-done.12.u1 = f32[64,512]{1,0:T(8,128)S(1)} collective-permute-done((f32[64,512]{1,0:T(8,128)S(1)}, f32[64,512]{1,0:T(8,128)S(1)}, u32[]{:S(2)}, u32[]{:S(2)}) %collective-permute-start.12) | collective-permute-done | bytes 131104 | tf_op jit(solution)/shard_map/ppermute | solution.py:28
  62.5 2.2 %collective-permute-done.16.z2 = f32[64,512]{1,0:T(8,128)S(1)} collective-permute-done((f32[64,512]{1,0:T(8,128)S(1)}, f32[64,512]{1,0:T(8,128)S(1)}, u32[]{:S(2)}, u32[]{:S(2)}) %collective-permute-start.16) | collective-permute-done | bytes 131104 | tf_op jit(solution)/shard_map/ppermute | solution.py:28
  66.1 6.7 %collective-permute-start.17 = (f32[8,3,8,128]{3,2,1,0:T(8,128)S(1)}, f32[8,3,8,128]{3,2,1,0:T(8,128)S(1)}, u32[]{:S(2)}, u32[]{:S(2)}) collective-permute-start(f32[8,3,8,128]{3,2,1,0:T(8,128)S(1)} %get-tuple-element.63), channel_id=1, source_target_pairs={{0,8},{8,0},{16,24},{24,16},{32,40},{40,32},{48,56},{56,48},{64,72... | collective-permute-start | bytes 294920 | tf_op jit(solution)/shard_map/ppermute | solution.py:28
  74.3 3.6 %all-to-all-start = ((f32[8,3,8,128]{3,2,1,0:T(8,128)}), f32[8,3,8,128]{3,2,1,0:T(8,128)S(1)}, u32[]{:S(2)}, u32[]{:S(2)}) async-start(f32[8,3,8,128]{3,2,1,0:T(8,128)} %add.50), calls=%async_computation | async-start | bytes 196608 | tf_op jit(solution)/shard_map/all_to_all | solution.py:47
  77.9 4.7 %collective-permute-start.19 = (f32[256,512]{1,0:T(8,128)S(1)}, f32[256,512]{1,0:T(8,128)S(1)}, u32[]{:S(2)}, u32[]{:S(2)}) collective-permute-start(f32[256,512]{1,0:T(8,128)S(1)} %get-tuple-element.64.m0), channel_id=1, source_target_pairs={{0,48},{8,56},{16,0},{24,8},{32,16},{40,24},{48,32},{56,40},{64,11... | collective-permute-start | bytes 1572872 | tf_op jit(solution)/shard_map/ppermute | solution.py:28
  83.9 6.1 %all-to-all-start.1 = ((f32[16,3,8,128]{3,2,1,0:T(8,128)}), f32[16,3,8,128]{3,2,1,0:T(8,128)S(1)}, u32[]{:S(2)}, u32[]{:S(2)}) async-start(f32[16,3,8,128]{3,2,1,0:T(8,128)} %spread.2), calls=%async_computation.1 | async-start | bytes 393216 | tf_op jit(solution)/shard_map/all_to_all | solution.py:47
  90.0 3.2 %collective-permute-done.19.m3 = f32[256,512]{1,0:T(8,128)S(1)} collective-permute-done((f32[256,512]{1,0:T(8,128)S(1)}, f32[256,512]{1,0:T(8,128)S(1)}, u32[]{:S(2)}, u32[]{:S(2)}) %collective-permute-start.19) | collective-permute-done | bytes 524320 | tf_op jit(solution)/shard_map/ppermute | solution.py:28
  93.2 3.4 %collective-permute-done.18.m1 = f32[256,512]{1,0:T(8,128)S(1)} collective-permute-done((f32[256,512]{1,0:T(8,128)S(1)}, f32[256,512]{1,0:T(8,128)S(1)}, u32[]{:S(2)}, u32[]{:S(2)}) %collective-permute-start.18) | collective-permute-done | bytes 524320 | tf_op jit(solution)/shard_map/ppermute | solution.py:28
  96.6 3.0 %all-to-all-done.1.x_ref = f32[16,3,8,128]{3,2,1,0:T(8,128)S(1)} async-done(((f32[16,3,8,128]{3,2,1,0:T(8,128)}), f32[16,3,8,128]{3,2,1,0:T(8,128)S(1)}, u32[]{:S(2)}, u32[]{:S(2)}) %all-to-all-start.1) | async-done | bytes 196640 | tf_op jit(solution)/shard_map/all_to_all | solution.py:47
  100.9 4.6 %all-to-all-start.2 = ((f32[8,16,3,8,128]{4,3,2,1,0:T(8,128)}), f32[8,16,3,8,128]{4,3,2,1,0:T(8,128)}, u32[]{:S(2)}, u32[]{:S(2)}) async-start(f32[8,16,3,8,128]{4,3,2,1,0:T(8,128)} %copy-done.6), calls=%async_computation.2 | async-start | bytes 3145728 | tf_op jit(solution)/shard_map/all_to_all | solution.py:47
  110.2 2.1 %merge_all.1 = (f32[1024,1024]{1,0:T(8,128)S(1)}, bf16[3,64,1024]{2,1,0:T(8,128)(2,1)S(1)}) custom-call(bf16[512,1024]{1,0:T(8,128)(2,1)S(1)} %copy-done.3, bf16[512,1024]{1,0:T(8,128)(2,1)S(1)} %copy-done.5, bf16[1,1024,1024]{2,1,0:T(8,128)(2,1)S(1)} %copy-done.1, f32[64,1024]{1,0:T(8,128)S(1)} %bitcast.5), custom_call_target="tpu_custom_call" | custom-call | flops 1073741824 | bytes 8388608 | tf_op jit(solution)/shard_map/merge_all/pallas_call | solution.py:120
  112.3 2.0 %copy-done.7 = f32[1024,1024]{1,0:T(8,128)} copy-done((f32[1024,1024]{1,0:T(8,128)}, f32[1024,1024]{1,0:T(8,128)S(1)}, u32[]{:S(2)}) %copy-start.7) | copy-done | bytes 4194328
  116.5 6.0 %all-to-all-done.2.own_ref = f32[8,16,3,8,128]{4,3,2,1,0:T(8,128)} async-done(((f32[8,16,3,8,128]{4,3,2,1,0:T(8,128)}), f32[8,16,3,8,128]{4,3,2,1,0:T(8,128)}, u32[]{:S(2)}, u32[]{:S(2)}) %all-to-all-start.2) | async-done | bytes 1572896 | tf_op jit(solution)/shard_map/all_to_all | solution.py:47
  122.6 4.6 %collective-permute-start.22 = (f32[8,16,3,8,128]{4,3,2,1,0:T(8,128)}, f32[8,16,3,8,128]{4,3,2,1,0:T(8,128)S(1)}, u32[]{:S(2)}, u32[]{:S(2)}) collective-permute-start(f32[8,16,3,8,128]{4,3,2,1,0:T(8,128)} %all-to-all-done.2.own_ref), channel_id=1, source_target_pairs={{0,8},{8,0},{16,24},{24,16},{32,40},{40,32},{48,56},{56,48},{64,72... | collective-permute-start | bytes 4718600 | tf_op jit(solution)/shard_map/ppermute | solution.py:28
  127.2 3.2 %collective-permute-done.22.away_ref = f32[8,16,3,8,128]{4,3,2,1,0:T(8,128)S(1)} collective-permute-done((f32[8,16,3,8,128]{4,3,2,1,0:T(8,128)}, f32[8,16,3,8,128]{4,3,2,1,0:T(8,128)S(1)}, u32[]{:S(2)}, u32[]{:S(2)}) %collective-permute-start.22) | collective-permute-done | bytes 1572896 | tf_op jit(solution)/shard_map/ppermute | solution.py:28
  131.4 13.6 %iterations.1 = (f32[64,1024]{1,0:T(8,128)}, f32[64,1024]{1,0:T(8,128)S(1)}) custom-call(s32[3]{0:T(128)S(1)} %pad_add_fusion.2.pos_ref, f32[8,16,3,8,128]{4,3,2,1,0:T(8,128)} %all-to-all-done.2.own_ref, f32[8,16,3,8,128]{4,3,2,1,0:T(8,128)S(1)} %collective-permute-done.22.away_ref, bf16[3,64,1024]{2,1,0:T(8,128)(2,1)S(1)} %copy-done.23), custom_call_target="tpu_custom_call" | custom-call | flops 2415919104 | bytes 4194304 | tf_op jit(solution)/shard_map/iterations/pallas_call | solution.py:331
  147.6 3.7 %finish.1 = (bf16[1,1024,1024]{2,1,0:T(8,128)(2,1)}, bf16[1024,1024]{1,0:T(8,128)(2,1)}) custom-call(s32[3]{0:T(128)S(1)} %pad_add_fusion.2.pos_ref, f32[1024,1024]{1,0:T(8,128)S(1)} %copy-done.8, bf16[1024,1024]{1,0:T(8,128)(2,1)S(1)} %copy-done.9, f32[64,512]{1,0:T(8,128)S(1)} %left.1.own, f32[64,512]{1,0:T(8,128)S(1)} %collective-permute-done.23.away, ...), custom_call_target="tpu_custom_call" | custom-call | flops 536870912 | bytes 12582912 | tf_op jit(solution)/shard_map/finish/pallas_call | solution.py:398
  (93 shorter events, 27.4 us)
Async XLA Ops:
  5.7 4.9 %collective-permute-start = (f32[1,512,256]{2,1,0:T(8,128)S(1)}, f32[1,512,256]{2,1,0:T(8,128)S(1)}, u32[]{:S(2)}, u32[]{:S(2)}) collective-permute-start(f32[1,512,256]{2,1,0:T(8,128)S(1)} %merge.4), channel_id=1, source_target_pairs={{0,8},{8,0},{16,24},{24,16},{32,40},{40,32},{48,56},{56,48},{64,72... | collective-permute-start | bytes 1572872 | tf_op jit(solution)/shard_map/ppermute | solution.py:28
  10.6 4.1 %collective-permute-start.1 = (f32[3,512,256]{2,1,0:T(8,128)S(1)}, f32[3,512,256]{2,1,0:T(8,128)S(1)}, u32[]{:S(2)}, u32[]{:S(2)}) collective-permute-start(f32[3,512,256]{2,1,0:T(8,128)S(1)} %merge.5), channel_id=1, source_target_pairs={{0,8},{8,0},{16,24},{24,16},{32,40},{40,32},{48,56},{56,48},{64,72... | collective-permute-start | bytes 4718600 | tf_op jit(solution)/shard_map/ppermute | solution.py:28
  11.9 9.1 %collective-permute-start.4 = (f32[256,256]{1,0:T(8,128)S(1)}, f32[256,256]{1,0:T(8,128)S(1)}, u32[]{:S(2)}, u32[]{:S(2)}) collective-permute-start(f32[256,256]{1,0:T(8,128)S(1)} %get-tuple-element.52), channel_id=1, source_target_pairs={{0,16},{8,24},{16,32},{24,40},{32,48},{40,56},{48,0},{56,8},{64,80... | collective-permute-start | bytes 786440 | tf_op jit(solution)/shard_map/ppermute | solution.py:28
  12.0 9.1 %collective-permute-start.6 = (f32[256,256]{1,0:T(8,128)S(1)}, f32[256,256]{1,0:T(8,128)S(1)}, u32[]{:S(2)}, u32[]{:S(2)}) collective-permute-start(f32[256,256]{1,0:T(8,128)S(1)} %get-tuple-element.54), channel_id=1, source_target_pairs={{0,48},{8,56},{16,0},{24,8},{32,16},{40,24},{48,32},{56,40},{64,11... | collective-permute-start | bytes 786440 | tf_op jit(solution)/shard_map/ppermute | solution.py:28
  15.9 9.6 %collective-permute-start.2 = (f32[256,256]{1,0:T(8,128)S(1)}, f32[256,256]{1,0:T(8,128)S(1)}, u32[]{:S(2)}, u32[]{:S(2)}) collective-permute-start(f32[256,256]{1,0:T(8,128)S(1)} %get-tuple-element.47), channel_id=1, source_target_pairs={{0,48},{8,56},{16,0},{24,8},{32,16},{40,24},{48,32},{56,40},{64,11... | collective-permute-start | bytes 786440 | tf_op jit(solution)/shard_map/ppermute | solution.py:28
  16.3 10.3 %collective-permute-start.3 = (f32[256,256]{1,0:T(8,128)S(1)}, f32[256,256]{1,0:T(8,128)S(1)}, u32[]{:S(2)}, u32[]{:S(2)}) collective-permute-start(f32[256,256]{1,0:T(8,128)S(1)} %get-tuple-element.49), channel_id=1, source_target_pairs={{0,16},{8,24},{16,32},{24,40},{32,48},{40,56},{48,0},{56,8},{64,80... | collective-permute-start | bytes 786440 | tf_op jit(solution)/shard_map/ppermute | solution.py:28
  21.0 11.2 %collective-permute-start.5 = (f32[256,256]{1,0:T(8,128)S(1)}, f32[256,256]{1,0:T(8,128)S(1)}, u32[]{:S(2)}, u32[]{:S(2)}) collective-permute-start(f32[256,256]{1,0:T(8,128)S(1)} %add.44), channel_id=1, source_target_pairs={{0,16},{8,24},{16,32},{24,40},{32,48},{40,56},{48,0},{56,8},{64,80... | collective-permute-start | bytes 786440 | tf_op jit(solution)/shard_map/ppermute | solution.py:28
  21.1 11.1 %collective-permute-start.7 = (f32[256,256]{1,0:T(8,128)S(1)}, f32[256,256]{1,0:T(8,128)S(1)}, u32[]{:S(2)}, u32[]{:S(2)}) collective-permute-start(f32[256,256]{1,0:T(8,128)S(1)} %add.45), channel_id=1, source_target_pairs={{0,48},{8,56},{16,0},{24,8},{32,16},{40,24},{48,32},{56,40},{64,11... | collective-permute-start | bytes 786440 | tf_op jit(solution)/shard_map/ppermute | solution.py:28
  33.0 5.6 %collective-permute-start.10 = (f32[32,512]{1,0:T(8,128)S(1)}, f32[32,512]{1,0:T(8,128)S(1)}, u32[]{:S(2)}, u32[]{:S(2)}) collective-permute-start(f32[32,512]{1,0:T(8,128)S(1)} %get-tuple-element.59), channel_id=1, source_target_pairs={{0,192},{8,200},{16,208},{24,216},{32,224},{40,232},{48,240},{56,2... | collective-permute-start | bytes 196616 | tf_op jit(solution)/shard_map/ppermute | solution.py:28
  37.2 6.0 %collective-permute-start.8 = (f32[32,512]{1,0:T(8,128)S(1)}, f32[32,512]{1,0:T(8,128)S(1)}, u32[]{:S(2)}, u32[]{:S(2)}) collective-permute-start(f32[32,512]{1,0:T(8,128)S(1)} %get-tuple-element.57), channel_id=1, source_target_pairs={{0,64},{8,72},{16,80},{24,88},{32,96},{40,104},{48,112},{56,120},{... | collective-permute-start | bytes 196616 | tf_op jit(solution)/shard_map/ppermute | solution.py:28
  38.6 8.0 %collective-permute-start.11 = (f32[64,512]{1,0:T(8,128)S(1)}, f32[64,512]{1,0:T(8,128)S(1)}, u32[]{:S(2)}, u32[]{:S(2)}) collective-permute-start(f32[64,512]{1,0:T(8,128)S(1)} %pad_add_fusion), channel_id=1, source_target_pairs={{0,192},{8,200},{16,208},{24,216},{32,224},{40,232},{48,240},{56,2... | collective-permute-start | bytes 393224 | tf_op jit(solution)/shard_map/ppermute | solution.py:28
  43.3 7.2 %collective-permute-start.9 = (f32[64,512]{1,0:T(8,128)S(1)}, f32[64,512]{1,0:T(8,128)S(1)}, u32[]{:S(2)}, u32[]{:S(2)}) collective-permute-start(f32[64,512]{1,0:T(8,128)S(1)} %pad_add_fusion.1), channel_id=1, source_target_pairs={{0,64},{8,72},{16,80},{24,88},{32,96},{40,104},{48,112},{56,120},{... | collective-permute-start | bytes 393224 | tf_op jit(solution)/shard_map/ppermute | solution.py:28
  50.5 6.7 %collective-permute-start.14 = (f32[64,512]{1,0:T(8,128)S(1)}, f32[64,512]{1,0:T(8,128)S(1)}, u32[]{:S(2)}, u32[]{:S(2)}) collective-permute-start(f32[64,512]{1,0:T(8,128)S(1)} %add_add_fusion.unit), channel_id=1, source_target_pairs={{0,64},{8,72},{16,80},{24,88},{32,96},{40,104},{48,112},{56,120},{... | collective-permute-start | bytes 393224 | tf_op jit(solution)/shard_map/ppermute | solution.py:28
  50.6 6.6 %collective-permute-start.15 = (f32[64,512]{1,0:T(8,128)S(1)}, f32[64,512]{1,0:T(8,128)S(1)}, u32[]{:S(2)}, u32[]{:S(2)}) collective-permute-start(f32[64,512]{1,0:T(8,128)S(1)} %add_add_fusion.unit), channel_id=1, source_target_pairs={{0,192},{8,200},{16,208},{24,216},{32,224},{40,232},{48,240},{56,2... | collective-permute-start | bytes 393224 | tf_op jit(solution)/shard_map/ppermute | solution.py:28
  54.2 5.4 %collective-permute-start.13 = (f32[64,512]{1,0:T(8,128)S(1)}, f32[64,512]{1,0:T(8,128)S(1)}, u32[]{:S(2)}, u32[]{:S(2)}) collective-permute-start(f32[64,512]{1,0:T(8,128)S(1)} %add_add_fusion.unit), channel_id=1, source_target_pairs={{0,32},{8,40},{16,48},{24,56},{32,0},{40,8},{48,16},{56,24},{64,96... | collective-permute-start | bytes 393224 | tf_op jit(solution)/shard_map/ppermute | solution.py:28
  57.2 5.3 %collective-permute-start.12 = (f32[64,512]{1,0:T(8,128)S(1)}, f32[64,512]{1,0:T(8,128)S(1)}, u32[]{:S(2)}, u32[]{:S(2)}) collective-permute-start(f32[64,512]{1,0:T(8,128)S(1)} %add_add_fusion.unit), channel_id=1, source_target_pairs={{0,16},{8,24},{16,32},{24,40},{32,48},{40,56},{48,0},{56,8},{64,80... | collective-permute-start | bytes 393224 | tf_op jit(solution)/shard_map/ppermute | solution.py:28
  57.2 7.5 %collective-permute-start.16 = (f32[64,512]{1,0:T(8,128)S(1)}, f32[64,512]{1,0:T(8,128)S(1)}, u32[]{:S(2)}, u32[]{:S(2)}) collective-permute-start(f32[64,512]{1,0:T(8,128)S(1)} %collective-permute-done.14.z1), channel_id=1, source_target_pairs={{0,64},{8,72},{16,80},{24,88},{32,96},{40,104},{48,112},{56,120},{... | collective-permute-start | bytes 393224 | tf_op jit(solution)/shard_map/ppermute | solution.py:28
  66.0 33.6 %copy-start.14 = (f32[256,512]{1,0:T(8,128)}, f32[256,512]{1,0:T(8,128)S(1)}, u32[]{:S(2)}) copy-start(f32[256,512]{1,0:T(8,128)S(1)} %get-tuple-element.64.m0) | copy-start | bytes 1572868
  66.1 7.6 %collective-permute-start.17 = (f32[8,3,8,128]{3,2,1,0:T(8,128)S(1)}, f32[8,3,8,128]{3,2,1,0:T(8,128)S(1)}, u32[]{:S(2)}, u32[]{:S(2)}) collective-permute-start(f32[8,3,8,128]{3,2,1,0:T(8,128)S(1)} %get-tuple-element.63), channel_id=1, source_target_pairs={{0,8},{8,0},{16,24},{24,16},{32,40},{40,32},{48,56},{56,48},{64,72... | collective-permute-start | bytes 294920 | tf_op jit(solution)/shard_map/ppermute | solution.py:28
  74.3 8.9 %all-to-all-start = ((f32[8,3,8,128]{3,2,1,0:T(8,128)}), f32[8,3,8,128]{3,2,1,0:T(8,128)S(1)}, u32[]{:S(2)}, u32[]{:S(2)}) async-start(f32[8,3,8,128]{3,2,1,0:T(8,128)} %add.50), calls=%async_computation | async-start | bytes 196608 | tf_op jit(solution)/shard_map/all_to_all | solution.py:47
  77.9 15.3 %collective-permute-start.19 = (f32[256,512]{1,0:T(8,128)S(1)}, f32[256,512]{1,0:T(8,128)S(1)}, u32[]{:S(2)}, u32[]{:S(2)}) collective-permute-start(f32[256,512]{1,0:T(8,128)S(1)} %get-tuple-element.64.m0), channel_id=1, source_target_pairs={{0,48},{8,56},{16,0},{24,8},{32,16},{40,24},{48,32},{56,40},{64,11... | collective-permute-start | bytes 1572872 | tf_op jit(solution)/shard_map/ppermute | solution.py:28
  82.6 14.0 %collective-permute-start.18 = (f32[256,512]{1,0:T(8,128)S(1)}, f32[256,512]{1,0:T(8,128)S(1)}, u32[]{:S(2)}, u32[]{:S(2)}) collective-permute-start(f32[256,512]{1,0:T(8,128)S(1)} %get-tuple-element.64.m0), channel_id=1, source_target_pairs={{0,16},{8,24},{16,32},{24,40},{32,48},{40,56},{48,0},{56,8},{64,80... | collective-permute-start | bytes 1572872 | tf_op jit(solution)/shard_map/ppermute | solution.py:28
  83.9 15.7 %all-to-all-start.1 = ((f32[16,3,8,128]{3,2,1,0:T(8,128)}), f32[16,3,8,128]{3,2,1,0:T(8,128)S(1)}, u32[]{:S(2)}, u32[]{:S(2)}) async-start(f32[16,3,8,128]{3,2,1,0:T(8,128)} %spread.2), calls=%async_computation.1 | async-start | bytes 393216 | tf_op jit(solution)/shard_map/all_to_all | solution.py:47
  100.9 21.7 %all-to-all-start.2 = ((f32[8,16,3,8,128]{4,3,2,1,0:T(8,128)}), f32[8,16,3,8,128]{4,3,2,1,0:T(8,128)}, u32[]{:S(2)}, u32[]{:S(2)}) async-start(f32[8,16,3,8,128]{4,3,2,1,0:T(8,128)} %copy-done.6), calls=%async_computation.2 | async-start | bytes 3145728 | tf_op jit(solution)/shard_map/all_to_all | solution.py:47
  107.4 7.7 %collective-permute-start.21 = (f32[128,512]{1,0:T(8,128)S(1)}, f32[128,512]{1,0:T(8,128)S(1)}, u32[]{:S(2)}, u32[]{:S(2)}) collective-permute-start(f32[128,512]{1,0:T(8,128)S(1)} %slice.7), channel_id=1, source_target_pairs={{0,48},{8,56},{16,0},{24,8},{32,16},{40,24},{48,32},{56,40},{64,11... | collective-permute-start | bytes 786440 | tf_op jit(solution)/shard_map/ppermute | solution.py:28
  108.3 7.5 %collective-permute-start.20 = (f32[128,512]{1,0:T(8,128)S(1)}, f32[128,512]{1,0:T(8,128)S(1)}, u32[]{:S(2)}, u32[]{:S(2)}) collective-permute-start(f32[128,512]{1,0:T(8,128)S(1)} %slice.6), channel_id=1, source_target_pairs={{0,16},{8,24},{16,32},{24,40},{32,48},{40,56},{48,0},{56,8},{64,80... | collective-permute-start | bytes 786440 | tf_op jit(solution)/shard_map/ppermute | solution.py:28
  122.6 22.5 %copy-start.13 = (f32[256,512]{1,0:T(8,128)S(1)}, f32[256,512]{1,0:T(8,128)}, u32[]{:S(2)}) copy-start(f32[256,512]{1,0:T(8,128)} %copy-done.12) | copy-start | bytes 1572868
  122.6 22.5 %copy-start.15 = (f32[256,512]{1,0:T(8,128)S(1)}, f32[256,512]{1,0:T(8,128)}, u32[]{:S(2)}) copy-start(f32[256,512]{1,0:T(8,128)} %copy-done.14) | copy-start | bytes 1572868
  122.6 22.5 %copy-start.19 = (f32[128,512]{1,0:T(8,128)S(1)}, f32[128,512]{1,0:T(8,128)}, u32[]{:S(2)}) copy-start(f32[128,512]{1,0:T(8,128)} %copy-done.18) | copy-start | bytes 786436
  122.6 22.5 %copy-start.21 = (f32[128,512]{1,0:T(8,128)S(1)}, f32[128,512]{1,0:T(8,128)}, u32[]{:S(2)}) copy-start(f32[128,512]{1,0:T(8,128)} %copy-done.20) | copy-start | bytes 786436
  122.6 7.8 %collective-permute-start.22 = (f32[8,16,3,8,128]{4,3,2,1,0:T(8,128)}, f32[8,16,3,8,128]{4,3,2,1,0:T(8,128)S(1)}, u32[]{:S(2)}, u32[]{:S(2)}) collective-permute-start(f32[8,16,3,8,128]{4,3,2,1,0:T(8,128)} %all-to-all-done.2.own_ref), channel_id=1, source_target_pairs={{0,8},{8,0},{16,24},{24,16},{32,40},{40,32},{48,56},{56,48},{64,72... | collective-permute-start | bytes 4718600 | tf_op jit(solution)/shard_map/ppermute | solution.py:28
  146.2 1.4 collective-permute-start.23
  (19 other events, 89.2 us)

commit v11 on v10

--- a/solution.py
+++ b/solution.py
@@ -335,7 +335,7 @@
         in_specs=[SMEM, part, part, pl.BlockSpec((3, n, k), lambda s: (0, 0, 0))],
         out_specs=(whole, whole),
         scratch_shapes=[pltpu.VMEM((k, k), BF16)] * 3,
-        compiler_params=params(20),
+        compiler_params=params(17),
         cost_estimate=cost(36 * n * k * k, 4 * k * k),
         name="iterations",
     )(pos, own, away, q_parts)

time: 152 us -> 152 us (level)
  no operation moved by 1% of the time
where the time goes in v11:
time: 152 us; the launch traced here: 151 us
  starting transfers between devices  58.7 us (39%)
  waiting for transfers between devices  49.5 us (33%)
  Pallas kernels  27.7 us (18%)
  local copies, waits for them, and re-layouts  13.6 us (9%)
    ppermute x24, starting transfers between devices, dp_shift(): return lax.ppermute(x, 'dp', pairs)  44.4 us
    ppermute x24, waiting for transfers between devices, dp_shift(): return lax.ppermute(x, 'dp', pairs)  39.8 us
    all_to_all x3, starting transfers between devices, exchange(): return lax.all_to_all(x, axis, 0, 0, axis_index_groups=groups)  14.2 us
    pallas_call x1, Pallas kernels, iterate(): pl.pallas_call(iterate_kernel, out_shape=(jax.ShapeDtypeStruct((n, k), F3...  13.6 us
    unnamed x48, local copies, waits for them, and re-layouts  11.7 us
    all_to_all x3, waiting for transfers between devices, exchange(): return lax.all_to_all(x, axis, 0, 0, axis_index_groups=groups)  9.66 us
    pallas_call x4, Pallas kernels, merge(): pl.pallas_call(functools.partial(merge_kernel, turns, own), out_shape=out...  4.3 us
    pallas_call x1, Pallas kernels, finish(): pl.pallas_call(finish_kernel, out_shape=(jax.ShapeDtypeStruct((1, d, k),...  3.69 us
  transfers between devices with their start and end apart: 27, of which 19 were waited for; matrix products, arithmetic and copies ran while one was open for 1% of the time, Pallas kernels for 4%

profile of v11, /device:TPU:1, one launch (start us, length us, event | category | flops | bytes accessed | tf_op | source)
XLA Modules:
  0.0 151.3 jit_solution(4368794760230083663)
XLA Ops:
  0.7 1.6 %copy-done = bf16[1,1024,1024]{2,1,0:T(8,128)(2,1)S(1)} copy-done((bf16[1,1024,1024]{2,1,0:T(8,128)(2,1)S(1)}, bf16[1,1024,1024]{2,1,0:T(8,128)(2,1)}, u32[]{:S(2)}) %copy-start) | copy-done | bytes 2097176
  5.7 3.3 %collective-permute-start = (f32[1,512,256]{2,1,0:T(8,128)S(1)}, f32[1,512,256]{2,1,0:T(8,128)S(1)}, u32[]{:S(2)}, u32[]{:S(2)}) collective-permute-start(f32[1,512,256]{2,1,0:T(8,128)S(1)} %merge.4), channel_id=1, source_target_pairs={{0,8},{8,0},{16,24},{24,16},{32,40},{40,32},{48,56},{56,48},{64,72... | collective-permute-start | bytes 1572872 | tf_op jit(solution)/shard_map/ppermute | solution.py:28
  12.0 2.7 %collective-permute-start.6 = (f32[256,256]{1,0:T(8,128)S(1)}, f32[256,256]{1,0:T(8,128)S(1)}, u32[]{:S(2)}, u32[]{:S(2)}) collective-permute-start(f32[256,256]{1,0:T(8,128)S(1)} %get-tuple-element.54), channel_id=1, source_target_pairs={{0,48},{8,56},{16,0},{24,8},{32,16},{40,24},{48,32},{56,40},{64,11... | collective-permute-start | bytes 786440 | tf_op jit(solution)/shard_map/ppermute | solution.py:28
  17.4 3.5 %collective-permute-done.4 = f32[256,256]{1,0:T(8,128)S(1)} collective-permute-done((f32[256,256]{1,0:T(8,128)S(1)}, f32[256,256]{1,0:T(8,128)S(1)}, u32[]{:S(2)}, u32[]{:S(2)}) %collective-permute-start.4) | collective-permute-done | bytes 262176 | tf_op jit(solution)/shard_map/ppermute | solution.py:28
  21.1 2.7 %collective-permute-start.7 = (f32[256,256]{1,0:T(8,128)S(1)}, f32[256,256]{1,0:T(8,128)S(1)}, u32[]{:S(2)}, u32[]{:S(2)}) collective-permute-start(f32[256,256]{1,0:T(8,128)S(1)} %add.45), channel_id=1, source_target_pairs={{0,48},{8,56},{16,0},{24,8},{32,16},{40,24},{48,32},{56,40},{64,11... | collective-permute-start | bytes 786440 | tf_op jit(solution)/shard_map/ppermute | solution.py:28
  23.9 1.7 %collective-permute-done.2 = f32[256,256]{1,0:T(8,128)S(1)} collective-permute-done((f32[256,256]{1,0:T(8,128)S(1)}, f32[256,256]{1,0:T(8,128)S(1)}, u32[]{:S(2)}, u32[]{:S(2)}) %collective-permute-start.2) | collective-permute-done | bytes 262176 | tf_op jit(solution)/shard_map/ppermute | solution.py:28
  26.6 5.6 %collective-permute-done.5.on = f32[256,256]{1,0:T(8,128)S(1)} collective-permute-done((f32[256,256]{1,0:T(8,128)S(1)}, f32[256,256]{1,0:T(8,128)S(1)}, u32[]{:S(2)}, u32[]{:S(2)}) %collective-permute-start.5) | collective-permute-done | bytes 262176 | tf_op jit(solution)/shard_map/ppermute | solution.py:28
  33.0 4.2 %collective-permute-start.10 = (f32[32,512]{1,0:T(8,128)S(1)}, f32[32,512]{1,0:T(8,128)S(1)}, u32[]{:S(2)}, u32[]{:S(2)}) collective-permute-start(f32[32,512]{1,0:T(8,128)S(1)} %get-tuple-element.59), channel_id=1, source_target_pairs={{0,192},{8,200},{16,208},{24,216},{32,224},{40,232},{48,240},{56,2... | collective-permute-start | bytes 196616 | tf_op jit(solution)/shard_map/ppermute | solution.py:28
  37.2 1.3 collective-permute-done.10
  38.6 4.7 %collective-permute-start.11 = (f32[64,512]{1,0:T(8,128)S(1)}, f32[64,512]{1,0:T(8,128)S(1)}, u32[]{:S(2)}, u32[]{:S(2)}) collective-permute-start(f32[64,512]{1,0:T(8,128)S(1)} %pad_add_fusion), channel_id=1, source_target_pairs={{0,192},{8,200},{16,208},{24,216},{32,224},{40,232},{48,240},{56,2... | collective-permute-start | bytes 393224 | tf_op jit(solution)/shard_map/ppermute | solution.py:28
  43.4 3.2 %collective-permute-done.11 = f32[64,512]{1,0:T(8,128)S(1)} collective-permute-done((f32[64,512]{1,0:T(8,128)S(1)}, f32[64,512]{1,0:T(8,128)S(1)}, u32[]{:S(2)}, u32[]{:S(2)}) %collective-permute-start.11) | collective-permute-done | bytes 131104 | tf_op jit(solution)/shard_map/ppermute | solution.py:28
  46.6 3.9 %collective-permute-done.9 = f32[64,512]{1,0:T(8,128)S(1)} collective-permute-done((f32[64,512]{1,0:T(8,128)S(1)}, f32[64,512]{1,0:T(8,128)S(1)}, u32[]{:S(2)}, u32[]{:S(2)}) %collective-permute-start.9) | collective-permute-done | bytes 131104 | tf_op jit(solution)/shard_map/ppermute | solution.py:28
  50.6 3.6 %collective-permute-start.15 = (f32[64,512]{1,0:T(8,128)S(1)}, f32[64,512]{1,0:T(8,128)S(1)}, u32[]{:S(2)}, u32[]{:S(2)}) collective-permute-start(f32[64,512]{1,0:T(8,128)S(1)} %add_add_fusion.unit), channel_id=1, source_target_pairs={{0,192},{8,200},{16,208},{24,216},{32,224},{40,232},{48,240},{56,2... | collective-permute-start | bytes 393224 | tf_op jit(solution)/shard_map/ppermute | solution.py:28
  54.2 3.0 %collective-permute-start.13 = (f32[64,512]{1,0:T(8,128)S(1)}, f32[64,512]{1,0:T(8,128)S(1)}, u32[]{:S(2)}, u32[]{:S(2)}) collective-permute-start(f32[64,512]{1,0:T(8,128)S(1)} %add_add_fusion.unit), channel_id=1, source_target_pairs={{0,32},{8,40},{16,48},{24,56},{32,0},{40,8},{48,16},{56,24},{64,96... | collective-permute-start | bytes 393224 | tf_op jit(solution)/shard_map/ppermute | solution.py:28
  57.2 2.3 %collective-permute-done.13.u2 = f32[64,512]{1,0:T(8,128)S(1)} collective-permute-done((f32[64,512]{1,0:T(8,128)S(1)}, f32[64,512]{1,0:T(8,128)S(1)}, u32[]{:S(2)}, u32[]{:S(2)}) %collective-permute-start.13) | collective-permute-done | bytes 131104 | tf_op jit(solution)/shard_map/ppermute | solution.py:28
  59.6 3.0 %collective-permute-done.12.u1 = f32[64,512]{1,0:T(8,128)S(1)} collective-permute-done((f32[64,512]{1,0:T(8,128)S(1)}, f32[64,512]{1,0:T(8,128)S(1)}, u32[]{:S(2)}, u32[]{:S(2)}) %collective-permute-start.12) | collective-permute-done | bytes 131104 | tf_op jit(solution)/shard_map/ppermute | solution.py:28
  62.5 2.2 %collective-permute-done.16.z2 = f32[64,512]{1,0:T(8,128)S(1)} collective-permute-done((f32[64,512]{1,0:T(8,128)S(1)}, f32[64,512]{1,0:T(8,128)S(1)}, u32[]{:S(2)}, u32[]{:S(2)}) %collective-permute-start.16) | collective-permute-done | bytes 131104 | tf_op jit(solution)/shard_map/ppermute | solution.py:28
  66.1 6.7 %collective-permute-start.17 = (f32[8,3,8,128]{3,2,1,0:T(8,128)S(1)}, f32[8,3,8,128]{3,2,1,0:T(8,128)S(1)}, u32[]{:S(2)}, u32[]{:S(2)}) collective-permute-start(f32[8,3,8,128]{3,2,1,0:T(8,128)S(1)} %get-tuple-element.63), channel_id=1, source_target_pairs={{0,8},{8,0},{16,24},{24,16},{32,40},{40,32},{48,56},{56,48},{64,72... | collective-permute-start | bytes 294920 | tf_op jit(solution)/shard_map/ppermute | solution.py:28
  74.3 3.6 %all-to-all-start = ((f32[8,3,8,128]{3,2,1,0:T(8,128)}), f32[8,3,8,128]{3,2,1,0:T(8,128)S(1)}, u32[]{:S(2)}, u32[]{:S(2)}) async-start(f32[8,3,8,128]{3,2,1,0:T(8,128)} %add.50), calls=%async_computation | async-start | bytes 196608 | tf_op jit(solution)/shard_map/all_to_all | solution.py:47
  77.9 4.7 %collective-permute-start.19 = (f32[256,512]{1,0:T(8,128)S(1)}, f32[256,512]{1,0:T(8,128)S(1)}, u32[]{:S(2)}, u32[]{:S(2)}) collective-permute-start(f32[256,512]{1,0:T(8,128)S(1)} %get-tuple-element.64.m0), channel_id=1, source_target_pairs={{0,48},{8,56},{16,0},{24,8},{32,16},{40,24},{48,32},{56,40},{64,11... | collective-permute-start | bytes 1572872 | tf_op jit(solution)/shard_map/ppermute | solution.py:28
  83.9 6.1 %all-to-all-start.1 = ((f32[16,3,8,128]{3,2,1,0:T(8,128)}), f32[16,3,8,128]{3,2,1,0:T(8,128)S(1)}, u32[]{:S(2)}, u32[]{:S(2)}) async-start(f32[16,3,8,128]{3,2,1,0:T(8,128)} %spread.2), calls=%async_computation.1 | async-start | bytes 393216 | tf_op jit(solution)/shard_map/all_to_all | solution.py:47
  90.0 3.2 %collective-permute-done.19.m3 = f32[256,512]{1,0:T(8,128)S(1)} collective-permute-done((f32[256,512]{1,0:T(8,128)S(1)}, f32[256,512]{1,0:T(8,128)S(1)}, u32[]{:S(2)}, u32[]{:S(2)}) %collective-permute-start.19) | collective-permute-done | bytes 524320 | tf_op jit(solution)/shard_map/ppermute | solution.py:28
  93.2 3.4 %collective-permute-done.18.m1 = f32[256,512]{1,0:T(8,128)S(1)} collective-permute-done((f32[256,512]{1,0:T(8,128)S(1)}, f32[256,512]{1,0:T(8,128)S(1)}, u32[]{:S(2)}, u32[]{:S(2)}) %collective-permute-start.18) | collective-permute-done | bytes 524320 | tf_op jit(solution)/shard_map/ppermute | solution.py:28
  96.6 3.0 %all-to-all-done.1.x_ref = f32[16,3,8,128]{3,2,1,0:T(8,128)S(1)} async-done(((f32[16,3,8,128]{3,2,1,0:T(8,128)}), f32[16,3,8,128]{3,2,1,0:T(8,128)S(1)}, u32[]{:S(2)}, u32[]{:S(2)}) %all-to-all-start.1) | async-done | bytes 196640 | tf_op jit(solution)/shard_map/all_to_all | solution.py:47
  100.9 4.6 %all-to-all-start.2 = ((f32[8,16,3,8,128]{4,3,2,1,0:T(8,128)}), f32[8,16,3,8,128]{4,3,2,1,0:T(8,128)}, u32[]{:S(2)}, u32[]{:S(2)}) async-start(f32[8,16,3,8,128]{4,3,2,1,0:T(8,128)} %copy-done.6), calls=%async_computation.2 | async-start | bytes 3145728 | tf_op jit(solution)/shard_map/all_to_all | solution.py:47
  110.2 2.1 %merge_all.1 = (f32[1024,1024]{1,0:T(8,128)S(1)}, bf16[3,64,1024]{2,1,0:T(8,128)(2,1)S(1)}) custom-call(bf16[512,1024]{1,0:T(8,128)(2,1)S(1)} %copy-done.3, bf16[512,1024]{1,0:T(8,128)(2,1)S(1)} %copy-done.5, bf16[1,1024,1024]{2,1,0:T(8,128)(2,1)S(1)} %copy-done.1, f32[64,1024]{1,0:T(8,128)S(1)} %bitcast.5), custom_call_target="tpu_custom_call" | custom-call | flops 1073741824 | bytes 8388608 | tf_op jit(solution)/shard_map/merge_all/pallas_call | solution.py:120
  112.3 2.0 %copy-done.7 = f32[1024,1024]{1,0:T(8,128)} copy-done((f32[1024,1024]{1,0:T(8,128)}, f32[1024,1024]{1,0:T(8,128)S(1)}, u32[]{:S(2)}) %copy-start.7) | copy-done | bytes 4194328
  116.5 6.0 %all-to-all-done.2.own_ref = f32[8,16,3,8,128]{4,3,2,1,0:T(8,128)} async-done(((f32[8,16,3,8,128]{4,3,2,1,0:T(8,128)}), f32[8,16,3,8,128]{4,3,2,1,0:T(8,128)}, u32[]{:S(2)}, u32[]{:S(2)}) %all-to-all-start.2) | async-done | bytes 1572896 | tf_op jit(solution)/shard_map/all_to_all | solution.py:47
  122.6 4.6 %collective-permute-start.22 = (f32[8,16,3,8,128]{4,3,2,1,0:T(8,128)}, f32[8,16,3,8,128]{4,3,2,1,0:T(8,128)S(1)}, u32[]{:S(2)}, u32[]{:S(2)}) collective-permute-start(f32[8,16,3,8,128]{4,3,2,1,0:T(8,128)} %all-to-all-done.2.own_ref), channel_id=1, source_target_pairs={{0,8},{8,0},{16,24},{24,16},{32,40},{40,32},{48,56},{56,48},{64,72... | collective-permute-start | bytes 4718600 | tf_op jit(solution)/shard_map/ppermute | solution.py:28
  127.2 3.2 %collective-permute-done.22.away_ref = f32[8,16,3,8,128]{4,3,2,1,0:T(8,128)S(1)} collective-permute-done((f32[8,16,3,8,128]{4,3,2,1,0:T(8,128)}, f32[8,16,3,8,128]{4,3,2,1,0:T(8,128)S(1)}, u32[]{:S(2)}, u32[]{:S(2)}) %collective-permute-start.22) | collective-permute-done | bytes 1572896 | tf_op jit(solution)/shard_map/ppermute | solution.py:28
  131.4 13.6 %iterations.1 = (f32[64,1024]{1,0:T(8,128)}, f32[64,1024]{1,0:T(8,128)S(1)}) custom-call(s32[3]{0:T(128)S(1)} %pad_add_fusion.2.pos_ref, f32[8,16,3,8,128]{4,3,2,1,0:T(8,128)} %all-to-all-done.2.own_ref, f32[8,16,3,8,128]{4,3,2,1,0:T(8,128)S(1)} %collective-permute-done.22.away_ref, bf16[3,64,1024]{2,1,0:T(8,128)(2,1)S(1)} %copy-done.23), custom_call_target="tpu_custom_call" | custom-call | flops 2415919104 | bytes 4194304 | tf_op jit(solution)/shard_map/iterations/pallas_call | solution.py:331
  147.6 3.7 %finish.1 = (bf16[1,1024,1024]{2,1,0:T(8,128)(2,1)}, bf16[1024,1024]{1,0:T(8,128)(2,1)}) custom-call(s32[3]{0:T(128)S(1)} %pad_add_fusion.2.pos_ref, f32[1024,1024]{1,0:T(8,128)S(1)} %copy-done.8, bf16[1024,1024]{1,0:T(8,128)(2,1)S(1)} %copy-done.9, f32[64,512]{1,0:T(8,128)S(1)} %left.1.own, f32[64,512]{1,0:T(8,128)S(1)} %collective-permute-done.23.away, ...), custom_call_target="tpu_custom_call" | custom-call | flops 536870912 | bytes 12582912 | tf_op jit(solution)/shard_map/finish/pallas_call | solution.py:398
  (93 shorter events, 27.4 us)
Async XLA Ops:
  5.7 4.9 %collective-permute-start = (f32[1,512,256]{2,1,0:T(8,128)S(1)}, f32[1,512,256]{2,1,0:T(8,128)S(1)}, u32[]{:S(2)}, u32[]{:S(2)}) collective-permute-start(f32[1,512,256]{2,1,0:T(8,128)S(1)} %merge.4), channel_id=1, source_target_pairs={{0,8},{8,0},{16,24},{24,16},{32,40},{40,32},{48,56},{56,48},{64,72... | collective-permute-start | bytes 1572872 | tf_op jit(solution)/shard_map/ppermute | solution.py:28
  10.6 4.1 %collective-permute-start.1 = (f32[3,512,256]{2,1,0:T(8,128)S(1)}, f32[3,512,256]{2,1,0:T(8,128)S(1)}, u32[]{:S(2)}, u32[]{:S(2)}) collective-permute-start(f32[3,512,256]{2,1,0:T(8,128)S(1)} %merge.5), channel_id=1, source_target_pairs={{0,8},{8,0},{16,24},{24,16},{32,40},{40,32},{48,56},{56,48},{64,72... | collective-permute-start | bytes 4718600 | tf_op jit(solution)/shard_map/ppermute | solution.py:28
  11.9 9.1 %collective-permute-start.4 = (f32[256,256]{1,0:T(8,128)S(1)}, f32[256,256]{1,0:T(8,128)S(1)}, u32[]{:S(2)}, u32[]{:S(2)}) collective-permute-start(f32[256,256]{1,0:T(8,128)S(1)} %get-tuple-element.52), channel_id=1, source_target_pairs={{0,16},{8,24},{16,32},{24,40},{32,48},{40,56},{48,0},{56,8},{64,80... | collective-permute-start | bytes 786440 | tf_op jit(solution)/shard_map/ppermute | solution.py:28
  12.0 9.1 %collective-permute-start.6 = (f32[256,256]{1,0:T(8,128)S(1)}, f32[256,256]{1,0:T(8,128)S(1)}, u32[]{:S(2)}, u32[]{:S(2)}) collective-permute-start(f32[256,256]{1,0:T(8,128)S(1)} %get-tuple-element.54), channel_id=1, source_target_pairs={{0,48},{8,56},{16,0},{24,8},{32,16},{40,24},{48,32},{56,40},{64,11... | collective-permute-start | bytes 786440 | tf_op jit(solution)/shard_map/ppermute | solution.py:28
  15.9 9.6 %collective-permute-start.2 = (f32[256,256]{1,0:T(8,128)S(1)}, f32[256,256]{1,0:T(8,128)S(1)}, u32[]{:S(2)}, u32[]{:S(2)}) collective-permute-start(f32[256,256]{1,0:T(8,128)S(1)} %get-tuple-element.47), channel_id=1, source_target_pairs={{0,48},{8,56},{16,0},{24,8},{32,16},{40,24},{48,32},{56,40},{64,11... | collective-permute-start | bytes 786440 | tf_op jit(solution)/shard_map/ppermute | solution.py:28
  16.3 10.3 %collective-permute-start.3 = (f32[256,256]{1,0:T(8,128)S(1)}, f32[256,256]{1,0:T(8,128)S(1)}, u32[]{:S(2)}, u32[]{:S(2)}) collective-permute-start(f32[256,256]{1,0:T(8,128)S(1)} %get-tuple-element.49), channel_id=1, source_target_pairs={{0,16},{8,24},{16,32},{24,40},{32,48},{40,56},{48,0},{56,8},{64,80... | collective-permute-start | bytes 786440 | tf_op jit(solution)/shard_map/ppermute | solution.py:28
  21.0 11.2 %collective-permute-start.5 = (f32[256,256]{1,0:T(8,128)S(1)}, f32[256,256]{1,0:T(8,128)S(1)}, u32[]{:S(2)}, u32[]{:S(2)}) collective-permute-start(f32[256,256]{1,0:T(8,128)S(1)} %add.44), channel_id=1, source_target_pairs={{0,16},{8,24},{16,32},{24,40},{32,48},{40,56},{48,0},{56,8},{64,80... | collective-permute-start | bytes 786440 | tf_op jit(solution)/shard_map/ppermute | solution.py:28
  21.1 11.1 %collective-permute-start.7 = (f32[256,256]{1,0:T(8,128)S(1)}, f32[256,256]{1,0:T(8,128)S(1)}, u32[]{:S(2)}, u32[]{:S(2)}) collective-permute-start(f32[256,256]{1,0:T(8,128)S(1)} %add.45), channel_id=1, source_target_pairs={{0,48},{8,56},{16,0},{24,8},{32,16},{40,24},{48,32},{56,40},{64,11... | collective-permute-start | bytes 786440 | tf_op jit(solution)/shard_map/ppermute | solution.py:28
  33.0 5.6 %collective-permute-start.10 = (f32[32,512]{1,0:T(8,128)S(1)}, f32[32,512]{1,0:T(8,128)S(1)}, u32[]{:S(2)}, u32[]{:S(2)}) collective-permute-start(f32[32,512]{1,0:T(8,128)S(1)} %get-tuple-element.59), channel_id=1, source_target_pairs={{0,192},{8,200},{16,208},{24,216},{32,224},{40,232},{48,240},{56,2... | collective-permute-start | bytes 196616 | tf_op jit(solution)/shard_map/ppermute | solution.py:28
  37.2 6.0 %collective-permute-start.8 = (f32[32,512]{1,0:T(8,128)S(1)}, f32[32,512]{1,0:T(8,128)S(1)}, u32[]{:S(2)}, u32[]{:S(2)}) collective-permute-start(f32[32,512]{1,0:T(8,128)S(1)} %get-tuple-element.57), channel_id=1, source_target_pairs={{0,64},{8,72},{16,80},{24,88},{32,96},{40,104},{48,112},{56,120},{... | collective-permute-start | bytes 196616 | tf_op jit(solution)/shard_map/ppermute | solution.py:28
  38.6 8.0 %collective-permute-start.11 = (f32[64,512]{1,0:T(8,128)S(1)}, f32[64,512]{1,0:T(8,128)S(1)}, u32[]{:S(2)}, u32[]{:S(2)}) collective-permute-start(f32[64,512]{1,0:T(8,128)S(1)} %pad_add_fusion), channel_id=1, source_target_pairs={{0,192},{8,200},{16,208},{24,216},{32,224},{40,232},{48,240},{56,2... | collective-permute-start | bytes 393224 | tf_op jit(solution)/shard_map/ppermute | solution.py:28
  43.3 7.2 %collective-permute-start.9 = (f32[64,512]{1,0:T(8,128)S(1)}, f32[64,512]{1,0:T(8,128)S(1)}, u32[]{:S(2)}, u32[]{:S(2)}) collective-permute-start(f32[64,512]{1,0:T(8,128)S(1)} %pad_add_fusion.1), channel_id=1, source_target_pairs={{0,64},{8,72},{16,80},{24,88},{32,96},{40,104},{48,112},{56,120},{... | collective-permute-start | bytes 393224 | tf_op jit(solution)/shard_map/ppermute | solution.py:28
  50.5 6.7 %collective-permute-start.14 = (f32[64,512]{1,0:T(8,128)S(1)}, f32[64,512]{1,0:T(8,128)S(1)}, u32[]{:S(2)}, u32[]{:S(2)}) collective-permute-start(f32[64,512]{1,0:T(8,128)S(1)} %add_add_fusion.unit), channel_id=1, source_target_pairs={{0,64},{8,72},{16,80},{24,88},{32,96},{40,104},{48,112},{56,120},{... | collective-permute-start | bytes 393224 | tf_op jit(solution)/shard_map/ppermute | solution.py:28
  50.6 6.6 %collective-permute-start.15 = (f32[64,512]{1,0:T(8,128)S(1)}, f32[64,512]{1,0:T(8,128)S(1)}, u32[]{:S(2)}, u32[]{:S(2)}) collective-permute-start(f32[64,512]{1,0:T(8,128)S(1)} %add_add_fusion.unit), channel_id=1, source_target_pairs={{0,192},{8,200},{16,208},{24,216},{32,224},{40,232},{48,240},{56,2... | collective-permute-start | bytes 393224 | tf_op jit(solution)/shard_map/ppermute | solution.py:28
  54.2 5.4 %collective-permute-start.13 = (f32[64,512]{1,0:T(8,128)S(1)}, f32[64,512]{1,0:T(8,128)S(1)}, u32[]{:S(2)}, u32[]{:S(2)}) collective-permute-start(f32[64,512]{1,0:T(8,128)S(1)} %add_add_fusion.unit), channel_id=1, source_target_pairs={{0,32},{8,40},{16,48},{24,56},{32,0},{40,8},{48,16},{56,24},{64,96... | collective-permute-start | bytes 393224 | tf_op jit(solution)/shard_map/ppermute | solution.py:28
  57.2 5.3 %collective-permute-start.12 = (f32[64,512]{1,0:T(8,128)S(1)}, f32[64,512]{1,0:T(8,128)S(1)}, u32[]{:S(2)}, u32[]{:S(2)}) collective-permute-start(f32[64,512]{1,0:T(8,128)S(1)} %add_add_fusion.unit), channel_id=1, source_target_pairs={{0,16},{8,24},{16,32},{24,40},{32,48},{40,56},{48,0},{56,8},{64,80... | collective-permute-start | bytes 393224 | tf_op jit(solution)/shard_map/ppermute | solution.py:28
  57.2 7.5 %collective-permute-start.16 = (f32[64,512]{1,0:T(8,128)S(1)}, f32[64,512]{1,0:T(8,128)S(1)}, u32[]{:S(2)}, u32[]{:S(2)}) collective-permute-start(f32[64,512]{1,0:T(8,128)S(1)} %collective-permute-done.14.z1), channel_id=1, source_target_pairs={{0,64},{8,72},{16,80},{24,88},{32,96},{40,104},{48,112},{56,120},{... | collective-permute-start | bytes 393224 | tf_op jit(solution)/shard_map/ppermute | solution.py:28
  66.0 33.6 %copy-start.14 = (f32[256,512]{1,0:T(8,128)}, f32[256,512]{1,0:T(8,128)S(1)}, u32[]{:S(2)}) copy-start(f32[256,512]{1,0:T(8,128)S(1)} %get-tuple-element.64.m0) | copy-start | bytes 1572868
  66.1 7.6 %collective-permute-start.17 = (f32[8,3,8,128]{3,2,1,0:T(8,128)S(1)}, f32[8,3,8,128]{3,2,1,0:T(8,128)S(1)}, u32[]{:S(2)}, u32[]{:S(2)}) collective-permute-start(f32[8,3,8,128]{3,2,1,0:T(8,128)S(1)} %get-tuple-element.63), channel_id=1, source_target_pairs={{0,8},{8,0},{16,24},{24,16},{32,40},{40,32},{48,56},{56,48},{64,72... | collective-permute-start | bytes 294920 | tf_op jit(solution)/shard_map/ppermute | solution.py:28
  74.3 8.9 %all-to-all-start = ((f32[8,3,8,128]{3,2,1,0:T(8,128)}), f32[8,3,8,128]{3,2,1,0:T(8,128)S(1)}, u32[]{:S(2)}, u32[]{:S(2)}) async-start(f32[8,3,8,128]{3,2,1,0:T(8,128)} %add.50), calls=%async_computation | async-start | bytes 196608 | tf_op jit(solution)/shard_map/all_to_all | solution.py:47
  77.9 15.3 %collective-permute-start.19 = (f32[256,512]{1,0:T(8,128)S(1)}, f32[256,512]{1,0:T(8,128)S(1)}, u32[]{:S(2)}, u32[]{:S(2)}) collective-permute-start(f32[256,512]{1,0:T(8,128)S(1)} %get-tuple-element.64.m0), channel_id=1, source_target_pairs={{0,48},{8,56},{16,0},{24,8},{32,16},{40,24},{48,32},{56,40},{64,11... | collective-permute-start | bytes 1572872 | tf_op jit(solution)/shard_map/ppermute | solution.py:28
  82.6 14.0 %collective-permute-start.18 = (f32[256,512]{1,0:T(8,128)S(1)}, f32[256,512]{1,0:T(8,128)S(1)}, u32[]{:S(2)}, u32[]{:S(2)}) collective-permute-start(f32[256,512]{1,0:T(8,128)S(1)} %get-tuple-element.64.m0), channel_id=1, source_target_pairs={{0,16},{8,24},{16,32},{24,40},{32,48},{40,56},{48,0},{56,8},{64,80... | collective-permute-start | bytes 1572872 | tf_op jit(solution)/shard_map/ppermute | solution.py:28
  83.9 15.7 %all-to-all-start.1 = ((f32[16,3,8,128]{3,2,1,0:T(8,128)}), f32[16,3,8,128]{3,2,1,0:T(8,128)S(1)}, u32[]{:S(2)}, u32[]{:S(2)}) async-start(f32[16,3,8,128]{3,2,1,0:T(8,128)} %spread.2), calls=%async_computation.1 | async-start | bytes 393216 | tf_op jit(solution)/shard_map/all_to_all | solution.py:47
  100.9 21.7 %all-to-all-start.2 = ((f32[8,16,3,8,128]{4,3,2,1,0:T(8,128)}), f32[8,16,3,8,128]{4,3,2,1,0:T(8,128)}, u32[]{:S(2)}, u32[]{:S(2)}) async-start(f32[8,16,3,8,128]{4,3,2,1,0:T(8,128)} %copy-done.6), calls=%async_computation.2 | async-start | bytes 3145728 | tf_op jit(solution)/shard_map/all_to_all | solution.py:47
  107.4 7.7 %collective-permute-start.21 = (f32[128,512]{1,0:T(8,128)S(1)}, f32[128,512]{1,0:T(8,128)S(1)}, u32[]{:S(2)}, u32[]{:S(2)}) collective-permute-start(f32[128,512]{1,0:T(8,128)S(1)} %slice.7), channel_id=1, source_target_pairs={{0,48},{8,56},{16,0},{24,8},{32,16},{40,24},{48,32},{56,40},{64,11... | collective-permute-start | bytes 786440 | tf_op jit(solution)/shard_map/ppermute | solution.py:28
  108.3 7.5 %collective-permute-start.20 = (f32[128,512]{1,0:T(8,128)S(1)}, f32[128,512]{1,0:T(8,128)S(1)}, u32[]{:S(2)}, u32[]{:S(2)}) collective-permute-start(f32[128,512]{1,0:T(8,128)S(1)} %slice.6), channel_id=1, source_target_pairs={{0,16},{8,24},{16,32},{24,40},{32,48},{40,56},{48,0},{56,8},{64,80... | collective-permute-start | bytes 786440 | tf_op jit(solution)/shard_map/ppermute | solution.py:28
  122.6 22.5 %copy-start.13 = (f32[256,512]{1,0:T(8,128)S(1)}, f32[256,512]{1,0:T(8,128)}, u32[]{:S(2)}) copy-start(f32[256,512]{1,0:T(8,128)} %copy-done.12) | copy-start | bytes 1572868
  122.6 22.5 %copy-start.15 = (f32[256,512]{1,0:T(8,128)S(1)}, f32[256,512]{1,0:T(8,128)}, u32[]{:S(2)}) copy-start(f32[256,512]{1,0:T(8,128)} %copy-done.14) | copy-start | bytes 1572868
  122.6 22.5 %copy-start.19 = (f32[128,512]{1,0:T(8,128)S(1)}, f32[128,512]{1,0:T(8,128)}, u32[]{:S(2)}) copy-start(f32[128,512]{1,0:T(8,128)} %copy-done.18) | copy-start | bytes 786436
  122.6 22.5 %copy-start.21 = (f32[128,512]{1,0:T(8,128)S(1)}, f32[128,512]{1,0:T(8,128)}, u32[]{:S(2)}) copy-start(f32[128,512]{1,0:T(8,128)} %copy-done.20) | copy-start | bytes 786436
  122.6 7.8 %collective-permute-start.22 = (f32[8,16,3,8,128]{4,3,2,1,0:T(8,128)}, f32[8,16,3,8,128]{4,3,2,1,0:T(8,128)S(1)}, u32[]{:S(2)}, u32[]{:S(2)}) collective-permute-start(f32[8,16,3,8,128]{4,3,2,1,0:T(8,128)} %all-to-all-done.2.own_ref), channel_id=1, source_target_pairs={{0,8},{8,0},{16,24},{24,16},{32,40},{40,32},{48,56},{56,48},{64,72... | collective-permute-start | bytes 4718600 | tf_op jit(solution)/shard_map/ppermute | solution.py:28
  146.2 1.4 collective-permute-start.23
  (19 other events, 89.2 us)
